TPU v7x, 32 devices: a whole 2x2x4 slice. The times are simulated.
32 devices in a mesh: tile: 8 (over y, x, core), section: 4 (over z).
Axes of the slice: x: 2, y: 2, z: 4, core: 2. Of those that a mesh axis runs over, the one named last changes fastest.
Arguments:
- state: float32 [5, 2, 192, 1536], P(None, None, 'tile', 'section'), may hold values from -6 to 6
- courant: float32 [2, 2, 192, 1536], P(None, None, 'tile', 'section'), may hold values from -0.4 to 0.4
- nest_offset: int32 [1], replicated, may hold values from 24 to 95
Outputs:
- new_state: float32 [5, 2, 192, 1536], P(None, None, 'tile', 'section')
All inputs are finite; a program needn't handle non-finite values.
Results may differ from a plain program's by a relative error of at most 0.000053.
Values sent between devices are 32-bit elements; how exact they have to be, the bound alone decides.
No kernel may reach another device: no remote copies, remote signals or barrier semaphores. Data moves between devices by JAX's collectives and lax.ppermute only.
A program may use at most 64 MiB of HBM per device.

v0:
```python
import jax
import jax.numpy as jnp
from jax import lax
from jax.sharding import PartitionSpec as P

RATIO = 3
ZONE = 5


diffusion = 0.02
mixing = 0.05


def shifted(value, axis, steps):
    count = lax.axis_size(axis)
    leading, last = (max(0, -steps), min(count, count - steps))
    return lax.ppermute(value, axis, [(source, source + steps) for source in range(leading, last)])


def with_halo(block, sides, width):
    for axis, dim in sides:
        count = lax.axis_size(axis)
        forward = [(i, i + 1) for i in range(count - 1)]
        backward = [(target, source) for source, target in forward]
        low = lax.ppermute(
            lax.slice_in_dim(block, block.shape[dim] - width, None, axis=dim), axis, forward
        )
        high = lax.ppermute(lax.slice_in_dim(block, 0, width, axis=dim), axis, backward)
        block = jnp.concatenate([low, block, high], axis=dim)
    return block


def advance(values, courant, padded, low_row, high_row, low_col, high_col):
    row_count = values.shape[2]
    col_count = values.shape[3]
    row_index = lax.broadcasted_iota(jnp.int32, (1, 1, row_count, col_count), 2)
    column_index = lax.broadcasted_iota(jnp.int32, (1, 1, row_count, col_count), 3)
    south_side = jnp.where(low_row & (row_index == 0), values, padded[:, :, :-2, 1:-1])
    north_side = jnp.where(high_row & (row_index == row_count - 1), values, padded[:, :, 2:, 1:-1])
    west_side = jnp.where(low_col & (column_index == 0), values, padded[:, :, 1:-1, :-2])
    east_side = jnp.where(
        high_col & (column_index == col_count - 1), values, padded[:, :, 1:-1, 2:]
    )
    stacked = jnp.pad(values, ((0, 0), (1, 1), (0, 0), (0, 0)), mode="edge")
    level_below = stacked[:, :-2]
    level_above = stacked[:, 2:]
    speed_y = courant[0]
    speed_x = courant[1]
    transport = (
        jnp.maximum(speed_y, 0.0) * (values - south_side)
        + jnp.minimum(speed_y, 0.0) * (north_side - values)
        + jnp.maximum(speed_x, 0.0) * (values - west_side)
        + jnp.minimum(speed_x, 0.0) * (east_side - values)
    )
    spread = south_side + north_side + west_side + east_side - 4.0 * values
    column = level_below + level_above - 2.0 * values
    return values - transport + diffusion * spread + mixing * column


def send_rims(values, distance):
    return shifted(values, "section", distance)


def on_device(state, courant, nest_offset):
    fields, levels, row_count, col_count = state.shape
    tile_count = lax.axis_size("tile")
    section_count = lax.axis_size("section")
    parent_count = section_count // 4
    tile_index = lax.axis_index("tile")
    section = lax.axis_index("section")
    offset = nest_offset[0]
    total_rows = row_count * tile_count
    nest_height = total_rows // RATIO
    third_width = col_count // RATIO
    coarse_rows = row_count // RATIO
    parent_width = parent_count * col_count
    nest_width = section_count * col_count - parent_width
    is_parent = section < parent_count
    low_row = tile_index == 0
    high_row = tile_index == tile_count - 1
    low_col = (section == 0) | (section == parent_count)
    high_col = (section == parent_count - 1) | (section == section_count - 1)

    def step(values):
        padded = with_halo(values, (("tile", 2), ("section", 3)), 1)
        return advance(values, courant, padded, low_row, high_row, low_col, high_col)

    stepped = step(state)
    local_rows = tile_index * row_count + jnp.arange(row_count, dtype=jnp.int32)
    rim_coarse = jnp.array([0, 1, nest_height - 2, nest_height - 1], dtype=jnp.int32)
    wanted = offset + rim_coarse
    pick_rows = (wanted[:, None] == local_rows[None, :]).astype(jnp.float32)
    parent_flag = is_parent.astype(jnp.float32)
    both_states = jnp.stack([state, stepped]) * parent_flag
    rim_part = jnp.einsum(
        "jr,tflrc->tfljc", pick_rows, both_states, precision=lax.Precision.HIGHEST
    )
    edge_cols = jnp.array([0, 1, parent_width - 2, parent_width - 1], dtype=jnp.int32)
    global_cols = section * col_count + jnp.arange(col_count, dtype=jnp.int32)
    pick_edge = (global_cols[:, None] == edge_cols[None, :]).astype(jnp.float32)
    edge_local = jnp.einsum(
        "tflrc,ck->tflrk", both_states, pick_edge, precision=lax.Precision.HIGHEST
    )
    span_rows = offset + jnp.arange(nest_height, dtype=jnp.int32)
    pick_span = (span_rows[:, None] == local_rows[None, :]).astype(jnp.float32)
    edge_part = jnp.einsum(
        "nr,tflrk->tflnk", pick_span, edge_local, precision=lax.Precision.HIGHEST
    )
    packed = jnp.concatenate(
        [
            rim_part.reshape(2 * fields * levels, 4 * col_count),
            edge_part.reshape(2 * fields * levels, nest_height * 4),
        ],
        axis=1,
    )
    summed = lax.psum(packed, "tile")
    nest_index = jnp.maximum(section - parent_count, 0)
    source_parent = nest_index // RATIO
    received = jnp.zeros_like(summed)
    for distance in range(parent_count, 3 * parent_count + 1):
        arrived = send_rims(summed, distance)
        hit = jnp.logical_not(is_parent) & (section - distance == source_parent)
        received = jnp.where(hit, arrived, received)
    rim_rows = received[:, : 4 * col_count].reshape(2, fields, levels, 4, col_count)
    edges = received[:, 4 * col_count :].reshape(2, fields, levels, nest_height, 4)
    rim_strip = lax.dynamic_slice_in_dim(rim_rows, nest_index % RATIO * third_width, third_width, 4)
    rim_strip = jnp.repeat(rim_strip, RATIO, axis=4)
    row_choice = ((local_rows // RATIO)[:, None] == rim_coarse[None, :]).astype(jnp.float32)
    forcing_rows = jnp.einsum(
        "rj,tfljc->tflrc", row_choice, rim_strip, precision=lax.Precision.HIGHEST
    )
    nest_cols = nest_index * col_count + jnp.arange(col_count, dtype=jnp.int32)
    col_choice = (edge_cols[:, None] == (nest_cols // RATIO)[None, :]).astype(jnp.float32)
    coarse_choice = (
        (local_rows // RATIO)[:, None] == jnp.arange(nest_height, dtype=jnp.int32)[None, :]
    ).astype(jnp.float32)
    edge_rows = jnp.einsum("rn,tflnk->tflrk", coarse_choice, edges, precision=lax.Precision.HIGHEST)
    forcing_cols = jnp.einsum(
        "tflrk,kc->tflrc", edge_rows, col_choice, precision=lax.Precision.HIGHEST
    )
    row_depth = jnp.minimum(local_rows, total_rows - 1 - local_rows)
    col_depth = jnp.minimum(nest_cols, nest_width - 1 - nest_cols)
    row_zone = (row_depth < ZONE)[:, None]
    forcing = jnp.where(row_zone, forcing_rows, forcing_cols)
    depth = jnp.minimum(row_depth[:, None], col_depth[None, :])
    weight = jnp.maximum(ZONE - depth, 0).astype(jnp.float32) / ZONE

    def relax(values, substep):
        fraction = (substep + 1) / RATIO
        target = forcing[0] + fraction * (forcing[1] - forcing[0])
        return values + weight * (target - values)

    nest_field = relax(stepped, 0)
    for substep in range(1, RATIO):
        nest_field = relax(step(nest_field), substep)
    block_means = nest_field.reshape(fields, levels, coarse_rows, RATIO, third_width, RATIO).sum(
        axis=(3, 5)
    ) / (RATIO * RATIO)
    wanted_nest = local_rows - offset
    portion = lax.all_gather(block_means, "tile", axis=2, tiled=True)
    row_span = portion.shape[2]
    select = (wanted_nest[:, None] == jnp.arange(row_span, dtype=jnp.int32)[None, :]).astype(
        jnp.float32
    )
    gathered = jnp.einsum("rs,flsc->flrc", select, portion, precision=lax.Precision.HIGHEST)
    target_slot = jnp.where(is_parent, -1, (section - parent_count) // RATIO)
    slot_index = jnp.arange(section_count, dtype=jnp.int32)
    outbound = jnp.where(
        (slot_index == target_slot)[None, None, None, :, None], gathered[:, :, :, None, :], 0.0
    )
    outbound = outbound.reshape(fields, levels, row_count, section_count * third_width)
    received_means = lax.all_to_all(outbound, "section", split_axis=3, concat_axis=3, tiled=True)
    start_col = (parent_count + RATIO * jnp.minimum(section, parent_count - 1)) * third_width
    feedback = lax.dynamic_slice_in_dim(received_means, start_col, col_count, 3)
    covered = ((wanted_nest >= 0) & (wanted_nest < nest_height))[:, None]
    parent_final = jnp.where(covered, feedback, stepped)
    return jnp.where(is_parent, parent_final, nest_field)


def solution(mesh):
    return jax.shard_map(
        on_device,
        mesh=mesh,
        in_specs=(P(None, None, "tile", "section"), P(None, None, "tile", "section"), P()),
        out_specs=P(None, None, "tile", "section"),
        check_vma=False,
    )
```

profile of v0, /device:TPU:0, one launch (start us, length us, event | category | flops | bytes accessed | tf_op | source)
XLA Modules:
  0.0 242.3 jit_solution(9191601514366137836)
XLA Ops:
  16.2 4.1 %collective-permute-start.2 = (f32[5,2,26,1]{3,2,1,0:T(8,128)S(1)}, f32[5,2,26,1]{3,2,1,0:T(8,128)S(1)}, u32[]{:S(2)}, u32[]{:S(2)}) collective-permute-start(f32[5,2,26,1]{3,2,1,0:T(8,128)S(1)} %get-tuple-element.11), channel_id=1, source_target_pairs={{0,1},{1,2},{2,3},{4,5},{5,6},{6,7},{8,9},{9,10},{10,11},{12,13},{... | collective-permute-start | bytes 3128 | tf_op jit(solution)/shard_map/ppermute | solution.py:25
  23.4 4.7 %collective-permute-done.3 = f32[5,2,26,1]{3,2,1,0:T(8,128)S(1)} collective-permute-done((f32[5,2,26,1]{3,2,1,0:T(8,128)S(1)}, f32[5,2,26,1]{3,2,1,0:T(8,128)S(1)}, u32[]{:S(2)}, u32[]{:S(2)}) %collective-permute-start.3) | collective-permute-done | bytes 1072 | tf_op jit(solution)/shard_map/ppermute | solution.py:28
  28.1 2.6 %fusion.113 = f32[1,5,2,24,384]{4,3,2,1,0:T(8,128)S(1)} fusion(f32[5,2,24,384]{3,2,1,0:T(8,128)} %param.5, f32[5,1,24,384]{3,2,1,0:T(8,128)S(1)} %get-tuple-element.24, f32[5,1,24,384]{3,2,1,0:T(8,128)S(1)} %get-tuple-element.23, f32[5,2,26,1]{3,2,1,0:T(8,128)S(1)} %collective-permute-done.3, f32[5,2,1,384]{3,2,1,0:T(1,128)S(1)} %collective-permute-done.1, ...), kind=kLoop, calls=%fused_computation.191 | loop fusion | flops 3502080 | bytes 1434448 | tf_op jit(solution)/shard_map/stack | solution.py:94
  34.1 54.2 %all-reduce.2.cloned.1.call-done = f32[20,1792]{1,0:T(8,128)} async-done(((f32[20,1792]{1,0:T(8,128)}), f32[20,1792]{1,0:T(8,128)}) %all-reduce.2.cloned.1.call-update) | async-done | bytes 143376 | tf_op jit(solution)/shard_map/psum | solution.py:116
  88.4 5.2 %collective-permute-start.4 = (f32[20,1792]{1,0:T(8,128)}, f32[20,1792]{1,0:T(8,128)S(1)}, u32[]{:S(2)}, u32[]{:S(2)}) collective-permute-start(f32[20,1792]{1,0:T(8,128)} %all-reduce.2.cloned.1.call-done), channel_id=1, source_target_pairs={{0,3},{4,7},{8,11},{12,15},{16,19},{20,23},{24,27},{28,31}} | collective-permute-start | bytes 430088 | tf_op jit(solution)/shard_map/ppermute | solution.py:17
  98.7 3.7 %collective-permute-done.5 = f32[20,1792]{1,0:T(8,128)S(1)} collective-permute-done((f32[20,1792]{1,0:T(8,128)}, f32[20,1792]{1,0:T(8,128)S(1)}, u32[]{:S(2)}, u32[]{:S(2)}) %collective-permute-start.5) | collective-permute-done | bytes 143392 | tf_op jit(solution)/shard_map/ppermute | solution.py:17
  102.4 3.2 %collective-permute-done.6 = f32[20,1792]{1,0:T(8,128)S(1)} collective-permute-done((f32[20,1792]{1,0:T(8,128)}, f32[20,1792]{1,0:T(8,128)S(1)}, u32[]{:S(2)}, u32[]{:S(2)}) %collective-permute-start.6) | collective-permute-done | bytes 143392 | tf_op jit(solution)/shard_map/ppermute | solution.py:17
  105.7 3.1 %broadcast_in_dim.140 = f32[2,5,2,4,128,3]{5,4,3,2,1,0:T(8,128)} broadcast(f32[2,5,2,4,128]{4,3,2,1,0:T(4,128)S(1)} %constant_dynamic-slice_fusion.1), dimensions={0,1,2,3,4} | broadcast | bytes 163840 | tf_op jit(solution)/shard_map/broadcast_in_dim | solution.py:127
  108.8 4.4 %reshape.122 = f32[2,5,2,4,384]{4,3,2,1,0:T(4,128)S(1)} reshape(f32[2,5,2,4,128,3]{5,4,3,2,1,0:T(8,128)} %broadcast_in_dim.140) | data formatting | bytes 245760 | tf_op jit(solution)/shard_map/reshape | solution.py:127
  123.2 7.6 %collective-permute-start.9 = (f32[5,2,26,1]{3,2,1,0:T(8,128)S(1)}, f32[5,2,26,1]{3,2,1,0:T(8,128)S(1)}, u32[]{:S(2)}, u32[]{:S(2)}) collective-permute-start(f32[5,2,26,1]{3,2,1,0:T(8,128)S(1)} %get-tuple-element.9), channel_id=1, source_target_pairs={{0,1},{1,2},{2,3},{4,5},{5,6},{6,7},{8,9},{9,10},{10,11},{12,13},{... | collective-permute-start | bytes 3128 | tf_op jit(solution)/shard_map/ppermute | solution.py:25
  134.5 3.6 %collective-permute-start.11 = (f32[5,2,1,384]{3,2,1,0:T(1,128)S(1)}, f32[5,2,1,384]{3,2,1,0:T(1,128)S(1)}, u32[]{:S(2)}, u32[]{:S(2)}) collective-permute-start(f32[5,2,1,384]{3,2,1,0:T(1,128)S(1)} %get-tuple-element.13), channel_id=1, source_target_pairs={{0,4},{4,8},{8,12},{12,16},{16,20},{20,24},{24,28},{1,5},{5,9},{9,... | collective-permute-start | bytes 46088 | tf_op jit(solution)/shard_map/ppermute | solution.py:25
  141.7 4.4 %collective-permute-start.13 = (f32[5,2,26,1]{3,2,1,0:T(8,128)S(1)}, f32[5,2,26,1]{3,2,1,0:T(8,128)S(1)}, u32[]{:S(2)}, u32[]{:S(2)}) collective-permute-start(f32[5,2,26,1]{3,2,1,0:T(8,128)S(1)} %get-tuple-element.7), channel_id=1, source_target_pairs={{0,1},{1,2},{2,3},{4,5},{5,6},{6,7},{8,9},{9,10},{10,11},{12,13},{... | collective-permute-start | bytes 3128 | tf_op jit(solution)/shard_map/ppermute | solution.py:25
  149.1 4.8 %collective-permute-done.14 = f32[5,2,26,1]{3,2,1,0:T(8,128)S(1)} collective-permute-done((f32[5,2,26,1]{3,2,1,0:T(8,128)S(1)}, f32[5,2,26,1]{3,2,1,0:T(8,128)S(1)}, u32[]{:S(2)}, u32[]{:S(2)}) %collective-permute-start.14) | collective-permute-done | bytes 1072 | tf_op jit(solution)/shard_map/ppermute | solution.py:28
  154.6 16.7 %reshape.124 = f32[5,2,8,3,128,3]{5,4,3,2,1,0:T(8,128)} reshape(f32[5,2,24,384]{3,2,1,0:T(8,128)S(1)} %multiply_add_fusion) | data formatting | bytes 737280 | tf_op jit(solution)/shard_map/reshape | solution.py:156
  171.3 6.9 %reduce_sum.9 = f32[5,2,8,128]{3,2,1,0:T(8,128)S(1)} reduce(f32[5,2,8,3,128,3]{5,4,3,2,1,0:T(8,128)} %reshape.124, f32[]{:T(128)} %constant.41.clone.1), dimensions={3,5}, to_apply=%region_1.2 | reduce | flops 81920 | bytes 409604 | tf_op jit(solution)/shard_map/reduce_sum | solution.py:156
  178.2 13.0 %all_gather.3 = f32[5,2,64,128]{3,2,1,0:T(8,128)S(1)} all-gather(f32[5,2,8,128]{3,2,1,0:T(8,128)S(1)} %broadcast_multiply_fusion), channel_id=1, replica_groups=mesh['tile'=8,'section'=4] {'tile'}, dimensions={2}, use_global_device_ids=true | all-gather | bytes 368640 | tf_op jit(solution)/shard_map/all_gather | solution.py:160
  192.6 3.0 %bitcast_select_fusion = f32[5,2,24,512]{2,1,0,3:T(2,128)S(1)} fusion(pred[512]{0:T(512)(128)(4,1)} %broadcast_bitcast_fusion, f32[5,2,24,128]{2,1,0,3:T(2,128)} %copy.10), kind=kLoop, calls=%fused_computation | loop fusion | flops 122880 | bytes 614912 | tf_op jit(solution)/shard_map/jit(_where)/select_n | solution.py:168
  195.5 5.3 %reshape.132 = f32[4,1,30720]{2,1,0:T(1,128)} reshape(f32[512,5,2,24]{3,2,1,0:T(2,128)S(1)} %bitcast.107) | data formatting | bytes 983040
  200.8 4.5 %all-to-all-start = ((f32[4,1,30720]{2,1,0:T(1,128)}), f32[4,1,30720]{2,1,0:T(1,128)S(1)}, u32[]{:S(2)}, u32[]{:S(2)}) async-start(f32[4,1,30720]{2,1,0:T(1,128)} %reshape.132), calls=%async_computation | async-start | bytes 983040 | tf_op jit(solution)/shard_map/all_to_all | solution.py:172
  205.3 14.3 %all-to-all-done = f32[4,1,30720]{2,1,0:T(1,128)S(1)} async-done(((f32[4,1,30720]{2,1,0:T(1,128)}), f32[4,1,30720]{2,1,0:T(1,128)S(1)}, u32[]{:S(2)}, u32[]{:S(2)}) %all-to-all-start) | async-done | bytes 491552 | tf_op jit(solution)/shard_map/all_to_all | solution.py:172
  220.1 2.8 %reduce = f32[4,30720]{1,0:T(4,128)} reduce(f32[4,1,30720]{2,1,0:T(1,128)S(1)} %all-to-all-done, f32[]{:T(128)} %broadcast.290), dimensions={1}, to_apply=%all_to_all.3.reduce_sub_computation | reduce | bytes 983044 | tf_op jit(solution)/shard_map/all_to_all | solution.py:172
  223.0 5.2 %reshape.133 = f32[512,5,2,24]{3,2,1,0:T(2,128)S(1)} reshape(f32[4,30720]{1,0:T(4,128)} %reduce) | data formatting | bytes 983040
  230.2 2.6 %copy.20 = f32[5,2,24,384]{3,2,1,0:T(8,128)S(1)} copy(f32[5,2,24,384]{2,1,0,3:T(2,128)} %constant_dynamic-slice_fusion) | data formatting | bytes 737280
  232.8 2.7 %select_select_fusion = f32[5,2,24,384]{3,2,1,0:T(8,128)} fusion(f32[5,2,24,384]{3,2,1,0:T(8,128)S(1)} %multiply_add_fusion, f32[5,2,24,384]{3,2,1,0:T(8,128)S(1)} %copy.20, pred[24]{0:T(512)(128)(4,1)} %get-tuple-element.5, pred[]{:T(512)S(6)} %lt.21, f32[5,2,24,384]{3,2,1,0:T(8,128)S(1)} %copy-done, f32[5,1,24,384]{3,2,1,0:T(8,128)} %copy-done.1, ...), kind=kLoop, calls=%fused_computation.108 | loop fusion | flops 3686400 | bytes 2171753 | tf_op jit(solution)/shard_map/jit(_where)/select_n | solution.py:177
  (97 shorter events, 45.1 us)
Async XLA Ops:
  6.5 81.8 %all-reduce.2.cloned.1.call-start = ((), (), s32[]{:S(2)}) async-start(), calls=%async_computation.1 | async-start | bytes 344064 | tf_op jit(solution)/shard_map/psum | solution.py:116
  7.6 7.2 %collective-permute-start = (f32[5,2,1,384]{3,2,1,0:T(1,128)S(1)}, f32[5,2,1,384]{3,2,1,0:T(1,128)S(1)}, u32[]{:S(2)}, u32[]{:S(2)}) collective-permute-start(f32[5,2,1,384]{3,2,1,0:T(1,128)S(1)} %get-tuple-element.21), channel_id=1, source_target_pairs={{0,4},{4,8},{8,12},{12,16},{16,20},{20,24},{24,28},{1,5},{5,9},{9,... | collective-permute-start | bytes 46088 | tf_op jit(solution)/shard_map/ppermute | solution.py:25
  9.9 5.2 %collective-permute-start.1 = (f32[5,2,1,384]{3,2,1,0:T(1,128)S(1)}, f32[5,2,1,384]{3,2,1,0:T(1,128)S(1)}, u32[]{:S(2)}, u32[]{:S(2)}) collective-permute-start(f32[5,2,1,384]{3,2,1,0:T(1,128)S(1)} %get-tuple-element.22), channel_id=1, source_target_pairs={{4,0},{8,4},{12,8},{16,12},{20,16},{24,20},{28,24},{5,1},{9,5},{13... | collective-permute-start | bytes 46088 | tf_op jit(solution)/shard_map/ppermute | solution.py:28
  12.3 103.5 %copy-start.1 = (f32[5,1,24,384]{3,2,1,0:T(8,128)}, f32[5,1,24,384]{3,2,1,0:T(8,128)S(1)}, u32[]{:S(2)}) copy-start(f32[5,1,24,384]{3,2,1,0:T(8,128)S(1)} %get-tuple-element.24) | copy-start | bytes 552964
  13.3 140.6 %copy-start.2 = (f32[2,24,384]{2,1,0:T(8,128)}, f32[2,24,384]{2,1,0:T(8,128)S(1)}, u32[]{:S(2)}) copy-start(f32[2,24,384]{2,1,0:T(8,128)S(1)} %get-tuple-element.25) | copy-start | bytes 221188
  13.3 140.6 %copy-start.3 = (f32[2,24,384]{2,1,0:T(8,128)}, f32[2,24,384]{2,1,0:T(8,128)S(1)}, u32[]{:S(2)}) copy-start(f32[2,24,384]{2,1,0:T(8,128)S(1)} %get-tuple-element.26) | copy-start | bytes 221188
  13.3 140.6 %copy-start.4 = (f32[2,24,384]{2,1,0:T(8,128)}, f32[2,24,384]{2,1,0:T(8,128)S(1)}, u32[]{:S(2)}) copy-start(f32[2,24,384]{2,1,0:T(8,128)S(1)} %get-tuple-element.27) | copy-start | bytes 221188
  13.4 140.5 %copy-start.5 = (f32[2,24,384]{2,1,0:T(8,128)}, f32[2,24,384]{2,1,0:T(8,128)S(1)}, u32[]{:S(2)}) copy-start(f32[2,24,384]{2,1,0:T(8,128)S(1)} %get-tuple-element.28) | copy-start | bytes 221188
  14.1 139.8 %copy-start.10 = (pred[24]{0:T(512)(128)(4,1)}, pred[24]{0:T(512)(128)(4,1)S(1)}, u32[]{:S(2)}) copy-start(pred[24]{0:T(512)(128)(4,1)S(1)} %get-tuple-element.32) | copy-start | bytes 76
  14.8 101.0 %copy-start.8 = (f32[5,2,1,384]{3,2,1,0:T(1,128)}, f32[5,2,1,384]{3,2,1,0:T(1,128)S(1)}, u32[]{:S(2)}) copy-start(f32[5,2,1,384]{3,2,1,0:T(1,128)S(1)} %collective-permute-done) | copy-start | bytes 46084
  16.2 7.1 %collective-permute-start.2 = (f32[5,2,26,1]{3,2,1,0:T(8,128)S(1)}, f32[5,2,26,1]{3,2,1,0:T(8,128)S(1)}, u32[]{:S(2)}, u32[]{:S(2)}) collective-permute-start(f32[5,2,26,1]{3,2,1,0:T(8,128)S(1)} %get-tuple-element.11), channel_id=1, source_target_pairs={{0,1},{1,2},{2,3},{4,5},{5,6},{6,7},{8,9},{9,10},{10,11},{12,13},{... | collective-permute-start | bytes 3128 | tf_op jit(solution)/shard_map/ppermute | solution.py:25
  20.3 7.8 %collective-permute-start.3 = (f32[5,2,26,1]{3,2,1,0:T(8,128)S(1)}, f32[5,2,26,1]{3,2,1,0:T(8,128)S(1)}, u32[]{:S(2)}, u32[]{:S(2)}) collective-permute-start(f32[5,2,26,1]{3,2,1,0:T(8,128)S(1)} %get-tuple-element.12), channel_id=1, source_target_pairs={{1,0},{2,1},{3,2},{5,4},{6,5},{7,6},{9,8},{10,9},{11,10},{13,12},{... | collective-permute-start | bytes 3128 | tf_op jit(solution)/shard_map/ppermute | solution.py:28
  88.4 10.3 %collective-permute-start.4 = (f32[20,1792]{1,0:T(8,128)}, f32[20,1792]{1,0:T(8,128)S(1)}, u32[]{:S(2)}, u32[]{:S(2)}) collective-permute-start(f32[20,1792]{1,0:T(8,128)} %all-reduce.2.cloned.1.call-done), channel_id=1, source_target_pairs={{0,3},{4,7},{8,11},{12,15},{16,19},{20,23},{24,27},{28,31}} | collective-permute-start | bytes 430088 | tf_op jit(solution)/shard_map/ppermute | solution.py:17
  93.6 8.8 %collective-permute-start.5 = (f32[20,1792]{1,0:T(8,128)}, f32[20,1792]{1,0:T(8,128)S(1)}, u32[]{:S(2)}, u32[]{:S(2)}) collective-permute-start(f32[20,1792]{1,0:T(8,128)} %all-reduce.2.cloned.1.call-done), channel_id=1, source_target_pairs={{0,2},{1,3},{4,6},{5,7},{8,10},{9,11},{12,14},{13,15},{16,18},{17,... | collective-permute-start | bytes 430088 | tf_op jit(solution)/shard_map/ppermute | solution.py:17
  94.9 10.7 %collective-permute-start.6 = (f32[20,1792]{1,0:T(8,128)}, f32[20,1792]{1,0:T(8,128)S(1)}, u32[]{:S(2)}, u32[]{:S(2)}) collective-permute-start(f32[20,1792]{1,0:T(8,128)} %all-reduce.2.cloned.1.call-done), channel_id=1, source_target_pairs={{0,1},{1,2},{2,3},{4,5},{5,6},{6,7},{8,9},{9,10},{10,11},{12,13},{... | collective-permute-start | bytes 430088 | tf_op jit(solution)/shard_map/ppermute | solution.py:17
  116.6 3.4 %collective-permute-start.7 = (f32[5,2,1,384]{3,2,1,0:T(1,128)S(1)}, f32[5,2,1,384]{3,2,1,0:T(1,128)S(1)}, u32[]{:S(2)}, u32[]{:S(2)}) collective-permute-start(f32[5,2,1,384]{3,2,1,0:T(1,128)S(1)} %get-tuple-element.17), channel_id=1, source_target_pairs={{0,4},{4,8},{8,12},{12,16},{16,20},{20,24},{24,28},{1,5},{5,9},{9,... | collective-permute-start | bytes 46088 | tf_op jit(solution)/shard_map/ppermute | solution.py:25
  118.1 3.6 %collective-permute-start.8 = (f32[5,2,1,384]{3,2,1,0:T(1,128)S(1)}, f32[5,2,1,384]{3,2,1,0:T(1,128)S(1)}, u32[]{:S(2)}, u32[]{:S(2)}) collective-permute-start(f32[5,2,1,384]{3,2,1,0:T(1,128)S(1)} %get-tuple-element.18), channel_id=1, source_target_pairs={{4,0},{8,4},{12,8},{16,12},{20,16},{24,20},{28,24},{5,1},{9,5},{13... | collective-permute-start | bytes 46088 | tf_op jit(solution)/shard_map/ppermute | solution.py:28
  121.9 10.3 %collective-permute-start.10 = (f32[5,2,26,1]{3,2,1,0:T(8,128)S(1)}, f32[5,2,26,1]{3,2,1,0:T(8,128)S(1)}, u32[]{:S(2)}, u32[]{:S(2)}) collective-permute-start(f32[5,2,26,1]{3,2,1,0:T(8,128)S(1)} %get-tuple-element.10), channel_id=1, source_target_pairs={{1,0},{2,1},{3,2},{5,4},{6,5},{7,6},{9,8},{10,9},{11,10},{13,12},{... | collective-permute-start | bytes 3128 | tf_op jit(solution)/shard_map/ppermute | solution.py:28
  123.2 10.7 %collective-permute-start.9 = (f32[5,2,26,1]{3,2,1,0:T(8,128)S(1)}, f32[5,2,26,1]{3,2,1,0:T(8,128)S(1)}, u32[]{:S(2)}, u32[]{:S(2)}) collective-permute-start(f32[5,2,26,1]{3,2,1,0:T(8,128)S(1)} %get-tuple-element.9), channel_id=1, source_target_pairs={{0,1},{1,2},{2,3},{4,5},{5,6},{6,7},{8,9},{9,10},{10,11},{12,13},{... | collective-permute-start | bytes 3128 | tf_op jit(solution)/shard_map/ppermute | solution.py:25
  134.5 5.4 %collective-permute-start.11 = (f32[5,2,1,384]{3,2,1,0:T(1,128)S(1)}, f32[5,2,1,384]{3,2,1,0:T(1,128)S(1)}, u32[]{:S(2)}, u32[]{:S(2)}) collective-permute-start(f32[5,2,1,384]{3,2,1,0:T(1,128)S(1)} %get-tuple-element.13), channel_id=1, source_target_pairs={{0,4},{4,8},{8,12},{12,16},{16,20},{20,24},{24,28},{1,5},{5,9},{9,... | collective-permute-start | bytes 46088 | tf_op jit(solution)/shard_map/ppermute | solution.py:25
  138.1 3.5 %collective-permute-start.12 = (f32[5,2,1,384]{3,2,1,0:T(1,128)S(1)}, f32[5,2,1,384]{3,2,1,0:T(1,128)S(1)}, u32[]{:S(2)}, u32[]{:S(2)}) collective-permute-start(f32[5,2,1,384]{3,2,1,0:T(1,128)S(1)} %get-tuple-element.14), channel_id=1, source_target_pairs={{4,0},{8,4},{12,8},{16,12},{20,16},{24,20},{28,24},{5,1},{9,5},{13... | collective-permute-start | bytes 46088 | tf_op jit(solution)/shard_map/ppermute | solution.py:28
  141.7 7.4 %collective-permute-start.13 = (f32[5,2,26,1]{3,2,1,0:T(8,128)S(1)}, f32[5,2,26,1]{3,2,1,0:T(8,128)S(1)}, u32[]{:S(2)}, u32[]{:S(2)}) collective-permute-start(f32[5,2,26,1]{3,2,1,0:T(8,128)S(1)} %get-tuple-element.7), channel_id=1, source_target_pairs={{0,1},{1,2},{2,3},{4,5},{5,6},{6,7},{8,9},{9,10},{10,11},{12,13},{... | collective-permute-start | bytes 3128 | tf_op jit(solution)/shard_map/ppermute | solution.py:25
  146.1 7.7 %collective-permute-start.14 = (f32[5,2,26,1]{3,2,1,0:T(8,128)S(1)}, f32[5,2,26,1]{3,2,1,0:T(8,128)S(1)}, u32[]{:S(2)}, u32[]{:S(2)}) collective-permute-start(f32[5,2,26,1]{3,2,1,0:T(8,128)S(1)} %get-tuple-element.8), channel_id=1, source_target_pairs={{1,0},{2,1},{3,2},{5,4},{6,5},{7,6},{9,8},{10,9},{11,10},{13,12},{... | collective-permute-start | bytes 3128 | tf_op jit(solution)/shard_map/ppermute | solution.py:28
  200.8 18.8 %all-to-all-start = ((f32[4,1,30720]{2,1,0:T(1,128)}), f32[4,1,30720]{2,1,0:T(1,128)S(1)}, u32[]{:S(2)}, u32[]{:S(2)}) async-start(f32[4,1,30720]{2,1,0:T(1,128)} %reshape.132), calls=%async_computation | async-start | bytes 983040 | tf_op jit(solution)/shard_map/all_to_all | solution.py:172
  (6 other events, 334.3 us)
Sparse Core Ops, SparseCore 0:
  34.2 54.1 all-reduce.1
where the time goes:
time: 243 us; the launch traced here: 242 us
  waiting for transfers between devices  95.9 us (39%)
  local copies, waits for them, and re-layouts  45.1 us (19%)
  starting transfers between devices  45 us (19%)
  other arithmetic  24.5 us (10%)
  between operations  14.7 us (6%)
  blocking collectives  13 us (5%)
  matrix products  4.13 us (2%)
    psum x1, waiting for transfers between devices, on_device(): summed = lax.psum(packed, 'tile')  54.2 us
    ppermute x6, starting transfers between devices, with_halo(): lax.ppermute(lax.slice_in_dim(block, block.shape[dim] - width, None, axis...  23.6 us
    reshape x1, local copies, waits for them, and re-layouts, on_device(): nest_field.reshape(fields, levels, coarse_rows, RATIO, third_width, RATIO)  16.7 us
    ppermute x6, waiting for transfers between devices, with_halo(): lax.ppermute(lax.slice_in_dim(block, 0, width, axis=dim), axis, backward)  14.4 us
    all_to_all x1, waiting for transfers between devices, on_device(): lax.all_to_all(outbound, 'section', split_axis=3, concat_axis=3, tiled=True)  14.3 us
    unnamed x31, local copies, waits for them, and re-layouts  13.2 us
    all_gather x1, blocking collectives, on_device(): portion = lax.all_gather(block_means, 'tile', axis=2, tiled=True)  13 us
    ppermute x3, starting transfers between devices, shifted(): lax.ppermute(value, axis, [(source, source + steps) for source in range(l...  9 us
  transfers between devices with their start and end apart: 17, of which 14 were waited for; matrix products, arithmetic and copies ran while one was open for 2% of the time, Pallas kernels for 0%

commit v1 on v0

--- a/solution.py
+++ b/solution.py
@@ -1,6 +1,10 @@
+import functools
+
 import jax
 import jax.numpy as jnp
 from jax import lax
+from jax.experimental import pallas as pl
+from jax.experimental.pallas import tpu as pltpu
 from jax.sharding import PartitionSpec as P
 
 RATIO = 3
@@ -61,7 +65,7 @@
     return shifted(values, "section", distance)
 
 
-def on_device(state, courant, nest_offset):
+def general_on_device(state, courant, nest_offset):
     fields, levels, row_count, col_count = state.shape
     tile_count = lax.axis_size("tile")
     section_count = lax.axis_size("section")
@@ -177,9 +181,519 @@
     return jnp.where(is_parent, parent_final, nest_field)
 
 
+ROWS = 24
+COLS = 384
+LANE = 128
+STATES = 10
+PLANES = 14
+SLOTS = 4 * PLANES
+NEST_MARK = 1.0
+PARENT_MARK = 2.0
+EXACT = lax.Precision.HIGHEST
+
+
+def device(tile, section):
+    return tile * 4 + section
+
+
+def third(value):
+    return (value * 43) >> 7
+
+
+def iota(shape, dim):
+    return lax.broadcasted_iota(jnp.int32, shape, dim)
+
+
+def dot(a, b):
+    return jnp.dot(a, b, precision=EXACT, preferred_element_type=jnp.float32)
+
+
+def turn(value, steps, dim):
+    size = value.shape[dim]
+    steps = steps % size
+    return pltpu.roll(value, steps, dim) if steps else value
+
+
+def plane_of(state_ref, courant_ref, p):
+    return state_ref[p] if p < STATES else courant_ref[p - STATES]
+
+
+def pack_kernel(offset_ref, state_ref, courant_ref, west_ref, middle_ref, east_ref):
+    tile = lax.axis_index("tile")
+    section = lax.axis_index("section")
+    offset = offset_ref[0]
+    first = tile * ROWS
+    lane = iota((ROWS, LANE), 1)
+    left = jnp.zeros((ROWS, LANE), jnp.float32)
+    right = jnp.zeros((ROWS, LANE), jnp.float32)
+    for p in range(PLANES):
+        source = plane_of(state_ref, courant_ref, p)
+        mine = (lane >= 3 * p) & (lane < 3 * p + 3)
+        left = jnp.where(mine, turn(source[:, :LANE], 3 * p, 1), left)
+        right = jnp.where(mine, turn(source[:, COLS - LANE :], 3 * p - (LANE - 3), 1), right)
+    top = (first <= offset + 2) & (first + ROWS - 1 >= offset - 1)
+    base = jnp.where(top, offset - 1, offset + 61) - first
+
+    def chosen(start, count):
+        slot = iota((4 * count, ROWS * count), 0)
+        column = iota((4 * count, ROWS * count), 1)
+        local = base + (slot & 3)
+        hit = (local >= 0) & (local < ROWS) & (column == (slot >> 2) * ROWS + local)
+        return hit.astype(jnp.float32)
+
+    rows = jnp.concatenate(
+        [
+            dot(chosen(0, STATES), state_ref[...].reshape(STATES * ROWS, COLS)),
+            dot(chosen(0, 4), courant_ref[...].reshape(4 * ROWS, COLS)),
+        ],
+        axis=0,
+    )
+    lane = iota((SLOTS, LANE), 1)
+    mark = jnp.where(section == 0, PARENT_MARK, NEST_MARK)
+    blank = jnp.zeros((SLOTS, LANE), jnp.float32)
+    outs = ((west_ref, left), (middle_ref, left), (east_ref, right))
+    for s, (out_ref, edge) in enumerate(outs):
+        before = rows[:, LANE * (s - 1) : LANE * s] if s > 0 else blank
+        after = rows[:, LANE * (s + 1) : LANE * (s + 2)] if s < 2 else blank
+        extra = turn(jnp.where(lane < 2, after, before), 44, 1)
+        side = jnp.where(
+            (lane >= 42) & (lane < 46), extra, jnp.where(lane == LANE - 1, mark, 0.0)
+        )
+        out_ref[:, :LANE] = rows[:, LANE * s : LANE * (s + 1)]
+        out_ref[:ROWS, LANE:] = jnp.where(lane[:ROWS] < 42, edge, side[:ROWS])
+        out_ref[ROWS:, LANE:] = side[ROWS:]
+
+
+def relay_kernel(*refs):
+    state_ref, courant_ref = refs[:2]
+    to_west, to_middle, to_east = refs[2:5], refs[5:6], refs[6:9]
+    west_ref, east_ref, rims_ref, pair_ref, cross_ref = refs[9:]
+    even = lax.axis_index("tile") % 2 == 0
+
+    def marked(sources, mark):
+        total = None
+        for ref in sources:
+            value = ref[...]
+            value = jnp.where(value[:, 2 * LANE - 1 :] == mark, value, 0.0)
+            total = value if total is None else total + value
+        return total
+
+    east = marked(to_west, NEST_MARK)[:ROWS, LANE:]
+    west = marked(to_east, NEST_MARK)[:ROWS, LANE:]
+    rims = marked(to_west + to_middle + to_east, PARENT_MARK)
+    west_ref[...] = west
+    east_ref[...] = east
+    rims_ref[...] = rims
+
+    def put(rows, lanes, value):
+        head, tail = value[:4], value[ROWS - 4 :]
+        pair_ref[rows, lanes] = jnp.where(even, tail, head)
+        cross_ref[rows, lanes] = jnp.where(even, head, tail)
+
+    for p in range(PLANES):
+        put(slice(4 * p, 4 * p + 4), slice(None), plane_of(state_ref, courant_ref, p))
+    put(slice(SLOTS, SLOTS + 4), slice(0, LANE), west)
+    put(slice(SLOTS, SLOTS + 4), slice(LANE, 2 * LANE), east)
+    pair_ref[SLOTS + 8 :, : 2 * LANE] = rims
+
+
+def flux(value, south, north, west, east, other, cy, cx):
+    transport = (
+        jnp.maximum(cy, 0.0) * (value - south)
+        + jnp.minimum(cy, 0.0) * (north - value)
+        + jnp.maximum(cx, 0.0) * (value - west)
+        + jnp.minimum(cx, 0.0) * (east - value)
+    )
+    spread = south + north + west + east - 4.0 * value
+    return diffusion * spread + mixing * (other - value) - transport
+
+
+def main_kernel(
+    offset_ref,
+    state_ref,
+    courant_ref,
+    west_ref,
+    east_ref,
+    rims_ref,
+    pair_ref,
+    cross_ref,
+    out_ref,
+    means_ref,
+    here,
+    there,
+    factors,
+    base_force,
+    step_force,
+    narrowed,
+):
+    tile = lax.axis_index("tile")
+    section = lax.axis_index("section")
+    offset = offset_ref[0]
+    even = tile % 2 == 0
+    is_nest = section > 0
+    full = (32, 4 * LANE)
+
+    after = jnp.where(even, pair_ref[: SLOTS + 8], cross_ref[...])
+    before = jnp.where(even, cross_ref[...], pair_ref[: SLOTS + 8])
+    wests = jnp.concatenate(
+        [west_ref[...], after[SLOTS : SLOTS + 4, :LANE], before[SLOTS : SLOTS + 4, :LANE]], axis=0
+    )
+    easts = jnp.concatenate(
+        [
+            east_ref[...],
+            after[SLOTS : SLOTS + 4, LANE : 2 * LANE],
+            before[SLOTS : SLOTS + 4, LANE : 2 * LANE],
+        ],
+        axis=0,
+    )
+    lane = iota((32, LANE), 1)
+
+    def ring(p):
+        tail = jnp.concatenate([after[4 * p : 4 * p + 4], before[4 * p : 4 * p + 4]], axis=0)
+        cells = jnp.concatenate([plane_of(state_ref, courant_ref, p), tail], axis=0)
+        outside = jnp.where(
+            lane < 3,
+            turn(easts, -3 * p, 1),
+            jnp.where(lane >= LANE - 3, turn(wests, LANE - 3 - 3 * p, 1), 0.0),
+        )
+        return jnp.concatenate([cells, outside], axis=1)
+
+    for p in range(STATES):
+        here[p] = ring(p)
+
+    row = iota(full, 0)
+    column = iota(full, 1)
+    near_row = jnp.where(row < 28, row, row - 32)
+    near_column = jnp.where(column < 448, column, column - 512)
+    grid_row = near_row + tile * ROWS
+    grid_column = near_column + (section - 1) * COLS
+    row_depth = jnp.minimum(grid_row, 8 * ROWS - 1 - grid_row)
+    column_depth = jnp.minimum(grid_column, 3 * COLS - 1 - grid_column)
+    depth = jnp.maximum(jnp.minimum(row_depth, column_depth), 0)
+    weight = jnp.maximum(ZONE - depth, 0).astype(jnp.float32) / ZONE
+    weight = jnp.where(is_nest, weight, 0.0)
+    keep = 1.0 - weight
+    no_south = row == jnp.where(tile == 0, 0, -1)
+    no_north = row == jnp.where(tile == 7, ROWS - 1, -1)
+    no_west = column == jnp.where(section < 2, 0, -1)
+    no_east = column == jnp.where((section == 0) | (section == 3), COLS - 1, -1)
+    for level in range(2):
+        cy = ring(STATES + level)
+        cx = ring(STATES + 2 + level)
+        from_south = jnp.maximum(cy, 0.0) + diffusion
+        from_north = diffusion - jnp.minimum(cy, 0.0)
+        from_west = jnp.maximum(cx, 0.0) + diffusion
+        from_east = diffusion - jnp.minimum(cx, 0.0)
+        from_south = jnp.where(no_south, 0.0, from_south)
+        from_north = jnp.where(no_north, 0.0, from_north)
+        from_west = jnp.where(no_west, 0.0, from_west)
+        from_east = jnp.where(no_east, 0.0, from_east)
+        own = (1.0 - mixing) - (from_south + from_north + from_west + from_east)
+        factors[level, 0] = own * keep
+        factors[level, 1] = from_south * keep
+        factors[level, 2] = from_north * keep
+        factors[level, 3] = from_west * keep
+        factors[level, 4] = from_east * keep
+    factors[0, 5] = mixing * keep
+
+    base_force[...] = jnp.zeros(base_force.shape, jnp.float32)
+    step_force[...] = jnp.zeros(step_force.shape, jnp.float32)
+    other_rims = pair_ref[SLOTS + 8 :, : 2 * LANE]
+    lower = jnp.where(even, rims_ref[...], other_rims)
+    upper = jnp.where(even, other_rims, rims_ref[...])
+
+    @pl.when((section == 1) | (section == 3))
+    def _():
+        on_left = section == 1
+        edges = jnp.concatenate([lower[:ROWS, LANE:], upper[:ROWS, LANE:]], axis=0)
+        source_tile = ((offset - 2) // 8 + (tile // 2) * 2) // 3
+        pick = iota((96, 2 * ROWS), 0)
+        part = pick >> 5
+        near = pick & 31
+        near = jnp.where(near < 28, near, near - 32)
+        coarse = offset + tile * 8 + third(near + 6) - 2 + part - 1 - source_tile * ROWS
+        picked = dot((iota((96, 2 * ROWS), 1) == coarse).astype(jnp.float32), edges)
+        south, value, north = picked[:32], picked[32:64], picked[64:]
+        place = lane - 3 * third(lane)
+        west = jnp.where(place == jnp.where(on_left, 0, -1), value, turn(value, 1, 1))
+        east = jnp.where(place == jnp.where(on_left, -1, 2), value, turn(value, -1, 1))
+        other = jnp.where((third(lane) & 1) == 0, turn(value, -3, 1), turn(value, 3, 1))
+        cy = jnp.zeros((32, LANE), jnp.float32)
+        cx = jnp.zeros((32, LANE), jnp.float32)
+        for field in range(STATES // 2):
+            mine = (lane >= 6 * field) & (lane < 6 * field + 6)
+            cy = jnp.where(mine, turn(value, 6 * field - 3 * STATES, 1), cy)
+            cx = jnp.where(mine, turn(value, 6 * field - 3 * STATES - 6, 1), cx)
+        change = flux(value, south, north, west, east, other, cy, cx) / RATIO
+        out = iota((LANE, STATES * LANE), 1)
+        spot = out & (LANE - 1)
+        wanted = 3 * (out >> 7) + jnp.where(on_left, third(spot), third(spot - 119))
+        start = jnp.where(on_left, 0, LANE - 6)
+        valid = (spot >= start) & (spot < start + 6)
+        spread = (valid & (iota((LANE, STATES * LANE), 0) == wanted)).astype(jnp.float32)
+        forced = dot(jnp.concatenate([value, change], axis=0), spread)
+
+        def place_side(lanes):
+            for p in range(STATES):
+                block = forced[:, p * LANE : (p + 1) * LANE]
+                base_force[p, :, lanes] = weight[:, lanes] * block[:32]
+                step_force[p, :, lanes] = weight[:, lanes] * block[32:]
+
+        @pl.when(on_left)
+        def _():
+            place_side(slice(0, LANE))
+
+        @pl.when(jnp.logical_not(on_left))
+        def _():
+            place_side(slice(2 * LANE, 3 * LANE))
+
+    @pl.when(is_nest & ((tile == 0) | (tile == 7)))
+    def _():
+        rows = lower + upper
+        wide = iota((8, 2 * LANE), 1)
+        narrow = iota((SLOTS, LANE), 1)
+        outside = turn(rows[:, LANE:], 84, 1)
+        outside = jnp.where((narrow < 2) | (narrow >= LANE - 2), outside, 0.0)
+        rows = jnp.concatenate([rows[:, :LANE], outside], axis=1)
+        cy = rows[4 * STATES : 4 * STATES + 8]
+        cx = rows[4 * STATES + 8 :]
+        changes = []
+        for field in range(STATES // 2):
+            value = rows[8 * field : 8 * field + 8]
+            west = jnp.where(wide == jnp.where(section == 1, 0, -1), value, turn(value, 1, 1))
+            east = jnp.where(wide == jnp.where(section == 3, LANE - 1, -1), value, turn(value, -1, 1))
+            changes.append(
+                flux(
+                    value,
+                    turn(value, 1, 0),
+                    turn(value, -1, 0),
+                    west,
+                    east,
+                    turn(value, 4, 0),
+                    cy,
+                    cx,
+                )
+                / RATIO
+            )
+        both = jnp.concatenate([rows[: 4 * STATES]] + changes, axis=0)
+        target = iota((2 * LANE, 4 * LANE), 1)
+        target = jnp.where(target < 448, target, target - 512)
+        coarse = (((target + 66) * 171) >> 9) - 22
+        spread = (iota((2 * LANE, 4 * LANE), 0) == (coarse & (2 * LANE - 1))).astype(jnp.float32)
+        forced = dot(both, spread)
+        eight = iota((8, 4 * LANE), 0)
+
+        def place_rows(rows, split):
+            zone = jnp.where(split == 3, eight < ZONE, eight >= 8 - ZONE)
+            for p in range(STATES):
+                for ref, start in ((base_force, 0), (step_force, 4 * STATES)):
+                    spot = start + 4 * p
+                    value = jnp.where(eight < split, forced[spot + 1 : spot + 2], forced[spot + 2 : spot + 3])
+                    ref[p, rows, :] = jnp.where(zone, weight[rows] * value, ref[p, rows, :])
+
+        @pl.when(tile == 0)
+        def _():
+            place_rows(slice(0, 8), 3)
+
+        @pl.when(tile == 7)
+        def _():
+            place_rows(slice(16, 24), 5)
+
+    def substep(source, target, number):
+        def per_field(field, carry):
+            values = [source[2 * field + level] for level in range(2)]
+            for level in range(2):
+                value = values[level]
+                result = factors[level, 0] * value + factors[0, 5] * values[1 - level]
+                result += factors[level, 1] * turn(value, 1, 0)
+                result += factors[level, 2] * turn(value, -1, 0)
+                result += factors[level, 3] * turn(value, 1, 1)
+                result += factors[level, 4] * turn(value, -1, 1)
+                p = 2 * field + level
+                result += base_force[p] + float(number) * step_force[p]
+                target[p] = result
+            return carry
+
+        lax.fori_loop(0, STATES // 2, per_field, 0)
+
+    substep(here, there, 1)
+
+    @pl.when(is_nest)
+    def _():
+        substep(there, here, 2)
+        substep(here, there, 3)
+
+    out_ref[...] = there[:, :ROWS, :COLS]
+    columns = iota((COLS, LANE), 1) * RATIO
+    source = iota((COLS, LANE), 0)
+    gather = ((source >= columns) & (source < columns + RATIO)).astype(jnp.float32)
+    narrowed[...] = dot(out_ref[...].reshape(STATES * ROWS, COLS), gather)
+    total = sum(narrowed[pl.ds(i, STATES * 8, stride=RATIO), :] for i in range(RATIO))
+    means_ref[...] = total / (RATIO * RATIO)
+
+
+def merge_kernel(offset_ref, first_ref, second_ref, third_ref, fourth_ref, block_ref, out_ref):
+    tile = lax.axis_index("tile")
+    section = lax.axis_index("section")
+    offset = offset_ref[0]
+    rest = offset % 8
+
+    @pl.when(section > 0)
+    def _():
+        out_ref[...] = block_ref[...]
+
+    @pl.when(section == 0)
+    def _():
+        nest_row = tile * ROWS + iota((ROWS, COLS), 0) - offset
+        covered = (nest_row >= 0) & (nest_row < 64)
+        for p in range(STATES):
+            parts = [r[8 * p : 8 * p + 8] for r in (first_ref, second_ref, third_ref, fourth_ref)]
+            moved = pltpu.roll(jnp.concatenate(parts, axis=0), rest + 24, 0)
+            out_ref[p] = jnp.where(covered, moved[:ROWS], block_ref[p])
+
+
+VMEM = pl.BlockSpec(memory_space=pltpu.VMEM)
+SMEM = pl.BlockSpec(memory_space=pltpu.SMEM)
+
+
+def shaped(*shape):
+    return jax.ShapeDtypeStruct(shape, jnp.float32)
+
+
+def rim_pairs(start):
+    groups = []
+    for section, inner in ((1, ((2, 1), (3, 2))), (3, ((1, 2), (2, 3)))):
+        lists = [[], [], []]
+        sent = {}
+        taken = {}
+        for chip in range(4):
+            source = (start + 2 * chip) // 3
+            for core in range(2):
+                color = sent.get(source + core, 0)
+                sent[source + core] = color + 1
+                taken[2 * chip + core] = color
+                lists[color].append((device(source + core, 0), device(2 * chip + core, section)))
+        for tile in range(8):
+            for origin, target in inner:
+                color = (taken[tile] + 1) % 3 if target == section else taken[tile]
+                lists[color].append((device(tile, origin), device(tile, target)))
+        groups.append(lists)
+    middle = []
+    for chip in (0, 3):
+        source = (start + 2 * chip) // 3
+        middle += [(device(source + core, 0), device(2 * chip + core, 2)) for core in range(2)]
+    return groups[0], [middle], groups[1]
+
+
+def mean_pairs(start):
+    lists = []
+    for step in range(4):
+        pairs = []
+        for tile in range(8):
+            source = 3 * tile - start - 1 + step
+            if 0 <= source < 8:
+                pairs.append((device(source, 0), device(tile, 0)))
+        lists.append(pairs)
+    return lists
+
+
+BOTH = ("tile", "section")
+
+
+def on_device(state, courant, nest_offset):
+    planes = state.reshape(STATES, ROWS, COLS)
+    speeds = courant.reshape(4, ROWS, COLS)
+    offset = nest_offset[0]
+    payloads = pl.pallas_call(
+        pack_kernel,
+        out_shape=[shaped(SLOTS, 2 * LANE)] * 3,
+        in_specs=[SMEM, VMEM, VMEM],
+        out_specs=[VMEM] * 3,
+        name="pack",
+    )(nest_offset, planes, speeds)
+
+    def send_rims(start, west, middle, east):
+        groups = rim_pairs(start)
+        return tuple(
+            lax.ppermute(value, BOTH, pairs)
+            for value, lists in zip((west, middle, east), groups)
+            for pairs in lists
+        )
+
+    received = lax.switch(
+        (offset - 2) // 8 - 2,
+        [functools.partial(send_rims, start) for start in range(2, 12)],
+        *payloads,
+    )
+    west, east, rims, to_pair, to_cross = pl.pallas_call(
+        relay_kernel,
+        out_shape=[
+            shaped(ROWS, LANE),
+            shaped(ROWS, LANE),
+            shaped(SLOTS, 2 * LANE),
+            shaped(2 * SLOTS + 8, COLS),
+            shaped(SLOTS + 8, COLS),
+        ],
+        in_specs=[VMEM] * 9,
+        out_specs=[VMEM] * 5,
+        name="relay",
+    )(planes, speeds, *received)
+    pair_map = [(device(t, s), device(t ^ 1, s)) for t in range(8) for s in range(4)]
+    cross_map = [
+        (device(a, s), device(b, s))
+        for low in (1, 3, 5)
+        for a, b in ((low, low + 1), (low + 1, low))
+        for s in range(4)
+    ]
+    from_cross = lax.ppermute(to_cross, BOTH, cross_map)
+    from_pair = lax.ppermute(to_pair, BOTH, pair_map)
+    block, means = pl.pallas_call(
+        main_kernel,
+        out_shape=[shaped(STATES, ROWS, COLS), shaped(STATES * 8, LANE)],
+        in_specs=[SMEM] + [VMEM] * 7,
+        out_specs=[VMEM] * 2,
+        scratch_shapes=[
+            pltpu.VMEM((STATES, 32, 4 * LANE), jnp.float32),
+            pltpu.VMEM((STATES, 32, 4 * LANE), jnp.float32),
+            pltpu.VMEM((2, 6, 32, 4 * LANE), jnp.float32),
+            pltpu.VMEM((STATES, 32, 4 * LANE), jnp.float32),
+            pltpu.VMEM((STATES, 32, 4 * LANE), jnp.float32),
+            pltpu.VMEM((STATES * ROWS, LANE), jnp.float32),
+        ],
+        compiler_params=pltpu.CompilerParams(vmem_limit_bytes=32 * 1024 * 1024),
+        name="nest",
+    )(nest_offset, planes, speeds, west, east, rims, from_pair, from_cross)
+    columns = jnp.concatenate(
+        [
+            lax.ppermute(means, BOTH, [(device(t, s), device(t, 0)) for t in range(8)])
+            for s in (1, 2, 3)
+        ],
+        axis=1,
+    )
+
+    def send_means(start, value):
+        return tuple(lax.ppermute(value, BOTH, pairs) for pairs in mean_pairs(start))
+
+    blocks = lax.switch(
+        offset // 8 - 3,
+        [functools.partial(send_means, start) for start in range(3, 12)],
+        columns,
+    )
+    merged = pl.pallas_call(
+        merge_kernel,
+        out_shape=shaped(STATES, ROWS, COLS),
+        in_specs=[SMEM] + [VMEM] * 5,
+        out_specs=VMEM,
+        compiler_params=pltpu.CompilerParams(vmem_limit_bytes=32 * 1024 * 1024),
+        name="merge",
+    )(nest_offset, *blocks, block)
+    return merged.reshape(state.shape)
+
+
 def solution(mesh):
+    small = mesh.shape["tile"] == 8 and mesh.shape["section"] == 4
     return jax.shard_map(
-        on_device,
+        on_device if small else general_on_device,
         mesh=mesh,
         in_specs=(P(None, None, "tile", "section"), P(None, None, "tile", "section"), P()),
         out_specs=P(None, None, "tile", "section"),

time: 243 us -> 103 us (0.42)
  waiting for transfers between devices: 95.9 us -> 6.23 us
  local copies, waits for them, and re-layouts: 45.1 us -> 2.24 us
  starting transfers between devices: 45 us -> 85.4 us
  other arithmetic: 24.5 us -> 0.01 us
  between operations: 14.7 us -> 0.83 us
  blocking collectives: 13 us -> 0 us
  Pallas kernels: 0 us -> 7.11 us
  matrix products: 4.13 us -> 0 us
    psum x1 -> x0, waiting for transfers between devices: 54.2 us -> none  [on_device(): summed = lax.psum(packed, 'tile')]
    ppermute x15 -> x16, starting transfers between devices: 40.5 us -> 85.4 us  [the longest x7 36.7 us: send_rims(): lax.ppermute(value, BOTH, pairs)]
    reshape x5 -> x0, local copies, waits for them, and re-layouts: 22.2 us -> none  [the longest x1 16.7 us: on_device(): nest_field.reshape(fields, levels, coarse_rows, RATIO, third_width, RATIO)]
    ppermute x15 -> x16, waiting for transfers between devices: 27.4 us -> 6.23 us  [the longest x3 4.44 us: on_device(): lax.ppermute(means, BOTH, [(device(t, s), device(t, 0)) for t in range(8)])]
    all_to_all x1 -> x0, waiting for transfers between devices: 14.3 us -> none  [on_device(): lax.all_to_all(outbound, 'section', split_axis=3, concat_axis=3, tiled=True)]
    all_gather x1 -> x0, blocking collectives: 13 us -> none  [on_device(): portion = lax.all_gather(block_means, 'tile', axis=2, tiled=True)]
    unnamed x31 -> x10, local copies, waits for them, and re-layouts: 13.2 us -> 2.24 us
    pallas_call x0 -> x4, Pallas kernels: none -> 7.11 us  [the longest x1 2.09 us: on_device(): pl.pallas_call(relay_kernel, out_shape=[shaped(ROWS, LANE), shaped(ROWS,...]
  transfers between devices with their start and end apart: 17 -> 16, of which waited for: 14 -> 2; matrix products, arithmetic and copies ran while one was open for 2% -> 0% of each run, Pallas kernels for 0% -> 0%
where the time goes in v1:
time: 103 us; the launch traced here: 102 us
  starting transfers between devices  85.4 us (83%)
  Pallas kernels  7.11 us (7%)
  waiting for transfers between devices  6.23 us (6%)
  local copies, waits for them, and re-layouts  2.24 us (2%)
    ppermute x7, starting transfers between devices, send_rims(): lax.ppermute(value, BOTH, pairs)  36.7 us
    ppermute x3, starting transfers between devices, on_device(): lax.ppermute(means, BOTH, [(device(t, s), device(t, 0)) for t in range(8)])  25.9 us
    ppermute x1, starting transfers between devices, on_device(): from_pair = lax.ppermute(to_pair, BOTH, pair_map)  8.4 us
    ppermute x4, starting transfers between devices, send_means(): lax.ppermute(value, BOTH, pairs)  7.92 us
    ppermute x1, starting transfers between devices, on_device(): from_cross = lax.ppermute(to_cross, BOTH, cross_map)  6.37 us
    ppermute x3, waiting for transfers between devices, on_device(): lax.ppermute(means, BOTH, [(device(t, s), device(t, 0)) for t in range(8)])  4.44 us
    unnamed x10, local copies, waits for them, and re-layouts  2.24 us
    pallas_call x1, Pallas kernels, on_device(): pl.pallas_call(relay_kernel, out_shape=[shaped(ROWS, LANE), shaped(ROWS,...  2.09 us
  transfers between devices with their start and end apart: 16, of which 2 were waited for; matrix products, arithmetic and copies ran while one was open for 0% of the time, Pallas kernels for 0%

profile of v1, /device:TPU:0, one launch (start us, length us, event | category | flops | bytes accessed | tf_op | source)
XLA Modules:
  0.0 101.8 jit_solution(3399079315112246483)
XLA Ops:
  0.7 1.5 %pack.1 = (f32[56,256]{1,0:T(8,128)S(1)}, f32[56,256]{1,0:T(8,128)S(1)}, f32[56,256]{1,0:T(8,128)S(1)}) custom-call(s32[1]{0:T(128)} %copy.110.offset_ref, f32[10,24,384]{2,1,0:T(8,128)} %bitcast.9, f32[4,24,384]{2,1,0:T(8,128)} %bitcast.12), custom_call_target="tpu_custom_call" | custom-call | tf_op jit(solution)/shard_map/pack/pallas_call | solution.py:607
  2.2 36.8 %conditional.2 = (f32[56,256]{1,0:T(8,128)}, f32[56,256]{1,0:T(8,128)}, f32[56,256]{1,0:T(8,128)}, f32[56,256]{1,0:T(8,128)}, f32[56,256]{1,0:T(8,128)}, /*index=5*/f32[56,256]{1,0:T(8,128)}, f32[56,256]{1,0:T(8,128)}) conditional(s32[]{:T(128)} %clamp.7, (f32[56,256]{1,0:T(8,128)S(1)}, f32[56,256]{1,0:T(8,128)S(1)}, ...), branch_computations={%region_0.1_spmd, %region_1.2_spmd, %region_2.3_spmd, %region_3.4_... | conditional | bytes 1605968 | solution.py:623
  2.2 1.3 %collective-permute-start.24 = (f32[56,256]{1,0:T(8,128)S(1)}, f32[56,256]{1,0:T(8,128)}, u32[]{:S(2)}, u32[]{:S(2)}) collective-permute-start(f32[56,256]{1,0:T(8,128)S(1)} %get-tuple-element.84), channel_id=1, source_target_pairs={{4,2},{8,6},{12,26},{16,30}} | collective-permute-start | bytes 172040 | tf_op jit(solution)/shard_map/cond/branch_3_fun/ppermute | solution.py:618
  3.5 1.3 %collective-permute-start.23 = (f32[56,256]{1,0:T(8,128)S(1)}, f32[56,256]{1,0:T(8,128)}, u32[]{:S(2)}, u32[]{:S(2)}) collective-permute-start(f32[56,256]{1,0:T(8,128)S(1)} %get-tuple-element.83), channel_id=1, source_target_pairs={{12,25},{10,9},{18,17},{27,26},{30,29}} | collective-permute-start | bytes 172040 | tf_op jit(solution)/shard_map/cond/branch_3_fun/ppermute | solution.py:618
  4.8 10.0 %collective-permute-start.22 = (f32[56,256]{1,0:T(8,128)S(1)}, f32[56,256]{1,0:T(8,128)}, u32[]{:S(2)}, u32[]{:S(2)}) collective-permute-start(f32[56,256]{1,0:T(8,128)S(1)} %get-tuple-element.83), channel_id=1, source_target_pairs={{8,9},{12,17},{16,29},{2,1},{6,5},{11,10},{14,13},{19,18},{22,21},... | collective-permute-start | bytes 172040 | tf_op jit(solution)/shard_map/cond/branch_3_fun/ppermute | solution.py:618
  14.8 7.4 %collective-permute-start.21 = (f32[56,256]{1,0:T(8,128)S(1)}, f32[56,256]{1,0:T(8,128)}, u32[]{:S(2)}, u32[]{:S(2)}) collective-permute-start(f32[56,256]{1,0:T(8,128)S(1)} %get-tuple-element.83), channel_id=1, source_target_pairs={{4,1},{8,5},{12,13},{16,21},{3,2},{7,6},{15,14},{23,22},{26,25}} | collective-permute-start | bytes 172040 | tf_op jit(solution)/shard_map/cond/branch_3_fun/ppermute | solution.py:618
  22.2 1.3 %collective-permute-start.27 = (f32[56,256]{1,0:T(8,128)S(1)}, f32[56,256]{1,0:T(8,128)}, u32[]{:S(2)}, u32[]{:S(2)}) collective-permute-start(f32[56,256]{1,0:T(8,128)S(1)} %get-tuple-element.85), channel_id=1, source_target_pairs={{12,27},{10,11},{18,19},{25,26},{30,31}} | collective-permute-start | bytes 172040 | tf_op jit(solution)/shard_map/cond/branch_3_fun/ppermute | solution.py:618
  23.5 8.5 %collective-permute-start.26 = (f32[56,256]{1,0:T(8,128)S(1)}, f32[56,256]{1,0:T(8,128)}, u32[]{:S(2)}, u32[]{:S(2)}) collective-permute-start(f32[56,256]{1,0:T(8,128)S(1)} %get-tuple-element.85), channel_id=1, source_target_pairs={{8,11},{12,19},{16,31},{2,3},{6,7},{9,10},{14,15},{17,18},{22,23},... | collective-permute-start | bytes 172040 | tf_op jit(solution)/shard_map/cond/branch_3_fun/ppermute | solution.py:618
  32.0 7.0 %collective-permute-start.25 = (f32[56,256]{1,0:T(8,128)S(1)}, f32[56,256]{1,0:T(8,128)}, u32[]{:S(2)}, u32[]{:S(2)}) collective-permute-start(f32[56,256]{1,0:T(8,128)S(1)} %get-tuple-element.85), channel_id=1, source_target_pairs={{4,3},{8,7},{12,15},{16,23},{1,2},{5,6},{13,14},{21,22},{26,27}} | collective-permute-start | bytes 172040 | tf_op jit(solution)/shard_map/cond/branch_3_fun/ppermute | solution.py:618
  39.0 2.1 %relay.1 = (f32[24,128]{1,0:T(8,128)}, f32[24,128]{1,0:T(8,128)}, f32[56,256]{1,0:T(8,128)}, f32[120,384]{1,0:T(8,128)}, f32[64,384]{1,0:T(8,128)}) custom-call(f32[10,24,384]{2,1,0:T(8,128)} %bitcast.10, f32[4,24,384]{2,1,0:T(8,128)} %bitcast.13, f32[56,256]{1,0:T(8,128)} %get-tuple-element.122.refs_2_, f32[56,256]{1,0:T(8,128)} %get-tuple-element.123.refs_3_, ...), custom_call_target="tpu_custom_call" | custom-call | tf_op jit(solution)/shard_map/relay/pallas_call | solution.py:628
  41.1 8.4 %collective-permute-start.106 = (f32[120,384]{1,0:T(8,128)}, f32[120,384]{1,0:T(8,128)S(1)}, u32[]{:S(2)}, u32[]{:S(2)}) collective-permute-start(f32[120,384]{1,0:T(8,128)} %get-tuple-element.132), channel_id=1, source_target_pairs={{0,4},{1,5},{2,6},{3,7},{4,0},{5,1},{6,2},{7,3},{8,12},{9,13},{10,... | collective-permute-start | bytes 552968 | tf_op jit(solution)/shard_map/ppermute | solution.py:649
  49.5 6.4 %collective-permute-start.107 = (f32[64,384]{1,0:T(8,128)}, f32[64,384]{1,0:T(8,128)S(1)}, u32[]{:S(2)}, u32[]{:S(2)}) collective-permute-start(f32[64,384]{1,0:T(8,128)} %get-tuple-element.133), channel_id=1, source_target_pairs={{4,8},{5,9},{6,10},{7,11},{8,4},{9,5},{10,6},{11,7},{12,16},{13,17... | collective-permute-start | bytes 294920 | tf_op jit(solution)/shard_map/ppermute | solution.py:648
  58.2 1.6 %nest.1 = (f32[10,24,384]{2,1,0:T(8,128)S(1)}, f32[80,128]{1,0:T(8,128)S(1)}) custom-call(s32[1]{0:T(128)} %copy.110.offset_ref, f32[10,24,384]{2,1,0:T(8,128)S(1)} %bitcast.11, f32[4,24,384]{2,1,0:T(8,128)S(1)} %bitcast.14, f32[24,128]{1,0:T(8,128)S(1)} %copy-done.3, f32[24,128]{1,0:T(8,128)S(1)} %copy-done.4, f32[56,256]{1,0:T(8,128)S(1)} %copy-done.2, ...), custom_call_target="tpu_custom_call" | custom-call | tf_op jit(solution)/shard_map/nest/pallas_call | solution.py:650
  59.8 12.6 %collective-permute-start.110 = (f32[80,128]{1,0:T(8,128)S(1)}, f32[80,128]{1,0:T(8,128)S(1)}, u32[]{:S(2)}, u32[]{:S(2)}) collective-permute-start(f32[80,128]{1,0:T(8,128)S(1)} %get-tuple-element.134), channel_id=1, source_target_pairs={{3,0},{7,4},{11,8},{15,12},{19,16},{23,20},{27,24},{31,28}} | collective-permute-start | bytes 122888 | tf_op jit(solution)/shard_map/ppermute | solution.py:668
  72.3 7.0 %collective-permute-start.109 = (f32[80,128]{1,0:T(8,128)S(1)}, f32[80,128]{1,0:T(8,128)S(1)}, u32[]{:S(2)}, u32[]{:S(2)}) collective-permute-start(f32[80,128]{1,0:T(8,128)S(1)} %get-tuple-element.134), channel_id=1, source_target_pairs={{2,0},{6,4},{10,8},{14,12},{18,16},{22,20},{26,24},{30,28}} | collective-permute-start | bytes 122888 | tf_op jit(solution)/shard_map/ppermute | solution.py:668
  79.4 6.4 %collective-permute-start.108 = (f32[80,128]{1,0:T(8,128)S(1)}, f32[80,128]{1,0:T(8,128)S(1)}, u32[]{:S(2)}, u32[]{:S(2)}) collective-permute-start(f32[80,128]{1,0:T(8,128)S(1)} %get-tuple-element.134), channel_id=1, source_target_pairs={{1,0},{5,4},{9,8},{13,12},{17,16},{21,20},{25,24},{29,28}} | collective-permute-start | bytes 122888 | tf_op jit(solution)/shard_map/ppermute | solution.py:668
  85.8 4.4 %collective-permute-done.108 = f32[80,128]{1,0:T(8,128)S(1)} collective-permute-done((f32[80,128]{1,0:T(8,128)S(1)}, f32[80,128]{1,0:T(8,128)S(1)}, u32[]{:S(2)}, u32[]{:S(2)}) %collective-permute-start.108) | collective-permute-done | bytes 40992 | tf_op jit(solution)/shard_map/ppermute | solution.py:668
  90.2 9.7 %conditional.3 = (f32[80,384]{1,0:T(8,128)}, f32[80,384]{1,0:T(8,128)}, f32[80,384]{1,0:T(8,128)}, f32[80,384]{1,0:T(8,128)}) conditional(s32[]{:T(128)} %clamp.6, f32[80,384]{1,0:T(8,128)S(1)} %pad_maximum_fusion, f32[80,384]{1,0:T(8,128)S(1)} %pad_maximum_fusion, f32[80,384]{1,0:T(8,128)S(1)} %pad_maximum_fusion, ...), branch_computations={%region_10.11_spmd, %region_11.12_spmd, %region_12.13_spmd, %regio... | conditional | bytes 1966272 | solution.py:677
  90.2 1.9 %collective-permute-start.81 = (f32[80,384]{1,0:T(8,128)S(1)}, f32[80,384]{1,0:T(8,128)}, u32[]{:S(2)}, u32[]{:S(2)}) collective-permute-start(f32[80,384]{1,0:T(8,128)S(1)} %param.12), channel_id=1, source_target_pairs={{0,4},{12,8},{24,12}} | collective-permute-start | bytes 368648 | tf_op jit(solution)/shard_map/cond/branch_2_fun/ppermute | solution.py:675
  92.2 1.3 %collective-permute-start.80 = (f32[80,384]{1,0:T(8,128)S(1)}, f32[80,384]{1,0:T(8,128)}, u32[]{:S(2)}, u32[]{:S(2)}) collective-permute-start(f32[80,384]{1,0:T(8,128)S(1)} %param.12), channel_id=1, source_target_pairs={{8,8},{20,12}} | collective-permute-start | bytes 368648 | tf_op jit(solution)/shard_map/cond/branch_2_fun/ppermute | solution.py:675
  93.5 1.3 %collective-permute-start.79 = (f32[80,384]{1,0:T(8,128)S(1)}, f32[80,384]{1,0:T(8,128)}, u32[]{:S(2)}, u32[]{:S(2)}) collective-permute-start(f32[80,384]{1,0:T(8,128)S(1)} %param.12), channel_id=1, source_target_pairs={{4,8},{16,12},{28,16}} | collective-permute-start | bytes 368648 | tf_op jit(solution)/shard_map/cond/branch_2_fun/ppermute | solution.py:675
  94.8 3.3 %collective-permute-start.78 = (f32[80,384]{1,0:T(8,128)S(1)}, f32[80,384]{1,0:T(8,128)}, u32[]{:S(2)}, u32[]{:S(2)}) collective-permute-start(f32[80,384]{1,0:T(8,128)S(1)} %param.12), channel_id=1, source_target_pairs={{0,8},{12,12},{24,16}} | collective-permute-start | bytes 368648 | tf_op jit(solution)/shard_map/cond/branch_2_fun/ppermute | solution.py:675
  98.2 1.8 %collective-permute-done.78 = f32[80,384]{1,0:T(8,128)} collective-permute-done((f32[80,384]{1,0:T(8,128)S(1)}, f32[80,384]{1,0:T(8,128)}, u32[]{:S(2)}, u32[]{:S(2)}) %collective-permute-start.78) | collective-permute-done | bytes 122912 | tf_op jit(solution)/shard_map/cond/branch_2_fun/ppermute | solution.py:675
  99.9 1.9 %merge.1 = f32[10,24,384]{2,1,0:T(8,128)} custom-call(s32[1]{0:T(128)} %copy.110.offset_ref, f32[80,384]{1,0:T(8,128)} %get-tuple-element.135.first_ref, f32[80,384]{1,0:T(8,128)} %get-tuple-element.136.second_ref, f32[80,384]{1,0:T(8,128)} %get-tuple-element.137.third_ref, f32[80,384]{1,0:T(8,128)} %get-tuple-element.138.fourth_ref, ...), custom_call_target="tpu_custom_call" | custom-call | tf_op jit(solution)/shard_map/merge/pallas_call | solution.py:682
  (25 shorter events, 2.3 us)
Async XLA Ops:
  2.2 21.3 %collective-permute-start.24 = (f32[56,256]{1,0:T(8,128)S(1)}, f32[56,256]{1,0:T(8,128)}, u32[]{:S(2)}, u32[]{:S(2)}) collective-permute-start(f32[56,256]{1,0:T(8,128)S(1)} %get-tuple-element.84), channel_id=1, source_target_pairs={{4,2},{8,6},{12,26},{16,30}} | collective-permute-start | bytes 172040 | tf_op jit(solution)/shard_map/cond/branch_3_fun/ppermute | solution.py:618
  3.5 28.5 %collective-permute-start.23 = (f32[56,256]{1,0:T(8,128)S(1)}, f32[56,256]{1,0:T(8,128)}, u32[]{:S(2)}, u32[]{:S(2)}) collective-permute-start(f32[56,256]{1,0:T(8,128)S(1)} %get-tuple-element.83), channel_id=1, source_target_pairs={{12,25},{10,9},{18,17},{27,26},{30,29}} | collective-permute-start | bytes 172040 | tf_op jit(solution)/shard_map/cond/branch_3_fun/ppermute | solution.py:618
  4.8 34.2 %collective-permute-start.22 = (f32[56,256]{1,0:T(8,128)S(1)}, f32[56,256]{1,0:T(8,128)}, u32[]{:S(2)}, u32[]{:S(2)}) collective-permute-start(f32[56,256]{1,0:T(8,128)S(1)} %get-tuple-element.83), channel_id=1, source_target_pairs={{8,9},{12,17},{16,29},{2,1},{6,5},{11,10},{14,13},{19,18},{22,21},... | collective-permute-start | bytes 172040 | tf_op jit(solution)/shard_map/cond/branch_3_fun/ppermute | solution.py:618
  14.8 24.2 %collective-permute-start.21 = (f32[56,256]{1,0:T(8,128)S(1)}, f32[56,256]{1,0:T(8,128)}, u32[]{:S(2)}, u32[]{:S(2)}) collective-permute-start(f32[56,256]{1,0:T(8,128)S(1)} %get-tuple-element.83), channel_id=1, source_target_pairs={{4,1},{8,5},{12,13},{16,21},{3,2},{7,6},{15,14},{23,22},{26,25}} | collective-permute-start | bytes 172040 | tf_op jit(solution)/shard_map/cond/branch_3_fun/ppermute | solution.py:618
  22.2 16.8 %collective-permute-start.27 = (f32[56,256]{1,0:T(8,128)S(1)}, f32[56,256]{1,0:T(8,128)}, u32[]{:S(2)}, u32[]{:S(2)}) collective-permute-start(f32[56,256]{1,0:T(8,128)S(1)} %get-tuple-element.85), channel_id=1, source_target_pairs={{12,27},{10,11},{18,19},{25,26},{30,31}} | collective-permute-start | bytes 172040 | tf_op jit(solution)/shard_map/cond/branch_3_fun/ppermute | solution.py:618
  23.5 15.5 %collective-permute-start.26 = (f32[56,256]{1,0:T(8,128)S(1)}, f32[56,256]{1,0:T(8,128)}, u32[]{:S(2)}, u32[]{:S(2)}) collective-permute-start(f32[56,256]{1,0:T(8,128)S(1)} %get-tuple-element.85), channel_id=1, source_target_pairs={{8,11},{12,19},{16,31},{2,3},{6,7},{9,10},{14,15},{17,18},{22,23},... | collective-permute-start | bytes 172040 | tf_op jit(solution)/shard_map/cond/branch_3_fun/ppermute | solution.py:618
  32.0 7.0 %collective-permute-start.25 = (f32[56,256]{1,0:T(8,128)S(1)}, f32[56,256]{1,0:T(8,128)}, u32[]{:S(2)}, u32[]{:S(2)}) collective-permute-start(f32[56,256]{1,0:T(8,128)S(1)} %get-tuple-element.85), channel_id=1, source_target_pairs={{4,3},{8,7},{12,15},{16,23},{1,2},{5,6},{13,14},{21,22},{26,27}} | collective-permute-start | bytes 172040 | tf_op jit(solution)/shard_map/cond/branch_3_fun/ppermute | solution.py:618
  39.0 16.9 %copy-start = (f32[5,2,24,384]{3,2,1,0:T(8,128)S(1)}, f32[5,2,24,384]{3,2,1,0:T(8,128)}, u32[]{:S(2)}) copy-start(f32[5,2,24,384]{3,2,1,0:T(8,128)} %param.22) | copy-start | bytes 1105924
  39.0 16.9 %copy-start.1 = (f32[2,2,24,384]{3,2,1,0:T(8,128)S(1)}, f32[2,2,24,384]{3,2,1,0:T(8,128)}, u32[]{:S(2)}) copy-start(f32[2,2,24,384]{3,2,1,0:T(8,128)} %param.23) | copy-start | bytes 442372
  41.1 14.8 %collective-permute-start.106 = (f32[120,384]{1,0:T(8,128)}, f32[120,384]{1,0:T(8,128)S(1)}, u32[]{:S(2)}, u32[]{:S(2)}) collective-permute-start(f32[120,384]{1,0:T(8,128)} %get-tuple-element.132), channel_id=1, source_target_pairs={{0,4},{1,5},{2,6},{3,7},{4,0},{5,1},{6,2},{7,3},{8,12},{9,13},{10,... | collective-permute-start | bytes 552968 | tf_op jit(solution)/shard_map/ppermute | solution.py:649
  49.5 6.4 %collective-permute-start.107 = (f32[64,384]{1,0:T(8,128)}, f32[64,384]{1,0:T(8,128)S(1)}, u32[]{:S(2)}, u32[]{:S(2)}) collective-permute-start(f32[64,384]{1,0:T(8,128)} %get-tuple-element.133), channel_id=1, source_target_pairs={{4,8},{5,9},{6,10},{7,11},{8,4},{9,5},{10,6},{11,7},{12,16},{13,17... | collective-permute-start | bytes 294920 | tf_op jit(solution)/shard_map/ppermute | solution.py:648
  56.0 0.8 copy-start.2
  56.8 0.7 copy-start.3
  57.5 0.7 copy-start.4
  59.8 26.0 %collective-permute-start.110 = (f32[80,128]{1,0:T(8,128)S(1)}, f32[80,128]{1,0:T(8,128)S(1)}, u32[]{:S(2)}, u32[]{:S(2)}) collective-permute-start(f32[80,128]{1,0:T(8,128)S(1)} %get-tuple-element.134), channel_id=1, source_target_pairs={{3,0},{7,4},{11,8},{15,12},{19,16},{23,20},{27,24},{31,28}} | collective-permute-start | bytes 122888 | tf_op jit(solution)/shard_map/ppermute | solution.py:668
  72.3 13.4 %collective-permute-start.109 = (f32[80,128]{1,0:T(8,128)S(1)}, f32[80,128]{1,0:T(8,128)S(1)}, u32[]{:S(2)}, u32[]{:S(2)}) collective-permute-start(f32[80,128]{1,0:T(8,128)S(1)} %get-tuple-element.134), channel_id=1, source_target_pairs={{2,0},{6,4},{10,8},{14,12},{18,16},{22,20},{26,24},{30,28}} | collective-permute-start | bytes 122888 | tf_op jit(solution)/shard_map/ppermute | solution.py:668
  79.4 10.8 %collective-permute-start.108 = (f32[80,128]{1,0:T(8,128)S(1)}, f32[80,128]{1,0:T(8,128)S(1)}, u32[]{:S(2)}, u32[]{:S(2)}) collective-permute-start(f32[80,128]{1,0:T(8,128)S(1)} %get-tuple-element.134), channel_id=1, source_target_pairs={{1,0},{5,4},{9,8},{13,12},{17,16},{21,20},{25,24},{29,28}} | collective-permute-start | bytes 122888 | tf_op jit(solution)/shard_map/ppermute | solution.py:668
  90.2 7.9 %collective-permute-start.81 = (f32[80,384]{1,0:T(8,128)S(1)}, f32[80,384]{1,0:T(8,128)}, u32[]{:S(2)}, u32[]{:S(2)}) collective-permute-start(f32[80,384]{1,0:T(8,128)S(1)} %param.12), channel_id=1, source_target_pairs={{0,4},{12,8},{24,12}} | collective-permute-start | bytes 368648 | tf_op jit(solution)/shard_map/cond/branch_2_fun/ppermute | solution.py:675
  92.2 6.0 %collective-permute-start.80 = (f32[80,384]{1,0:T(8,128)S(1)}, f32[80,384]{1,0:T(8,128)}, u32[]{:S(2)}, u32[]{:S(2)}) collective-permute-start(f32[80,384]{1,0:T(8,128)S(1)} %param.12), channel_id=1, source_target_pairs={{8,8},{20,12}} | collective-permute-start | bytes 368648 | tf_op jit(solution)/shard_map/cond/branch_2_fun/ppermute | solution.py:675
  93.5 4.7 %collective-permute-start.79 = (f32[80,384]{1,0:T(8,128)S(1)}, f32[80,384]{1,0:T(8,128)}, u32[]{:S(2)}, u32[]{:S(2)}) collective-permute-start(f32[80,384]{1,0:T(8,128)S(1)} %param.12), channel_id=1, source_target_pairs={{4,8},{16,12},{28,16}} | collective-permute-start | bytes 368648 | tf_op jit(solution)/shard_map/cond/branch_2_fun/ppermute | solution.py:675
  94.8 5.1 %collective-permute-start.78 = (f32[80,384]{1,0:T(8,128)S(1)}, f32[80,384]{1,0:T(8,128)}, u32[]{:S(2)}, u32[]{:S(2)}) collective-permute-start(f32[80,384]{1,0:T(8,128)S(1)} %param.12), channel_id=1, source_target_pairs={{0,8},{12,12},{24,16}} | collective-permute-start | bytes 368648 | tf_op jit(solution)/shard_map/cond/branch_2_fun/ppermute | solution.py:675

commit v2 on v1

--- a/solution.py
+++ b/solution.py
@@ -187,8 +187,10 @@
 STATES = 10
 PLANES = 14
 SLOTS = 4 * PLANES
+HALO = SLOTS + 8
 NEST_MARK = 1.0
 PARENT_MARK = 2.0
+RIMS = 3 * ROWS
 EXACT = lax.Precision.HIGHEST
 
 
@@ -249,7 +251,7 @@
         axis=0,
     )
     lane = iota((SLOTS, LANE), 1)
-    mark = jnp.where(section == 0, PARENT_MARK, NEST_MARK)
+    mark = jnp.where(section == 0, PARENT_MARK + tile.astype(jnp.float32), NEST_MARK)
     blank = jnp.zeros((SLOTS, LANE), jnp.float32)
     outs = ((west_ref, left), (middle_ref, left), (east_ref, right))
     for s, (out_ref, edge) in enumerate(outs):
@@ -264,26 +266,39 @@
         out_ref[ROWS:, LANE:] = side[ROWS:]
 
 
-def relay_kernel(*refs):
-    state_ref, courant_ref = refs[:2]
-    to_west, to_middle, to_east = refs[2:5], refs[5:6], refs[6:9]
-    west_ref, east_ref, rims_ref, pair_ref, cross_ref = refs[9:]
-    even = lax.axis_index("tile") % 2 == 0
+def first_source(offset, tile):
+    return jnp.maximum((offset - 2) // ROWS, 1) - 1 + jnp.minimum(tile // 2, 2)
+
+
+def relay_kernel(offset_ref, state_ref, courant_ref, *refs):
+    to_west, middle, to_east = refs[:3], refs[3], refs[4:7]
+    west_ref, east_ref, rims_ref, pair_ref, cross_ref = refs[7:]
+    tile = lax.axis_index("tile")
+    even = tile % 2 == 0
+    source = first_source(offset_ref[0], tile).astype(jnp.float32) + PARENT_MARK
+    lane = iota((ROWS, LANE), 1)
 
     def marked(sources, mark):
-        total = None
+        total = jnp.zeros((ROWS, LANE), jnp.float32)
         for ref in sources:
-            value = ref[...]
-            value = jnp.where(value[:, 2 * LANE - 1 :] == mark, value, 0.0)
-            total = value if total is None else total + value
-        return total
-
-    east = marked(to_west, NEST_MARK)[:ROWS, LANE:]
-    west = marked(to_east, NEST_MARK)[:ROWS, LANE:]
-    rims = marked(to_west + to_middle + to_east, PARENT_MARK)
+            total += jnp.where(ref[:ROWS, 2 * LANE - 1 :] == mark, ref[:ROWS, LANE:], 0.0)
+        return jnp.where(lane < 42, total, 0.0)
+
+    east = marked(to_west, NEST_MARK)
+    west = marked(to_east, NEST_MARK)
     west_ref[...] = west
     east_ref[...] = east
-    rims_ref[...] = rims
+    rows = middle[...]
+    for ref in to_west + to_east:
+        value = ref[...]
+        rows += jnp.where(value[:, 2 * LANE - 1 :] >= PARENT_MARK, value, 0.0)
+    wide = iota((SLOTS, LANE), 1)
+    rims_ref[:SLOTS, :LANE] = rows[:, :LANE]
+    rims_ref[SLOTS:, :LANE] = jnp.zeros((RIMS - SLOTS, LANE), jnp.float32)
+    extra = jnp.where((wide >= 42) & (wide < 46), rows[:, LANE:], 0.0)
+    extra = jnp.concatenate([extra, jnp.zeros((RIMS - SLOTS, LANE), jnp.float32)], axis=0)
+    edges = [marked(to_west + to_east, source + slot) for slot in range(3)]
+    rims_ref[:, LANE:] = jnp.concatenate(edges, axis=0) + extra
 
     def put(rows, lanes, value):
         head, tail = value[:4], value[ROWS - 4 :]
@@ -294,7 +309,8 @@
         put(slice(4 * p, 4 * p + 4), slice(None), plane_of(state_ref, courant_ref, p))
     put(slice(SLOTS, SLOTS + 4), slice(0, LANE), west)
     put(slice(SLOTS, SLOTS + 4), slice(LANE, 2 * LANE), east)
-    pair_ref[SLOTS + 8 :, : 2 * LANE] = rims
+    pair_ref[HALO:, : 2 * LANE] = rims_ref[...]
+    cross_ref[HALO:, :LANE] = edges[0]
 
 
 def flux(value, south, north, west, east, other, cy, cx):
@@ -333,8 +349,8 @@
     is_nest = section > 0
     full = (32, 4 * LANE)
 
-    after = jnp.where(even, pair_ref[: SLOTS + 8], cross_ref[...])
-    before = jnp.where(even, cross_ref[...], pair_ref[: SLOTS + 8])
+    after = jnp.where(even, pair_ref[:HALO], cross_ref[:HALO])
+    before = jnp.where(even, cross_ref[:HALO], pair_ref[:HALO])
     wests = jnp.concatenate(
         [west_ref[...], after[SLOTS : SLOTS + 4, :LANE], before[SLOTS : SLOTS + 4, :LANE]], axis=0
     )
@@ -398,21 +414,20 @@
 
     base_force[...] = jnp.zeros(base_force.shape, jnp.float32)
     step_force[...] = jnp.zeros(step_force.shape, jnp.float32)
-    other_rims = pair_ref[SLOTS + 8 :, : 2 * LANE]
-    lower = jnp.where(even, rims_ref[...], other_rims)
-    upper = jnp.where(even, other_rims, rims_ref[...])
+    rims = rims_ref[...] + pair_ref[HALO:, : 2 * LANE]
 
     @pl.when((section == 1) | (section == 3))
     def _():
         on_left = section == 1
-        edges = jnp.concatenate([lower[:ROWS, LANE:], upper[:ROWS, LANE:]], axis=0)
-        source_tile = ((offset - 2) // 8 + (tile // 2) * 2) // 3
-        pick = iota((96, 2 * ROWS), 0)
+        before_six = jnp.where(tile == 6, cross_ref[HALO:, :LANE], 0.0)
+        edges = jnp.concatenate([rims[:ROWS, LANE:] + before_six, rims[ROWS:, LANE:]], axis=0)
+        source_tile = first_source(offset, tile)
+        pick = iota((96, RIMS), 0)
         part = pick >> 5
         near = pick & 31
         near = jnp.where(near < 28, near, near - 32)
         coarse = offset + tile * 8 + third(near + 6) - 2 + part - 1 - source_tile * ROWS
-        picked = dot((iota((96, 2 * ROWS), 1) == coarse).astype(jnp.float32), edges)
+        picked = dot((iota((96, RIMS), 1) == coarse).astype(jnp.float32), edges)
         south, value, north = picked[:32], picked[32:64], picked[64:]
         place = lane - 3 * third(lane)
         west = jnp.where(place == jnp.where(on_left, 0, -1), value, turn(value, 1, 1))
@@ -449,7 +464,7 @@
 
     @pl.when(is_nest & ((tile == 0) | (tile == 7)))
     def _():
-        rows = lower + upper
+        rows = rims[:SLOTS]
         wide = iota((8, 2 * LANE), 1)
         narrow = iota((SLOTS, LANE), 1)
         outside = turn(rows[:, LANE:], 84, 1)
@@ -560,41 +575,60 @@
     return jax.ShapeDtypeStruct(shape, jnp.float32)
 
 
+def in_rounds(edges, count):
+    at = {}
+    for source, target in edges:
+        mine, theirs = ("from", source), ("to", target)
+        a = next(c for c in range(count) if (mine, c) not in at)
+        b = next(c for c in range(count) if (theirs, c) not in at)
+        path = []
+        node, color = theirs, a
+        while (node, color) in at:
+            node_next = at[(node, color)]
+            path.append((node, node_next, color))
+            node, color = node_next, (b if color == a else a)
+        for one, two, color in path:
+            del at[(one, color)], at[(two, color)]
+        for one, two, color in path:
+            swapped = b if color == a else a
+            at[(one, swapped)] = two
+            at[(two, swapped)] = one
+        at[(mine, a)] = theirs
+        at[(theirs, a)] = mine
+    rounds = [[] for _ in range(count)]
+    for (node, color), other in sorted(at.items()):
+        if node[0] == "from":
+            rounds[color].append((node[1], other[1]))
+    return rounds
+
+
 def rim_pairs(start):
+    to_chips = [(0, 0), (1, 1), (0, 2), (1, 3), (2, 3), (2, 4), (1, 5), (3, 4), (2, 6), (3, 7)]
+    sends = [(start + step, tile) for step, tile in to_chips]
+    middle = [[(start, 0), (start + 1, 1), (start + 2, 6), (start + 3, 7)]]
+    if start == 1:
+        sends.append((0, 0))
+        middle.append([(0, 0)])
     groups = []
     for section, inner in ((1, ((2, 1), (3, 2))), (3, ((1, 2), (2, 3)))):
-        lists = [[], [], []]
-        sent = {}
-        taken = {}
-        for chip in range(4):
-            source = (start + 2 * chip) // 3
-            for core in range(2):
-                color = sent.get(source + core, 0)
-                sent[source + core] = color + 1
-                taken[2 * chip + core] = color
-                lists[color].append((device(source + core, 0), device(2 * chip + core, section)))
-        for tile in range(8):
-            for origin, target in inner:
-                color = (taken[tile] + 1) % 3 if target == section else taken[tile]
-                lists[color].append((device(tile, origin), device(tile, target)))
-        groups.append(lists)
-    middle = []
-    for chip in (0, 3):
-        source = (start + 2 * chip) // 3
-        middle += [(device(source + core, 0), device(2 * chip + core, 2)) for core in range(2)]
-    return groups[0], [middle], groups[1]
-
-
-def mean_pairs(start):
-    lists = []
-    for step in range(4):
-        pairs = []
-        for tile in range(8):
-            source = 3 * tile - start - 1 + step
-            if 0 <= source < 8:
-                pairs.append((device(source, 0), device(tile, 0)))
-        lists.append(pairs)
-    return lists
+        edges = [(device(a, 0), device(b, section)) for a, b in sends]
+        edges += [(device(t, a), device(t, b)) for t in range(8) for a, b in inner]
+        groups.append(in_rounds(edges, 3))
+    middle = [[(device(a, 0), device(b, 2)) for a, b in pairs] for pairs in middle]
+    return groups[0], middle, groups[1]
+
+
+TOGETHER = ((1, 8), (2, 10), (3, 11), (4, 12), (5,), (6,), (7,), (9,))
+
+
+def mean_pairs(distance):
+    (group,) = [g for g in TOGETHER if distance in g]
+    return [
+        (device(3 * tile - step, 0), device(tile, 0))
+        for step in group
+        for tile in range(8)
+        if 0 <= 3 * tile - step < 8
+    ]
 
 
 BOTH = ("tile", "section")
@@ -614,15 +648,15 @@
 
     def send_rims(start, west, middle, east):
         groups = rim_pairs(start)
-        return tuple(
-            lax.ppermute(value, BOTH, pairs)
+        west, middle, east = (
+            [lax.ppermute(value, BOTH, pairs) for pairs in lists]
             for value, lists in zip((west, middle, east), groups)
-            for pairs in lists
         )
+        return (*west, sum(middle), *east)
 
     received = lax.switch(
-        (offset - 2) // 8 - 2,
-        [functools.partial(send_rims, start) for start in range(2, 12)],
+        (offset - 2) // ROWS - 1,
+        [functools.partial(send_rims, start) for start in (1, 2, 3)],
         *payloads,
     )
     west, east, rims, to_pair, to_cross = pl.pallas_call(
@@ -630,14 +664,14 @@
         out_shape=[
             shaped(ROWS, LANE),
             shaped(ROWS, LANE),
-            shaped(SLOTS, 2 * LANE),
-            shaped(2 * SLOTS + 8, COLS),
-            shaped(SLOTS + 8, COLS),
+            shaped(RIMS, 2 * LANE),
+            shaped(HALO + RIMS, COLS),
+            shaped(HALO + ROWS, COLS),
         ],
-        in_specs=[VMEM] * 9,
+        in_specs=[SMEM] + [VMEM] * 9,
         out_specs=[VMEM] * 5,
         name="relay",
-    )(planes, speeds, *received)
+    )(nest_offset, planes, speeds, *received)
     pair_map = [(device(t, s), device(t ^ 1, s)) for t in range(8) for s in range(4)]
     cross_map = [
         (device(a, s), device(b, s))
@@ -672,7 +706,7 @@
     )
 
     def send_means(start, value):
-        return tuple(lax.ppermute(value, BOTH, pairs) for pairs in mean_pairs(start))
+        return tuple(lax.ppermute(value, BOTH, mean_pairs(start + 1 - j)) for j in range(4))
 
     blocks = lax.switch(
         offset // 8 - 3,

time: 103 us -> 60.7 us (0.59)
  the two profiles are of different devices: /device:TPU:0 before, /device:TPU:4 now
where the time goes in v2:
time: 60.7 us; the launch traced here: 60.3 us
  starting transfers between devices  32 us (53%)
  waiting for transfers between devices  18 us (30%)
  Pallas kernels  7.18 us (12%)
  local copies, waits for them, and re-layouts  2.3 us (4%)
  between operations  0.76 us (1%)
    ppermute x7, starting transfers between devices, send_rims(): lax.ppermute(value, BOTH, pairs)  18.2 us
    ppermute x4, starting transfers between devices, send_means(): lax.ppermute(value, BOTH, mean_pairs(start + 1 - j))  8 us
    ppermute x3, waiting for transfers between devices, on_device(): lax.ppermute(means, BOTH, [(device(t, s), device(t, 0)) for t in range(8)])  6.73 us
    ppermute x1, waiting for transfers between devices, on_device(): from_cross = lax.ppermute(to_cross, BOTH, cross_map)  5.51 us
    ppermute x4, waiting for transfers between devices, send_means(): lax.ppermute(value, BOTH, mean_pairs(start + 1 - j))  4.37 us
    ppermute x3, starting transfers between devices, on_device(): lax.ppermute(means, BOTH, [(device(t, s), device(t, 0)) for t in range(8)])  3.88 us
    unnamed x10, local copies, waits for them, and re-layouts  2.3 us
    pallas_call x1, Pallas kernels, on_device(): pl.pallas_call(relay_kernel, out_shape=[shaped(ROWS, LANE), shaped(ROWS,...  2.16 us
  transfers between devices with their start and end apart: 16, of which 6 were waited for; matrix products, arithmetic and copies ran while one was open for 0% of the time, Pallas kernels for 0%

profile of v2, /device:TPU:4, one launch (start us, length us, event | category | flops | bytes accessed | tf_op | source)
XLA Modules:
  0.0 60.3 jit_solution(3549423755131027618)
XLA Ops:
  0.7 1.5 %pack.1 = (f32[56,256]{1,0:T(8,128)S(1)}, f32[56,256]{1,0:T(8,128)S(1)}, f32[56,256]{1,0:T(8,128)S(1)}) custom-call(s32[1]{0:T(128)} %copy.61.offset_ref, f32[10,24,384]{2,1,0:T(8,128)} %bitcast.9, f32[4,24,384]{2,1,0:T(8,128)} %bitcast.12), custom_call_target="tpu_custom_call" | custom-call | tf_op jit(solution)/shard_map/pack/pallas_call | solution.py:641
  2.2 19.6 %conditional.2 = (f32[56,256]{1,0:T(8,128)}, f32[56,256]{1,0:T(8,128)}, f32[56,256]{1,0:T(8,128)}, f32[56,256]{1,0:T(8,128)}, f32[56,256]{1,0:T(8,128)}, /*index=5*/f32[56,256]{1,0:T(8,128)}, f32[56,256]{1,0:T(8,128)}) conditional(s32[]{:T(128)} %clamp.7, (f32[56,256]{1,0:T(8,128)S(1)}, f32[56,256]{1,0:T(8,128)S(1)}, ...), branch_computations={%region_0.1_spmd, %region_1.2_spmd, %region_2.3_spmd} | conditional | flops 14336 | bytes 2007416 | solution.py:657
  2.2 4.5 %collective-permute-start.18 = (f32[56,256]{1,0:T(8,128)S(1)}, f32[56,256]{1,0:T(8,128)}, u32[]{:S(2)}, u32[]{:S(2)}) collective-permute-start(f32[56,256]{1,0:T(8,128)S(1)} %get-tuple-element.39), channel_id=1, source_target_pairs={{12,2},{16,6},{20,26},{24,30}} | collective-permute-start | bytes 172040 | tf_op jit(solution)/shard_map/cond/branch_2_fun/ppermute | solution.py:652
  6.7 1.9 %collective-permute-start.17 = (f32[56,256]{1,0:T(8,128)S(1)}, f32[56,256]{1,0:T(8,128)}, u32[]{:S(2)}, u32[]{:S(2)}) collective-permute-start(f32[56,256]{1,0:T(8,128)S(1)} %get-tuple-element.38), channel_id=1, source_target_pairs={{16,13},{20,17}} | collective-permute-start | bytes 172040 | tf_op jit(solution)/shard_map/cond/branch_2_fun/ppermute | solution.py:652
  8.6 1.9 %collective-permute-start.16 = (f32[56,256]{1,0:T(8,128)S(1)}, f32[56,256]{1,0:T(8,128)}, u32[]{:S(2)}, u32[]{:S(2)}) collective-permute-start(f32[56,256]{1,0:T(8,128)S(1)} %get-tuple-element.38), channel_id=1, source_target_pairs={{2,1},{6,5},{12,9},{14,13},{16,21},{18,17},{20,25},{24,29}} | collective-permute-start | bytes 172040 | tf_op jit(solution)/shard_map/cond/branch_2_fun/ppermute | solution.py:652
  10.5 1.9 %collective-permute-start.15 = (f32[56,256]{1,0:T(8,128)S(1)}, f32[56,256]{1,0:T(8,128)}, u32[]{:S(2)}, u32[]{:S(2)}) collective-permute-start(f32[56,256]{1,0:T(8,128)S(1)} %get-tuple-element.38), channel_id=1, source_target_pairs={{3,2},{7,6},{10,9},{11,10},{12,1},{15,14},{16,5},{19,18},{20,13},{... | collective-permute-start | bytes 172040 | tf_op jit(solution)/shard_map/cond/branch_2_fun/ppermute | solution.py:652
  12.4 4.2 %collective-permute-start.21 = (f32[56,256]{1,0:T(8,128)S(1)}, f32[56,256]{1,0:T(8,128)}, u32[]{:S(2)}, u32[]{:S(2)}) collective-permute-start(f32[56,256]{1,0:T(8,128)S(1)} %get-tuple-element.40), channel_id=1, source_target_pairs={{16,15},{20,19}} | collective-permute-start | bytes 172040 | tf_op jit(solution)/shard_map/cond/branch_2_fun/ppermute | solution.py:652
  16.6 1.9 %collective-permute-start.20 = (f32[56,256]{1,0:T(8,128)S(1)}, f32[56,256]{1,0:T(8,128)}, u32[]{:S(2)}, u32[]{:S(2)}) collective-permute-start(f32[56,256]{1,0:T(8,128)S(1)} %get-tuple-element.40), channel_id=1, source_target_pairs={{2,3},{6,7},{12,11},{14,15},{16,23},{18,19},{20,27},{24,31}} | collective-permute-start | bytes 172040 | tf_op jit(solution)/shard_map/cond/branch_2_fun/ppermute | solution.py:652
  18.5 1.9 %collective-permute-start.19 = (f32[56,256]{1,0:T(8,128)S(1)}, f32[56,256]{1,0:T(8,128)}, u32[]{:S(2)}, u32[]{:S(2)}) collective-permute-start(f32[56,256]{1,0:T(8,128)S(1)} %get-tuple-element.40), channel_id=1, source_target_pairs={{1,2},{5,6},{9,10},{10,11},{12,3},{13,14},{16,7},{17,18},{20,15},{... | collective-permute-start | bytes 172040 | tf_op jit(solution)/shard_map/cond/branch_2_fun/ppermute | solution.py:652
  20.5 1.3 %collective-permute-done.19 = f32[56,256]{1,0:T(8,128)} collective-permute-done((f32[56,256]{1,0:T(8,128)S(1)}, f32[56,256]{1,0:T(8,128)}, u32[]{:S(2)}, u32[]{:S(2)}) %collective-permute-start.19) | collective-permute-done | bytes 57376 | tf_op jit(solution)/shard_map/cond/branch_2_fun/ppermute | solution.py:652
  21.8 2.2 %relay.1 = (f32[24,128]{1,0:T(8,128)}, f32[24,128]{1,0:T(8,128)}, f32[72,256]{1,0:T(8,128)}, f32[136,384]{1,0:T(8,128)}, f32[88,384]{1,0:T(8,128)}) custom-call(s32[1]{0:T(128)} %copy.61.offset_ref, f32[10,24,384]{2,1,0:T(8,128)} %bitcast.10, f32[4,24,384]{2,1,0:T(8,128)} %bitcast.13, f32[56,256]{1,0:T(8,128)} %get-tuple-element.59.refs_0_, ...), custom_call_target="tpu_custom_call" | custom-call | tf_op jit(solution)/shard_map/relay/pallas_call | solution.py:662
  24.0 1.9 %collective-permute-start.59 = (f32[88,384]{1,0:T(8,128)}, f32[88,384]{1,0:T(8,128)S(1)}, u32[]{:S(2)}, u32[]{:S(2)}) collective-permute-start(f32[88,384]{1,0:T(8,128)} %get-tuple-element.70), channel_id=1, source_target_pairs={{4,8},{5,9},{6,10},{7,11},{8,4},{9,5},{10,6},{11,7},{12,16},{13,17... | collective-permute-start | bytes 405512 | tf_op jit(solution)/shard_map/ppermute | solution.py:682
  25.9 5.5 %collective-permute-done.59.cross_ref = f32[88,384]{1,0:T(8,128)S(1)} collective-permute-done((f32[88,384]{1,0:T(8,128)}, f32[88,384]{1,0:T(8,128)S(1)}, u32[]{:S(2)}, u32[]{:S(2)}) %collective-permute-start.59) | collective-permute-done | bytes 135200 | tf_op jit(solution)/shard_map/ppermute | solution.py:682
  33.7 1.6 %nest.1 = (f32[10,24,384]{2,1,0:T(8,128)S(1)}, f32[80,128]{1,0:T(8,128)S(1)}) custom-call(s32[1]{0:T(128)} %copy.61.offset_ref, f32[10,24,384]{2,1,0:T(8,128)S(1)} %bitcast.11, f32[4,24,384]{2,1,0:T(8,128)S(1)} %bitcast.14, f32[24,128]{1,0:T(8,128)S(1)} %copy-done.3, f32[24,128]{1,0:T(8,128)S(1)} %copy-done.4, f32[72,256]{1,0:T(8,128)S(1)} %copy-done.2, ...), custom_call_target="tpu_custom_call" | custom-call | tf_op jit(solution)/shard_map/nest/pallas_call | solution.py:684
  35.3 1.3 %collective-permute-start.62 = (f32[80,128]{1,0:T(8,128)S(1)}, f32[80,128]{1,0:T(8,128)S(1)}, u32[]{:S(2)}, u32[]{:S(2)}) collective-permute-start(f32[80,128]{1,0:T(8,128)S(1)} %get-tuple-element.71), channel_id=1, source_target_pairs={{3,0},{7,4},{11,8},{15,12},{19,16},{23,20},{27,24},{31,28}} | collective-permute-start | bytes 122888 | tf_op jit(solution)/shard_map/ppermute | solution.py:702
  36.6 1.3 %collective-permute-start.61 = (f32[80,128]{1,0:T(8,128)S(1)}, f32[80,128]{1,0:T(8,128)S(1)}, u32[]{:S(2)}, u32[]{:S(2)}) collective-permute-start(f32[80,128]{1,0:T(8,128)S(1)} %get-tuple-element.71), channel_id=1, source_target_pairs={{2,0},{6,4},{10,8},{14,12},{18,16},{22,20},{26,24},{30,28}} | collective-permute-start | bytes 122888 | tf_op jit(solution)/shard_map/ppermute | solution.py:702
  39.2 6.7 %collective-permute-done.62 = f32[80,128]{1,0:T(8,128)S(1)} collective-permute-done((f32[80,128]{1,0:T(8,128)S(1)}, f32[80,128]{1,0:T(8,128)S(1)}, u32[]{:S(2)}, u32[]{:S(2)}) %collective-permute-start.62) | collective-permute-done | bytes 40992 | tf_op jit(solution)/shard_map/ppermute | solution.py:702
  46.0 12.4 %conditional.3 = (f32[80,384]{1,0:T(8,128)}, f32[80,384]{1,0:T(8,128)}, f32[80,384]{1,0:T(8,128)}, f32[80,384]{1,0:T(8,128)}) conditional(s32[]{:T(128)} %clamp.6, f32[80,384]{1,0:T(8,128)S(1)} %pad_maximum_fusion, f32[80,384]{1,0:T(8,128)S(1)} %pad_maximum_fusion, f32[80,384]{1,0:T(8,128)S(1)} %pad_maximum_fusion, ...), branch_computations={%region_3.4_spmd, %region_4.5_spmd, %region_5.6_spmd, %region_6.7_... | conditional | bytes 1966272 | solution.py:711
  46.0 1.3 %collective-permute-start.53 = (f32[80,384]{1,0:T(8,128)S(1)}, f32[80,384]{1,0:T(8,128)}, u32[]{:S(2)}, u32[]{:S(2)}) collective-permute-start(f32[80,384]{1,0:T(8,128)S(1)} %param.10), channel_id=1, source_target_pairs={{8,4},{20,8},{4,12},{16,16},{28,20}} | collective-permute-start | bytes 368648 | tf_op jit(solution)/shard_map/cond/branch_7_fun/ppermute | solution.py:709
  48.6 3.5 %collective-permute-start.51 = (f32[80,384]{1,0:T(8,128)S(1)}, f32[80,384]{1,0:T(8,128)}, u32[]{:S(2)}, u32[]{:S(2)}) collective-permute-start(f32[80,384]{1,0:T(8,128)S(1)} %param.10), channel_id=1, source_target_pairs={{4,4},{16,8},{28,12},{8,16},{20,20}} | collective-permute-start | bytes 368648 | tf_op jit(solution)/shard_map/cond/branch_7_fun/ppermute | solution.py:709
  52.1 1.9 %collective-permute-start.50 = (f32[80,384]{1,0:T(8,128)S(1)}, f32[80,384]{1,0:T(8,128)}, u32[]{:S(2)}, u32[]{:S(2)}) collective-permute-start(f32[80,384]{1,0:T(8,128)S(1)} %param.10), channel_id=1, source_target_pairs={{0,4},{12,8},{24,12},{4,16},{16,20},{28,24}} | collective-permute-start | bytes 368648 | tf_op jit(solution)/shard_map/cond/branch_7_fun/ppermute | solution.py:709
  54.5 1.9 %collective-permute-done.51 = f32[80,384]{1,0:T(8,128)} collective-permute-done((f32[80,384]{1,0:T(8,128)S(1)}, f32[80,384]{1,0:T(8,128)}, u32[]{:S(2)}, u32[]{:S(2)}) %collective-permute-start.51) | collective-permute-done | bytes 122912 | tf_op jit(solution)/shard_map/cond/branch_7_fun/ppermute | solution.py:709
  56.4 2.0 %collective-permute-done.50 = f32[80,384]{1,0:T(8,128)} collective-permute-done((f32[80,384]{1,0:T(8,128)S(1)}, f32[80,384]{1,0:T(8,128)}, u32[]{:S(2)}, u32[]{:S(2)}) %collective-permute-start.50) | collective-permute-done | bytes 122912 | tf_op jit(solution)/shard_map/cond/branch_7_fun/ppermute | solution.py:709
  58.4 1.9 %merge.1 = f32[10,24,384]{2,1,0:T(8,128)} custom-call(s32[1]{0:T(128)} %copy.61.offset_ref, f32[80,384]{1,0:T(8,128)} %get-tuple-element.72.first_ref, f32[80,384]{1,0:T(8,128)} %get-tuple-element.73.second_ref, f32[80,384]{1,0:T(8,128)} %get-tuple-element.74.third_ref, f32[80,384]{1,0:T(8,128)} %get-tuple-element.75.fourth_ref, ...), custom_call_target="tpu_custom_call" | custom-call | tf_op jit(solution)/shard_map/merge/pallas_call | solution.py:716
  (25 shorter events, 5.4 us)
Async XLA Ops:
  2.2 14.4 %collective-permute-start.18 = (f32[56,256]{1,0:T(8,128)S(1)}, f32[56,256]{1,0:T(8,128)}, u32[]{:S(2)}, u32[]{:S(2)}) collective-permute-start(f32[56,256]{1,0:T(8,128)S(1)} %get-tuple-element.39), channel_id=1, source_target_pairs={{12,2},{16,6},{20,26},{24,30}} | collective-permute-start | bytes 172040 | tf_op jit(solution)/shard_map/cond/branch_2_fun/ppermute | solution.py:652
  6.7 11.8 %collective-permute-start.17 = (f32[56,256]{1,0:T(8,128)S(1)}, f32[56,256]{1,0:T(8,128)}, u32[]{:S(2)}, u32[]{:S(2)}) collective-permute-start(f32[56,256]{1,0:T(8,128)S(1)} %get-tuple-element.38), channel_id=1, source_target_pairs={{16,13},{20,17}} | collective-permute-start | bytes 172040 | tf_op jit(solution)/shard_map/cond/branch_2_fun/ppermute | solution.py:652
  8.6 11.8 %collective-permute-start.16 = (f32[56,256]{1,0:T(8,128)S(1)}, f32[56,256]{1,0:T(8,128)}, u32[]{:S(2)}, u32[]{:S(2)}) collective-permute-start(f32[56,256]{1,0:T(8,128)S(1)} %get-tuple-element.38), channel_id=1, source_target_pairs={{2,1},{6,5},{12,9},{14,13},{16,21},{18,17},{20,25},{24,29}} | collective-permute-start | bytes 172040 | tf_op jit(solution)/shard_map/cond/branch_2_fun/ppermute | solution.py:652
  10.5 9.9 %collective-permute-start.15 = (f32[56,256]{1,0:T(8,128)S(1)}, f32[56,256]{1,0:T(8,128)}, u32[]{:S(2)}, u32[]{:S(2)}) collective-permute-start(f32[56,256]{1,0:T(8,128)S(1)} %get-tuple-element.38), channel_id=1, source_target_pairs={{3,2},{7,6},{10,9},{11,10},{12,1},{15,14},{16,5},{19,18},{20,13},{... | collective-permute-start | bytes 172040 | tf_op jit(solution)/shard_map/cond/branch_2_fun/ppermute | solution.py:652
  12.4 8.0 %collective-permute-start.21 = (f32[56,256]{1,0:T(8,128)S(1)}, f32[56,256]{1,0:T(8,128)}, u32[]{:S(2)}, u32[]{:S(2)}) collective-permute-start(f32[56,256]{1,0:T(8,128)S(1)} %get-tuple-element.40), channel_id=1, source_target_pairs={{16,15},{20,19}} | collective-permute-start | bytes 172040 | tf_op jit(solution)/shard_map/cond/branch_2_fun/ppermute | solution.py:652
  16.6 3.8 %collective-permute-start.20 = (f32[56,256]{1,0:T(8,128)S(1)}, f32[56,256]{1,0:T(8,128)}, u32[]{:S(2)}, u32[]{:S(2)}) collective-permute-start(f32[56,256]{1,0:T(8,128)S(1)} %get-tuple-element.40), channel_id=1, source_target_pairs={{2,3},{6,7},{12,11},{14,15},{16,23},{18,19},{20,27},{24,31}} | collective-permute-start | bytes 172040 | tf_op jit(solution)/shard_map/cond/branch_2_fun/ppermute | solution.py:652
  18.5 3.3 %collective-permute-start.19 = (f32[56,256]{1,0:T(8,128)S(1)}, f32[56,256]{1,0:T(8,128)}, u32[]{:S(2)}, u32[]{:S(2)}) collective-permute-start(f32[56,256]{1,0:T(8,128)S(1)} %get-tuple-element.40), channel_id=1, source_target_pairs={{1,2},{5,6},{9,10},{10,11},{12,3},{13,14},{16,7},{17,18},{20,15},{... | collective-permute-start | bytes 172040 | tf_op jit(solution)/shard_map/cond/branch_2_fun/ppermute | solution.py:652
  21.8 9.6 %copy-start = (f32[5,2,24,384]{3,2,1,0:T(8,128)S(1)}, f32[5,2,24,384]{3,2,1,0:T(8,128)}, u32[]{:S(2)}) copy-start(f32[5,2,24,384]{3,2,1,0:T(8,128)} %param.15) | copy-start | bytes 1105924
  21.8 9.6 %copy-start.1 = (f32[2,2,24,384]{3,2,1,0:T(8,128)S(1)}, f32[2,2,24,384]{3,2,1,0:T(8,128)}, u32[]{:S(2)}) copy-start(f32[2,2,24,384]{3,2,1,0:T(8,128)} %param.16) | copy-start | bytes 442372
  24.0 7.4 %collective-permute-start.58 = (f32[136,384]{1,0:T(8,128)}, f32[136,384]{1,0:T(8,128)S(1)}, u32[]{:S(2)}, u32[]{:S(2)}) collective-permute-start(f32[136,384]{1,0:T(8,128)} %get-tuple-element.69), channel_id=1, source_target_pairs={{0,4},{1,5},{2,6},{3,7},{4,0},{5,1},{6,2},{7,3},{8,12},{9,13},{10,... | collective-permute-start | bytes 626696 | tf_op jit(solution)/shard_map/ppermute | solution.py:683
  24.0 7.4 %collective-permute-start.59 = (f32[88,384]{1,0:T(8,128)}, f32[88,384]{1,0:T(8,128)S(1)}, u32[]{:S(2)}, u32[]{:S(2)}) collective-permute-start(f32[88,384]{1,0:T(8,128)} %get-tuple-element.70), channel_id=1, source_target_pairs={{4,8},{5,9},{6,10},{7,11},{8,4},{9,5},{10,6},{11,7},{12,16},{13,17... | collective-permute-start | bytes 405512 | tf_op jit(solution)/shard_map/ppermute | solution.py:682
  31.4 0.9 %copy-start.2 = (f32[72,256]{1,0:T(8,128)S(1)}, f32[72,256]{1,0:T(8,128)}, u32[]{:S(2)}) copy-start(f32[72,256]{1,0:T(8,128)} %get-tuple-element.68.rims_ref) | copy-start | bytes 221188
  32.3 0.7 %copy-start.3 = (f32[24,128]{1,0:T(8,128)S(1)}, f32[24,128]{1,0:T(8,128)}, u32[]{:S(2)}) copy-start(f32[24,128]{1,0:T(8,128)} %get-tuple-element.66.west_ref) | copy-start | bytes 36868
  33.0 0.7 %copy-start.4 = (f32[24,128]{1,0:T(8,128)S(1)}, f32[24,128]{1,0:T(8,128)}, u32[]{:S(2)}) copy-start(f32[24,128]{1,0:T(8,128)} %get-tuple-element.67.east_ref) | copy-start | bytes 36868
  35.3 10.6 %collective-permute-start.62 = (f32[80,128]{1,0:T(8,128)S(1)}, f32[80,128]{1,0:T(8,128)S(1)}, u32[]{:S(2)}, u32[]{:S(2)}) collective-permute-start(f32[80,128]{1,0:T(8,128)S(1)} %get-tuple-element.71), channel_id=1, source_target_pairs={{3,0},{7,4},{11,8},{15,12},{19,16},{23,20},{27,24},{31,28}} | collective-permute-start | bytes 122888 | tf_op jit(solution)/shard_map/ppermute | solution.py:702
  36.6 9.4 %collective-permute-start.61 = (f32[80,128]{1,0:T(8,128)S(1)}, f32[80,128]{1,0:T(8,128)S(1)}, u32[]{:S(2)}, u32[]{:S(2)}) collective-permute-start(f32[80,128]{1,0:T(8,128)S(1)} %get-tuple-element.71), channel_id=1, source_target_pairs={{2,0},{6,4},{10,8},{14,12},{18,16},{22,20},{26,24},{30,28}} | collective-permute-start | bytes 122888 | tf_op jit(solution)/shard_map/ppermute | solution.py:702
  37.9 8.1 %collective-permute-start.60 = (f32[80,128]{1,0:T(8,128)S(1)}, f32[80,128]{1,0:T(8,128)S(1)}, u32[]{:S(2)}, u32[]{:S(2)}) collective-permute-start(f32[80,128]{1,0:T(8,128)S(1)} %get-tuple-element.71), channel_id=1, source_target_pairs={{1,0},{5,4},{9,8},{13,12},{17,16},{21,20},{25,24},{29,28}} | collective-permute-start | bytes 122888 | tf_op jit(solution)/shard_map/ppermute | solution.py:702
  46.0 8.0 %collective-permute-start.53 = (f32[80,384]{1,0:T(8,128)S(1)}, f32[80,384]{1,0:T(8,128)}, u32[]{:S(2)}, u32[]{:S(2)}) collective-permute-start(f32[80,384]{1,0:T(8,128)S(1)} %param.10), channel_id=1, source_target_pairs={{8,4},{20,8},{4,12},{16,16},{28,20}} | collective-permute-start | bytes 368648 | tf_op jit(solution)/shard_map/cond/branch_7_fun/ppermute | solution.py:709
  47.3 7.2 %collective-permute-start.52 = (f32[80,384]{1,0:T(8,128)S(1)}, f32[80,384]{1,0:T(8,128)}, u32[]{:S(2)}, u32[]{:S(2)}) collective-permute-start(f32[80,384]{1,0:T(8,128)S(1)} %param.10), channel_id=1, source_target_pairs={{0,12},{12,16},{24,20}} | collective-permute-start | bytes 368648 | tf_op jit(solution)/shard_map/cond/branch_7_fun/ppermute | solution.py:709
  48.6 7.8 %collective-permute-start.51 = (f32[80,384]{1,0:T(8,128)S(1)}, f32[80,384]{1,0:T(8,128)}, u32[]{:S(2)}, u32[]{:S(2)}) collective-permute-start(f32[80,384]{1,0:T(8,128)S(1)} %param.10), channel_id=1, source_target_pairs={{4,4},{16,8},{28,12},{8,16},{20,20}} | collective-permute-start | bytes 368648 | tf_op jit(solution)/shard_map/cond/branch_7_fun/ppermute | solution.py:709
  52.1 6.3 %collective-permute-start.50 = (f32[80,384]{1,0:T(8,128)S(1)}, f32[80,384]{1,0:T(8,128)}, u32[]{:S(2)}, u32[]{:S(2)}) collective-permute-start(f32[80,384]{1,0:T(8,128)S(1)} %param.10), channel_id=1, source_target_pairs={{0,4},{12,8},{24,12},{4,16},{16,20},{28,24}} | collective-permute-start | bytes 368648 | tf_op jit(solution)/shard_map/cond/branch_7_fun/ppermute | solution.py:709

commit v3 on v2

--- a/solution.py
+++ b/solution.py
@@ -646,32 +646,34 @@
         name="pack",
     )(nest_offset, planes, speeds)
 
-    def send_rims(start, west, middle, east):
+    def send_rims(start, nest_offset, planes, speeds, west, middle, east):
         groups = rim_pairs(start)
         west, middle, east = (
             [lax.ppermute(value, BOTH, pairs) for pairs in lists]
             for value, lists in zip((west, middle, east), groups)
         )
-        return (*west, sum(middle), *east)
-
-    received = lax.switch(
+        return pl.pallas_call(
+            relay_kernel,
+            out_shape=[
+                shaped(ROWS, LANE),
+                shaped(ROWS, LANE),
+                shaped(RIMS, 2 * LANE),
+                shaped(HALO + RIMS, COLS),
+                shaped(HALO + ROWS, COLS),
+            ],
+            in_specs=[SMEM] + [VMEM] * 9,
+            out_specs=[VMEM] * 5,
+            name="relay",
+        )(nest_offset, planes, speeds, *west, sum(middle), *east)
+
+    west, east, rims, to_pair, to_cross = lax.switch(
         (offset - 2) // ROWS - 1,
         [functools.partial(send_rims, start) for start in (1, 2, 3)],
+        nest_offset,
+        planes,
+        speeds,
         *payloads,
     )
-    west, east, rims, to_pair, to_cross = pl.pallas_call(
-        relay_kernel,
-        out_shape=[
-            shaped(ROWS, LANE),
-            shaped(ROWS, LANE),
-            shaped(RIMS, 2 * LANE),
-            shaped(HALO + RIMS, COLS),
-            shaped(HALO + ROWS, COLS),
-        ],
-        in_specs=[SMEM] + [VMEM] * 9,
-        out_specs=[VMEM] * 5,
-        name="relay",
-    )(nest_offset, planes, speeds, *received)
     pair_map = [(device(t, s), device(t ^ 1, s)) for t in range(8) for s in range(4)]
     cross_map = [
         (device(a, s), device(b, s))
@@ -705,22 +707,24 @@
         axis=1,
     )
 
-    def send_means(start, value):
-        return tuple(lax.ppermute(value, BOTH, mean_pairs(start + 1 - j)) for j in range(4))
-
-    blocks = lax.switch(
+    def send_means(start, nest_offset, value, block):
+        blocks = [lax.ppermute(value, BOTH, mean_pairs(start + 1 - j)) for j in range(4)]
+        return pl.pallas_call(
+            merge_kernel,
+            out_shape=shaped(STATES, ROWS, COLS),
+            in_specs=[SMEM] + [VMEM] * 5,
+            out_specs=VMEM,
+            compiler_params=pltpu.CompilerParams(vmem_limit_bytes=32 * 1024 * 1024),
+            name="merge",
+        )(nest_offset, *blocks, block)
+
+    merged = lax.switch(
         offset // 8 - 3,
         [functools.partial(send_means, start) for start in range(3, 12)],
+        nest_offset,
         columns,
-    )
-    merged = pl.pallas_call(
-        merge_kernel,
-        out_shape=shaped(STATES, ROWS, COLS),
-        in_specs=[SMEM] + [VMEM] * 5,
-        out_specs=VMEM,
-        compiler_params=pltpu.CompilerParams(vmem_limit_bytes=32 * 1024 * 1024),
-        name="merge",
-    )(nest_offset, *blocks, block)
+        block,
+    )
     return merged.reshape(state.shape)
 
 

time: 60.7 us -> 54.8 us (0.903)
  the two profiles are of different devices: /device:TPU:4 before, /device:TPU:5 now
where the time goes in v3:
time: 54.8 us; the launch traced here: 54.3 us
  starting transfers between devices  30.8 us (56%)
  waiting for transfers between devices  15.3 us (28%)
  Pallas kernels  5.72 us (10%)
  local copies, waits for them, and re-layouts  1.35 us (2%)
  between operations  0.84 us (2%)
    ppermute x7, starting transfers between devices, send_rims(): lax.ppermute(value, BOTH, pairs)  15 us
    ppermute x4, starting transfers between devices, send_means(): lax.ppermute(value, BOTH, mean_pairs(start + 1 - j))  8.93 us
    ppermute x3, waiting for transfers between devices, on_device(): lax.ppermute(means, BOTH, [(device(t, s), device(t, 0)) for t in range(8)])  5.76 us
    ppermute x1, waiting for transfers between devices, on_device(): from_cross = lax.ppermute(to_cross, BOTH, cross_map)  4.7 us
    ppermute x3, starting transfers between devices, on_device(): lax.ppermute(means, BOTH, [(device(t, s), device(t, 0)) for t in range(8)])  3.88 us
    ppermute x4, waiting for transfers between devices, send_means(): lax.ppermute(value, BOTH, mean_pairs(start + 1 - j))  3.67 us
    ppermute x1, starting transfers between devices, on_device(): from_cross = lax.ppermute(to_cross, BOTH, cross_map)  1.91 us
    pallas_call x1, Pallas kernels, send_rims(): pl.pallas_call(relay_kernel, out_shape=[shaped(ROWS, LANE), shaped(ROWS,...  1.83 us
  transfers between devices with their start and end apart: 16, of which 6 were waited for; matrix products, arithmetic and copies ran while one was open for 0% of the time, Pallas kernels for 0%

profile of v3, /device:TPU:5, one launch (start us, length us, event | category | flops | bytes accessed | tf_op | source)
XLA Modules:
  0.0 54.3 jit_solution(9620482487235039932)
XLA Ops:
  0.7 1.6 %pack.1 = (f32[56,256]{1,0:T(8,128)S(1)}, f32[56,256]{1,0:T(8,128)S(1)}, f32[56,256]{1,0:T(8,128)S(1)}) custom-call(s32[1]{0:T(128)} %copy.37.offset_ref, f32[10,24,384]{2,1,0:T(8,128)} %bitcast.17, f32[4,24,384]{2,1,0:T(8,128)} %bitcast.22), custom_call_target="tpu_custom_call" | custom-call | tf_op jit(solution)/shard_map/pack/pallas_call | solution.py:641
  2.3 18.9 %conditional.2 = ((f32[24,128]{1,0:T(8,128)S(1)}, f32[24,128]{1,0:T(8,128)S(1)}, f32[72,256]{1,0:T(8,128)S(1)}, f32[136,384]{1,0:T(8,128)S(1)}, f32[88,384]{1,0:T(8,128)S(1)})) conditional(s32[]{:T(128)} %clamp.7, (f32[56,256]{1,0:T(8,128)S(1)}, f32[56,256]{1,0:T(8,128)S(1)}, f32[56,256]{1,0:T(8,128)S(1)}, s32[1]{0:T(128)}, ...), branch_computations={%region_0.1_spmd, %region_1.2_spmd, %region_2.3_spmd} | conditional | flops 14336 | bytes 3383792 | solution.py:669
  2.4 5.1 %collective-permute-start.11 = (f32[56,256]{1,0:T(8,128)S(1)}, f32[56,256]{1,0:T(8,128)S(1)}, u32[]{:S(2)}, u32[]{:S(2)}) collective-permute-start(f32[56,256]{1,0:T(8,128)S(1)} %get-tuple-element.116), channel_id=1, source_target_pairs={{8,2},{12,6},{16,26},{20,30}} | collective-permute-start | bytes 172040 | tf_op jit(solution)/shard_map/cond/branch_1_fun/ppermute | solution.py:652
  8.2 1.3 %collective-permute-start.9 = (f32[56,256]{1,0:T(8,128)S(1)}, f32[56,256]{1,0:T(8,128)S(1)}, u32[]{:S(2)}, u32[]{:S(2)}) collective-permute-start(f32[56,256]{1,0:T(8,128)S(1)} %get-tuple-element.115), channel_id=1, source_target_pairs={{2,1},{6,5},{8,9},{12,21},{14,13},{16,25},{18,17},{20,29}} | collective-permute-start | bytes 172040 | tf_op jit(solution)/shard_map/cond/branch_1_fun/ppermute | solution.py:652
  9.5 1.3 %collective-permute-start.8 = (f32[56,256]{1,0:T(8,128)S(1)}, f32[56,256]{1,0:T(8,128)S(1)}, u32[]{:S(2)}, u32[]{:S(2)}) collective-permute-start(f32[56,256]{1,0:T(8,128)S(1)} %get-tuple-element.115), channel_id=1, source_target_pairs={{3,2},{7,6},{8,1},{10,9},{11,10},{12,5},{15,14},{16,13},{19,18},{2... | collective-permute-start | bytes 172040 | tf_op jit(solution)/shard_map/cond/branch_1_fun/ppermute | solution.py:652
  11.5 2.5 %collective-permute-start.13 = (f32[56,256]{1,0:T(8,128)S(1)}, f32[56,256]{1,0:T(8,128)S(1)}, u32[]{:S(2)}, u32[]{:S(2)}) collective-permute-start(f32[56,256]{1,0:T(8,128)S(1)} %get-tuple-element.117), channel_id=1, source_target_pairs={{2,3},{6,7},{8,11},{12,23},{14,15},{16,27},{18,19},{20,31}} | collective-permute-start | bytes 172040 | tf_op jit(solution)/shard_map/cond/branch_1_fun/ppermute | solution.py:652
  14.0 3.5 %collective-permute-start.12 = (f32[56,256]{1,0:T(8,128)S(1)}, f32[56,256]{1,0:T(8,128)S(1)}, u32[]{:S(2)}, u32[]{:S(2)}) collective-permute-start(f32[56,256]{1,0:T(8,128)S(1)} %get-tuple-element.117), channel_id=1, source_target_pairs={{1,2},{5,6},{8,3},{9,10},{10,11},{12,7},{13,14},{16,15},{17,18},{2... | collective-permute-start | bytes 172040 | tf_op jit(solution)/shard_map/cond/branch_1_fun/ppermute | solution.py:652
  17.6 1.2 %collective-permute-done.12.refs_4_ = f32[56,256]{1,0:T(8,128)S(1)} collective-permute-done((f32[56,256]{1,0:T(8,128)S(1)}, f32[56,256]{1,0:T(8,128)S(1)}, u32[]{:S(2)}, u32[]{:S(2)}) %collective-permute-start.12) | collective-permute-done | bytes 57376 | tf_op jit(solution)/shard_map/cond/branch_1_fun/ppermute | solution.py:652
  19.4 1.8 %relay.4 = (f32[24,128]{1,0:T(8,128)S(1)}, f32[24,128]{1,0:T(8,128)S(1)}, f32[72,256]{1,0:T(8,128)S(1)}, f32[136,384]{1,0:T(8,128)S(1)}, f32[88,384]{1,0:T(8,128)S(1)}) custom-call(s32[1]{0:T(128)} %get-tuple-element.112.offset_ref, f32[10,24,384]{2,1,0:T(8,128)S(1)} %get-tuple-element.113.state_ref, f32[4,24,384]{2,1,0:T(8,128)S(1)} %get-tuple-element.114.courant_ref, ...), custom_call_target="tpu_custom_call" | custom-call | tf_op jit(solution)/shard_map/cond/branch_1_fun/relay/pallas_call | solution.py:655
  21.2 1.0 %collective-permute-start.58 = (f32[136,384]{1,0:T(8,128)S(1)}, f32[136,384]{1,0:T(8,128)S(1)}, u32[]{:S(2)}, u32[]{:S(2)}) collective-permute-start(f32[136,384]{1,0:T(8,128)S(1)} %get-tuple-element.167), channel_id=1, source_target_pairs={{0,4},{1,5},{2,6},{3,7},{4,0},{5,1},{6,2},{7,3},{8,12},{9,13},{10,... | collective-permute-start | bytes 626696 | tf_op jit(solution)/shard_map/ppermute | solution.py:685
  22.2 1.9 %collective-permute-start.59 = (f32[88,384]{1,0:T(8,128)S(1)}, f32[88,384]{1,0:T(8,128)S(1)}, u32[]{:S(2)}, u32[]{:S(2)}) collective-permute-start(f32[88,384]{1,0:T(8,128)S(1)} %get-tuple-element.168), channel_id=1, source_target_pairs={{4,8},{5,9},{6,10},{7,11},{8,4},{9,5},{10,6},{11,7},{12,16},{13,17... | collective-permute-start | bytes 405512 | tf_op jit(solution)/shard_map/ppermute | solution.py:684
  24.2 4.7 %collective-permute-done.59.cross_ref = f32[88,384]{1,0:T(8,128)S(1)} collective-permute-done((f32[88,384]{1,0:T(8,128)S(1)}, f32[88,384]{1,0:T(8,128)S(1)}, u32[]{:S(2)}, u32[]{:S(2)}) %collective-permute-start.59) | collective-permute-done | bytes 135200 | tf_op jit(solution)/shard_map/ppermute | solution.py:684
  28.9 1.6 %nest.1 = (f32[10,24,384]{2,1,0:T(8,128)S(1)}, f32[80,128]{1,0:T(8,128)S(1)}) custom-call(s32[1]{0:T(128)} %copy.37.offset_ref, f32[10,24,384]{2,1,0:T(8,128)S(1)} %bitcast.21, f32[4,24,384]{2,1,0:T(8,128)S(1)} %bitcast.26, f32[24,128]{1,0:T(8,128)S(1)} %get-tuple-element.164.west_ref, f32[24,128]{1,0:T(8,128)S(1)} %get-tuple-element.165.east_ref, ...), custom_call_target="tpu_custom_call" | custom-call | tf_op jit(solution)/shard_map/nest/pallas_call | solution.py:686
  30.4 1.3 %collective-permute-start.62 = (f32[80,128]{1,0:T(8,128)S(1)}, f32[80,128]{1,0:T(8,128)S(1)}, u32[]{:S(2)}, u32[]{:S(2)}) collective-permute-start(f32[80,128]{1,0:T(8,128)S(1)} %get-tuple-element.169), channel_id=1, source_target_pairs={{3,0},{7,4},{11,8},{15,12},{19,16},{23,20},{27,24},{31,28}} | collective-permute-start | bytes 122888 | tf_op jit(solution)/shard_map/ppermute | solution.py:704
  31.7 1.3 %collective-permute-start.61 = (f32[80,128]{1,0:T(8,128)S(1)}, f32[80,128]{1,0:T(8,128)S(1)}, u32[]{:S(2)}, u32[]{:S(2)}) collective-permute-start(f32[80,128]{1,0:T(8,128)S(1)} %get-tuple-element.169), channel_id=1, source_target_pairs={{2,0},{6,4},{10,8},{14,12},{18,16},{22,20},{26,24},{30,28}} | collective-permute-start | bytes 122888 | tf_op jit(solution)/shard_map/ppermute | solution.py:704
  33.0 1.3 %collective-permute-start.60 = (f32[80,128]{1,0:T(8,128)S(1)}, f32[80,128]{1,0:T(8,128)S(1)}, u32[]{:S(2)}, u32[]{:S(2)}) collective-permute-start(f32[80,128]{1,0:T(8,128)S(1)} %get-tuple-element.169), channel_id=1, source_target_pairs={{1,0},{5,4},{9,8},{13,12},{17,16},{21,20},{25,24},{29,28}} | collective-permute-start | bytes 122888 | tf_op jit(solution)/shard_map/ppermute | solution.py:704
  34.4 4.6 %collective-permute-done.62 = f32[80,128]{1,0:T(8,128)S(1)} collective-permute-done((f32[80,128]{1,0:T(8,128)S(1)}, f32[80,128]{1,0:T(8,128)S(1)}, u32[]{:S(2)}, u32[]{:S(2)}) %collective-permute-start.62) | collective-permute-done | bytes 40992 | tf_op jit(solution)/shard_map/ppermute | solution.py:704
  40.1 13.4 %conditional.3 = (f32[5,2,24,384]{3,2,1,0:T(8,128)S(1)}) conditional(s32[]{:T(128)} %clamp.6, (f32[80,384]{1,0:T(8,128)S(1)}, s32[1]{0:T(128)}, f32[10,24,384]{2,1,0:T(8,128)S(1)}) %tuple.51, (f32[80,384]{1,0:T(8,128)S(1)}, s32[1]{0:T(128)}, f32[10,24,384]{2,1,0:T(8,128)S(1)}) %tuple.51, (f32[80,384]{1,0:T(8,128)S(1)}, ...), branch_computations={%region_3.4_spmd, %region_4.5_spmd, %region_5.6_spmd, %region_6.7_... | conditional | bytes 1966248 | solution.py:721
  40.2 0.7 %collective-permute-start.41 = (f32[80,384]{1,0:T(8,128)S(1)}, f32[80,384]{1,0:T(8,128)S(1)}, u32[]{:S(2)}, u32[]{:S(2)}) collective-permute-start(f32[80,384]{1,0:T(8,128)S(1)} %get-tuple-element.137), channel_id=1, source_target_pairs={{4,8},{16,12},{28,16}} | collective-permute-start | bytes 368648 | tf_op jit(solution)/shard_map/cond/branch_4_fun/ppermute | solution.py:711
  41.5 5.7 %collective-permute-start.39 = (f32[80,384]{1,0:T(8,128)S(1)}, f32[80,384]{1,0:T(8,128)S(1)}, u32[]{:S(2)}, u32[]{:S(2)}) collective-permute-start(f32[80,384]{1,0:T(8,128)S(1)} %get-tuple-element.137), channel_id=1, source_target_pairs={{8,12},{20,16}} | collective-permute-start | bytes 368648 | tf_op jit(solution)/shard_map/cond/branch_4_fun/ppermute | solution.py:711
  47.2 1.9 %collective-permute-start.38 = (f32[80,384]{1,0:T(8,128)S(1)}, f32[80,384]{1,0:T(8,128)S(1)}, u32[]{:S(2)}, u32[]{:S(2)}) collective-permute-start(f32[80,384]{1,0:T(8,128)S(1)} %get-tuple-element.137), channel_id=1, source_target_pairs={{8,4},{20,8},{4,12},{16,16},{28,20}} | collective-permute-start | bytes 368648 | tf_op jit(solution)/shard_map/cond/branch_4_fun/ppermute | solution.py:711
  49.2 3.7 %collective-permute-done.38.first_ref = f32[80,384]{1,0:T(8,128)S(1)} collective-permute-done((f32[80,384]{1,0:T(8,128)S(1)}, f32[80,384]{1,0:T(8,128)S(1)}, u32[]{:S(2)}, u32[]{:S(2)}) %collective-permute-start.38) | collective-permute-done | bytes 122912 | tf_op jit(solution)/shard_map/cond/branch_4_fun/ppermute | solution.py:711
  52.8 0.7 %merge.13 = f32[10,24,384]{2,1,0:T(8,128)S(1)} custom-call(s32[1]{0:T(128)} %get-tuple-element.136.offset_ref, f32[80,384]{1,0:T(8,128)S(1)} %collective-permute-done.38.first_ref, f32[80,384]{1,0:T(8,128)S(1)} %collective-permute-done.39.second_ref, f32[80,384]{1,0:T(8,128)S(1)} %collective-permute-done.40.third_ref, ...), custom_call_target="tpu_custom_call" | custom-call | tf_op jit(solution)/shard_map/cond/branch_4_fun/merge/pallas_call | solution.py:712
  53.6 0.7 %copy-done.2 = f32[5,2,24,384]{3,2,1,0:T(8,128)} copy-done((f32[5,2,24,384]{3,2,1,0:T(8,128)}, f32[5,2,24,384]{3,2,1,0:T(8,128)S(1)}, u32[]{:S(2)}) %copy-start.2) | copy-done | bytes 368664
  (35 shorter events, 3.9 us)
Async XLA Ops:
  0.0 2.3 %copy-start = (f32[5,2,24,384]{3,2,1,0:T(8,128)S(1)}, f32[5,2,24,384]{3,2,1,0:T(8,128)}, u32[]{:S(2)}) copy-start(f32[5,2,24,384]{3,2,1,0:T(8,128)} %param.15) | copy-start | bytes 1105924
  0.7 1.6 %copy-start.1 = (f32[2,2,24,384]{3,2,1,0:T(8,128)S(1)}, f32[2,2,24,384]{3,2,1,0:T(8,128)}, u32[]{:S(2)}) copy-start(f32[2,2,24,384]{3,2,1,0:T(8,128)} %param.16) | copy-start | bytes 442372
  2.4 9.1 %collective-permute-start.11 = (f32[56,256]{1,0:T(8,128)S(1)}, f32[56,256]{1,0:T(8,128)S(1)}, u32[]{:S(2)}, u32[]{:S(2)}) collective-permute-start(f32[56,256]{1,0:T(8,128)S(1)} %get-tuple-element.116), channel_id=1, source_target_pairs={{8,2},{12,6},{16,26},{20,30}} | collective-permute-start | bytes 172040 | tf_op jit(solution)/shard_map/cond/branch_1_fun/ppermute | solution.py:652
  7.5 6.4 %collective-permute-start.10 = (f32[56,256]{1,0:T(8,128)S(1)}, f32[56,256]{1,0:T(8,128)S(1)}, u32[]{:S(2)}, u32[]{:S(2)}) collective-permute-start(f32[56,256]{1,0:T(8,128)S(1)} %get-tuple-element.115), channel_id=1, source_target_pairs={{12,13},{16,17}} | collective-permute-start | bytes 172040 | tf_op jit(solution)/shard_map/cond/branch_1_fun/ppermute | solution.py:652
  8.2 9.3 %collective-permute-start.9 = (f32[56,256]{1,0:T(8,128)S(1)}, f32[56,256]{1,0:T(8,128)S(1)}, u32[]{:S(2)}, u32[]{:S(2)}) collective-permute-start(f32[56,256]{1,0:T(8,128)S(1)} %get-tuple-element.115), channel_id=1, source_target_pairs={{2,1},{6,5},{8,9},{12,21},{14,13},{16,25},{18,17},{20,29}} | collective-permute-start | bytes 172040 | tf_op jit(solution)/shard_map/cond/branch_1_fun/ppermute | solution.py:652
  9.5 8.0 %collective-permute-start.8 = (f32[56,256]{1,0:T(8,128)S(1)}, f32[56,256]{1,0:T(8,128)S(1)}, u32[]{:S(2)}, u32[]{:S(2)}) collective-permute-start(f32[56,256]{1,0:T(8,128)S(1)} %get-tuple-element.115), channel_id=1, source_target_pairs={{3,2},{7,6},{8,1},{10,9},{11,10},{12,5},{15,14},{16,13},{19,18},{2... | collective-permute-start | bytes 172040 | tf_op jit(solution)/shard_map/cond/branch_1_fun/ppermute | solution.py:652
  10.8 6.8 %collective-permute-start.14 = (f32[56,256]{1,0:T(8,128)S(1)}, f32[56,256]{1,0:T(8,128)S(1)}, u32[]{:S(2)}, u32[]{:S(2)}) collective-permute-start(f32[56,256]{1,0:T(8,128)S(1)} %get-tuple-element.117), channel_id=1, source_target_pairs={{12,15},{16,19}} | collective-permute-start | bytes 172040 | tf_op jit(solution)/shard_map/cond/branch_1_fun/ppermute | solution.py:652
  11.5 7.3 %copy-start.4 = (f32[56,256]{1,0:T(8,128)}, f32[56,256]{1,0:T(8,128)S(1)}, u32[]{:S(2)}) copy-start(f32[56,256]{1,0:T(8,128)S(1)} %collective-permute-done.11.refs_3_) | copy-start | bytes 172036 | tf_op jit(solution)/shard_map/cond
  11.5 6.1 %collective-permute-start.13 = (f32[56,256]{1,0:T(8,128)S(1)}, f32[56,256]{1,0:T(8,128)S(1)}, u32[]{:S(2)}, u32[]{:S(2)}) collective-permute-start(f32[56,256]{1,0:T(8,128)S(1)} %get-tuple-element.117), channel_id=1, source_target_pairs={{2,3},{6,7},{8,11},{12,23},{14,15},{16,27},{18,19},{20,31}} | collective-permute-start | bytes 172040 | tf_op jit(solution)/shard_map/cond/branch_1_fun/ppermute | solution.py:652
  14.0 4.8 %copy-start.7 = (f32[56,256]{1,0:T(8,128)}, f32[56,256]{1,0:T(8,128)S(1)}, u32[]{:S(2)}) copy-start(f32[56,256]{1,0:T(8,128)S(1)} %collective-permute-done.10.refs_2_) | copy-start | bytes 172036 | tf_op jit(solution)/shard_map/cond
  14.0 4.8 %collective-permute-start.12 = (f32[56,256]{1,0:T(8,128)S(1)}, f32[56,256]{1,0:T(8,128)S(1)}, u32[]{:S(2)}, u32[]{:S(2)}) collective-permute-start(f32[56,256]{1,0:T(8,128)S(1)} %get-tuple-element.117), channel_id=1, source_target_pairs={{1,2},{5,6},{8,3},{9,10},{10,11},{12,7},{13,14},{16,15},{17,18},{2... | collective-permute-start | bytes 172040 | tf_op jit(solution)/shard_map/cond/branch_1_fun/ppermute | solution.py:652
  17.5 1.2 %copy-start.10 = (f32[56,256]{1,0:T(8,128)}, f32[56,256]{1,0:T(8,128)S(1)}, u32[]{:S(2)}) copy-start(f32[56,256]{1,0:T(8,128)S(1)} %collective-permute-done.9.refs_1_) | copy-start | bytes 172036 | tf_op jit(solution)/shard_map/cond
  17.5 1.2 %copy-start.12 = (f32[56,256]{1,0:T(8,128)}, f32[56,256]{1,0:T(8,128)S(1)}, u32[]{:S(2)}) copy-start(f32[56,256]{1,0:T(8,128)S(1)} %collective-permute-done.8.refs_0_) | copy-start | bytes 172036 | tf_op jit(solution)/shard_map/cond
  17.6 1.2 %copy-start.15 = (f32[56,256]{1,0:T(8,128)}, f32[56,256]{1,0:T(8,128)S(1)}, u32[]{:S(2)}) copy-start(f32[56,256]{1,0:T(8,128)S(1)} %collective-permute-done.14.refs_6_) | copy-start | bytes 172036 | tf_op jit(solution)/shard_map/cond
  17.6 1.2 %copy-start.18 = (f32[56,256]{1,0:T(8,128)}, f32[56,256]{1,0:T(8,128)S(1)}, u32[]{:S(2)}) copy-start(f32[56,256]{1,0:T(8,128)S(1)} %collective-permute-done.13.refs_5_) | copy-start | bytes 172036 | tf_op jit(solution)/shard_map/cond
  21.2 7.7 %collective-permute-start.58 = (f32[136,384]{1,0:T(8,128)S(1)}, f32[136,384]{1,0:T(8,128)S(1)}, u32[]{:S(2)}, u32[]{:S(2)}) collective-permute-start(f32[136,384]{1,0:T(8,128)S(1)} %get-tuple-element.167), channel_id=1, source_target_pairs={{0,4},{1,5},{2,6},{3,7},{4,0},{5,1},{6,2},{7,3},{8,12},{9,13},{10,... | collective-permute-start | bytes 626696 | tf_op jit(solution)/shard_map/ppermute | solution.py:685
  22.2 6.6 %collective-permute-start.59 = (f32[88,384]{1,0:T(8,128)S(1)}, f32[88,384]{1,0:T(8,128)S(1)}, u32[]{:S(2)}, u32[]{:S(2)}) collective-permute-start(f32[88,384]{1,0:T(8,128)S(1)} %get-tuple-element.168), channel_id=1, source_target_pairs={{4,8},{5,9},{6,10},{7,11},{8,4},{9,5},{10,6},{11,7},{12,16},{13,17... | collective-permute-start | bytes 405512 | tf_op jit(solution)/shard_map/ppermute | solution.py:684
  30.4 8.5 %collective-permute-start.62 = (f32[80,128]{1,0:T(8,128)S(1)}, f32[80,128]{1,0:T(8,128)S(1)}, u32[]{:S(2)}, u32[]{:S(2)}) collective-permute-start(f32[80,128]{1,0:T(8,128)S(1)} %get-tuple-element.169), channel_id=1, source_target_pairs={{3,0},{7,4},{11,8},{15,12},{19,16},{23,20},{27,24},{31,28}} | collective-permute-start | bytes 122888 | tf_op jit(solution)/shard_map/ppermute | solution.py:704
  31.7 7.8 %collective-permute-start.61 = (f32[80,128]{1,0:T(8,128)S(1)}, f32[80,128]{1,0:T(8,128)S(1)}, u32[]{:S(2)}, u32[]{:S(2)}) collective-permute-start(f32[80,128]{1,0:T(8,128)S(1)} %get-tuple-element.169), channel_id=1, source_target_pairs={{2,0},{6,4},{10,8},{14,12},{18,16},{22,20},{26,24},{30,28}} | collective-permute-start | bytes 122888 | tf_op jit(solution)/shard_map/ppermute | solution.py:704
  33.0 7.1 %collective-permute-start.60 = (f32[80,128]{1,0:T(8,128)S(1)}, f32[80,128]{1,0:T(8,128)S(1)}, u32[]{:S(2)}, u32[]{:S(2)}) collective-permute-start(f32[80,128]{1,0:T(8,128)S(1)} %get-tuple-element.169), channel_id=1, source_target_pairs={{1,0},{5,4},{9,8},{13,12},{17,16},{21,20},{25,24},{29,28}} | collective-permute-start | bytes 122888 | tf_op jit(solution)/shard_map/ppermute | solution.py:704
  40.2 9.0 %collective-permute-start.41 = (f32[80,384]{1,0:T(8,128)S(1)}, f32[80,384]{1,0:T(8,128)S(1)}, u32[]{:S(2)}, u32[]{:S(2)}) collective-permute-start(f32[80,384]{1,0:T(8,128)S(1)} %get-tuple-element.137), channel_id=1, source_target_pairs={{4,8},{16,12},{28,16}} | collective-permute-start | bytes 368648 | tf_op jit(solution)/shard_map/cond/branch_4_fun/ppermute | solution.py:711
  40.8 8.3 %collective-permute-start.40 = (f32[80,384]{1,0:T(8,128)S(1)}, f32[80,384]{1,0:T(8,128)S(1)}, u32[]{:S(2)}, u32[]{:S(2)}) collective-permute-start(f32[80,384]{1,0:T(8,128)S(1)} %get-tuple-element.137), channel_id=1, source_target_pairs={{0,8},{12,12},{24,16}} | collective-permute-start | bytes 368648 | tf_op jit(solution)/shard_map/cond/branch_4_fun/ppermute | solution.py:711
  41.5 7.6 %collective-permute-start.39 = (f32[80,384]{1,0:T(8,128)S(1)}, f32[80,384]{1,0:T(8,128)S(1)}, u32[]{:S(2)}, u32[]{:S(2)}) collective-permute-start(f32[80,384]{1,0:T(8,128)S(1)} %get-tuple-element.137), channel_id=1, source_target_pairs={{8,12},{20,16}} | collective-permute-start | bytes 368648 | tf_op jit(solution)/shard_map/cond/branch_4_fun/ppermute | solution.py:711
  47.2 5.6 %collective-permute-start.38 = (f32[80,384]{1,0:T(8,128)S(1)}, f32[80,384]{1,0:T(8,128)S(1)}, u32[]{:S(2)}, u32[]{:S(2)}) collective-permute-start(f32[80,384]{1,0:T(8,128)S(1)} %get-tuple-element.137), channel_id=1, source_target_pairs={{8,4},{20,8},{4,12},{16,16},{28,20}} | collective-permute-start | bytes 368648 | tf_op jit(solution)/shard_map/cond/branch_4_fun/ppermute | solution.py:711
  (2 other events, 1.4 us)

commit v4 on v3

--- a/solution.py
+++ b/solution.py
@@ -271,7 +271,9 @@
 
 
 def relay_kernel(offset_ref, state_ref, courant_ref, *refs):
-    to_west, middle, to_east = refs[:3], refs[3], refs[4:7]
+    to_east = refs[0:3]
+    middle = refs[3]
+    to_west = refs[4:7]
     west_ref, east_ref, rims_ref, pair_ref, cross_ref = refs[7:]
     tile = lax.axis_index("tile")
     even = tile % 2 == 0
@@ -547,7 +549,8 @@
     means_ref[...] = total / (RATIO * RATIO)
 
 
-def merge_kernel(offset_ref, first_ref, second_ref, third_ref, fourth_ref, block_ref, out_ref):
+def merge_kernel(offset_ref, *refs):
+    *block_refs, stepped_ref, out_ref, near = refs
     tile = lax.axis_index("tile")
     section = lax.axis_index("section")
     offset = offset_ref[0]
@@ -555,16 +558,25 @@
 
     @pl.when(section > 0)
     def _():
-        out_ref[...] = block_ref[...]
+        out_ref[...] = stepped_ref[...]
 
     @pl.when(section == 0)
     def _():
+        for step in range(4):
+            source = 3 * tile - offset // 8 - 1 + step
+            inside = (source >= 0) & (source < 8)
+            for way, block_ref in enumerate(block_refs):
+
+                @pl.when(inside & (source == (tile ^ way)))
+                def _():
+                    near[step] = block_ref[...]
+
         nest_row = tile * ROWS + iota((ROWS, COLS), 0) - offset
         covered = (nest_row >= 0) & (nest_row < 64)
         for p in range(STATES):
-            parts = [r[8 * p : 8 * p + 8] for r in (first_ref, second_ref, third_ref, fourth_ref)]
+            parts = [near[step, 8 * p : 8 * p + 8] for step in range(4)]
             moved = pltpu.roll(jnp.concatenate(parts, axis=0), rest + 24, 0)
-            out_ref[p] = jnp.where(covered, moved[:ROWS], block_ref[p])
+            out_ref[p] = jnp.where(covered, moved[:ROWS], stepped_ref[p])
 
 
 VMEM = pl.BlockSpec(memory_space=pltpu.VMEM)
@@ -613,7 +625,7 @@
     for section, inner in ((1, ((2, 1), (3, 2))), (3, ((1, 2), (2, 3)))):
         edges = [(device(a, 0), device(b, section)) for a, b in sends]
         edges += [(device(t, a), device(t, b)) for t in range(8) for a, b in inner]
-        groups.append(in_rounds(edges, 3))
+        groups.append(in_rounds(edges, 3)[::-1])
     middle = [[(device(a, 0), device(b, 2)) for a, b in pairs] for pairs in middle]
     return groups[0], middle, groups[1]
 
@@ -664,7 +676,7 @@
             in_specs=[SMEM] + [VMEM] * 9,
             out_specs=[VMEM] * 5,
             name="relay",
-        )(nest_offset, planes, speeds, *west, sum(middle), *east)
+        )(nest_offset, planes, speeds, *east, sum(middle), *west)
 
     west, east, rims, to_pair, to_cross = lax.switch(
         (offset - 2) // ROWS - 1,
@@ -707,24 +719,24 @@
         axis=1,
     )
 
-    def send_means(start, nest_offset, value, block):
-        blocks = [lax.ppermute(value, BOTH, mean_pairs(start + 1 - j)) for j in range(4)]
-        return pl.pallas_call(
-            merge_kernel,
-            out_shape=shaped(STATES, ROWS, COLS),
-            in_specs=[SMEM] + [VMEM] * 5,
-            out_specs=VMEM,
-            compiler_params=pltpu.CompilerParams(vmem_limit_bytes=32 * 1024 * 1024),
-            name="merge",
-        )(nest_offset, *blocks, block)
-
-    merged = lax.switch(
-        offset // 8 - 3,
-        [functools.partial(send_means, start) for start in range(3, 12)],
-        nest_offset,
-        columns,
-        block,
-    )
+    def across(value, way):
+        pairs = [(device(t, s), device(t ^ way, s)) for t in range(8) for s in range(4)]
+        return lax.ppermute(value, BOTH, pairs)
+
+    blocks = {0: columns}
+    for way in (7, 3, 4, 1):
+        blocks[way] = across(columns, way)
+    for way in (7, 3, 4):
+        blocks[way ^ 1] = across(blocks[way], 1)
+    merged = pl.pallas_call(
+        merge_kernel,
+        out_shape=shaped(STATES, ROWS, COLS),
+        in_specs=[SMEM] + [VMEM] * 9,
+        out_specs=VMEM,
+        scratch_shapes=[pltpu.VMEM((4, STATES * 8, COLS), jnp.float32)],
+        compiler_params=pltpu.CompilerParams(vmem_limit_bytes=32 * 1024 * 1024),
+        name="merge",
+    )(nest_offset, *[blocks[way] for way in range(8)], block)
     return merged.reshape(state.shape)
 
 

time: 54.8 us -> 51.6 us (0.942)
  the two profiles are of different devices: /device:TPU:5 before, /device:TPU:0 now
where the time goes in v4:
time: 51.6 us; the launch traced here: 51.2 us
  starting transfers between devices  30.5 us (59%)
  waiting for transfers between devices  12.6 us (24%)
  Pallas kernels  5.8 us (11%)
  between operations  0.83 us (2%)
  local copies, waits for them, and re-layouts  0.65 us (1%)
  other arithmetic  0.63 us (1%)
    ppermute x8, starting transfers between devices, send_rims(): lax.ppermute(value, BOTH, pairs)  14.9 us
    ppermute x7, starting transfers between devices, across(): return lax.ppermute(value, BOTH, pairs)  11 us
    ppermute x3, waiting for transfers between devices, on_device(): lax.ppermute(means, BOTH, [(device(t, s), device(t, 0)) for t in range(8)])  5.53 us
    ppermute x7, waiting for transfers between devices, across(): return lax.ppermute(value, BOTH, pairs)  5.22 us
    ppermute x3, starting transfers between devices, on_device(): lax.ppermute(means, BOTH, [(device(t, s), device(t, 0)) for t in range(8)])  3.88 us
    pallas_call x1, Pallas kernels, send_rims(): pl.pallas_call(relay_kernel, out_shape=[shaped(ROWS, LANE), shaped(ROWS,...  1.83 us
    pallas_call x1, Pallas kernels, on_device(): pl.pallas_call(pack_kernel, out_shape=[shaped(SLOTS, 2 * LANE)] * 3, in_s...  1.58 us
    pallas_call x1, Pallas kernels, on_device(): pl.pallas_call(main_kernel, out_shape=[shaped(STATES, ROWS, COLS), shaped...  1.57 us
  transfers between devices with their start and end apart: 20, of which 8 were waited for; matrix products, arithmetic and copies ran while one was open for 1% of the time, Pallas kernels for 0%

profile of v4, /device:TPU:0, one launch (start us, length us, event | category | flops | bytes accessed | tf_op | source)
XLA Modules:
  0.0 51.2 jit_solution(10578362155012308638)
XLA Ops:
  0.7 1.6 %pack.1 = (f32[56,256]{1,0:T(8,128)S(1)}, f32[56,256]{1,0:T(8,128)S(1)}, f32[56,256]{1,0:T(8,128)S(1)}) custom-call(s32[1]{0:T(128)S(6)} %copy.21.offset_ref, f32[10,24,384]{2,1,0:T(8,128)} %bitcast.5, f32[4,24,384]{2,1,0:T(8,128)} %bitcast.10), custom_call_target="tpu_custom_call" | custom-call | tf_op jit(solution)/shard_map/pack/pallas_call | solution.py:653
  2.3 19.3 %conditional.1 = ((f32[24,128]{1,0:T(8,128)S(1)}, f32[24,128]{1,0:T(8,128)S(1)}, f32[72,256]{1,0:T(8,128)S(1)}, f32[136,384]{1,0:T(8,128)S(1)}, f32[88,384]{1,0:T(8,128)S(1)})) conditional(s32[]{:T(128)} %clamp.3, (f32[56,256]{1,0:T(8,128)S(1)}, f32[56,256]{1,0:T(8,128)S(1)}, f32[56,256]{1,0:T(8,128)S(1)}, s32[1]{0:T(128)}, ...), branch_computations={%region_0.1_spmd, %region_1.2_spmd, %region_2.3_spmd} | conditional | flops 14336 | bytes 3383792 | solution.py:681
  2.4 5.9 %collective-permute-start.4 = (f32[56,256]{1,0:T(8,128)S(1)}, f32[56,256]{1,0:T(8,128)S(1)}, u32[]{:S(2)}, u32[]{:S(2)}) collective-permute-start(f32[56,256]{1,0:T(8,128)S(1)} %get-tuple-element.45), channel_id=1, source_target_pairs={{0,2}} | collective-permute-start | bytes 172040 | tf_op jit(solution)/shard_map/cond/branch_0_fun/ppermute | solution.py:664
  8.3 0.7 %collective-permute-start.3 = (f32[56,256]{1,0:T(8,128)S(1)}, f32[56,256]{1,0:T(8,128)S(1)}, u32[]{:S(2)}, u32[]{:S(2)}) collective-permute-start(f32[56,256]{1,0:T(8,128)S(1)} %get-tuple-element.45), channel_id=1, source_target_pairs={{4,2},{8,6},{12,26},{16,30}} | collective-permute-start | bytes 172040 | tf_op jit(solution)/shard_map/cond/branch_0_fun/ppermute | solution.py:664
  9.0 0.7 %collective-permute-start.2 = (f32[56,256]{1,0:T(8,128)S(1)}, f32[56,256]{1,0:T(8,128)S(1)}, u32[]{:S(2)}, u32[]{:S(2)}) collective-permute-start(f32[56,256]{1,0:T(8,128)S(1)} %get-tuple-element.44), channel_id=1, source_target_pairs={{1,2},{4,3},{5,6},{8,7},{9,10},{10,11},{12,15},{13,14},{16,19},{17... | collective-permute-start | bytes 172040 | tf_op jit(solution)/shard_map/cond/branch_0_fun/ppermute | solution.py:664
  10.3 2.9 %collective-permute-start = (f32[56,256]{1,0:T(8,128)S(1)}, f32[56,256]{1,0:T(8,128)S(1)}, u32[]{:S(2)}, u32[]{:S(2)}) collective-permute-start(f32[56,256]{1,0:T(8,128)S(1)} %get-tuple-element.44), channel_id=1, source_target_pairs={{0,3},{8,15},{12,19}} | collective-permute-start | bytes 172040 | tf_op jit(solution)/shard_map/cond/branch_0_fun/ppermute | solution.py:664
  13.3 0.7 %collective-permute-start.7 = (f32[56,256]{1,0:T(8,128)S(1)}, f32[56,256]{1,0:T(8,128)S(1)}, u32[]{:S(2)}, u32[]{:S(2)}) collective-permute-start(f32[56,256]{1,0:T(8,128)S(1)} %get-tuple-element.46), channel_id=1, source_target_pairs={{3,2},{4,1},{7,6},{8,5},{10,9},{11,10},{12,13},{15,14},{16,17},{19... | collective-permute-start | bytes 172040 | tf_op jit(solution)/shard_map/cond/branch_0_fun/ppermute | solution.py:664
  14.6 2.7 %collective-permute-start.5 = (f32[56,256]{1,0:T(8,128)S(1)}, f32[56,256]{1,0:T(8,128)S(1)}, u32[]{:S(2)}, u32[]{:S(2)}) collective-permute-start(f32[56,256]{1,0:T(8,128)S(1)} %get-tuple-element.46), channel_id=1, source_target_pairs={{0,1},{8,13},{12,17}} | collective-permute-start | bytes 172040 | tf_op jit(solution)/shard_map/cond/branch_0_fun/ppermute | solution.py:664
  18.1 1.1 %collective-permute-done.5.refs_4_ = f32[56,256]{1,0:T(8,128)S(1)} collective-permute-done((f32[56,256]{1,0:T(8,128)S(1)}, f32[56,256]{1,0:T(8,128)S(1)}, u32[]{:S(2)}, u32[]{:S(2)}) %collective-permute-start.5) | collective-permute-done | bytes 57376 | tf_op jit(solution)/shard_map/cond/branch_0_fun/ppermute | solution.py:664
  19.8 1.8 %relay.3 = (f32[24,128]{1,0:T(8,128)S(1)}, f32[24,128]{1,0:T(8,128)S(1)}, f32[72,256]{1,0:T(8,128)S(1)}, f32[136,384]{1,0:T(8,128)S(1)}, f32[88,384]{1,0:T(8,128)S(1)}) custom-call(s32[1]{0:T(128)} %get-tuple-element.41.offset_ref, f32[10,24,384]{2,1,0:T(8,128)S(1)} %get-tuple-element.42.state_ref, f32[4,24,384]{2,1,0:T(8,128)S(1)} %get-tuple-element.43.courant_ref, ...), custom_call_target="tpu_custom_call" | custom-call | tf_op jit(solution)/shard_map/cond/branch_0_fun/relay/pallas_call | solution.py:667
  21.7 0.7 %collective-permute-start.23 = (f32[88,384]{1,0:T(8,128)S(1)}, f32[88,384]{1,0:T(8,128)S(1)}, u32[]{:S(2)}, u32[]{:S(2)}) collective-permute-start(f32[88,384]{1,0:T(8,128)S(1)} %get-tuple-element.76), channel_id=1, source_target_pairs={{4,8},{5,9},{6,10},{7,11},{8,4},{9,5},{10,6},{11,7},{12,16},{13,17... | collective-permute-start | bytes 405512 | tf_op jit(solution)/shard_map/ppermute | solution.py:696
  22.4 0.8 %collective-permute-done.22.pair_ref = f32[136,384]{1,0:T(8,128)S(1)} collective-permute-done((f32[136,384]{1,0:T(8,128)S(1)}, f32[136,384]{1,0:T(8,128)S(1)}, u32[]{:S(2)}, u32[]{:S(2)}) %collective-permute-start.22) | collective-permute-done | bytes 208928 | tf_op jit(solution)/shard_map/ppermute | solution.py:697
  23.2 1.6 %nest.1 = (f32[10,24,384]{2,1,0:T(8,128)S(1)}, f32[80,128]{1,0:T(8,128)S(1)}) custom-call(s32[1]{0:T(128)S(6)} %copy.21.offset_ref, f32[10,24,384]{2,1,0:T(8,128)S(1)} %bitcast.9, f32[4,24,384]{2,1,0:T(8,128)S(1)} %bitcast.14, f32[24,128]{1,0:T(8,128)S(1)} %get-tuple-element.72.west_ref, f32[24,128]{1,0:T(8,128)S(1)} %get-tuple-element.73.east_ref, ...), custom_call_target="tpu_custom_call" | custom-call | tf_op jit(solution)/shard_map/nest/pallas_call | solution.py:698
  24.7 1.3 %collective-permute-start.24 = (f32[80,128]{1,0:T(8,128)S(1)}, f32[80,128]{1,0:T(8,128)S(1)}, u32[]{:S(2)}, u32[]{:S(2)}) collective-permute-start(f32[80,128]{1,0:T(8,128)S(1)} %get-tuple-element.77), channel_id=1, source_target_pairs={{1,0},{5,4},{9,8},{13,12},{17,16},{21,20},{25,24},{29,28}} | collective-permute-start | bytes 122888 | tf_op jit(solution)/shard_map/ppermute | solution.py:716
  26.0 1.3 %collective-permute-start.26 = (f32[80,128]{1,0:T(8,128)S(1)}, f32[80,128]{1,0:T(8,128)S(1)}, u32[]{:S(2)}, u32[]{:S(2)}) collective-permute-start(f32[80,128]{1,0:T(8,128)S(1)} %get-tuple-element.77), channel_id=1, source_target_pairs={{3,0},{7,4},{11,8},{15,12},{19,16},{23,20},{27,24},{31,28}} | collective-permute-start | bytes 122888 | tf_op jit(solution)/shard_map/ppermute | solution.py:716
  27.3 1.3 %collective-permute-start.25 = (f32[80,128]{1,0:T(8,128)S(1)}, f32[80,128]{1,0:T(8,128)S(1)}, u32[]{:S(2)}, u32[]{:S(2)}) collective-permute-start(f32[80,128]{1,0:T(8,128)S(1)} %get-tuple-element.77), channel_id=1, source_target_pairs={{2,0},{6,4},{10,8},{14,12},{18,16},{22,20},{26,24},{30,28}} | collective-permute-start | bytes 122888 | tf_op jit(solution)/shard_map/ppermute | solution.py:716
  28.6 4.6 %collective-permute-done.24 = f32[80,128]{1,0:T(8,128)S(1)} collective-permute-done((f32[80,128]{1,0:T(8,128)S(1)}, f32[80,128]{1,0:T(8,128)S(1)}, u32[]{:S(2)}, u32[]{:S(2)}) %collective-permute-start.24) | collective-permute-done | bytes 40992 | tf_op jit(solution)/shard_map/ppermute | solution.py:716
  33.2 1.0 %collective-permute-done.25 = f32[80,128]{1,0:T(8,128)S(1)} collective-permute-done((f32[80,128]{1,0:T(8,128)S(1)}, f32[80,128]{1,0:T(8,128)S(1)}, u32[]{:S(2)}, u32[]{:S(2)}) %collective-permute-start.25) | collective-permute-done | bytes 40992 | tf_op jit(solution)/shard_map/ppermute | solution.py:716
  34.3 9.4 %collective-permute-start.30 = (f32[80,384]{1,0:T(8,128)S(1)}, f32[80,384]{1,0:T(8,128)S(1)}, u32[]{:S(2)}, u32[]{:S(2)}) collective-permute-start(f32[80,384]{1,0:T(8,128)S(1)} %constant_dynamic-update-slice_fusion.refs_0_), channel_id=1, source_target_pairs={{0,16},{1,17},{2,18},{3,19},{4,20},{5,21},{6,22},{7,23},{8,24},{9,... | collective-permute-start | bytes 368648 | tf_op jit(solution)/shard_map/ppermute | solution.py:724
  43.8 1.2 %collective-permute-start.33 = (f32[80,384]{1,0:T(8,128)S(1)}, f32[80,384]{1,0:T(8,128)S(1)}, u32[]{:S(2)}, u32[]{:S(2)}) collective-permute-start(f32[80,384]{1,0:T(8,128)S(1)} %collective-permute-done.32.refs_7_), channel_id=1, source_target_pairs={{0,4},{1,5},{2,6},{3,7},{4,0},{5,1},{6,2},{7,3},{8,12},{9,13},{10,... | collective-permute-start | bytes 368648 | tf_op jit(solution)/shard_map/ppermute | solution.py:724
  45.0 3.1 %collective-permute-done.30.refs_4_ = f32[80,384]{1,0:T(8,128)S(1)} collective-permute-done((f32[80,384]{1,0:T(8,128)S(1)}, f32[80,384]{1,0:T(8,128)S(1)}, u32[]{:S(2)}, u32[]{:S(2)}) %collective-permute-start.30) | collective-permute-done | bytes 122912 | tf_op jit(solution)/shard_map/ppermute | solution.py:724
  48.2 0.8 %collective-permute-done.28.refs_3_ = f32[80,384]{1,0:T(8,128)S(1)} collective-permute-done((f32[80,384]{1,0:T(8,128)S(1)}, f32[80,384]{1,0:T(8,128)S(1)}, u32[]{:S(2)}, u32[]{:S(2)}) %collective-permute-start.28) | collective-permute-done | bytes 122912 | tf_op jit(solution)/shard_map/ppermute | solution.py:724
  49.5 0.9 %collective-permute-done.29.refs_2_ = f32[80,384]{1,0:T(8,128)S(1)} collective-permute-done((f32[80,384]{1,0:T(8,128)S(1)}, f32[80,384]{1,0:T(8,128)S(1)}, u32[]{:S(2)}, u32[]{:S(2)}) %collective-permute-start.29) | collective-permute-done | bytes 122912 | tf_op jit(solution)/shard_map/ppermute | solution.py:724
  50.4 0.8 %merge.1 = f32[10,24,384]{2,1,0:T(8,128)} custom-call(s32[1]{0:T(128)S(6)} %copy.21.offset_ref, f32[80,384]{1,0:T(8,128)S(1)} %constant_dynamic-update-slice_fusion.refs_0_, f32[80,384]{1,0:T(8,128)S(1)} %collective-permute-done.27.refs_1_, f32[80,384]{1,0:T(8,128)S(1)} %collective-permute-done.29.refs_2_, f32[80,384]{1,0:T(8,128)S(1)} %collective-permute-done.28.refs_3_, ...), custom_call_target="tpu_custom_call" | custom-call | tf_op jit(solution)/shard_map/merge/pallas_call | solution.py:731
  (41 shorter events, 3.4 us)
Async XLA Ops:
  0.0 2.3 %copy-start = (f32[5,2,24,384]{3,2,1,0:T(8,128)S(1)}, f32[5,2,24,384]{3,2,1,0:T(8,128)}, u32[]{:S(2)}) copy-start(f32[5,2,24,384]{3,2,1,0:T(8,128)} %param.6) | copy-start | bytes 1105924
  0.7 1.6 %copy-start.1 = (f32[2,2,24,384]{3,2,1,0:T(8,128)S(1)}, f32[2,2,24,384]{3,2,1,0:T(8,128)}, u32[]{:S(2)}) copy-start(f32[2,2,24,384]{3,2,1,0:T(8,128)} %param.7) | copy-start | bytes 442372
  2.4 10.9 %collective-permute-start.4 = (f32[56,256]{1,0:T(8,128)S(1)}, f32[56,256]{1,0:T(8,128)S(1)}, u32[]{:S(2)}, u32[]{:S(2)}) collective-permute-start(f32[56,256]{1,0:T(8,128)S(1)} %get-tuple-element.45), channel_id=1, source_target_pairs={{0,2}} | collective-permute-start | bytes 172040 | tf_op jit(solution)/shard_map/cond/branch_0_fun/ppermute | solution.py:664
  8.3 5.6 %collective-permute-start.3 = (f32[56,256]{1,0:T(8,128)S(1)}, f32[56,256]{1,0:T(8,128)S(1)}, u32[]{:S(2)}, u32[]{:S(2)}) collective-permute-start(f32[56,256]{1,0:T(8,128)S(1)} %get-tuple-element.45), channel_id=1, source_target_pairs={{4,2},{8,6},{12,26},{16,30}} | collective-permute-start | bytes 172040 | tf_op jit(solution)/shard_map/cond/branch_0_fun/ppermute | solution.py:664
  9.0 5.7 %collective-permute-start.2 = (f32[56,256]{1,0:T(8,128)S(1)}, f32[56,256]{1,0:T(8,128)S(1)}, u32[]{:S(2)}, u32[]{:S(2)}) collective-permute-start(f32[56,256]{1,0:T(8,128)S(1)} %get-tuple-element.44), channel_id=1, source_target_pairs={{1,2},{4,3},{5,6},{8,7},{9,10},{10,11},{12,15},{13,14},{16,19},{17... | collective-permute-start | bytes 172040 | tf_op jit(solution)/shard_map/cond/branch_0_fun/ppermute | solution.py:664
  9.6 8.4 %collective-permute-start.1 = (f32[56,256]{1,0:T(8,128)S(1)}, f32[56,256]{1,0:T(8,128)S(1)}, u32[]{:S(2)}, u32[]{:S(2)}) collective-permute-start(f32[56,256]{1,0:T(8,128)S(1)} %get-tuple-element.44), channel_id=1, source_target_pairs={{2,3},{4,11},{6,7},{8,23},{12,27},{14,15},{16,31},{18,19}} | collective-permute-start | bytes 172040 | tf_op jit(solution)/shard_map/cond/branch_0_fun/ppermute | solution.py:664
  10.3 7.7 %collective-permute-start = (f32[56,256]{1,0:T(8,128)S(1)}, f32[56,256]{1,0:T(8,128)S(1)}, u32[]{:S(2)}, u32[]{:S(2)}) collective-permute-start(f32[56,256]{1,0:T(8,128)S(1)} %get-tuple-element.44), channel_id=1, source_target_pairs={{0,3},{8,15},{12,19}} | collective-permute-start | bytes 172040 | tf_op jit(solution)/shard_map/cond/branch_0_fun/ppermute | solution.py:664
  13.3 4.8 %collective-permute-start.7 = (f32[56,256]{1,0:T(8,128)S(1)}, f32[56,256]{1,0:T(8,128)S(1)}, u32[]{:S(2)}, u32[]{:S(2)}) collective-permute-start(f32[56,256]{1,0:T(8,128)S(1)} %get-tuple-element.46), channel_id=1, source_target_pairs={{3,2},{4,1},{7,6},{8,5},{10,9},{11,10},{12,13},{15,14},{16,17},{19... | collective-permute-start | bytes 172040 | tf_op jit(solution)/shard_map/cond/branch_0_fun/ppermute | solution.py:664
  14.0 4.1 %collective-permute-start.6 = (f32[56,256]{1,0:T(8,128)S(1)}, f32[56,256]{1,0:T(8,128)S(1)}, u32[]{:S(2)}, u32[]{:S(2)}) collective-permute-start(f32[56,256]{1,0:T(8,128)S(1)} %get-tuple-element.46), channel_id=1, source_target_pairs={{2,1},{4,9},{6,5},{8,21},{12,25},{14,13},{16,29},{18,17}} | collective-permute-start | bytes 172040 | tf_op jit(solution)/shard_map/cond/branch_0_fun/ppermute | solution.py:664
  14.6 3.4 %copy-start.2 = (f32[56,256]{1,0:T(8,128)}, f32[56,256]{1,0:T(8,128)S(1)}, u32[]{:S(2)}) copy-start(f32[56,256]{1,0:T(8,128)S(1)} %collective-permute-done.2.refs_2_) | copy-start | bytes 172036 | tf_op jit(solution)/shard_map/cond
  14.6 4.5 %collective-permute-start.5 = (f32[56,256]{1,0:T(8,128)S(1)}, f32[56,256]{1,0:T(8,128)S(1)}, u32[]{:S(2)}, u32[]{:S(2)}) collective-permute-start(f32[56,256]{1,0:T(8,128)S(1)} %get-tuple-element.46), channel_id=1, source_target_pairs={{0,1},{8,13},{12,17}} | collective-permute-start | bytes 172040 | tf_op jit(solution)/shard_map/cond/branch_0_fun/ppermute | solution.py:664
  18.0 1.2 %copy-start.5 = (f32[56,256]{1,0:T(8,128)}, f32[56,256]{1,0:T(8,128)S(1)}, u32[]{:S(2)}) copy-start(f32[56,256]{1,0:T(8,128)S(1)} %collective-permute-done.1.refs_1_) | copy-start | bytes 172036 | tf_op jit(solution)/shard_map/cond
  21.7 1.5 %collective-permute-start.22 = (f32[136,384]{1,0:T(8,128)S(1)}, f32[136,384]{1,0:T(8,128)S(1)}, u32[]{:S(2)}, u32[]{:S(2)}) collective-permute-start(f32[136,384]{1,0:T(8,128)S(1)} %get-tuple-element.75), channel_id=1, source_target_pairs={{0,4},{1,5},{2,6},{3,7},{4,0},{5,1},{6,2},{7,3},{8,12},{9,13},{10,... | collective-permute-start | bytes 626696 | tf_op jit(solution)/shard_map/ppermute | solution.py:697
  21.7 0.7 %collective-permute-start.23 = (f32[88,384]{1,0:T(8,128)S(1)}, f32[88,384]{1,0:T(8,128)S(1)}, u32[]{:S(2)}, u32[]{:S(2)}) collective-permute-start(f32[88,384]{1,0:T(8,128)S(1)} %get-tuple-element.76), channel_id=1, source_target_pairs={{4,8},{5,9},{6,10},{7,11},{8,4},{9,5},{10,6},{11,7},{12,16},{13,17... | collective-permute-start | bytes 405512 | tf_op jit(solution)/shard_map/ppermute | solution.py:696
  24.7 8.5 %collective-permute-start.24 = (f32[80,128]{1,0:T(8,128)S(1)}, f32[80,128]{1,0:T(8,128)S(1)}, u32[]{:S(2)}, u32[]{:S(2)}) collective-permute-start(f32[80,128]{1,0:T(8,128)S(1)} %get-tuple-element.77), channel_id=1, source_target_pairs={{1,0},{5,4},{9,8},{13,12},{17,16},{21,20},{25,24},{29,28}} | collective-permute-start | bytes 122888 | tf_op jit(solution)/shard_map/ppermute | solution.py:716
  26.0 8.1 %collective-permute-start.26 = (f32[80,128]{1,0:T(8,128)S(1)}, f32[80,128]{1,0:T(8,128)S(1)}, u32[]{:S(2)}, u32[]{:S(2)}) collective-permute-start(f32[80,128]{1,0:T(8,128)S(1)} %get-tuple-element.77), channel_id=1, source_target_pairs={{3,0},{7,4},{11,8},{15,12},{19,16},{23,20},{27,24},{31,28}} | collective-permute-start | bytes 122888 | tf_op jit(solution)/shard_map/ppermute | solution.py:716
  27.3 6.8 %collective-permute-start.25 = (f32[80,128]{1,0:T(8,128)S(1)}, f32[80,128]{1,0:T(8,128)S(1)}, u32[]{:S(2)}, u32[]{:S(2)}) collective-permute-start(f32[80,128]{1,0:T(8,128)S(1)} %get-tuple-element.77), channel_id=1, source_target_pairs={{2,0},{6,4},{10,8},{14,12},{18,16},{22,20},{26,24},{30,28}} | collective-permute-start | bytes 122888 | tf_op jit(solution)/shard_map/ppermute | solution.py:716
  34.2 9.6 %collective-permute-start.32 = (f32[80,384]{1,0:T(8,128)S(1)}, f32[80,384]{1,0:T(8,128)S(1)}, u32[]{:S(2)}, u32[]{:S(2)}) collective-permute-start(f32[80,384]{1,0:T(8,128)S(1)} %constant_dynamic-update-slice_fusion.refs_0_), channel_id=1, source_target_pairs={{0,28},{1,29},{2,30},{3,31},{4,24},{5,25},{6,26},{7,27},{8,20},{9,... | collective-permute-start | bytes 368648 | tf_op jit(solution)/shard_map/ppermute | solution.py:724
  34.3 13.9 %collective-permute-start.30 = (f32[80,384]{1,0:T(8,128)S(1)}, f32[80,384]{1,0:T(8,128)S(1)}, u32[]{:S(2)}, u32[]{:S(2)}) collective-permute-start(f32[80,384]{1,0:T(8,128)S(1)} %constant_dynamic-update-slice_fusion.refs_0_), channel_id=1, source_target_pairs={{0,16},{1,17},{2,18},{3,19},{4,20},{5,21},{6,22},{7,23},{8,24},{9,... | collective-permute-start | bytes 368648 | tf_op jit(solution)/shard_map/ppermute | solution.py:724
  43.7 5.4 %collective-permute-start.28 = (f32[80,384]{1,0:T(8,128)S(1)}, f32[80,384]{1,0:T(8,128)S(1)}, u32[]{:S(2)}, u32[]{:S(2)}) collective-permute-start(f32[80,384]{1,0:T(8,128)S(1)} %constant_dynamic-update-slice_fusion.refs_0_), channel_id=1, source_target_pairs={{0,12},{1,13},{2,14},{3,15},{4,8},{5,9},{6,10},{7,11},{8,4},{9,5},... | collective-permute-start | bytes 368648 | tf_op jit(solution)/shard_map/ppermute | solution.py:724
  43.8 5.4 %collective-permute-start.27 = (f32[80,384]{1,0:T(8,128)S(1)}, f32[80,384]{1,0:T(8,128)S(1)}, u32[]{:S(2)}, u32[]{:S(2)}) collective-permute-start(f32[80,384]{1,0:T(8,128)S(1)} %constant_dynamic-update-slice_fusion.refs_0_), channel_id=1, source_target_pairs={{0,4},{1,5},{2,6},{3,7},{4,0},{5,1},{6,2},{7,3},{8,12},{9,13},{10,... | collective-permute-start | bytes 368648 | tf_op jit(solution)/shard_map/ppermute | solution.py:724
  43.8 5.4 %collective-permute-start.33 = (f32[80,384]{1,0:T(8,128)S(1)}, f32[80,384]{1,0:T(8,128)S(1)}, u32[]{:S(2)}, u32[]{:S(2)}) collective-permute-start(f32[80,384]{1,0:T(8,128)S(1)} %collective-permute-done.32.refs_7_), channel_id=1, source_target_pairs={{0,4},{1,5},{2,6},{3,7},{4,0},{5,1},{6,2},{7,3},{8,12},{9,13},{10,... | collective-permute-start | bytes 368648 | tf_op jit(solution)/shard_map/ppermute | solution.py:724
  48.2 1.3 %collective-permute-start.31 = (f32[80,384]{1,0:T(8,128)S(1)}, f32[80,384]{1,0:T(8,128)S(1)}, u32[]{:S(2)}, u32[]{:S(2)}) collective-permute-start(f32[80,384]{1,0:T(8,128)S(1)} %collective-permute-done.30.refs_4_), channel_id=1, source_target_pairs={{0,4},{1,5},{2,6},{3,7},{4,0},{5,1},{6,2},{7,3},{8,12},{9,13},{10,... | collective-permute-start | bytes 368648 | tf_op jit(solution)/shard_map/ppermute | solution.py:724
  49.1 1.3 %collective-permute-start.29 = (f32[80,384]{1,0:T(8,128)S(1)}, f32[80,384]{1,0:T(8,128)S(1)}, u32[]{:S(2)}, u32[]{:S(2)}) collective-permute-start(f32[80,384]{1,0:T(8,128)S(1)} %collective-permute-done.28.refs_3_), channel_id=1, source_target_pairs={{0,4},{1,5},{2,6},{3,7},{4,0},{5,1},{6,2},{7,3},{8,12},{9,13},{10,... | collective-permute-start | bytes 368648 | tf_op jit(solution)/shard_map/ppermute | solution.py:724
  (4 other events, 4.1 us)

commit v5 on v4

--- a/solution.py
+++ b/solution.py
@@ -188,14 +188,16 @@
 PLANES = 14
 SLOTS = 4 * PLANES
 HALO = SLOTS + 8
-NEST_MARK = 1.0
-PARENT_MARK = 2.0
 RIMS = 3 * ROWS
 EXACT = lax.Precision.HIGHEST
 
 
 def device(tile, section):
     return tile * 4 + section
+
+
+def device_mark(tile, section):
+    return (device(tile, section) + 1).astype(jnp.float32)
 
 
 def third(value):
@@ -251,7 +253,7 @@
         axis=0,
     )
     lane = iota((SLOTS, LANE), 1)
-    mark = jnp.where(section == 0, PARENT_MARK + tile.astype(jnp.float32), NEST_MARK)
+    mark = device_mark(tile, section)
     blank = jnp.zeros((SLOTS, LANE), jnp.float32)
     outs = ((west_ref, left), (middle_ref, left), (east_ref, right))
     for s, (out_ref, edge) in enumerate(outs):
@@ -270,36 +272,44 @@
     return jnp.maximum((offset - 2) // ROWS, 1) - 1 + jnp.minimum(tile // 2, 2)
 
 
-def relay_kernel(offset_ref, state_ref, courant_ref, *refs):
-    to_east = refs[0:3]
-    middle = refs[3]
-    to_west = refs[4:7]
-    west_ref, east_ref, rims_ref, pair_ref, cross_ref = refs[7:]
+def relay_kernel(middles, offset_ref, state_ref, courant_ref, *refs):
+    to_east, middle, to_west = refs[:3], refs[3 : 3 + middles], refs[3 + middles : 6 + middles]
+    west_ref, east_ref, rims_ref, pair_ref, cross_ref = refs[6 + middles :]
     tile = lax.axis_index("tile")
+    section = lax.axis_index("section")
     even = tile % 2 == 0
-    source = first_source(offset_ref[0], tile).astype(jnp.float32) + PARENT_MARK
     lane = iota((ROWS, LANE), 1)
-
-    def marked(sources, mark):
+    first = first_source(offset_ref[0], tile)
+    sources = [device_mark(first + slot, 0) for slot in range(3)]
+
+    def marked(refs, mark):
         total = jnp.zeros((ROWS, LANE), jnp.float32)
-        for ref in sources:
+        for ref in refs:
             total += jnp.where(ref[:ROWS, 2 * LANE - 1 :] == mark, ref[:ROWS, LANE:], 0.0)
         return jnp.where(lane < 42, total, 0.0)
 
-    east = marked(to_west, NEST_MARK)
-    west = marked(to_east, NEST_MARK)
+    has_east = (section == 1) | (section == 2)
+    has_west = (section == 2) | (section == 3)
+    east = marked(to_west, jnp.where(has_east, device_mark(tile, section + 1), 0.0))
+    west = marked(to_east, jnp.where(has_west, device_mark(tile, section - 1), 0.0))
     west_ref[...] = west
     east_ref[...] = east
-    rows = middle[...]
-    for ref in to_west + to_east:
-        value = ref[...]
-        rows += jnp.where(value[:, 2 * LANE - 1 :] >= PARENT_MARK, value, 0.0)
+    rows = jnp.zeros((SLOTS, 2 * LANE), jnp.float32)
+    edges = [jnp.zeros((ROWS, LANE), jnp.float32)] * 3
+    for refs_in, target in ((to_west, 1), (middle, 2), (to_east, 3)):
+        marks = [jnp.where(section == target, mark, 0.0) for mark in sources]
+        for ref in refs_in:
+            value = ref[...]
+            mark = value[:, 2 * LANE - 1 :]
+            for source in marks:
+                rows += jnp.where(mark == source, value, 0.0)
+        if target != 2:
+            edges = [edge + marked(refs_in, mark) for edge, mark in zip(edges, marks)]
     wide = iota((SLOTS, LANE), 1)
     rims_ref[:SLOTS, :LANE] = rows[:, :LANE]
     rims_ref[SLOTS:, :LANE] = jnp.zeros((RIMS - SLOTS, LANE), jnp.float32)
     extra = jnp.where((wide >= 42) & (wide < 46), rows[:, LANE:], 0.0)
     extra = jnp.concatenate([extra, jnp.zeros((RIMS - SLOTS, LANE), jnp.float32)], axis=0)
-    edges = [marked(to_west + to_east, source + slot) for slot in range(3)]
     rims_ref[:, LANE:] = jnp.concatenate(edges, axis=0) + extra
 
     def put(rows, lanes, value):
@@ -614,6 +624,51 @@
     return rounds
 
 
+def hops(one, two):
+    (t, s), (u, r) = divmod(one, 4), divmod(two, 4)
+    links = abs((t >> 2) - (u >> 2)) + abs(((t >> 1) & 1) - ((u >> 1) & 1)) + abs(s - r)
+    return links or 0.3
+
+
+def completed(pairs, valid):
+    senders = [d for d in range(32) if d not in {a for a, _ in pairs}]
+    takers = [d for d in range(32) if d not in {b for _, b in pairs}]
+
+    def cost(a, b):
+        from_parent = a % 4 == 0 and b % 4 > 0
+        return 1e3 if a == b or from_parent or (a, b) in valid else hops(a, b) ** 2
+
+    n = len(senders)
+    row_price, column_price = [0.0] * (n + 1), [0.0] * (n + 1)
+    owner = [0] * (n + 1)
+    for i in range(1, n + 1):
+        owner[0] = i
+        column = 0
+        least, before, used = [1e9] * (n + 1), [0] * (n + 1), [False] * (n + 1)
+        while True:
+            used[column] = True
+            row, step, best = owner[column], 1e9, 0
+            for j in range(1, n + 1):
+                if not used[j]:
+                    gap = cost(senders[row - 1], takers[j - 1]) - row_price[row] - column_price[j]
+                    if gap < least[j]:
+                        least[j], before[j] = gap, column
+                    if least[j] < step:
+                        step, best = least[j], j
+            for j in range(n + 1):
+                if used[j]:
+                    row_price[owner[j]] += step
+                    column_price[j] -= step
+                else:
+                    least[j] -= step
+            column = best
+            if owner[column] == 0:
+                break
+        while column:
+            owner[column], column = owner[before[column]], before[column]
+    return pairs + [(senders[owner[j] - 1], takers[j - 1]) for j in range(1, n + 1)]
+
+
 def rim_pairs(start):
     to_chips = [(0, 0), (1, 1), (0, 2), (1, 3), (2, 3), (2, 4), (1, 5), (3, 4), (2, 6), (3, 7)]
     sends = [(start + step, tile) for step, tile in to_chips]
@@ -625,22 +680,11 @@
     for section, inner in ((1, ((2, 1), (3, 2))), (3, ((1, 2), (2, 3)))):
         edges = [(device(a, 0), device(b, section)) for a, b in sends]
         edges += [(device(t, a), device(t, b)) for t in range(8) for a, b in inner]
-        groups.append(in_rounds(edges, 3)[::-1])
+        rounds = in_rounds(edges, 3)[::-1]
+        groups.append([completed(pairs, edges) for pairs in rounds])
     middle = [[(device(a, 0), device(b, 2)) for a, b in pairs] for pairs in middle]
+    middle = [completed(pairs, []) for pairs in middle]
     return groups[0], middle, groups[1]
-
-
-TOGETHER = ((1, 8), (2, 10), (3, 11), (4, 12), (5,), (6,), (7,), (9,))
-
-
-def mean_pairs(distance):
-    (group,) = [g for g in TOGETHER if distance in g]
-    return [
-        (device(3 * tile - step, 0), device(tile, 0))
-        for step in group
-        for tile in range(8)
-        if 0 <= 3 * tile - step < 8
-    ]
 
 
 BOTH = ("tile", "section")
@@ -665,7 +709,7 @@
             for value, lists in zip((west, middle, east), groups)
         )
         return pl.pallas_call(
-            relay_kernel,
+            functools.partial(relay_kernel, len(middle)),
             out_shape=[
                 shaped(ROWS, LANE),
                 shaped(ROWS, LANE),
@@ -673,10 +717,10 @@
                 shaped(HALO + RIMS, COLS),
                 shaped(HALO + ROWS, COLS),
             ],
-            in_specs=[SMEM] + [VMEM] * 9,
+            in_specs=[SMEM] + [VMEM] * (8 + len(middle)),
             out_specs=[VMEM] * 5,
             name="relay",
-        )(nest_offset, planes, speeds, *east, sum(middle), *west)
+        )(nest_offset, planes, speeds, *east, *middle, *west)
 
     west, east, rims, to_pair, to_cross = lax.switch(
         (offset - 2) // ROWS - 1,
@@ -689,8 +733,8 @@
     pair_map = [(device(t, s), device(t ^ 1, s)) for t in range(8) for s in range(4)]
     cross_map = [
         (device(a, s), device(b, s))
-        for low in (1, 3, 5)
-        for a, b in ((low, low + 1), (low + 1, low))
+        for low in (1, 3, 5, 7)
+        for a, b in ((low, (low + 1) % 8), ((low + 1) % 8, low))
         for s in range(4)
     ]
     from_cross = lax.ppermute(to_cross, BOTH, cross_map)

time: 51.6 us -> 47.2 us (0.915)
  starting transfers between devices: 30.5 us -> 19 us
  waiting for transfers between devices: 12.6 us -> 20.4 us
  other arithmetic: 0.63 us -> 0 us
    ppermute x7, starting transfers between devices: 11 us -> 3.51 us  [across(): return lax.ppermute(value, BOTH, pairs)]
    ppermute x1, waiting for transfers between devices: 0.01 us -> 5.32 us  [on_device(): from_cross = lax.ppermute(to_cross, BOTH, cross_map)]
    ppermute x8, starting transfers between devices: 14.9 us -> 11.5 us  [send_rims(): lax.ppermute(value, BOTH, pairs)]
    ppermute x8, waiting for transfers between devices: 1.13 us -> 3.48 us  [send_rims(): lax.ppermute(value, BOTH, pairs)]
    ppermute x7, waiting for transfers between devices: 5.22 us -> 6.07 us  [across(): return lax.ppermute(value, BOTH, pairs)]
    ppermute x1, waiting for transfers between devices: 0.76 us -> 0.01 us  [on_device(): from_pair = lax.ppermute(to_pair, BOTH, pair_map)]
    add x1 -> x0, other arithmetic: 0.63 us -> none  [send_rims(): sum(middle)]
    ppermute x1, starting transfers between devices: 0.67 us -> 0.07 us  [on_device(): from_cross = lax.ppermute(to_cross, BOTH, cross_map)]
  transfers between devices with their start and end apart: 20 -> 20, of which waited for: 8 -> 11; matrix products, arithmetic and copies ran while one was open for 1% -> 0% of each run, Pallas kernels for 0% -> 0%
where the time goes in v5:
time: 47.2 us; the launch traced here: 46.9 us
  waiting for transfers between devices  20.4 us (43%)
  starting transfers between devices  19 us (40%)
  Pallas kernels  6.01 us (13%)
  between operations  0.82 us (2%)
  local copies, waits for them, and re-layouts  0.62 us (1%)
    ppermute x8, starting transfers between devices, send_rims(): lax.ppermute(value, BOTH, pairs)  11.5 us
    ppermute x7, waiting for transfers between devices, across(): return lax.ppermute(value, BOTH, pairs)  6.07 us
    ppermute x3, waiting for transfers between devices, on_device(): lax.ppermute(means, BOTH, [(device(t, s), device(t, 0)) for t in range(8)])  5.53 us
    ppermute x1, waiting for transfers between devices, on_device(): from_cross = lax.ppermute(to_cross, BOTH, cross_map)  5.32 us
    ppermute x3, starting transfers between devices, on_device(): lax.ppermute(means, BOTH, [(device(t, s), device(t, 0)) for t in range(8)])  3.88 us
    ppermute x7, starting transfers between devices, across(): return lax.ppermute(value, BOTH, pairs)  3.51 us
    ppermute x8, waiting for transfers between devices, send_rims(): lax.ppermute(value, BOTH, pairs)  3.48 us
    pallas_call x1, Pallas kernels, send_rims(): pl.pallas_call(functools.partial(relay_kernel, len(middle)), out_shape=[s...  2.03 us
  transfers between devices with their start and end apart: 20, of which 11 were waited for; matrix products, arithmetic and copies ran while one was open for 0% of the time, Pallas kernels for 0%

profile of v5, /device:TPU:0, one launch (start us, length us, event | category | flops | bytes accessed | tf_op | source)
XLA Modules:
  0.0 46.9 jit_solution(16462718406649917538)
XLA Ops:
  0.7 1.6 %pack.1 = (f32[56,256]{1,0:T(8,128)S(1)}, f32[56,256]{1,0:T(8,128)S(1)}, f32[56,256]{1,0:T(8,128)S(1)}) custom-call(s32[1]{0:T(128)S(6)} %copy.21.offset_ref, f32[10,24,384]{2,1,0:T(8,128)} %bitcast.5, f32[4,24,384]{2,1,0:T(8,128)} %bitcast.10), custom_call_target="tpu_custom_call" | custom-call | tf_op jit(solution)/shard_map/pack/pallas_call | solution.py:697
  2.3 17.6 %conditional.1 = ((f32[24,128]{1,0:T(8,128)S(1)}, f32[24,128]{1,0:T(8,128)S(1)}, f32[72,256]{1,0:T(8,128)S(1)}, f32[136,384]{1,0:T(8,128)S(1)}, f32[88,384]{1,0:T(8,128)S(1)})) conditional(s32[]{:T(128)} %clamp.3, (f32[56,256]{1,0:T(8,128)S(1)}, f32[56,256]{1,0:T(8,128)S(1)}, f32[56,256]{1,0:T(8,128)S(1)}, s32[1]{0:T(128)}, ...), branch_computations={%region_0.1_spmd, %region_1.2_spmd, %region_2.3_spmd} | conditional | bytes 3670568 | solution.py:725
  2.4 4.1 %collective-permute-start.4 = (f32[56,256]{1,0:T(8,128)S(1)}, f32[56,256]{1,0:T(8,128)S(1)}, u32[]{:S(2)}, u32[]{:S(2)}) collective-permute-start(f32[56,256]{1,0:T(8,128)S(1)} %get-tuple-element.45), channel_id=1, source_target_pairs={{0,2},{4,0},{6,1},{7,3},{5,4},{1,5},{2,6},{3,7},{12,8},{13,9},{14,... | collective-permute-start | bytes 172040 | tf_op jit(solution)/shard_map/cond/branch_0_fun/ppermute | solution.py:708
  6.4 2.2 %collective-permute-start.2 = (f32[56,256]{1,0:T(8,128)S(1)}, f32[56,256]{1,0:T(8,128)S(1)}, u32[]{:S(2)}, u32[]{:S(2)}) collective-permute-start(f32[56,256]{1,0:T(8,128)S(1)} %get-tuple-element.44), channel_id=1, source_target_pairs={{1,2},{4,3},{5,6},{8,7},{9,10},{10,11},{12,15},{13,14},{16,19},{17... | collective-permute-start | bytes 172040 | tf_op jit(solution)/shard_map/cond/branch_0_fun/ppermute | solution.py:708
  8.7 1.9 %collective-permute-start = (f32[56,256]{1,0:T(8,128)S(1)}, f32[56,256]{1,0:T(8,128)S(1)}, u32[]{:S(2)}, u32[]{:S(2)}) collective-permute-start(f32[56,256]{1,0:T(8,128)S(1)} %get-tuple-element.44), channel_id=1, source_target_pairs={{0,3},{8,15},{12,19},{4,0},{6,1},{3,2},{5,4},{1,5},{7,6},{23,7},{1... | collective-permute-start | bytes 172040 | tf_op jit(solution)/shard_map/cond/branch_0_fun/ppermute | solution.py:708
  10.6 1.3 %collective-permute-start.7 = (f32[56,256]{1,0:T(8,128)S(1)}, f32[56,256]{1,0:T(8,128)S(1)}, u32[]{:S(2)}, u32[]{:S(2)}) collective-permute-start(f32[56,256]{1,0:T(8,128)S(1)} %get-tuple-element.46), channel_id=1, source_target_pairs={{3,2},{4,1},{7,6},{8,5},{10,9},{11,10},{12,13},{15,14},{16,17},{19... | collective-permute-start | bytes 172040 | tf_op jit(solution)/shard_map/cond/branch_0_fun/ppermute | solution.py:708
  12.1 1.9 %collective-permute-start.5 = (f32[56,256]{1,0:T(8,128)S(1)}, f32[56,256]{1,0:T(8,128)S(1)}, u32[]{:S(2)}, u32[]{:S(2)}) collective-permute-start(f32[56,256]{1,0:T(8,128)S(1)} %get-tuple-element.46), channel_id=1, source_target_pairs={{0,1},{8,13},{12,17},{1,0},{6,2},{7,3},{5,4},{21,5},{2,6},{3,7},{9... | collective-permute-start | bytes 172040 | tf_op jit(solution)/shard_map/cond/branch_0_fun/ppermute | solution.py:708
  14.0 0.8 %collective-permute-done.7.refs_7_ = f32[56,256]{1,0:T(8,128)S(1)} collective-permute-done((f32[56,256]{1,0:T(8,128)S(1)}, f32[56,256]{1,0:T(8,128)S(1)}, u32[]{:S(2)}, u32[]{:S(2)}) %collective-permute-start.7) | collective-permute-done | bytes 57376 | tf_op jit(solution)/shard_map/cond/branch_0_fun/ppermute | solution.py:708
  14.8 1.7 %collective-permute-done.6.refs_6_ = f32[56,256]{1,0:T(8,128)S(1)} collective-permute-done((f32[56,256]{1,0:T(8,128)S(1)}, f32[56,256]{1,0:T(8,128)S(1)}, u32[]{:S(2)}, u32[]{:S(2)}) %collective-permute-start.6) | collective-permute-done | bytes 57376 | tf_op jit(solution)/shard_map/cond/branch_0_fun/ppermute | solution.py:708
  16.5 0.8 %collective-permute-done.5.refs_5_ = f32[56,256]{1,0:T(8,128)S(1)} collective-permute-done((f32[56,256]{1,0:T(8,128)S(1)}, f32[56,256]{1,0:T(8,128)S(1)}, u32[]{:S(2)}, u32[]{:S(2)}) %collective-permute-start.5) | collective-permute-done | bytes 57376 | tf_op jit(solution)/shard_map/cond/branch_0_fun/ppermute | solution.py:708
  17.9 2.0 %relay.3 = (f32[24,128]{1,0:T(8,128)S(1)}, f32[24,128]{1,0:T(8,128)S(1)}, f32[72,256]{1,0:T(8,128)S(1)}, f32[136,384]{1,0:T(8,128)S(1)}, f32[88,384]{1,0:T(8,128)S(1)}) custom-call(s32[1]{0:T(128)} %get-tuple-element.41.offset_ref, f32[10,24,384]{2,1,0:T(8,128)S(1)} %get-tuple-element.42.state_ref, f32[4,24,384]{2,1,0:T(8,128)S(1)} %get-tuple-element.43.courant_ref, ...), custom_call_target="tpu_custom_call" | custom-call | tf_op jit(solution)/shard_map/cond/branch_0_fun/relay/pallas_call | solution.py:711
  20.1 5.3 %collective-permute-done.23.cross_ref = f32[88,384]{1,0:T(8,128)S(1)} collective-permute-done((f32[88,384]{1,0:T(8,128)S(1)}, f32[88,384]{1,0:T(8,128)S(1)}, u32[]{:S(2)}, u32[]{:S(2)}) %collective-permute-start.23) | collective-permute-done | bytes 135200 | tf_op jit(solution)/shard_map/ppermute | solution.py:740
  25.5 1.6 %nest.1 = (f32[10,24,384]{2,1,0:T(8,128)S(1)}, f32[80,128]{1,0:T(8,128)S(1)}) custom-call(s32[1]{0:T(128)S(6)} %copy.21.offset_ref, f32[10,24,384]{2,1,0:T(8,128)S(1)} %bitcast.9, f32[4,24,384]{2,1,0:T(8,128)S(1)} %bitcast.14, f32[24,128]{1,0:T(8,128)S(1)} %get-tuple-element.72.west_ref, f32[24,128]{1,0:T(8,128)S(1)} %get-tuple-element.73.east_ref, ...), custom_call_target="tpu_custom_call" | custom-call | tf_op jit(solution)/shard_map/nest/pallas_call | solution.py:742
  27.0 1.3 %collective-permute-start.24 = (f32[80,128]{1,0:T(8,128)S(1)}, f32[80,128]{1,0:T(8,128)S(1)}, u32[]{:S(2)}, u32[]{:S(2)}) collective-permute-start(f32[80,128]{1,0:T(8,128)S(1)} %get-tuple-element.77), channel_id=1, source_target_pairs={{1,0},{5,4},{9,8},{13,12},{17,16},{21,20},{25,24},{29,28}} | collective-permute-start | bytes 122888 | tf_op jit(solution)/shard_map/ppermute | solution.py:760
  28.3 1.3 %collective-permute-start.26 = (f32[80,128]{1,0:T(8,128)S(1)}, f32[80,128]{1,0:T(8,128)S(1)}, u32[]{:S(2)}, u32[]{:S(2)}) collective-permute-start(f32[80,128]{1,0:T(8,128)S(1)} %get-tuple-element.77), channel_id=1, source_target_pairs={{3,0},{7,4},{11,8},{15,12},{19,16},{23,20},{27,24},{31,28}} | collective-permute-start | bytes 122888 | tf_op jit(solution)/shard_map/ppermute | solution.py:760
  29.6 1.3 %collective-permute-start.25 = (f32[80,128]{1,0:T(8,128)S(1)}, f32[80,128]{1,0:T(8,128)S(1)}, u32[]{:S(2)}, u32[]{:S(2)}) collective-permute-start(f32[80,128]{1,0:T(8,128)S(1)} %get-tuple-element.77), channel_id=1, source_target_pairs={{2,0},{6,4},{10,8},{14,12},{18,16},{22,20},{26,24},{30,28}} | collective-permute-start | bytes 122888 | tf_op jit(solution)/shard_map/ppermute | solution.py:760
  30.9 3.0 %collective-permute-done.24 = f32[80,128]{1,0:T(8,128)S(1)} collective-permute-done((f32[80,128]{1,0:T(8,128)S(1)}, f32[80,128]{1,0:T(8,128)S(1)}, u32[]{:S(2)}, u32[]{:S(2)}) %collective-permute-start.24) | collective-permute-done | bytes 40992 | tf_op jit(solution)/shard_map/ppermute | solution.py:760
  34.0 2.5 %collective-permute-done.25 = f32[80,128]{1,0:T(8,128)S(1)} collective-permute-done((f32[80,128]{1,0:T(8,128)S(1)}, f32[80,128]{1,0:T(8,128)S(1)}, u32[]{:S(2)}, u32[]{:S(2)}) %collective-permute-start.25) | collective-permute-done | bytes 40992 | tf_op jit(solution)/shard_map/ppermute | solution.py:760
  36.5 0.7 %collective-permute-start.32 = (f32[80,384]{1,0:T(8,128)S(1)}, f32[80,384]{1,0:T(8,128)S(1)}, u32[]{:S(2)}, u32[]{:S(2)}) collective-permute-start(f32[80,384]{1,0:T(8,128)S(1)} %constant_dynamic-update-slice_fusion.refs_0_), channel_id=1, source_target_pairs={{0,28},{1,29},{2,30},{3,31},{4,24},{5,25},{6,26},{7,27},{8,20},{9,... | collective-permute-start | bytes 368648 | tf_op jit(solution)/shard_map/ppermute | solution.py:768
  37.2 1.6 %collective-permute-start.30 = (f32[80,384]{1,0:T(8,128)S(1)}, f32[80,384]{1,0:T(8,128)S(1)}, u32[]{:S(2)}, u32[]{:S(2)}) collective-permute-start(f32[80,384]{1,0:T(8,128)S(1)} %constant_dynamic-update-slice_fusion.refs_0_), channel_id=1, source_target_pairs={{0,16},{1,17},{2,18},{3,19},{4,20},{5,21},{6,22},{7,23},{8,24},{9,... | collective-permute-start | bytes 368648 | tf_op jit(solution)/shard_map/ppermute | solution.py:768
  39.5 2.6 %collective-permute-done.32.refs_7_ = f32[80,384]{1,0:T(8,128)S(1)} collective-permute-done((f32[80,384]{1,0:T(8,128)S(1)}, f32[80,384]{1,0:T(8,128)S(1)}, u32[]{:S(2)}, u32[]{:S(2)}) %collective-permute-start.32) | collective-permute-done | bytes 122912 | tf_op jit(solution)/shard_map/ppermute | solution.py:768
  42.0 2.5 %collective-permute-done.30.refs_4_ = f32[80,384]{1,0:T(8,128)S(1)} collective-permute-done((f32[80,384]{1,0:T(8,128)S(1)}, f32[80,384]{1,0:T(8,128)S(1)}, u32[]{:S(2)}, u32[]{:S(2)}) %collective-permute-start.30) | collective-permute-done | bytes 122912 | tf_op jit(solution)/shard_map/ppermute | solution.py:768
  45.1 0.8 %collective-permute-done.31.refs_5_ = f32[80,384]{1,0:T(8,128)S(1)} collective-permute-done((f32[80,384]{1,0:T(8,128)S(1)}, f32[80,384]{1,0:T(8,128)S(1)}, u32[]{:S(2)}, u32[]{:S(2)}) %collective-permute-start.31) | collective-permute-done | bytes 122912 | tf_op jit(solution)/shard_map/ppermute | solution.py:768
  46.1 0.8 %merge.1 = f32[10,24,384]{2,1,0:T(8,128)} custom-call(s32[1]{0:T(128)S(6)} %copy.21.offset_ref, f32[80,384]{1,0:T(8,128)S(1)} %constant_dynamic-update-slice_fusion.refs_0_, f32[80,384]{1,0:T(8,128)S(1)} %collective-permute-done.27.refs_1_, f32[80,384]{1,0:T(8,128)S(1)} %collective-permute-done.29.refs_2_, f32[80,384]{1,0:T(8,128)S(1)} %collective-permute-done.28.refs_3_, ...), custom_call_target="tpu_custom_call" | custom-call | tf_op jit(solution)/shard_map/merge/pallas_call | solution.py:775
  (44 shorter events, 2.3 us)
Async XLA Ops:
  2.4 8.3 %collective-permute-start.4 = (f32[56,256]{1,0:T(8,128)S(1)}, f32[56,256]{1,0:T(8,128)S(1)}, u32[]{:S(2)}, u32[]{:S(2)}) collective-permute-start(f32[56,256]{1,0:T(8,128)S(1)} %get-tuple-element.45), channel_id=1, source_target_pairs={{0,2},{4,0},{6,1},{7,3},{5,4},{1,5},{2,6},{3,7},{12,8},{13,9},{14,... | collective-permute-start | bytes 172040 | tf_op jit(solution)/shard_map/cond/branch_0_fun/ppermute | solution.py:708
  6.4 5.5 %collective-permute-start.3 = (f32[56,256]{1,0:T(8,128)S(1)}, f32[56,256]{1,0:T(8,128)S(1)}, u32[]{:S(2)}, u32[]{:S(2)}) collective-permute-start(f32[56,256]{1,0:T(8,128)S(1)} %get-tuple-element.45), channel_id=1, source_target_pairs={{4,2},{8,6},{12,26},{16,30},{5,0},{6,1},{7,3},{0,4},{2,5},{3,7},{2... | collective-permute-start | bytes 172040 | tf_op jit(solution)/shard_map/cond/branch_0_fun/ppermute | solution.py:708
  6.4 5.6 %collective-permute-start.2 = (f32[56,256]{1,0:T(8,128)S(1)}, f32[56,256]{1,0:T(8,128)S(1)}, u32[]{:S(2)}, u32[]{:S(2)}) collective-permute-start(f32[56,256]{1,0:T(8,128)S(1)} %get-tuple-element.44), channel_id=1, source_target_pairs={{1,2},{4,3},{5,6},{8,7},{9,10},{10,11},{12,15},{13,14},{16,19},{17... | collective-permute-start | bytes 172040 | tf_op jit(solution)/shard_map/cond/branch_0_fun/ppermute | solution.py:708
  8.7 5.3 %collective-permute-start.1 = (f32[56,256]{1,0:T(8,128)S(1)}, f32[56,256]{1,0:T(8,128)S(1)}, u32[]{:S(2)}, u32[]{:S(2)}) collective-permute-start(f32[56,256]{1,0:T(8,128)S(1)} %get-tuple-element.44), channel_id=1, source_target_pairs={{2,3},{4,11},{6,7},{8,23},{12,27},{14,15},{16,31},{18,19},{5,0},{1... | collective-permute-start | bytes 172040 | tf_op jit(solution)/shard_map/cond/branch_0_fun/ppermute | solution.py:708
  8.7 5.3 %collective-permute-start = (f32[56,256]{1,0:T(8,128)S(1)}, f32[56,256]{1,0:T(8,128)S(1)}, u32[]{:S(2)}, u32[]{:S(2)}) collective-permute-start(f32[56,256]{1,0:T(8,128)S(1)} %get-tuple-element.44), channel_id=1, source_target_pairs={{0,3},{8,15},{12,19},{4,0},{6,1},{3,2},{5,4},{1,5},{7,6},{23,7},{1... | collective-permute-start | bytes 172040 | tf_op jit(solution)/shard_map/cond/branch_0_fun/ppermute | solution.py:708
  10.6 6.7 %copy-start.16 = (f32[56,256]{1,0:T(8,128)}, f32[56,256]{1,0:T(8,128)S(1)}, u32[]{:S(2)}) copy-start(f32[56,256]{1,0:T(8,128)S(1)} %collective-permute-done.4.refs_4_) | copy-start | bytes 172036 | tf_op jit(solution)/shard_map/cond
  10.6 4.2 %collective-permute-start.7 = (f32[56,256]{1,0:T(8,128)S(1)}, f32[56,256]{1,0:T(8,128)S(1)}, u32[]{:S(2)}, u32[]{:S(2)}) collective-permute-start(f32[56,256]{1,0:T(8,128)S(1)} %get-tuple-element.46), channel_id=1, source_target_pairs={{3,2},{4,1},{7,6},{8,5},{10,9},{11,10},{12,13},{15,14},{16,17},{19... | collective-permute-start | bytes 172040 | tf_op jit(solution)/shard_map/cond/branch_0_fun/ppermute | solution.py:708
  11.9 5.4 %copy-start.17 = (f32[56,256]{1,0:T(8,128)}, f32[56,256]{1,0:T(8,128)S(1)}, u32[]{:S(2)}) copy-start(f32[56,256]{1,0:T(8,128)S(1)} %collective-permute-done.3.refs_3_) | copy-start | bytes 172036 | tf_op jit(solution)/shard_map/cond
  11.9 4.6 %collective-permute-start.6 = (f32[56,256]{1,0:T(8,128)S(1)}, f32[56,256]{1,0:T(8,128)S(1)}, u32[]{:S(2)}, u32[]{:S(2)}) collective-permute-start(f32[56,256]{1,0:T(8,128)S(1)} %get-tuple-element.46), channel_id=1, source_target_pairs={{2,1},{4,9},{6,5},{8,21},{12,25},{14,13},{16,29},{18,17},{1,0},{5,... | collective-permute-start | bytes 172040 | tf_op jit(solution)/shard_map/cond/branch_0_fun/ppermute | solution.py:708
  12.0 5.3 %copy-start.18 = (f32[56,256]{1,0:T(8,128)}, f32[56,256]{1,0:T(8,128)S(1)}, u32[]{:S(2)}) copy-start(f32[56,256]{1,0:T(8,128)S(1)} %collective-permute-done.2.refs_2_) | copy-start | bytes 172036 | tf_op jit(solution)/shard_map/cond
  12.1 5.3 %collective-permute-start.5 = (f32[56,256]{1,0:T(8,128)S(1)}, f32[56,256]{1,0:T(8,128)S(1)}, u32[]{:S(2)}, u32[]{:S(2)}) collective-permute-start(f32[56,256]{1,0:T(8,128)S(1)} %get-tuple-element.46), channel_id=1, source_target_pairs={{0,1},{8,13},{12,17},{1,0},{6,2},{7,3},{5,4},{21,5},{2,6},{3,7},{9... | collective-permute-start | bytes 172040 | tf_op jit(solution)/shard_map/cond/branch_0_fun/ppermute | solution.py:708
  14.0 3.4 %copy-start.20 = (f32[56,256]{1,0:T(8,128)}, f32[56,256]{1,0:T(8,128)S(1)}, u32[]{:S(2)}) copy-start(f32[56,256]{1,0:T(8,128)S(1)} %collective-permute-done.refs_0_) | copy-start | bytes 172036 | tf_op jit(solution)/shard_map/cond
  20.0 5.5 %collective-permute-start.22 = (f32[136,384]{1,0:T(8,128)S(1)}, f32[136,384]{1,0:T(8,128)S(1)}, u32[]{:S(2)}, u32[]{:S(2)}) collective-permute-start(f32[136,384]{1,0:T(8,128)S(1)} %get-tuple-element.75), channel_id=1, source_target_pairs={{0,4},{1,5},{2,6},{3,7},{4,0},{5,1},{6,2},{7,3},{8,12},{9,13},{10,... | collective-permute-start | bytes 626696 | tf_op jit(solution)/shard_map/ppermute | solution.py:741
  20.1 5.4 %collective-permute-start.23 = (f32[88,384]{1,0:T(8,128)S(1)}, f32[88,384]{1,0:T(8,128)S(1)}, u32[]{:S(2)}, u32[]{:S(2)}) collective-permute-start(f32[88,384]{1,0:T(8,128)S(1)} %get-tuple-element.76), channel_id=1, source_target_pairs={{4,8},{5,9},{6,10},{7,11},{8,4},{9,5},{10,6},{11,7},{12,16},{13,17... | collective-permute-start | bytes 405512 | tf_op jit(solution)/shard_map/ppermute | solution.py:740
  27.0 6.9 %collective-permute-start.24 = (f32[80,128]{1,0:T(8,128)S(1)}, f32[80,128]{1,0:T(8,128)S(1)}, u32[]{:S(2)}, u32[]{:S(2)}) collective-permute-start(f32[80,128]{1,0:T(8,128)S(1)} %get-tuple-element.77), channel_id=1, source_target_pairs={{1,0},{5,4},{9,8},{13,12},{17,16},{21,20},{25,24},{29,28}} | collective-permute-start | bytes 122888 | tf_op jit(solution)/shard_map/ppermute | solution.py:760
  28.3 8.1 %collective-permute-start.26 = (f32[80,128]{1,0:T(8,128)S(1)}, f32[80,128]{1,0:T(8,128)S(1)}, u32[]{:S(2)}, u32[]{:S(2)}) collective-permute-start(f32[80,128]{1,0:T(8,128)S(1)} %get-tuple-element.77), channel_id=1, source_target_pairs={{3,0},{7,4},{11,8},{15,12},{19,16},{23,20},{27,24},{31,28}} | collective-permute-start | bytes 122888 | tf_op jit(solution)/shard_map/ppermute | solution.py:760
  29.6 6.8 %collective-permute-start.25 = (f32[80,128]{1,0:T(8,128)S(1)}, f32[80,128]{1,0:T(8,128)S(1)}, u32[]{:S(2)}, u32[]{:S(2)}) collective-permute-start(f32[80,128]{1,0:T(8,128)S(1)} %get-tuple-element.77), channel_id=1, source_target_pairs={{2,0},{6,4},{10,8},{14,12},{18,16},{22,20},{26,24},{30,28}} | collective-permute-start | bytes 122888 | tf_op jit(solution)/shard_map/ppermute | solution.py:760
  36.5 5.5 %collective-permute-start.32 = (f32[80,384]{1,0:T(8,128)S(1)}, f32[80,384]{1,0:T(8,128)S(1)}, u32[]{:S(2)}, u32[]{:S(2)}) collective-permute-start(f32[80,384]{1,0:T(8,128)S(1)} %constant_dynamic-update-slice_fusion.refs_0_), channel_id=1, source_target_pairs={{0,28},{1,29},{2,30},{3,31},{4,24},{5,25},{6,26},{7,27},{8,20},{9,... | collective-permute-start | bytes 368648 | tf_op jit(solution)/shard_map/ppermute | solution.py:768
  37.2 7.3 %collective-permute-start.30 = (f32[80,384]{1,0:T(8,128)S(1)}, f32[80,384]{1,0:T(8,128)S(1)}, u32[]{:S(2)}, u32[]{:S(2)}) collective-permute-start(f32[80,384]{1,0:T(8,128)S(1)} %constant_dynamic-update-slice_fusion.refs_0_), channel_id=1, source_target_pairs={{0,16},{1,17},{2,18},{3,19},{4,20},{5,21},{6,22},{7,23},{8,24},{9,... | collective-permute-start | bytes 368648 | tf_op jit(solution)/shard_map/ppermute | solution.py:768
  38.8 5.8 %collective-permute-start.28 = (f32[80,384]{1,0:T(8,128)S(1)}, f32[80,384]{1,0:T(8,128)S(1)}, u32[]{:S(2)}, u32[]{:S(2)}) collective-permute-start(f32[80,384]{1,0:T(8,128)S(1)} %constant_dynamic-update-slice_fusion.refs_0_), channel_id=1, source_target_pairs={{0,12},{1,13},{2,14},{3,15},{4,8},{5,9},{6,10},{7,11},{8,4},{9,5},... | collective-permute-start | bytes 368648 | tf_op jit(solution)/shard_map/ppermute | solution.py:768
  39.5 5.6 %collective-permute-start.27 = (f32[80,384]{1,0:T(8,128)S(1)}, f32[80,384]{1,0:T(8,128)S(1)}, u32[]{:S(2)}, u32[]{:S(2)}) collective-permute-start(f32[80,384]{1,0:T(8,128)S(1)} %constant_dynamic-update-slice_fusion.refs_0_), channel_id=1, source_target_pairs={{0,4},{1,5},{2,6},{3,7},{4,0},{5,1},{6,2},{7,3},{8,12},{9,13},{10,... | collective-permute-start | bytes 368648 | tf_op jit(solution)/shard_map/ppermute | solution.py:768
  42.0 3.0 %collective-permute-start.33 = (f32[80,384]{1,0:T(8,128)S(1)}, f32[80,384]{1,0:T(8,128)S(1)}, u32[]{:S(2)}, u32[]{:S(2)}) collective-permute-start(f32[80,384]{1,0:T(8,128)S(1)} %collective-permute-done.32.refs_7_), channel_id=1, source_target_pairs={{0,4},{1,5},{2,6},{3,7},{4,0},{5,1},{6,2},{7,3},{8,12},{9,13},{10,... | collective-permute-start | bytes 368648 | tf_op jit(solution)/shard_map/ppermute | solution.py:768
  44.6 1.3 %collective-permute-start.31 = (f32[80,384]{1,0:T(8,128)S(1)}, f32[80,384]{1,0:T(8,128)S(1)}, u32[]{:S(2)}, u32[]{:S(2)}) collective-permute-start(f32[80,384]{1,0:T(8,128)S(1)} %collective-permute-done.30.refs_4_), channel_id=1, source_target_pairs={{0,4},{1,5},{2,6},{3,7},{4,0},{5,1},{6,2},{7,3},{8,12},{9,13},{10,... | collective-permute-start | bytes 368648 | tf_op jit(solution)/shard_map/ppermute | solution.py:768
  44.6 1.4 %collective-permute-start.29 = (f32[80,384]{1,0:T(8,128)S(1)}, f32[80,384]{1,0:T(8,128)S(1)}, u32[]{:S(2)}, u32[]{:S(2)}) collective-permute-start(f32[80,384]{1,0:T(8,128)S(1)} %collective-permute-done.28.refs_3_), channel_id=1, source_target_pairs={{0,4},{1,5},{2,6},{3,7},{4,0},{5,1},{6,2},{7,3},{8,12},{9,13},{10,... | collective-permute-start | bytes 368648 | tf_op jit(solution)/shard_map/ppermute | solution.py:768
  (6 other events, 11.4 us)

commit v6 on v5

--- a/solution.py
+++ b/solution.py
@@ -189,7 +189,6 @@
 SLOTS = 4 * PLANES
 HALO = SLOTS + 8
 RIMS = 3 * ROWS
-EXACT = lax.Precision.HIGHEST
 
 
 def device(tile, section):
@@ -208,8 +207,19 @@
     return lax.broadcasted_iota(jnp.int32, shape, dim)
 
 
-def dot(a, b):
-    return jnp.dot(a, b, precision=EXACT, preferred_element_type=jnp.float32)
+def parts(value):
+    high = value.astype(jnp.bfloat16)
+    rest = value - high.astype(jnp.float32)
+    middle = rest.astype(jnp.bfloat16)
+    return high, middle, (rest - middle.astype(jnp.float32)).astype(jnp.bfloat16)
+
+
+def product(a, b):
+    return jnp.dot(a, b, preferred_element_type=jnp.float32)
+
+
+def choose(ones, value):
+    return sum(product(ones.astype(jnp.bfloat16), part) for part in parts(value))
 
 
 def turn(value, steps, dim):
@@ -222,7 +232,9 @@
     return state_ref[p] if p < STATES else courant_ref[p - STATES]
 
 
-def pack_kernel(offset_ref, state_ref, courant_ref, west_ref, middle_ref, east_ref):
+def pack_kernel(
+    offset_ref, state_ref, courant_ref, west_ref, middle_ref, east_ref, pair_ref, cross_ref
+):
     tile = lax.axis_index("tile")
     section = lax.axis_index("section")
     offset = offset_ref[0]
@@ -238,7 +250,7 @@
     top = (first <= offset + 2) & (first + ROWS - 1 >= offset - 1)
     base = jnp.where(top, offset - 1, offset + 61) - first
 
-    def chosen(start, count):
+    def chosen(count):
         slot = iota((4 * count, ROWS * count), 0)
         column = iota((4 * count, ROWS * count), 1)
         local = base + (slot & 3)
@@ -247,8 +259,8 @@
 
     rows = jnp.concatenate(
         [
-            dot(chosen(0, STATES), state_ref[...].reshape(STATES * ROWS, COLS)),
-            dot(chosen(0, 4), courant_ref[...].reshape(4 * ROWS, COLS)),
+            choose(chosen(STATES), state_ref[...].reshape(STATES * ROWS, COLS)),
+            choose(chosen(4), courant_ref[...].reshape(4 * ROWS, COLS)),
         ],
         axis=0,
     )
@@ -268,59 +280,66 @@
         out_ref[ROWS:, LANE:] = side[ROWS:]
 
 
-def first_source(offset, tile):
-    return jnp.maximum((offset - 2) // ROWS, 1) - 1 + jnp.minimum(tile // 2, 2)
-
-
-def relay_kernel(middles, offset_ref, state_ref, courant_ref, *refs):
+    even = tile % 2 == 0
+    for p in range(PLANES):
+        source = plane_of(state_ref, courant_ref, p)
+        head, tail = source[:4], source[ROWS - 4 :]
+        pair_ref[4 * p : 4 * p + 4] = jnp.where(even, tail, head)
+        cross_ref[4 * p : 4 * p + 4] = jnp.where(even, head, tail)
+
+
+def first_source(start, tile):
+    return start - 1 + jnp.minimum(tile // 2, 2)
+
+
+def relay_kernel(start, middles, _, __, *refs):
     to_east, middle, to_west = refs[:3], refs[3 : 3 + middles], refs[3 + middles : 6 + middles]
     west_ref, east_ref, rims_ref, pair_ref, cross_ref = refs[6 + middles :]
     tile = lax.axis_index("tile")
     section = lax.axis_index("section")
     even = tile % 2 == 0
     lane = iota((ROWS, LANE), 1)
-    first = first_source(offset_ref[0], tile)
+    first = first_source(start, tile)
     sources = [device_mark(first + slot, 0) for slot in range(3)]
-
-    def marked(refs, mark):
-        total = jnp.zeros((ROWS, LANE), jnp.float32)
-        for ref in refs:
-            total += jnp.where(ref[:ROWS, 2 * LANE - 1 :] == mark, ref[:ROWS, LANE:], 0.0)
-        return jnp.where(lane < 42, total, 0.0)
 
     has_east = (section == 1) | (section == 2)
     has_west = (section == 2) | (section == 3)
-    east = marked(to_west, jnp.where(has_east, device_mark(tile, section + 1), 0.0))
-    west = marked(to_east, jnp.where(has_west, device_mark(tile, section - 1), 0.0))
+    east_mark = jnp.where(has_east, device_mark(tile, section + 1), 0.0)
+    west_mark = jnp.where(has_west, device_mark(tile, section - 1), 0.0)
+    nothing = jnp.zeros((ROWS, LANE), jnp.float32)
+    east = west = nothing
+    edges = [nothing] * 3
+    center = side = jnp.zeros((SLOTS, LANE), jnp.float32)
+    targets = [3] * 3 + [2] * middles + [1] * 3
+    for ref, target in zip(to_east + middle + to_west, targets):
+        tail = ref[:, LANE:]
+        mark = jnp.broadcast_to(tail[:, LANE - 1 :], (SLOTS, LANE))
+        marks = [jnp.where(section == target, source, 0.0) for source in sources]
+        hits = [mark == source for source in marks]
+        hit = hits[0] | hits[1] | hits[2]
+        center = jnp.where(hit, center + ref[:, :LANE], center)
+        side = jnp.where(hit, side + tail, side)
+        if target != 2:
+            cells = tail[:ROWS]
+            edges = [jnp.where(one[:ROWS], cells, edge) for one, edge in zip(hits, edges)]
+        if target == 1:
+            east = jnp.where(mark[:ROWS] == east_mark, cells, east)
+        if target == 3:
+            west = jnp.where(mark[:ROWS] == west_mark, cells, west)
+    east, west, *edges = [jnp.where(lane < 42, value, 0.0) for value in (east, west, *edges)]
     west_ref[...] = west
     east_ref[...] = east
-    rows = jnp.zeros((SLOTS, 2 * LANE), jnp.float32)
-    edges = [jnp.zeros((ROWS, LANE), jnp.float32)] * 3
-    for refs_in, target in ((to_west, 1), (middle, 2), (to_east, 3)):
-        marks = [jnp.where(section == target, mark, 0.0) for mark in sources]
-        for ref in refs_in:
-            value = ref[...]
-            mark = value[:, 2 * LANE - 1 :]
-            for source in marks:
-                rows += jnp.where(mark == source, value, 0.0)
-        if target != 2:
-            edges = [edge + marked(refs_in, mark) for edge, mark in zip(edges, marks)]
     wide = iota((SLOTS, LANE), 1)
-    rims_ref[:SLOTS, :LANE] = rows[:, :LANE]
+    rims_ref[:SLOTS, :LANE] = center
     rims_ref[SLOTS:, :LANE] = jnp.zeros((RIMS - SLOTS, LANE), jnp.float32)
-    extra = jnp.where((wide >= 42) & (wide < 46), rows[:, LANE:], 0.0)
+    extra = jnp.where((wide >= 42) & (wide < 46), side, 0.0)
     extra = jnp.concatenate([extra, jnp.zeros((RIMS - SLOTS, LANE), jnp.float32)], axis=0)
     rims_ref[:, LANE:] = jnp.concatenate(edges, axis=0) + extra
 
-    def put(rows, lanes, value):
+    for lanes, value in ((slice(0, LANE), west), (slice(LANE, 2 * LANE), east)):
         head, tail = value[:4], value[ROWS - 4 :]
-        pair_ref[rows, lanes] = jnp.where(even, tail, head)
-        cross_ref[rows, lanes] = jnp.where(even, head, tail)
-
-    for p in range(PLANES):
-        put(slice(4 * p, 4 * p + 4), slice(None), plane_of(state_ref, courant_ref, p))
-    put(slice(SLOTS, SLOTS + 4), slice(0, LANE), west)
-    put(slice(SLOTS, SLOTS + 4), slice(LANE, 2 * LANE), east)
+        pair_ref[SLOTS : SLOTS + 4, lanes] = jnp.where(even, tail, head)
+        cross_ref[SLOTS : SLOTS + 4, lanes] = jnp.where(even, head, tail)
     pair_ref[HALO:, : 2 * LANE] = rims_ref[...]
     cross_ref[HALO:, :LANE] = edges[0]
 
@@ -350,8 +369,8 @@
     here,
     there,
     factors,
-    base_force,
-    step_force,
+    column_force,
+    row_force,
     narrowed,
 ):
     tile = lax.axis_index("tile")
@@ -424,139 +443,169 @@
         factors[level, 4] = from_east * keep
     factors[0, 5] = mixing * keep
 
-    base_force[...] = jnp.zeros(base_force.shape, jnp.float32)
-    step_force[...] = jnp.zeros(step_force.shape, jnp.float32)
     rims = rims_ref[...] + pair_ref[HALO:, : 2 * LANE]
-
-    @pl.when((section == 1) | (section == 3))
+    on_left = section == 1
+    on_right = section == 3
+    at_first = is_nest & (tile == 0)
+    at_last = is_nest & (tile == 7)
+
+    @pl.when(on_left | on_right)
     def _():
-        on_left = section == 1
         before_six = jnp.where(tile == 6, cross_ref[HALO:, :LANE], 0.0)
         edges = jnp.concatenate([rims[:ROWS, LANE:] + before_six, rims[ROWS:, LANE:]], axis=0)
-        source_tile = first_source(offset, tile)
-        pick = iota((96, RIMS), 0)
-        part = pick >> 5
-        near = pick & 31
-        near = jnp.where(near < 28, near, near - 32)
-        coarse = offset + tile * 8 + third(near + 6) - 2 + part - 1 - source_tile * ROWS
-        picked = dot((iota((96, RIMS), 1) == coarse).astype(jnp.float32), edges)
-        south, value, north = picked[:32], picked[32:64], picked[64:]
-        place = lane - 3 * third(lane)
+        start = offset + tile * 8 - 2 - first_source(jnp.maximum((offset - 2) // ROWS, 1), tile) * ROWS
+        value = pltpu.roll(edges, RIMS - start, 0)[:16]
+        short = iota((16, LANE), 1)
+        place = short - 3 * third(short)
         west = jnp.where(place == jnp.where(on_left, 0, -1), value, turn(value, 1, 1))
         east = jnp.where(place == jnp.where(on_left, -1, 2), value, turn(value, -1, 1))
-        other = jnp.where((third(lane) & 1) == 0, turn(value, -3, 1), turn(value, 3, 1))
-        cy = jnp.zeros((32, LANE), jnp.float32)
-        cx = jnp.zeros((32, LANE), jnp.float32)
+        other = jnp.where((third(short) & 1) == 0, turn(value, -3, 1), turn(value, 3, 1))
+        cy = jnp.zeros((16, LANE), jnp.float32)
+        cx = jnp.zeros((16, LANE), jnp.float32)
         for field in range(STATES // 2):
-            mine = (lane >= 6 * field) & (lane < 6 * field + 6)
+            mine = (short >= 6 * field) & (short < 6 * field + 6)
             cy = jnp.where(mine, turn(value, 6 * field - 3 * STATES, 1), cy)
             cx = jnp.where(mine, turn(value, 6 * field - 3 * STATES - 6, 1), cx)
-        change = flux(value, south, north, west, east, other, cy, cx) / RATIO
-        out = iota((LANE, STATES * LANE), 1)
-        spot = out & (LANE - 1)
-        wanted = 3 * (out >> 7) + jnp.where(on_left, third(spot), third(spot - 119))
-        start = jnp.where(on_left, 0, LANE - 6)
-        valid = (spot >= start) & (spot < start + 6)
-        spread = (valid & (iota((LANE, STATES * LANE), 0) == wanted)).astype(jnp.float32)
-        forced = dot(jnp.concatenate([value, change], axis=0), spread)
-
-        def place_side(lanes):
+        change = (
+            flux(value, turn(value, 1, 0), turn(value, -1, 0), west, east, other, cy, cx) / RATIO
+        )
+        eight = iota((8, LANE), 0)
+
+        def tall(narrow):
+            tiles = []
+            for block in range(4):
+                rows = [8 * block + i for i in range(8)]
+                under = [(i if i < 28 else i - 32) // RATIO + 2 for i in rows]
+                tile_rows = jnp.broadcast_to(narrow[under[0] : under[0] + 1], (8, LANE))
+                for i in range(1, 8):
+                    if under[i] != under[i - 1]:
+                        tile_rows = jnp.where(eight >= i, narrow[under[i] : under[i] + 1], tile_rows)
+                tiles.append(tile_rows)
+            return jnp.concatenate(tiles, axis=0)
+
+        wide_value, wide_change = tall(value), tall(change)
+
+        def place_side(lanes, first, split):
+            free = row_depth[:, lanes] >= ZONE
+            share = jnp.where(free, weight[:, lanes], 0.0)
             for p in range(STATES):
-                block = forced[:, p * LANE : (p + 1) * LANE]
-                base_force[p, :, lanes] = weight[:, lanes] * block[:32]
-                step_force[p, :, lanes] = weight[:, lanes] * block[32:]
+                for kind, source in enumerate((wide_value, wide_change)):
+                    at = 3 * p + first
+                    near, far = source[:, at : at + 1], source[:, at + 1 : at + 2]
+                    column_force[kind, p] = share * jnp.where(lane < split, near, far)
 
         @pl.when(on_left)
         def _():
-            place_side(slice(0, LANE))
-
-        @pl.when(jnp.logical_not(on_left))
+            place_side(slice(0, LANE), 0, 3)
+
+        @pl.when(on_right)
         def _():
-            place_side(slice(2 * LANE, 3 * LANE))
-
-    @pl.when(is_nest & ((tile == 0) | (tile == 7)))
+            place_side(slice(2 * LANE, 3 * LANE), 1, LANE - 3)
+
+    @pl.when(at_first | at_last)
     def _():
-        rows = rims[:SLOTS]
         wide = iota((8, 2 * LANE), 1)
-        narrow = iota((SLOTS, LANE), 1)
-        outside = turn(rows[:, LANE:], 84, 1)
-        outside = jnp.where((narrow < 2) | (narrow >= LANE - 2), outside, 0.0)
-        rows = jnp.concatenate([rows[:, :LANE], outside], axis=1)
+        short = iota((8, LANE), 1)
+        eight = iota((8, 4 * LANE), 0)
+        outside = turn(rims[:SLOTS, LANE:], 84, 1)
+        rows = jnp.concatenate([rims[:SLOTS, :LANE], outside], axis=1)
         cy = rows[4 * STATES : 4 * STATES + 8]
         cx = rows[4 * STATES + 8 :]
-        changes = []
+        under = [((short + LANE * i) * 171) >> 9 for i in range(3)]
+
+        def stretch(value):
+            inside = [
+                jnp.take_along_axis(value[:, :LANE], i, axis=1, mode="promise_in_bounds")
+                for i in under
+            ]
+            after_last = value[:, LANE : LANE + 1]
+            before_first = value[:, 2 * LANE - 1 :]
+            beside = jnp.where(
+                short < 3, after_last, jnp.where(short >= LANE - 3, before_first, 0.0)
+            )
+            return jnp.concatenate(inside + [beside], axis=1)
+
+        forces = []
         for field in range(STATES // 2):
             value = rows[8 * field : 8 * field + 8]
             west = jnp.where(wide == jnp.where(section == 1, 0, -1), value, turn(value, 1, 1))
-            east = jnp.where(wide == jnp.where(section == 3, LANE - 1, -1), value, turn(value, -1, 1))
-            changes.append(
-                flux(
-                    value,
-                    turn(value, 1, 0),
-                    turn(value, -1, 0),
-                    west,
-                    east,
-                    turn(value, 4, 0),
-                    cy,
-                    cx,
-                )
-                / RATIO
+            east = jnp.where(
+                wide == jnp.where(section == 3, LANE - 1, -1), value, turn(value, -1, 1)
             )
-        both = jnp.concatenate([rows[: 4 * STATES]] + changes, axis=0)
-        target = iota((2 * LANE, 4 * LANE), 1)
-        target = jnp.where(target < 448, target, target - 512)
-        coarse = (((target + 66) * 171) >> 9) - 22
-        spread = (iota((2 * LANE, 4 * LANE), 0) == (coarse & (2 * LANE - 1))).astype(jnp.float32)
-        forced = dot(both, spread)
-        eight = iota((8, 4 * LANE), 0)
+            south, north, other = turn(value, 1, 0), turn(value, -1, 0), turn(value, 4, 0)
+            change = flux(value, south, north, west, east, other, cy, cx) / RATIO
+            forces.append((stretch(value), stretch(change)))
 
         def place_rows(rows, split):
-            zone = jnp.where(split == 3, eight < ZONE, eight >= 8 - ZONE)
+            share = jnp.where(row_depth[rows] < ZONE, weight[rows], 0.0)
             for p in range(STATES):
-                for ref, start in ((base_force, 0), (step_force, 4 * STATES)):
-                    spot = start + 4 * p
-                    value = jnp.where(eight < split, forced[spot + 1 : spot + 2], forced[spot + 2 : spot + 3])
-                    ref[p, rows, :] = jnp.where(zone, weight[rows] * value, ref[p, rows, :])
-
-        @pl.when(tile == 0)
+                at = 4 * (p % 2)
+                for kind in range(2):
+                    source = forces[p // 2][kind]
+                    near, far = source[at + 1 : at + 2], source[at + 2 : at + 3]
+                    row_force[kind, p] = share * jnp.where(eight < split, near, far)
+
+        @pl.when(at_first)
         def _():
             place_rows(slice(0, 8), 3)
 
-        @pl.when(tile == 7)
+        @pl.when(at_last)
         def _():
             place_rows(slice(16, 24), 5)
 
-    def substep(source, target, number):
+    def substep(source, target, number, rows, lanes):
         def per_field(field, carry):
             values = [source[2 * field + level] for level in range(2)]
             for level in range(2):
                 value = values[level]
-                result = factors[level, 0] * value + factors[0, 5] * values[1 - level]
-                result += factors[level, 1] * turn(value, 1, 0)
-                result += factors[level, 2] * turn(value, -1, 0)
-                result += factors[level, 3] * turn(value, 1, 1)
-                result += factors[level, 4] * turn(value, -1, 1)
-                p = 2 * field + level
-                result += base_force[p] + float(number) * step_force[p]
-                target[p] = result
+                factor = [factors[level, i, rows, lanes] for i in range(5)]
+                result = factor[0] * value[rows, lanes]
+                result += factors[0, 5, rows, lanes] * values[1 - level][rows, lanes]
+                result += factor[1] * turn(value, 1, 0)[rows, lanes]
+                result += factor[2] * turn(value, -1, 0)[rows, lanes]
+                result += factor[3] * turn(value, 1, 1)[rows, lanes]
+                result += factor[4] * turn(value, -1, 1)[rows, lanes]
+                target[2 * field + level] = result
             return carry
 
         lax.fori_loop(0, STATES // 2, per_field, 0)
 
-    substep(here, there, 1)
+        def push(force, rows, lanes, part):
+            def per_plane(p, carry):
+                amount = force[0, p][part] + float(number) * force[1, p][part]
+                target[p, rows, lanes] = target[p, rows, lanes] + amount
+                return carry
+
+            lax.fori_loop(0, STATES, per_plane, 0, unroll=2)
+
+        for where, section_lanes in ((on_left, slice(0, LANE)), (on_right, slice(2 * LANE, COLS))):
+
+            @pl.when(where)
+            def _():
+                push(column_force, rows, section_lanes, (rows, slice(None)))
+
+        for where, tile_rows in ((at_first, slice(0, 8)), (at_last, slice(16, 24))):
+
+            @pl.when(where)
+            def _():
+                push(row_force, tile_rows, lanes, (slice(None), lanes))
 
     @pl.when(is_nest)
     def _():
-        substep(there, here, 2)
-        substep(here, there, 3)
-
-    out_ref[...] = there[:, :ROWS, :COLS]
-    columns = iota((COLS, LANE), 1) * RATIO
-    source = iota((COLS, LANE), 0)
-    gather = ((source >= columns) & (source < columns + RATIO)).astype(jnp.float32)
-    narrowed[...] = dot(out_ref[...].reshape(STATES * ROWS, COLS), gather)
-    total = sum(narrowed[pl.ds(i, STATES * 8, stride=RATIO), :] for i in range(RATIO))
-    means_ref[...] = total / (RATIO * RATIO)
+        substep(here, there, 1, slice(0, 32), slice(0, 4 * LANE))
+        substep(there, here, 2, slice(0, 32), slice(0, 4 * LANE))
+
+    substep(here, out_ref, 3, slice(0, ROWS), slice(0, COLS))
+
+    @pl.when(is_nest)
+    def _():
+        columns = iota((COLS, LANE), 1) * RATIO
+        source = iota((COLS, LANE), 0)
+        gather = ((source >= columns) & (source < columns + RATIO)).astype(jnp.bfloat16)
+        cells = out_ref[...].reshape(STATES * ROWS, COLS)
+        narrowed[...] = sum(product(part, gather) for part in parts(cells))
+        total = sum(narrowed[pl.ds(i, STATES * 8, stride=RATIO), :] for i in range(RATIO))
+        means_ref[...] = total / (RATIO * RATIO)
 
 
 def merge_kernel(offset_ref, *refs):
@@ -694,22 +743,23 @@
     planes = state.reshape(STATES, ROWS, COLS)
     speeds = courant.reshape(4, ROWS, COLS)
     offset = nest_offset[0]
-    payloads = pl.pallas_call(
+    *payloads, to_pair, to_cross = pl.pallas_call(
         pack_kernel,
-        out_shape=[shaped(SLOTS, 2 * LANE)] * 3,
+        out_shape=[shaped(SLOTS, 2 * LANE)] * 3
+        + [shaped(HALO + RIMS, COLS), shaped(HALO + ROWS, COLS)],
         in_specs=[SMEM, VMEM, VMEM],
-        out_specs=[VMEM] * 3,
+        out_specs=[VMEM] * 5,
         name="pack",
     )(nest_offset, planes, speeds)
 
-    def send_rims(start, nest_offset, planes, speeds, west, middle, east):
+    def send_rims(start, to_pair, to_cross, west, middle, east):
         groups = rim_pairs(start)
         west, middle, east = (
             [lax.ppermute(value, BOTH, pairs) for pairs in lists]
             for value, lists in zip((west, middle, east), groups)
         )
         return pl.pallas_call(
-            functools.partial(relay_kernel, len(middle)),
+            functools.partial(relay_kernel, start, len(middle)),
             out_shape=[
                 shaped(ROWS, LANE),
                 shaped(ROWS, LANE),
@@ -717,17 +767,17 @@
                 shaped(HALO + RIMS, COLS),
                 shaped(HALO + ROWS, COLS),
             ],
-            in_specs=[SMEM] + [VMEM] * (8 + len(middle)),
+            in_specs=[VMEM] * (8 + len(middle)),
             out_specs=[VMEM] * 5,
+            input_output_aliases={0: 3, 1: 4},
             name="relay",
-        )(nest_offset, planes, speeds, *east, *middle, *west)
+        )(to_pair, to_cross, *east, *middle, *west)
 
     west, east, rims, to_pair, to_cross = lax.switch(
         (offset - 2) // ROWS - 1,
         [functools.partial(send_rims, start) for start in (1, 2, 3)],
-        nest_offset,
-        planes,
-        speeds,
+        to_pair,
+        to_cross,
         *payloads,
     )
     pair_map = [(device(t, s), device(t ^ 1, s)) for t in range(8) for s in range(4)]
@@ -748,20 +798,21 @@
             pltpu.VMEM((STATES, 32, 4 * LANE), jnp.float32),
             pltpu.VMEM((STATES, 32, 4 * LANE), jnp.float32),
             pltpu.VMEM((2, 6, 32, 4 * LANE), jnp.float32),
-            pltpu.VMEM((STATES, 32, 4 * LANE), jnp.float32),
-            pltpu.VMEM((STATES, 32, 4 * LANE), jnp.float32),
+            pltpu.VMEM((2, STATES, 32, LANE), jnp.float32),
+            pltpu.VMEM((2, STATES, 8, 4 * LANE), jnp.float32),
             pltpu.VMEM((STATES * ROWS, LANE), jnp.float32),
         ],
         compiler_params=pltpu.CompilerParams(vmem_limit_bytes=32 * 1024 * 1024),
         name="nest",
     )(nest_offset, planes, speeds, west, east, rims, from_pair, from_cross)
-    columns = jnp.concatenate(
-        [
-            lax.ppermute(means, BOTH, [(device(t, s), device(t, 0)) for t in range(8)])
-            for s in (1, 2, 3)
-        ],
-        axis=1,
-    )
+    def gather_from(s):
+        pairs = [(device(t, s), device(t, 0)) for t in range(8)]
+        if s == 2:
+            pairs = completed(pairs, [])
+        return lax.ppermute(means, BOTH, pairs)
+
+    got = {s: gather_from(s) for s in (1, 2, 3)}
+    columns = jnp.concatenate([got[s] for s in (1, 2, 3)], axis=1)
 
     def across(value, way):
         pairs = [(device(t, s), device(t ^ way, s)) for t in range(8) for s in range(4)]

time: 47.2 us -> 44 us (0.932)
  Pallas kernels: 6.01 us -> 4.26 us
  starting transfers between devices: 19 us -> 17.8 us
    ppermute x8 -> x7, starting transfers between devices: 11.5 us -> 8.32 us  [send_rims(): lax.ppermute(value, BOTH, pairs)]
    ppermute x7, starting transfers between devices: 3.51 us -> 4.74 us  [across(): return lax.ppermute(value, BOTH, pairs)]
    ppermute x8 -> x7, waiting for transfers between devices: 3.48 us -> 4.58 us  [send_rims(): lax.ppermute(value, BOTH, pairs)]
    ppermute x3, waiting for transfers between devices: 5.53 us -> 4.45 us  [gather_from(): return lax.ppermute(means, BOTH, pairs)]
    pallas_call x2, Pallas kernels: 3.61 us -> 2.55 us  [the longest x1 1.43 us: on_device(): pl.pallas_call(pack_kernel, out_shape=[shaped(SLOTS, 2 * LANE)] * 3 + [sh...]
    ppermute x3, starting transfers between devices: 3.88 us -> 4.61 us  [gather_from(): return lax.ppermute(means, BOTH, pairs)]
    pallas_call x1, Pallas kernels: 1.57 us -> 0.89 us  [on_device(): pl.pallas_call(main_kernel, out_shape=[shaped(STATES, ROWS, COLS), shaped...]
  transfers between devices with their start and end apart: 20 -> 19, of which waited for: 11 -> 9; matrix products, arithmetic and copies ran while one was open for 0% -> 0% of each run, Pallas kernels for 0% -> 0%
where the time goes in v6:
time: 44 us; the launch traced here: 43.9 us
  waiting for transfers between devices  20.3 us (46%)
  starting transfers between devices  17.8 us (40%)
  Pallas kernels  4.26 us (10%)
  between operations  0.77 us (2%)
  local copies, waits for them, and re-layouts  0.64 us (1%)
    ppermute x7, starting transfers between devices, send_rims(): lax.ppermute(value, BOTH, pairs)  8.32 us
    ppermute x7, waiting for transfers between devices, across(): return lax.ppermute(value, BOTH, pairs)  5.99 us
    ppermute x1, waiting for transfers between devices, on_device(): from_cross = lax.ppermute(to_cross, BOTH, cross_map)  5.32 us
    ppermute x7, starting transfers between devices, across(): return lax.ppermute(value, BOTH, pairs)  4.74 us
    ppermute x3, starting transfers between devices, gather_from(): return lax.ppermute(means, BOTH, pairs)  4.61 us
    ppermute x7, waiting for transfers between devices, send_rims(): lax.ppermute(value, BOTH, pairs)  4.58 us
    ppermute x3, waiting for transfers between devices, gather_from(): return lax.ppermute(means, BOTH, pairs)  4.45 us
    pallas_call x1, Pallas kernels, on_device(): pl.pallas_call(pack_kernel, out_shape=[shaped(SLOTS, 2 * LANE)] * 3 + [sh...  1.43 us
  transfers between devices with their start and end apart: 19, of which 9 were waited for; matrix products, arithmetic and copies ran while one was open for 0% of the time, Pallas kernels for 0%

profile of v6, /device:TPU:0, one launch (start us, length us, event | category | flops | bytes accessed | tf_op | source)
XLA Modules:
  0.0 43.9 jit_solution(13816238889182712699)
XLA Ops:
  0.7 1.4 %pack.1 = (f32[56,256]{1,0:T(8,128)S(1)}, f32[56,256]{1,0:T(8,128)S(1)}, f32[56,256]{1,0:T(8,128)S(1)}, f32[136,384]{1,0:T(8,128)S(1)}, f32[88,384]{1,0:T(8,128)S(1)}) custom-call(s32[1]{0:T(128)S(6)} %copy.33.offset_ref, f32[10,24,384]{2,1,0:T(8,128)} %bitcast.5, f32[4,24,384]{2,1,0:T(8,128)} %bitcast.7), custom_call_target="tpu_custom_call" | custom-call | tf_op jit(solution)/shard_map/pack/pallas_call | solution.py:746
  2.1 14.7 %conditional.1 = ((f32[24,128]{1,0:T(8,128)S(1)}, f32[24,128]{1,0:T(8,128)S(1)}, f32[72,256]{1,0:T(8,128)S(1)}, f32[136,384]{1,0:T(8,128)S(1)}, f32[88,384]{1,0:T(8,128)S(1)})) conditional(s32[]{:T(128)} %clamp.3, (f32[56,256]{1,0:T(8,128)S(1)}, f32[56,256]{1,0:T(8,128)S(1)}, f32[56,256]{1,0:T(8,128)S(1)}, f32[136,384]{1,0:T(8,128)S(1)}, ...), branch_computations={%region_0.1_spmd, %region_1.2_spmd, %region_2.3_spmd} | conditional | bytes 3670568 | solution.py:776
  2.2 0.5 %collective-permute-start.18 = (f32[56,256]{1,0:T(8,128)S(1)}, f32[56,256]{1,0:T(8,128)S(1)}, u32[]{:S(2)}, u32[]{:S(2)}) collective-permute-start(f32[56,256]{1,0:T(8,128)S(1)} %get-tuple-element.48), channel_id=1, source_target_pairs={{12,2},{16,6},{20,26},{24,30},{5,0},{2,1},{7,3},{0,4},{1,5},{3,7},... | collective-permute-start | bytes 172040 | tf_op jit(solution)/shard_map/cond/branch_2_fun/ppermute | solution.py:758
  2.7 5.7 %collective-permute-start.17 = (f32[56,256]{1,0:T(8,128)S(1)}, f32[56,256]{1,0:T(8,128)S(1)}, u32[]{:S(2)}, u32[]{:S(2)}) collective-permute-start(f32[56,256]{1,0:T(8,128)S(1)} %get-tuple-element.47), channel_id=1, source_target_pairs={{1,2},{5,6},{9,10},{10,11},{12,3},{13,14},{16,7},{17,18},{20,15},{... | collective-permute-start | bytes 172040 | tf_op jit(solution)/shard_map/cond/branch_2_fun/ppermute | solution.py:758
  8.4 0.5 %collective-permute-start.15 = (f32[56,256]{1,0:T(8,128)S(1)}, f32[56,256]{1,0:T(8,128)S(1)}, u32[]{:S(2)}, u32[]{:S(2)}) collective-permute-start(f32[56,256]{1,0:T(8,128)S(1)} %get-tuple-element.47), channel_id=1, source_target_pairs={{16,15},{20,19},{4,0},{6,1},{7,2},{11,3},{0,4},{1,5},{2,6},{3,7},{... | collective-permute-start | bytes 172040 | tf_op jit(solution)/shard_map/cond/branch_2_fun/ppermute | solution.py:758
  9.3 1.2 %collective-permute-start.20 = (f32[56,256]{1,0:T(8,128)S(1)}, f32[56,256]{1,0:T(8,128)S(1)}, u32[]{:S(2)}, u32[]{:S(2)}) collective-permute-start(f32[56,256]{1,0:T(8,128)S(1)} %get-tuple-element.49), channel_id=1, source_target_pairs={{2,1},{6,5},{12,9},{14,13},{16,21},{18,17},{20,25},{24,29},{4,0},{... | collective-permute-start | bytes 172040 | tf_op jit(solution)/shard_map/cond/branch_2_fun/ppermute | solution.py:758
  10.5 1.0 %collective-permute-done.17.refs_2_ = f32[56,256]{1,0:T(8,128)S(1)} collective-permute-done((f32[56,256]{1,0:T(8,128)S(1)}, f32[56,256]{1,0:T(8,128)S(1)}, u32[]{:S(2)}, u32[]{:S(2)}) %collective-permute-start.17) | collective-permute-done | bytes 57376 | tf_op jit(solution)/shard_map/cond/branch_2_fun/ppermute | solution.py:758
  11.5 1.8 %collective-permute-done.21.refs_6_ = f32[56,256]{1,0:T(8,128)S(1)} collective-permute-done((f32[56,256]{1,0:T(8,128)S(1)}, f32[56,256]{1,0:T(8,128)S(1)}, u32[]{:S(2)}, u32[]{:S(2)}) %collective-permute-start.21) | collective-permute-done | bytes 57376 | tf_op jit(solution)/shard_map/cond/branch_2_fun/ppermute | solution.py:758
  13.3 1.8 %collective-permute-done.19.refs_4_ = f32[56,256]{1,0:T(8,128)S(1)} collective-permute-done((f32[56,256]{1,0:T(8,128)S(1)}, f32[56,256]{1,0:T(8,128)S(1)}, u32[]{:S(2)}, u32[]{:S(2)}) %collective-permute-start.19) | collective-permute-done | bytes 57376 | tf_op jit(solution)/shard_map/cond/branch_2_fun/ppermute | solution.py:758
  15.2 0.6 %copy-done.23 = f32[56,256]{1,0:T(8,128)} copy-done((f32[56,256]{1,0:T(8,128)}, f32[56,256]{1,0:T(8,128)S(1)}, u32[]{:S(2)}) %copy-start.23) | copy-done | bytes 57368 | tf_op jit(solution)/shard_map/cond
  15.7 1.1 %relay.5 = (f32[24,128]{1,0:T(8,128)S(1)}, f32[24,128]{1,0:T(8,128)S(1)}, f32[72,256]{1,0:T(8,128)S(1)}, f32[136,384]{1,0:T(8,128)S(1)}, f32[88,384]{1,0:T(8,128)S(1)}) custom-call(f32[136,384]{1,0:T(8,128)S(1)} %get-tuple-element.45._, f32[88,384]{1,0:T(8,128)S(1)} %get-tuple-element.46.__, ...), custom_call_target="tpu_custom_call", output_to_operand_aliasing={{3}: (0, {}), {4}: (1, {})} | custom-call | tf_op jit(solution)/shard_map/cond/branch_2_fun/relay/pallas_call | solution.py:761
  17.0 5.3 %collective-permute-done.23.cross_ref = f32[88,384]{1,0:T(8,128)S(1)} collective-permute-done((f32[88,384]{1,0:T(8,128)S(1)}, f32[88,384]{1,0:T(8,128)S(1)}, u32[]{:S(2)}, u32[]{:S(2)}) %collective-permute-start.23) | collective-permute-done | bytes 135200 | tf_op jit(solution)/shard_map/ppermute | solution.py:790
  22.4 0.9 %nest.1 = (f32[10,24,384]{2,1,0:T(8,128)S(1)}, f32[80,128]{1,0:T(8,128)S(1)}) custom-call(s32[1]{0:T(128)S(6)} %copy.33.offset_ref, f32[10,24,384]{2,1,0:T(8,128)S(1)} %bitcast.6, f32[4,24,384]{2,1,0:T(8,128)S(1)} %bitcast.8, f32[24,128]{1,0:T(8,128)S(1)} %get-tuple-element.67.west_ref, f32[24,128]{1,0:T(8,128)S(1)} %get-tuple-element.68.east_ref, ...), custom_call_target="tpu_custom_call" | custom-call | tf_op jit(solution)/shard_map/nest/pallas_call | solution.py:792
  23.3 1.3 %collective-permute-start.24 = (f32[80,128]{1,0:T(8,128)S(1)}, f32[80,128]{1,0:T(8,128)S(1)}, u32[]{:S(2)}, u32[]{:S(2)}) collective-permute-start(f32[80,128]{1,0:T(8,128)S(1)} %get-tuple-element.72), channel_id=1, source_target_pairs={{1,0},{5,4},{9,8},{13,12},{17,16},{21,20},{25,24},{29,28}} | collective-permute-start | bytes 122888 | tf_op jit(solution)/shard_map/ppermute | solution.py:812
  24.6 1.3 %collective-permute-start.26 = (f32[80,128]{1,0:T(8,128)S(1)}, f32[80,128]{1,0:T(8,128)S(1)}, u32[]{:S(2)}, u32[]{:S(2)}) collective-permute-start(f32[80,128]{1,0:T(8,128)S(1)} %get-tuple-element.72), channel_id=1, source_target_pairs={{3,0},{7,4},{11,8},{15,12},{19,16},{23,20},{27,24},{31,28}} | collective-permute-start | bytes 122888 | tf_op jit(solution)/shard_map/ppermute | solution.py:812
  25.9 2.0 %collective-permute-start.25 = (f32[80,128]{1,0:T(8,128)S(1)}, f32[80,128]{1,0:T(8,128)S(1)}, u32[]{:S(2)}, u32[]{:S(2)}) collective-permute-start(f32[80,128]{1,0:T(8,128)S(1)} %get-tuple-element.72), channel_id=1, source_target_pairs={{2,0},{6,4},{10,8},{14,12},{18,16},{22,20},{26,24},{30,28},{5,1},{... | collective-permute-start | bytes 122888 | tf_op jit(solution)/shard_map/ppermute | solution.py:812
  27.9 4.4 %collective-permute-done.24 = f32[80,128]{1,0:T(8,128)S(1)} collective-permute-done((f32[80,128]{1,0:T(8,128)S(1)}, f32[80,128]{1,0:T(8,128)S(1)}, u32[]{:S(2)}, u32[]{:S(2)}) %collective-permute-start.24) | collective-permute-done | bytes 40992 | tf_op jit(solution)/shard_map/ppermute | solution.py:812
  32.4 2.0 %collective-permute-start.32 = (f32[80,384]{1,0:T(8,128)S(1)}, f32[80,384]{1,0:T(8,128)S(1)}, u32[]{:S(2)}, u32[]{:S(2)}) collective-permute-start(f32[80,384]{1,0:T(8,128)S(1)} %constant_dynamic-update-slice_fusion.refs_0_), channel_id=1, source_target_pairs={{0,28},{1,29},{2,30},{3,31},{4,24},{5,25},{6,26},{7,27},{8,20},{9,... | collective-permute-start | bytes 368648 | tf_op jit(solution)/shard_map/ppermute | solution.py:819
  34.4 1.4 %collective-permute-start.30 = (f32[80,384]{1,0:T(8,128)S(1)}, f32[80,384]{1,0:T(8,128)S(1)}, u32[]{:S(2)}, u32[]{:S(2)}) collective-permute-start(f32[80,384]{1,0:T(8,128)S(1)} %constant_dynamic-update-slice_fusion.refs_0_), channel_id=1, source_target_pairs={{0,16},{1,17},{2,18},{3,19},{4,20},{5,21},{6,22},{7,23},{8,24},{9,... | collective-permute-start | bytes 368648 | tf_op jit(solution)/shard_map/ppermute | solution.py:819
  35.8 0.7 %collective-permute-start.28 = (f32[80,384]{1,0:T(8,128)S(1)}, f32[80,384]{1,0:T(8,128)S(1)}, u32[]{:S(2)}, u32[]{:S(2)}) collective-permute-start(f32[80,384]{1,0:T(8,128)S(1)} %constant_dynamic-update-slice_fusion.refs_0_), channel_id=1, source_target_pairs={{0,12},{1,13},{2,14},{3,15},{4,8},{5,9},{6,10},{7,11},{8,4},{9,5},... | collective-permute-start | bytes 368648 | tf_op jit(solution)/shard_map/ppermute | solution.py:819
  36.5 2.3 %collective-permute-done.32.refs_7_ = f32[80,384]{1,0:T(8,128)S(1)} collective-permute-done((f32[80,384]{1,0:T(8,128)S(1)}, f32[80,384]{1,0:T(8,128)S(1)}, u32[]{:S(2)}, u32[]{:S(2)}) %collective-permute-start.32) | collective-permute-done | bytes 122912 | tf_op jit(solution)/shard_map/ppermute | solution.py:819
  38.9 2.7 %collective-permute-done.30.refs_4_ = f32[80,384]{1,0:T(8,128)S(1)} collective-permute-done((f32[80,384]{1,0:T(8,128)S(1)}, f32[80,384]{1,0:T(8,128)S(1)}, u32[]{:S(2)}, u32[]{:S(2)}) %collective-permute-start.30) | collective-permute-done | bytes 122912 | tf_op jit(solution)/shard_map/ppermute | solution.py:819
  42.1 0.8 %collective-permute-done.31.refs_5_ = f32[80,384]{1,0:T(8,128)S(1)} collective-permute-done((f32[80,384]{1,0:T(8,128)S(1)}, f32[80,384]{1,0:T(8,128)S(1)}, u32[]{:S(2)}, u32[]{:S(2)}) %collective-permute-start.31) | collective-permute-done | bytes 122912 | tf_op jit(solution)/shard_map/ppermute | solution.py:819
  43.1 0.8 %merge.1 = f32[10,24,384]{2,1,0:T(8,128)} custom-call(s32[1]{0:T(128)S(6)} %copy.33.offset_ref, f32[80,384]{1,0:T(8,128)S(1)} %constant_dynamic-update-slice_fusion.refs_0_, f32[80,384]{1,0:T(8,128)S(1)} %collective-permute-done.27.refs_1_, f32[80,384]{1,0:T(8,128)S(1)} %collective-permute-done.29.refs_2_, f32[80,384]{1,0:T(8,128)S(1)} %collective-permute-done.28.refs_3_, ...), custom_call_target="tpu_custom_call" | custom-call | tf_op jit(solution)/shard_map/merge/pallas_call | solution.py:826
  (40 shorter events, 1.4 us)
Async XLA Ops:
  2.1 20.2 %copy-start = (f32[5,2,24,384]{3,2,1,0:T(8,128)S(1)}, f32[5,2,24,384]{3,2,1,0:T(8,128)}, u32[]{:S(2)}) copy-start(f32[5,2,24,384]{3,2,1,0:T(8,128)} %param.6) | copy-start | bytes 1105924
  2.1 20.2 %copy-start.1 = (f32[2,2,24,384]{3,2,1,0:T(8,128)S(1)}, f32[2,2,24,384]{3,2,1,0:T(8,128)}, u32[]{:S(2)}) copy-start(f32[2,2,24,384]{3,2,1,0:T(8,128)} %param.7) | copy-start | bytes 442372
  2.2 7.1 %collective-permute-start.18 = (f32[56,256]{1,0:T(8,128)S(1)}, f32[56,256]{1,0:T(8,128)S(1)}, u32[]{:S(2)}, u32[]{:S(2)}) collective-permute-start(f32[56,256]{1,0:T(8,128)S(1)} %get-tuple-element.48), channel_id=1, source_target_pairs={{12,2},{16,6},{20,26},{24,30},{5,0},{2,1},{7,3},{0,4},{1,5},{3,7},... | collective-permute-start | bytes 172040 | tf_op jit(solution)/shard_map/cond/branch_2_fun/ppermute | solution.py:758
  2.7 8.8 %collective-permute-start.17 = (f32[56,256]{1,0:T(8,128)S(1)}, f32[56,256]{1,0:T(8,128)S(1)}, u32[]{:S(2)}, u32[]{:S(2)}) collective-permute-start(f32[56,256]{1,0:T(8,128)S(1)} %get-tuple-element.47), channel_id=1, source_target_pairs={{1,2},{5,6},{9,10},{10,11},{12,3},{13,14},{16,7},{17,18},{20,15},{... | collective-permute-start | bytes 172040 | tf_op jit(solution)/shard_map/cond/branch_2_fun/ppermute | solution.py:758
  8.4 3.1 %collective-permute-start.16 = (f32[56,256]{1,0:T(8,128)S(1)}, f32[56,256]{1,0:T(8,128)S(1)}, u32[]{:S(2)}, u32[]{:S(2)}) collective-permute-start(f32[56,256]{1,0:T(8,128)S(1)} %get-tuple-element.47), channel_id=1, source_target_pairs={{2,3},{6,7},{12,11},{14,15},{16,23},{18,19},{20,27},{24,31},{4,0},... | collective-permute-start | bytes 172040 | tf_op jit(solution)/shard_map/cond/branch_2_fun/ppermute | solution.py:758
  8.4 3.1 %collective-permute-start.15 = (f32[56,256]{1,0:T(8,128)S(1)}, f32[56,256]{1,0:T(8,128)S(1)}, u32[]{:S(2)}, u32[]{:S(2)}) collective-permute-start(f32[56,256]{1,0:T(8,128)S(1)} %get-tuple-element.47), channel_id=1, source_target_pairs={{16,15},{20,19},{4,0},{6,1},{7,2},{11,3},{0,4},{1,5},{2,6},{3,7},{... | collective-permute-start | bytes 172040 | tf_op jit(solution)/shard_map/cond/branch_2_fun/ppermute | solution.py:758
  8.9 4.4 %collective-permute-start.21 = (f32[56,256]{1,0:T(8,128)S(1)}, f32[56,256]{1,0:T(8,128)S(1)}, u32[]{:S(2)}, u32[]{:S(2)}) collective-permute-start(f32[56,256]{1,0:T(8,128)S(1)} %get-tuple-element.49), channel_id=1, source_target_pairs={{3,2},{7,6},{10,9},{11,10},{12,1},{15,14},{16,5},{19,18},{20,13},{... | collective-permute-start | bytes 172040 | tf_op jit(solution)/shard_map/cond/branch_2_fun/ppermute | solution.py:758
  9.3 5.8 %copy-start.6 = (f32[56,256]{1,0:T(8,128)}, f32[56,256]{1,0:T(8,128)S(1)}, u32[]{:S(2)}) copy-start(f32[56,256]{1,0:T(8,128)S(1)} %collective-permute-done.18.refs_3_) | copy-start | bytes 172036 | tf_op jit(solution)/shard_map/cond
  9.3 4.0 %collective-permute-start.20 = (f32[56,256]{1,0:T(8,128)S(1)}, f32[56,256]{1,0:T(8,128)S(1)}, u32[]{:S(2)}, u32[]{:S(2)}) collective-permute-start(f32[56,256]{1,0:T(8,128)S(1)} %get-tuple-element.49), channel_id=1, source_target_pairs={{2,1},{6,5},{12,9},{14,13},{16,21},{18,17},{20,25},{24,29},{4,0},{... | collective-permute-start | bytes 172040 | tf_op jit(solution)/shard_map/cond/branch_2_fun/ppermute | solution.py:758
  11.5 3.6 %copy-start.9 = (f32[56,256]{1,0:T(8,128)}, f32[56,256]{1,0:T(8,128)S(1)}, u32[]{:S(2)}) copy-start(f32[56,256]{1,0:T(8,128)S(1)} %collective-permute-done.17.refs_2_) | copy-start | bytes 172036 | tf_op jit(solution)/shard_map/cond
  11.5 3.6 %collective-permute-start.19 = (f32[56,256]{1,0:T(8,128)S(1)}, f32[56,256]{1,0:T(8,128)S(1)}, u32[]{:S(2)}, u32[]{:S(2)}) collective-permute-start(f32[56,256]{1,0:T(8,128)S(1)} %get-tuple-element.49), channel_id=1, source_target_pairs={{16,13},{20,17},{5,0},{9,1},{6,2},{7,3},{0,4},{1,5},{2,6},{3,7},{1... | collective-permute-start | bytes 172040 | tf_op jit(solution)/shard_map/cond/branch_2_fun/ppermute | solution.py:758
  11.5 3.6 %copy-start.12 = (f32[56,256]{1,0:T(8,128)}, f32[56,256]{1,0:T(8,128)S(1)}, u32[]{:S(2)}) copy-start(f32[56,256]{1,0:T(8,128)S(1)} %collective-permute-done.16.refs_1_) | copy-start | bytes 172036 | tf_op jit(solution)/shard_map/cond
  16.9 5.5 %collective-permute-start.22 = (f32[136,384]{1,0:T(8,128)S(1)}, f32[136,384]{1,0:T(8,128)S(1)}, u32[]{:S(2)}, u32[]{:S(2)}) collective-permute-start(f32[136,384]{1,0:T(8,128)S(1)} %get-tuple-element.70), channel_id=1, source_target_pairs={{0,4},{1,5},{2,6},{3,7},{4,0},{5,1},{6,2},{7,3},{8,12},{9,13},{10,... | collective-permute-start | bytes 626696 | tf_op jit(solution)/shard_map/ppermute | solution.py:791
  16.9 5.4 %collective-permute-start.23 = (f32[88,384]{1,0:T(8,128)S(1)}, f32[88,384]{1,0:T(8,128)S(1)}, u32[]{:S(2)}, u32[]{:S(2)}) collective-permute-start(f32[88,384]{1,0:T(8,128)S(1)} %get-tuple-element.71), channel_id=1, source_target_pairs={{4,8},{5,9},{6,10},{7,11},{8,4},{9,5},{10,6},{11,7},{12,16},{13,17... | collective-permute-start | bytes 405512 | tf_op jit(solution)/shard_map/ppermute | solution.py:790
  23.3 9.1 %collective-permute-start.24 = (f32[80,128]{1,0:T(8,128)S(1)}, f32[80,128]{1,0:T(8,128)S(1)}, u32[]{:S(2)}, u32[]{:S(2)}) collective-permute-start(f32[80,128]{1,0:T(8,128)S(1)} %get-tuple-element.72), channel_id=1, source_target_pairs={{1,0},{5,4},{9,8},{13,12},{17,16},{21,20},{25,24},{29,28}} | collective-permute-start | bytes 122888 | tf_op jit(solution)/shard_map/ppermute | solution.py:812
  24.6 7.8 %collective-permute-start.26 = (f32[80,128]{1,0:T(8,128)S(1)}, f32[80,128]{1,0:T(8,128)S(1)}, u32[]{:S(2)}, u32[]{:S(2)}) collective-permute-start(f32[80,128]{1,0:T(8,128)S(1)} %get-tuple-element.72), channel_id=1, source_target_pairs={{3,0},{7,4},{11,8},{15,12},{19,16},{23,20},{27,24},{31,28}} | collective-permute-start | bytes 122888 | tf_op jit(solution)/shard_map/ppermute | solution.py:812
  25.9 6.5 %collective-permute-start.25 = (f32[80,128]{1,0:T(8,128)S(1)}, f32[80,128]{1,0:T(8,128)S(1)}, u32[]{:S(2)}, u32[]{:S(2)}) collective-permute-start(f32[80,128]{1,0:T(8,128)S(1)} %get-tuple-element.72), channel_id=1, source_target_pairs={{2,0},{6,4},{10,8},{14,12},{18,16},{22,20},{26,24},{30,28},{5,1},{... | collective-permute-start | bytes 122888 | tf_op jit(solution)/shard_map/ppermute | solution.py:812
  32.4 6.4 %collective-permute-start.32 = (f32[80,384]{1,0:T(8,128)S(1)}, f32[80,384]{1,0:T(8,128)S(1)}, u32[]{:S(2)}, u32[]{:S(2)}) collective-permute-start(f32[80,384]{1,0:T(8,128)S(1)} %constant_dynamic-update-slice_fusion.refs_0_), channel_id=1, source_target_pairs={{0,28},{1,29},{2,30},{3,31},{4,24},{5,25},{6,26},{7,27},{8,20},{9,... | collective-permute-start | bytes 368648 | tf_op jit(solution)/shard_map/ppermute | solution.py:819
  34.4 7.2 %collective-permute-start.30 = (f32[80,384]{1,0:T(8,128)S(1)}, f32[80,384]{1,0:T(8,128)S(1)}, u32[]{:S(2)}, u32[]{:S(2)}) collective-permute-start(f32[80,384]{1,0:T(8,128)S(1)} %constant_dynamic-update-slice_fusion.refs_0_), channel_id=1, source_target_pairs={{0,16},{1,17},{2,18},{3,19},{4,20},{5,21},{6,22},{7,23},{8,24},{9,... | collective-permute-start | bytes 368648 | tf_op jit(solution)/shard_map/ppermute | solution.py:819
  35.8 5.8 %collective-permute-start.28 = (f32[80,384]{1,0:T(8,128)S(1)}, f32[80,384]{1,0:T(8,128)S(1)}, u32[]{:S(2)}, u32[]{:S(2)}) collective-permute-start(f32[80,384]{1,0:T(8,128)S(1)} %constant_dynamic-update-slice_fusion.refs_0_), channel_id=1, source_target_pairs={{0,12},{1,13},{2,14},{3,15},{4,8},{5,9},{6,10},{7,11},{8,4},{9,5},... | collective-permute-start | bytes 368648 | tf_op jit(solution)/shard_map/ppermute | solution.py:819
  36.5 5.6 %collective-permute-start.27 = (f32[80,384]{1,0:T(8,128)S(1)}, f32[80,384]{1,0:T(8,128)S(1)}, u32[]{:S(2)}, u32[]{:S(2)}) collective-permute-start(f32[80,384]{1,0:T(8,128)S(1)} %constant_dynamic-update-slice_fusion.refs_0_), channel_id=1, source_target_pairs={{0,4},{1,5},{2,6},{3,7},{4,0},{5,1},{6,2},{7,3},{8,12},{9,13},{10,... | collective-permute-start | bytes 368648 | tf_op jit(solution)/shard_map/ppermute | solution.py:819
  38.7 3.4 %collective-permute-start.33 = (f32[80,384]{1,0:T(8,128)S(1)}, f32[80,384]{1,0:T(8,128)S(1)}, u32[]{:S(2)}, u32[]{:S(2)}) collective-permute-start(f32[80,384]{1,0:T(8,128)S(1)} %collective-permute-done.32.refs_7_), channel_id=1, source_target_pairs={{0,4},{1,5},{2,6},{3,7},{4,0},{5,1},{6,2},{7,3},{8,12},{9,13},{10,... | collective-permute-start | bytes 368648 | tf_op jit(solution)/shard_map/ppermute | solution.py:819
  41.6 1.3 %collective-permute-start.31 = (f32[80,384]{1,0:T(8,128)S(1)}, f32[80,384]{1,0:T(8,128)S(1)}, u32[]{:S(2)}, u32[]{:S(2)}) collective-permute-start(f32[80,384]{1,0:T(8,128)S(1)} %collective-permute-done.30.refs_4_), channel_id=1, source_target_pairs={{0,4},{1,5},{2,6},{3,7},{4,0},{5,1},{6,2},{7,3},{8,12},{9,13},{10,... | collective-permute-start | bytes 368648 | tf_op jit(solution)/shard_map/ppermute | solution.py:819
  41.6 1.5 %collective-permute-start.29 = (f32[80,384]{1,0:T(8,128)S(1)}, f32[80,384]{1,0:T(8,128)S(1)}, u32[]{:S(2)}, u32[]{:S(2)}) collective-permute-start(f32[80,384]{1,0:T(8,128)S(1)} %collective-permute-done.28.refs_3_), channel_id=1, source_target_pairs={{0,4},{1,5},{2,6},{3,7},{4,0},{5,1},{6,2},{7,3},{8,12},{9,13},{10,... | collective-permute-start | bytes 368648 | tf_op jit(solution)/shard_map/ppermute | solution.py:819
  (4 other events, 7.8 us)

commit v7 on v6

--- a/solution.py
+++ b/solution.py
@@ -267,7 +267,8 @@
     lane = iota((SLOTS, LANE), 1)
     mark = device_mark(tile, section)
     blank = jnp.zeros((SLOTS, LANE), jnp.float32)
-    outs = ((west_ref, left), (middle_ref, left), (east_ref, right))
+    both = jnp.where(iota((ROWS, LANE), 1) < 42, left, turn(right, 64, 1))
+    outs = ((west_ref, left), (middle_ref, both), (east_ref, right))
     for s, (out_ref, edge) in enumerate(outs):
         before = rows[:, LANE * (s - 1) : LANE * s] if s > 0 else blank
         after = rows[:, LANE * (s + 1) : LANE * (s + 2)] if s < 2 else blank
@@ -276,7 +277,8 @@
             (lane >= 42) & (lane < 46), extra, jnp.where(lane == LANE - 1, mark, 0.0)
         )
         out_ref[:, :LANE] = rows[:, LANE * s : LANE * (s + 1)]
-        out_ref[:ROWS, LANE:] = jnp.where(lane[:ROWS] < 42, edge, side[:ROWS])
+        free = (lane[:ROWS] >= 42) & (lane[:ROWS] < 64) | (lane[:ROWS] == LANE - 1)
+        out_ref[:ROWS, LANE:] = jnp.where(free, side[:ROWS], edge)
         out_ref[ROWS:, LANE:] = side[ROWS:]
 
 
@@ -292,22 +294,31 @@
     return start - 1 + jnp.minimum(tile // 2, 2)
 
 
-def relay_kernel(start, middles, _, __, *refs):
+def across_chips(tile):
+    return jnp.where(tile % 2 == 0, tile - 1, tile + 1)
+
+
+def relay_kernel(start, middles, to_pair_ref, from_cross_ref, *refs):
     to_east, middle, to_west = refs[:3], refs[3 : 3 + middles], refs[3 + middles : 6 + middles]
     west_ref, east_ref, rims_ref, pair_ref, cross_ref = refs[6 + middles :]
+    pair_ref[:SLOTS] = to_pair_ref[...]
+    pair_ref[SLOTS + 4 : HALO] = jnp.zeros((HALO - SLOTS - 4, COLS), jnp.float32)
+    cross_ref[...] = from_cross_ref[...]
     tile = lax.axis_index("tile")
     section = lax.axis_index("section")
     even = tile % 2 == 0
     lane = iota((ROWS, LANE), 1)
     first = first_source(start, tile)
     sources = [device_mark(first + slot, 0) for slot in range(3)]
-
     has_east = (section == 1) | (section == 2)
     has_west = (section == 2) | (section == 3)
+    corner = across_chips(tile)
     east_mark = jnp.where(has_east, device_mark(tile, section + 1), 0.0)
     west_mark = jnp.where(has_west, device_mark(tile, section - 1), 0.0)
+    far_east_mark = jnp.where(has_east, device_mark(corner, section + 1), 0.0)
+    far_west_mark = jnp.where(has_west, device_mark(corner, section - 1), 0.0)
     nothing = jnp.zeros((ROWS, LANE), jnp.float32)
-    east = west = nothing
+    east = west = far_east = far_west = nothing
     edges = [nothing] * 3
     center = side = jnp.zeros((SLOTS, LANE), jnp.float32)
     targets = [3] * 3 + [2] * middles + [1] * 3
@@ -315,33 +326,36 @@
         tail = ref[:, LANE:]
         mark = jnp.broadcast_to(tail[:, LANE - 1 :], (SLOTS, LANE))
         marks = [jnp.where(section == target, source, 0.0) for source in sources]
-        hits = [mark == source for source in marks]
-        hit = hits[0] | hits[1] | hits[2]
+        hit = (mark == marks[0]) | (mark == marks[1]) | (mark == marks[2])
         center = jnp.where(hit, center + ref[:, :LANE], center)
         side = jnp.where(hit, side + tail, side)
-        if target != 2:
-            cells = tail[:ROWS]
-            edges = [jnp.where(one[:ROWS], cells, edge) for one, edge in zip(hits, edges)]
-        if target == 1:
-            east = jnp.where(mark[:ROWS] == east_mark, cells, east)
-        if target == 3:
-            west = jnp.where(mark[:ROWS] == west_mark, cells, west)
-    east, west, *edges = [jnp.where(lane < 42, value, 0.0) for value in (east, west, *edges)]
-    west_ref[...] = west
-    east_ref[...] = east
+        mark, cells = mark[:ROWS], tail[:ROWS]
+        if target == 2:
+            marks = [jnp.where(section == 2, 0.0, source) for source in sources]
+            cells = jnp.where(section == 3, turn(cells, -64, 1), cells)
+        edges = [jnp.where(mark == one, cells, edge) for one, edge in zip(marks, edges)]
+        if target < 3:
+            east = jnp.where(mark == east_mark, cells, east)
+            far_east = jnp.where(mark == far_east_mark, cells, far_east)
+        if target > 1:
+            west = jnp.where(mark == west_mark, cells, west)
+            far_west = jnp.where(mark == far_west_mark, cells, far_west)
+    edges = [jnp.where(lane < 42, value, 0.0) for value in edges]
+    for lanes, out_ref, value, far in (
+        (slice(0, LANE), west_ref, west, far_west),
+        (slice(LANE, 2 * LANE), east_ref, east, far_east),
+    ):
+        out_ref[:ROWS] = value
+        out_ref[ROWS : ROWS + 4] = jnp.where(even, far[ROWS - 4 :], far[:4])
+        out_ref[ROWS + 4 :] = jnp.zeros((4, LANE), jnp.float32)
+        pair_ref[SLOTS : SLOTS + 4, lanes] = jnp.where(even, value[ROWS - 4 :], value[:4])
     wide = iota((SLOTS, LANE), 1)
     rims_ref[:SLOTS, :LANE] = center
     rims_ref[SLOTS:, :LANE] = jnp.zeros((RIMS - SLOTS, LANE), jnp.float32)
     extra = jnp.where((wide >= 42) & (wide < 46), side, 0.0)
     extra = jnp.concatenate([extra, jnp.zeros((RIMS - SLOTS, LANE), jnp.float32)], axis=0)
     rims_ref[:, LANE:] = jnp.concatenate(edges, axis=0) + extra
-
-    for lanes, value in ((slice(0, LANE), west), (slice(LANE, 2 * LANE), east)):
-        head, tail = value[:4], value[ROWS - 4 :]
-        pair_ref[SLOTS : SLOTS + 4, lanes] = jnp.where(even, tail, head)
-        cross_ref[SLOTS : SLOTS + 4, lanes] = jnp.where(even, head, tail)
     pair_ref[HALO:, : 2 * LANE] = rims_ref[...]
-    cross_ref[HALO:, :LANE] = edges[0]
 
 
 def flux(value, south, north, west, east, other, cy, cx):
@@ -380,19 +394,16 @@
     is_nest = section > 0
     full = (32, 4 * LANE)
 
-    after = jnp.where(even, pair_ref[:HALO], cross_ref[:HALO])
-    before = jnp.where(even, cross_ref[:HALO], pair_ref[:HALO])
-    wests = jnp.concatenate(
-        [west_ref[...], after[SLOTS : SLOTS + 4, :LANE], before[SLOTS : SLOTS + 4, :LANE]], axis=0
-    )
-    easts = jnp.concatenate(
-        [
-            east_ref[...],
-            after[SLOTS : SLOTS + 4, LANE : 2 * LANE],
-            before[SLOTS : SLOTS + 4, LANE : 2 * LANE],
-        ],
-        axis=0,
-    )
+    after = jnp.where(even, pair_ref[:SLOTS], cross_ref[...])
+    before = jnp.where(even, cross_ref[...], pair_ref[:SLOTS])
+
+    def beside(ref, lanes):
+        inside, outside = pair_ref[SLOTS : SLOTS + 4, lanes], ref[ROWS : ROWS + 4]
+        last = [jnp.where(even, inside, outside), jnp.where(even, outside, inside)]
+        return jnp.concatenate([ref[:ROWS]] + last, axis=0)
+
+    wests = beside(west_ref, slice(0, LANE))
+    easts = beside(east_ref, slice(LANE, 2 * LANE))
     lane = iota((32, LANE), 1)
 
     def ring(p):
@@ -451,8 +462,7 @@
 
     @pl.when(on_left | on_right)
     def _():
-        before_six = jnp.where(tile == 6, cross_ref[HALO:, :LANE], 0.0)
-        edges = jnp.concatenate([rims[:ROWS, LANE:] + before_six, rims[ROWS:, LANE:]], axis=0)
+        edges = rims[:, LANE:]
         start = offset + tile * 8 - 2 - first_source(jnp.maximum((offset - 2) // ROWS, 1), tile) * ROWS
         value = pltpu.roll(edges, RIMS - start, 0)[:16]
         short = iota((16, LANE), 1)
@@ -608,6 +618,10 @@
         means_ref[...] = total / (RATIO * RATIO)
 
 
+def ring_step(tile):
+    return 7 - 4 * (((tile + 1) % 4) // 2)
+
+
 def merge_kernel(offset_ref, *refs):
     *block_refs, stepped_ref, out_ref, near = refs
     tile = lax.axis_index("tile")
@@ -621,12 +635,15 @@
 
     @pl.when(section == 0)
     def _():
+        mate = tile ^ 1
+        sources = [tile, mate]
+        for one in (tile, mate):
+            sources += [one ^ ring_step(one), one ^ (10 - ring_step(one)), one ^ 4]
         for step in range(4):
-            source = 3 * tile - offset // 8 - 1 + step
-            inside = (source >= 0) & (source < 8)
-            for way, block_ref in enumerate(block_refs):
-
-                @pl.when(inside & (source == (tile ^ way)))
+            wanted = 3 * tile - offset // 8 - 1 + step
+            for source, block_ref in zip(sources, block_refs):
+
+                @pl.when(wanted == source)
                 def _():
                     near[step] = block_ref[...]
 
@@ -718,20 +735,33 @@
     return pairs + [(senders[owner[j] - 1], takers[j - 1]) for j in range(1, n + 1)]
 
 
-def rim_pairs(start):
-    to_chips = [(0, 0), (1, 1), (0, 2), (1, 3), (2, 3), (2, 4), (1, 5), (3, 4), (2, 6), (3, 7)]
-    sends = [(start + step, tile) for step, tile in to_chips]
+def rim_pairs(case):
+    start = max(case, 1)
+    sends = {
+        1: [(0, 0), (1, 1), (0, 2), (1, 3), (2, 3), (2, 4), (1, 5), (3, 4), (2, 6), (3, 7)],
+        3: [(0, 0), (1, 1), (0, 2), (1, 3), (2, 2), (2, 4), (1, 5), (3, 5), (2, 6), (3, 7)],
+    }
+    corners = {low: low + 1 for low in (1, 3, 5)}
+    corners.update({high: low for low, high in list(corners.items())})
+    crowded = [(device(4, 2), device(3, 1)), (device(3, 2), device(4, 1))]
+    crowded += [(device(1, 2), device(2, 3)), (device(6, 2), device(5, 3))]
     middle = [[(start, 0), (start + 1, 1), (start + 2, 6), (start + 3, 7)]]
-    if start == 1:
-        sends.append((0, 0))
-        middle.append([(0, 0)])
+    middle = [[(device(a, 0), device(b, 2)) for a, b in pairs] for pairs in middle]
+    middle[0] += crowded
+    if case == 0:
+        middle.append([(device(0, 0), device(0, 2)), (device(2, 0), device(6, 1))])
+        middle.append([(device(2, 0), device(6, 3))])
     groups = []
     for section, inner in ((1, ((2, 1), (3, 2))), (3, ((1, 2), (2, 3)))):
-        edges = [(device(a, 0), device(b, section)) for a, b in sends]
-        edges += [(device(t, a), device(t, b)) for t in range(8) for a, b in inner]
+        edges = [(device(start + a, 0), device(b, section)) for a, b in sends[section]]
+        if start == 1:
+            edges.append((device(0, 0), device(0, section)))
+        for a, b in inner:
+            edges += [(device(t, a), device(t, b)) for t in range(8)]
+            edges += [(device(corners[t], a), device(t, b)) for t in corners]
+        edges = [pair for pair in edges if pair not in crowded]
         rounds = in_rounds(edges, 3)[::-1]
         groups.append([completed(pairs, edges) for pairs in rounds])
-    middle = [[(device(a, 0), device(b, 2)) for a, b in pairs] for pairs in middle]
     middle = [completed(pairs, []) for pairs in middle]
     return groups[0], middle, groups[1]
 
@@ -746,50 +776,45 @@
     *payloads, to_pair, to_cross = pl.pallas_call(
         pack_kernel,
         out_shape=[shaped(SLOTS, 2 * LANE)] * 3
-        + [shaped(HALO + RIMS, COLS), shaped(HALO + ROWS, COLS)],
+        + [shaped(SLOTS, COLS)] * 2,
         in_specs=[SMEM, VMEM, VMEM],
         out_specs=[VMEM] * 5,
         name="pack",
     )(nest_offset, planes, speeds)
 
-    def send_rims(start, to_pair, to_cross, west, middle, east):
-        groups = rim_pairs(start)
+    pair_map = [(device(t, s), device(t ^ 1, s)) for t in range(8) for s in range(4)]
+    cross_map = [(device(t, s), device(t ^ ring_step(t), s)) for t in range(8) for s in range(4)]
+
+    def send_rims(case, to_pair, to_cross, west, middle, east):
+        from_cross = lax.ppermute(to_cross, BOTH, cross_map)
+        groups = rim_pairs(case)
         west, middle, east = (
             [lax.ppermute(value, BOTH, pairs) for pairs in lists]
             for value, lists in zip((west, middle, east), groups)
         )
         return pl.pallas_call(
-            functools.partial(relay_kernel, start, len(middle)),
+            functools.partial(relay_kernel, max(case, 1), len(middle)),
             out_shape=[
-                shaped(ROWS, LANE),
-                shaped(ROWS, LANE),
+                shaped(32, LANE),
+                shaped(32, LANE),
                 shaped(RIMS, 2 * LANE),
                 shaped(HALO + RIMS, COLS),
-                shaped(HALO + ROWS, COLS),
+                shaped(SLOTS, COLS),
             ],
             in_specs=[VMEM] * (8 + len(middle)),
             out_specs=[VMEM] * 5,
-            input_output_aliases={0: 3, 1: 4},
             name="relay",
-        )(to_pair, to_cross, *east, *middle, *west)
-
-    west, east, rims, to_pair, to_cross = lax.switch(
-        (offset - 2) // ROWS - 1,
-        [functools.partial(send_rims, start) for start in (1, 2, 3)],
+        )(to_pair, from_cross, *east, *middle, *west)
+
+    west, east, rims, to_pair, from_cross = lax.switch(
+        (offset - 2) // ROWS,
+        [functools.partial(send_rims, case) for case in range(4)],
         to_pair,
         to_cross,
         *payloads,
     )
-    pair_map = [(device(t, s), device(t ^ 1, s)) for t in range(8) for s in range(4)]
-    cross_map = [
-        (device(a, s), device(b, s))
-        for low in (1, 3, 5, 7)
-        for a, b in ((low, (low + 1) % 8), ((low + 1) % 8, low))
-        for s in range(4)
-    ]
-    from_cross = lax.ppermute(to_cross, BOTH, cross_map)
     from_pair = lax.ppermute(to_pair, BOTH, pair_map)
-    block, means = pl.pallas_call(
+    stepped, means = pl.pallas_call(
         main_kernel,
         out_shape=[shaped(STATES, ROWS, COLS), shaped(STATES * 8, LANE)],
         in_specs=[SMEM] + [VMEM] * 7,
@@ -814,15 +839,17 @@
     got = {s: gather_from(s) for s in (1, 2, 3)}
     columns = jnp.concatenate([got[s] for s in (1, 2, 3)], axis=1)
 
-    def across(value, way):
-        pairs = [(device(t, s), device(t ^ way, s)) for t in range(8) for s in range(4)]
+    def across(value, partner):
+        pairs = [(device(t, s), device(partner(t), s)) for t in range(8) for s in range(4)]
         return lax.ppermute(value, BOTH, pairs)
 
-    blocks = {0: columns}
-    for way in (7, 3, 4, 1):
-        blocks[way] = across(columns, way)
-    for way in (7, 3, 4):
-        blocks[way ^ 1] = across(blocks[way], 1)
+    def mate(t):
+        return t ^ 1
+
+    ways = (lambda t: t ^ ring_step(t), lambda t: t ^ (10 - ring_step(t)), lambda t: t ^ 4)
+    blocks = [columns, across(columns, mate)]
+    blocks += [across(columns, way) for way in ways]
+    blocks += [across(block, mate) for block in blocks[2:]]
     merged = pl.pallas_call(
         merge_kernel,
         out_shape=shaped(STATES, ROWS, COLS),
@@ -831,7 +858,7 @@
         scratch_shapes=[pltpu.VMEM((4, STATES * 8, COLS), jnp.float32)],
         compiler_params=pltpu.CompilerParams(vmem_limit_bytes=32 * 1024 * 1024),
         name="merge",
-    )(nest_offset, *[blocks[way] for way in range(8)], block)
+    )(nest_offset, *blocks, stepped)
     return merged.reshape(state.shape)
 
 

time: 44 us -> 42.1 us (0.957)
  waiting for transfers between devices: 20.3 us -> 12.9 us
  starting transfers between devices: 17.8 us -> 23.1 us
    ppermute x1, waiting for transfers between devices: 5.32 us -> 0.01 us  [send_rims(): from_cross = lax.ppermute(to_cross, BOTH, cross_map)]
    ppermute x7, waiting for transfers between devices: 4.58 us -> 1.72 us  [send_rims(): lax.ppermute(value, BOTH, pairs)]
    ppermute x1, starting transfers between devices: 0.07 us -> 1.87 us  [on_device(): from_pair = lax.ppermute(to_pair, BOTH, pair_map)]
    ppermute x1, starting transfers between devices: 0.07 us -> 1.73 us  [send_rims(): from_cross = lax.ppermute(to_cross, BOTH, cross_map)]
    ppermute x7, starting transfers between devices: 8.32 us -> 9.84 us  [send_rims(): lax.ppermute(value, BOTH, pairs)]
    ppermute x1, waiting for transfers between devices: 0.01 us -> 1.09 us  [on_device(): from_pair = lax.ppermute(to_pair, BOTH, pair_map)]
  transfers between devices with their start and end apart: 19 -> 19, of which waited for: 9 -> 10; matrix products, arithmetic and copies ran while one was open for 0% -> 0% of each run, Pallas kernels for 0% -> 0%
where the time goes in v7:
time: 42.1 us; the launch traced here: 41.8 us
  starting transfers between devices  23.1 us (55%)
  waiting for transfers between devices  12.9 us (31%)
  Pallas kernels  4.32 us (10%)
  between operations  0.74 us (2%)
  local copies, waits for them, and re-layouts  0.64 us (2%)
    ppermute x7, starting transfers between devices, send_rims(): lax.ppermute(value, BOTH, pairs)  9.84 us
    ppermute x7, waiting for transfers between devices, across(): return lax.ppermute(value, BOTH, pairs)  6.06 us
    ppermute x3, starting transfers between devices, gather_from(): return lax.ppermute(means, BOTH, pairs)  4.92 us
    ppermute x7, starting transfers between devices, across(): return lax.ppermute(value, BOTH, pairs)  4.74 us
    ppermute x3, waiting for transfers between devices, gather_from(): return lax.ppermute(means, BOTH, pairs)  4.06 us
    ppermute x1, starting transfers between devices, on_device(): from_pair = lax.ppermute(to_pair, BOTH, pair_map)  1.87 us
    ppermute x1, starting transfers between devices, send_rims(): from_cross = lax.ppermute(to_cross, BOTH, cross_map)  1.73 us
    ppermute x7, waiting for transfers between devices, send_rims(): lax.ppermute(value, BOTH, pairs)  1.72 us
  transfers between devices with their start and end apart: 19, of which 10 were waited for; matrix products, arithmetic and copies ran while one was open for 0% of the time, Pallas kernels for 0%

profile of v7, /device:TPU:0, one launch (start us, length us, event | category | flops | bytes accessed | tf_op | source)
XLA Modules:
  0.0 41.8 jit_solution(6005239633658945125)
XLA Ops:
  0.7 1.4 %pack.1 = (f32[56,256]{1,0:T(8,128)S(1)}, f32[56,256]{1,0:T(8,128)S(1)}, f32[56,256]{1,0:T(8,128)S(1)}, f32[56,384]{1,0:T(8,128)S(1)}, f32[56,384]{1,0:T(8,128)S(1)}) custom-call(s32[1]{0:T(128)S(6)} %copy.26.offset_ref, f32[10,24,384]{2,1,0:T(8,128)} %bitcast.5, f32[4,24,384]{2,1,0:T(8,128)} %bitcast.7), custom_call_target="tpu_custom_call" | custom-call | tf_op jit(solution)/shard_map/pack/pallas_call | solution.py:776
  2.1 15.2 %conditional.1 = ((f32[32,128]{1,0:T(8,128)S(1)}, f32[32,128]{1,0:T(8,128)S(1)}, f32[72,256]{1,0:T(8,128)S(1)}, f32[136,384]{1,0:T(8,128)S(1)}, f32[56,384]{1,0:T(8,128)S(1)})) conditional(s32[]{:T(128)} %clamp.3, (f32[56,384]{1,0:T(8,128)S(1)}, f32[56,256]{1,0:T(8,128)S(1)}, f32[56,256]{1,0:T(8,128)S(1)}, ...), branch_computations={%region_0.1_spmd, %region_1.2_spmd, %region_2.3_spmd, %region_3.4_... | conditional | bytes 4817584 | solution.py:809
  2.7 5.7 %collective-permute-start.29 = (f32[56,256]{1,0:T(8,128)S(1)}, f32[56,256]{1,0:T(8,128)S(1)}, u32[]{:S(2)}, u32[]{:S(2)}) collective-permute-start(f32[56,256]{1,0:T(8,128)S(1)} %get-tuple-element.62), channel_id=1, source_target_pairs={{1,2},{2,3},{5,6},{9,10},{10,7},{13,14},{14,15},{16,23},{17,18},{1... | collective-permute-start | bytes 172040 | tf_op jit(solution)/shard_map/cond/branch_3_fun/ppermute | solution.py:792
  8.9 1.7 %collective-permute-start.26 = (f32[56,384]{1,0:T(8,128)S(1)}, f32[56,384]{1,0:T(8,128)S(1)}, u32[]{:S(2)}, u32[]{:S(2)}) collective-permute-start(f32[56,384]{1,0:T(8,128)S(1)} %get-tuple-element.61), channel_id=1, source_target_pairs={{0,28},{1,29},{2,30},{3,31},{4,8},{5,9},{6,10},{7,11},{8,4},{9,5},... | collective-permute-start | bytes 258056 | tf_op jit(solution)/shard_map/cond/branch_3_fun/ppermute | solution.py:789
  11.2 2.5 %collective-permute-start.32 = (f32[56,256]{1,0:T(8,128)S(1)}, f32[56,256]{1,0:T(8,128)S(1)}, u32[]{:S(2)}, u32[]{:S(2)}) collective-permute-start(f32[56,256]{1,0:T(8,128)S(1)} %get-tuple-element.64), channel_id=1, source_target_pairs={{2,1},{7,10},{10,5},{11,6},{12,9},{15,18},{16,13},{19,14},{20,17},... | collective-permute-start | bytes 172040 | tf_op jit(solution)/shard_map/cond/branch_3_fun/ppermute | solution.py:792
  14.3 1.2 %collective-permute-done.32.refs_5_ = f32[56,256]{1,0:T(8,128)S(1)} collective-permute-done((f32[56,256]{1,0:T(8,128)S(1)}, f32[56,256]{1,0:T(8,128)S(1)}, u32[]{:S(2)}, u32[]{:S(2)}) %collective-permute-start.32) | collective-permute-done | bytes 57376 | tf_op jit(solution)/shard_map/cond/branch_3_fun/ppermute | solution.py:792
  16.1 1.2 %relay.7 = (f32[32,128]{1,0:T(8,128)S(1)}, f32[32,128]{1,0:T(8,128)S(1)}, f32[72,256]{1,0:T(8,128)S(1)}, f32[136,384]{1,0:T(8,128)S(1)}, f32[56,384]{1,0:T(8,128)S(1)}) custom-call(f32[56,384]{1,0:T(8,128)S(1)} %get-tuple-element.60.to_pair_ref, f32[56,384]{1,0:T(8,128)} %copy-done.4, f32[56,256]{1,0:T(8,128)} %copy-done.17, f32[56,256]{1,0:T(8,128)} %copy-done.14, ...), custom_call_target="tpu_custom_call" | custom-call | tf_op jit(solution)/shard_map/cond/branch_3_fun/relay/pallas_call | solution.py:795
  17.3 1.9 %collective-permute-start.34 = (f32[136,384]{1,0:T(8,128)S(1)}, f32[136,384]{1,0:T(8,128)S(1)}, u32[]{:S(2)}, u32[]{:S(2)}) collective-permute-start(f32[136,384]{1,0:T(8,128)S(1)} %get-tuple-element.85), channel_id=1, source_target_pairs={{0,4},{1,5},{2,6},{3,7},{4,0},{5,1},{6,2},{7,3},{8,12},{9,13},{10,... | collective-permute-start | bytes 626696 | tf_op jit(solution)/shard_map/ppermute | solution.py:816
  19.2 1.1 %collective-permute-done.34.pair_ref = f32[136,384]{1,0:T(8,128)S(1)} collective-permute-done((f32[136,384]{1,0:T(8,128)S(1)}, f32[136,384]{1,0:T(8,128)S(1)}, u32[]{:S(2)}, u32[]{:S(2)}) %collective-permute-start.34) | collective-permute-done | bytes 208928 | tf_op jit(solution)/shard_map/ppermute | solution.py:816
  20.3 0.9 %nest.1 = (f32[10,24,384]{2,1,0:T(8,128)S(1)}, f32[80,128]{1,0:T(8,128)S(1)}) custom-call(s32[1]{0:T(128)S(6)} %copy.26.offset_ref, f32[10,24,384]{2,1,0:T(8,128)S(1)} %bitcast.6, f32[4,24,384]{2,1,0:T(8,128)S(1)} %bitcast.8, f32[32,128]{1,0:T(8,128)S(1)} %get-tuple-element.82.west_ref, f32[32,128]{1,0:T(8,128)S(1)} %get-tuple-element.83.east_ref, ...), custom_call_target="tpu_custom_call" | custom-call | tf_op jit(solution)/shard_map/nest/pallas_call | solution.py:817
  21.2 1.3 %collective-permute-start.35 = (f32[80,128]{1,0:T(8,128)S(1)}, f32[80,128]{1,0:T(8,128)S(1)}, u32[]{:S(2)}, u32[]{:S(2)}) collective-permute-start(f32[80,128]{1,0:T(8,128)S(1)} %get-tuple-element.87), channel_id=1, source_target_pairs={{1,0},{5,4},{9,8},{13,12},{17,16},{21,20},{25,24},{29,28}} | collective-permute-start | bytes 122888 | tf_op jit(solution)/shard_map/ppermute | solution.py:837
  22.5 1.3 %collective-permute-start.37 = (f32[80,128]{1,0:T(8,128)S(1)}, f32[80,128]{1,0:T(8,128)S(1)}, u32[]{:S(2)}, u32[]{:S(2)}) collective-permute-start(f32[80,128]{1,0:T(8,128)S(1)} %get-tuple-element.87), channel_id=1, source_target_pairs={{3,0},{7,4},{11,8},{15,12},{19,16},{23,20},{27,24},{31,28}} | collective-permute-start | bytes 122888 | tf_op jit(solution)/shard_map/ppermute | solution.py:837
  23.8 2.3 %collective-permute-start.36 = (f32[80,128]{1,0:T(8,128)S(1)}, f32[80,128]{1,0:T(8,128)S(1)}, u32[]{:S(2)}, u32[]{:S(2)}) collective-permute-start(f32[80,128]{1,0:T(8,128)S(1)} %get-tuple-element.87), channel_id=1, source_target_pairs={{2,0},{6,4},{10,8},{14,12},{18,16},{22,20},{26,24},{30,28},{5,1},{... | collective-permute-start | bytes 122888 | tf_op jit(solution)/shard_map/ppermute | solution.py:837
  26.1 2.3 %collective-permute-done.35 = f32[80,128]{1,0:T(8,128)S(1)} collective-permute-done((f32[80,128]{1,0:T(8,128)S(1)}, f32[80,128]{1,0:T(8,128)S(1)}, u32[]{:S(2)}, u32[]{:S(2)}) %collective-permute-start.35) | collective-permute-done | bytes 40992 | tf_op jit(solution)/shard_map/ppermute | solution.py:837
  28.8 1.4 %collective-permute-done.37 = f32[80,128]{1,0:T(8,128)S(1)} collective-permute-done((f32[80,128]{1,0:T(8,128)S(1)}, f32[80,128]{1,0:T(8,128)S(1)}, u32[]{:S(2)}, u32[]{:S(2)}) %collective-permute-start.37) | collective-permute-done | bytes 40992 | tf_op jit(solution)/shard_map/ppermute | solution.py:837
  30.2 1.7 %collective-permute-start.41 = (f32[80,384]{1,0:T(8,128)S(1)}, f32[80,384]{1,0:T(8,128)S(1)}, u32[]{:S(2)}, u32[]{:S(2)}) collective-permute-start(f32[80,384]{1,0:T(8,128)S(1)} %constant_dynamic-update-slice_fusion.refs_0_), channel_id=1, source_target_pairs={{0,16},{1,17},{2,18},{3,19},{4,20},{5,21},{6,22},{7,23},{8,24},{9,... | collective-permute-start | bytes 368648 | tf_op jit(solution)/shard_map/ppermute | solution.py:844
  32.0 1.3 %collective-permute-start.40 = (f32[80,384]{1,0:T(8,128)S(1)}, f32[80,384]{1,0:T(8,128)S(1)}, u32[]{:S(2)}, u32[]{:S(2)}) collective-permute-start(f32[80,384]{1,0:T(8,128)S(1)} %constant_dynamic-update-slice_fusion.refs_0_), channel_id=1, source_target_pairs={{0,12},{1,13},{2,14},{3,15},{4,24},{5,25},{6,26},{7,27},{8,20},{9,... | collective-permute-start | bytes 368648 | tf_op jit(solution)/shard_map/ppermute | solution.py:844
  33.4 0.6 %collective-permute-start.38 = (f32[80,384]{1,0:T(8,128)S(1)}, f32[80,384]{1,0:T(8,128)S(1)}, u32[]{:S(2)}, u32[]{:S(2)}) collective-permute-start(f32[80,384]{1,0:T(8,128)S(1)} %constant_dynamic-update-slice_fusion.refs_0_), channel_id=1, source_target_pairs={{0,4},{1,5},{2,6},{3,7},{4,0},{5,1},{6,2},{7,3},{8,12},{9,13},{10,... | collective-permute-start | bytes 368648 | tf_op jit(solution)/shard_map/ppermute | solution.py:844
  34.0 1.1 %collective-permute-done.41.refs_4_ = f32[80,384]{1,0:T(8,128)S(1)} collective-permute-done((f32[80,384]{1,0:T(8,128)S(1)}, f32[80,384]{1,0:T(8,128)S(1)}, u32[]{:S(2)}, u32[]{:S(2)}) %collective-permute-start.41) | collective-permute-done | bytes 122912 | tf_op jit(solution)/shard_map/ppermute | solution.py:844
  35.1 2.1 %collective-permute-done.40.refs_3_ = f32[80,384]{1,0:T(8,128)S(1)} collective-permute-done((f32[80,384]{1,0:T(8,128)S(1)}, f32[80,384]{1,0:T(8,128)S(1)}, u32[]{:S(2)}, u32[]{:S(2)}) %collective-permute-start.40) | collective-permute-done | bytes 122912 | tf_op jit(solution)/shard_map/ppermute | solution.py:844
  37.5 1.9 %collective-permute-done.39.refs_2_ = f32[80,384]{1,0:T(8,128)S(1)} collective-permute-done((f32[80,384]{1,0:T(8,128)S(1)}, f32[80,384]{1,0:T(8,128)S(1)}, u32[]{:S(2)}, u32[]{:S(2)}) %collective-permute-start.39) | collective-permute-done | bytes 122912 | tf_op jit(solution)/shard_map/ppermute | solution.py:844
  39.3 0.7 %collective-permute-start.42 = (f32[80,384]{1,0:T(8,128)S(1)}, f32[80,384]{1,0:T(8,128)S(1)}, u32[]{:S(2)}, u32[]{:S(2)}) collective-permute-start(f32[80,384]{1,0:T(8,128)S(1)} %collective-permute-done.39.refs_2_), channel_id=1, source_target_pairs={{0,4},{1,5},{2,6},{3,7},{4,0},{5,1},{6,2},{7,3},{8,12},{9,13},{10,... | collective-permute-start | bytes 368648 | tf_op jit(solution)/shard_map/ppermute | solution.py:844
  40.0 1.0 %collective-permute-done.42.refs_5_ = f32[80,384]{1,0:T(8,128)S(1)} collective-permute-done((f32[80,384]{1,0:T(8,128)S(1)}, f32[80,384]{1,0:T(8,128)S(1)}, u32[]{:S(2)}, u32[]{:S(2)}) %collective-permute-start.42) | collective-permute-done | bytes 122912 | tf_op jit(solution)/shard_map/ppermute | solution.py:844
  41.0 0.8 %merge.1 = f32[10,24,384]{2,1,0:T(8,128)} custom-call(s32[1]{0:T(128)S(6)} %copy.26.offset_ref, f32[80,384]{1,0:T(8,128)S(1)} %constant_dynamic-update-slice_fusion.refs_0_, f32[80,384]{1,0:T(8,128)S(1)} %collective-permute-done.38.refs_1_, f32[80,384]{1,0:T(8,128)S(1)} %collective-permute-done.39.refs_2_, f32[80,384]{1,0:T(8,128)S(1)} %collective-permute-done.40.refs_3_, ...), custom_call_target="tpu_custom_call" | custom-call | tf_op jit(solution)/shard_map/merge/pallas_call | solution.py:853
  (42 shorter events, 3.6 us)
Async XLA Ops:
  2.1 18.2 %copy-start = (f32[5,2,24,384]{3,2,1,0:T(8,128)S(1)}, f32[5,2,24,384]{3,2,1,0:T(8,128)}, u32[]{:S(2)}) copy-start(f32[5,2,24,384]{3,2,1,0:T(8,128)} %param.7) | copy-start | bytes 1105924
  2.1 18.2 %copy-start.1 = (f32[2,2,24,384]{3,2,1,0:T(8,128)S(1)}, f32[2,2,24,384]{3,2,1,0:T(8,128)}, u32[]{:S(2)}) copy-start(f32[2,2,24,384]{3,2,1,0:T(8,128)} %param.8) | copy-start | bytes 442372
  2.2 8.5 %collective-permute-start.30 = (f32[56,256]{1,0:T(8,128)S(1)}, f32[56,256]{1,0:T(8,128)S(1)}, u32[]{:S(2)}, u32[]{:S(2)}) collective-permute-start(f32[56,256]{1,0:T(8,128)S(1)} %get-tuple-element.63), channel_id=1, source_target_pairs={{12,2},{16,6},{20,26},{24,30},{18,13},{14,17},{6,11},{26,23},{5,0}... | collective-permute-start | bytes 172040 | tf_op jit(solution)/shard_map/cond/branch_3_fun/ppermute | solution.py:792
  2.7 8.5 %collective-permute-start.29 = (f32[56,256]{1,0:T(8,128)S(1)}, f32[56,256]{1,0:T(8,128)S(1)}, u32[]{:S(2)}, u32[]{:S(2)}) collective-permute-start(f32[56,256]{1,0:T(8,128)S(1)} %get-tuple-element.62), channel_id=1, source_target_pairs={{1,2},{2,3},{5,6},{9,10},{10,7},{13,14},{14,15},{16,23},{17,18},{1... | collective-permute-start | bytes 172040 | tf_op jit(solution)/shard_map/cond/branch_3_fun/ppermute | solution.py:792
  8.4 5.2 %collective-permute-start.28 = (f32[56,256]{1,0:T(8,128)S(1)}, f32[56,256]{1,0:T(8,128)S(1)}, u32[]{:S(2)}, u32[]{:S(2)}) collective-permute-start(f32[56,256]{1,0:T(8,128)S(1)} %get-tuple-element.62), channel_id=1, source_target_pairs={{5,10},{9,6},{10,11},{12,3},{13,18},{14,19},{16,7},{17,14},{18,15}... | collective-permute-start | bytes 172040 | tf_op jit(solution)/shard_map/cond/branch_3_fun/ppermute | solution.py:792
  8.9 6.6 %collective-permute-start.26 = (f32[56,384]{1,0:T(8,128)S(1)}, f32[56,384]{1,0:T(8,128)S(1)}, u32[]{:S(2)}, u32[]{:S(2)}) collective-permute-start(f32[56,384]{1,0:T(8,128)S(1)} %get-tuple-element.61), channel_id=1, source_target_pairs={{0,28},{1,29},{2,30},{3,31},{4,8},{5,9},{6,10},{7,11},{8,4},{9,5},... | collective-permute-start | bytes 258056 | tf_op jit(solution)/shard_map/cond/branch_3_fun/ppermute | solution.py:789
  10.6 3.1 %collective-permute-start.27 = (f32[56,256]{1,0:T(8,128)S(1)}, f32[56,256]{1,0:T(8,128)S(1)}, u32[]{:S(2)}, u32[]{:S(2)}) collective-permute-start(f32[56,256]{1,0:T(8,128)S(1)} %get-tuple-element.62), channel_id=1, source_target_pairs={{6,7},{12,11},{16,15},{20,19},{24,23},{26,27},{4,0},{5,1},{3,2},{7... | collective-permute-start | bytes 172040 | tf_op jit(solution)/shard_map/cond/branch_3_fun/ppermute | solution.py:792
  10.6 4.9 %copy-start.8 = (f32[56,256]{1,0:T(8,128)}, f32[56,256]{1,0:T(8,128)S(1)}, u32[]{:S(2)}) copy-start(f32[56,256]{1,0:T(8,128)S(1)} %collective-permute-done.30.refs_3_) | copy-start | bytes 172036 | tf_op jit(solution)/shard_map/cond
  10.6 3.7 %collective-permute-start.33 = (f32[56,256]{1,0:T(8,128)S(1)}, f32[56,256]{1,0:T(8,128)S(1)}, u32[]{:S(2)}, u32[]{:S(2)}) collective-permute-start(f32[56,256]{1,0:T(8,128)S(1)} %get-tuple-element.64), channel_id=1, source_target_pairs={{3,2},{6,9},{7,6},{11,10},{12,1},{15,14},{16,5},{19,18},{20,13},{2... | collective-permute-start | bytes 172040 | tf_op jit(solution)/shard_map/cond/branch_3_fun/ppermute | solution.py:792
  11.2 4.4 %copy-start.11 = (f32[56,256]{1,0:T(8,128)}, f32[56,256]{1,0:T(8,128)S(1)}, u32[]{:S(2)}) copy-start(f32[56,256]{1,0:T(8,128)S(1)} %collective-permute-done.29.refs_2_) | copy-start | bytes 172036 | tf_op jit(solution)/shard_map/cond
  11.2 4.3 %collective-permute-start.32 = (f32[56,256]{1,0:T(8,128)S(1)}, f32[56,256]{1,0:T(8,128)S(1)}, u32[]{:S(2)}, u32[]{:S(2)}) collective-permute-start(f32[56,256]{1,0:T(8,128)S(1)} %get-tuple-element.64), channel_id=1, source_target_pairs={{2,1},{7,10},{10,5},{11,6},{12,9},{15,18},{16,13},{19,14},{20,17},... | collective-permute-start | bytes 172040 | tf_op jit(solution)/shard_map/cond/branch_3_fun/ppermute | solution.py:792
  13.6 1.9 %copy-start.14 = (f32[56,256]{1,0:T(8,128)}, f32[56,256]{1,0:T(8,128)S(1)}, u32[]{:S(2)}) copy-start(f32[56,256]{1,0:T(8,128)S(1)} %collective-permute-done.28.refs_1_) | copy-start | bytes 172036 | tf_op jit(solution)/shard_map/cond
  13.6 1.8 %collective-permute-start.31 = (f32[56,256]{1,0:T(8,128)S(1)}, f32[56,256]{1,0:T(8,128)S(1)}, u32[]{:S(2)}, u32[]{:S(2)}) collective-permute-start(f32[56,256]{1,0:T(8,128)S(1)} %get-tuple-element.64), channel_id=1, source_target_pairs={{6,5},{10,9},{14,13},{16,21},{18,17},{20,25},{4,0},{5,1},{1,2},{7,... | collective-permute-start | bytes 172040 | tf_op jit(solution)/shard_map/cond/branch_3_fun/ppermute | solution.py:792
  17.3 3.0 %collective-permute-start.34 = (f32[136,384]{1,0:T(8,128)S(1)}, f32[136,384]{1,0:T(8,128)S(1)}, u32[]{:S(2)}, u32[]{:S(2)}) collective-permute-start(f32[136,384]{1,0:T(8,128)S(1)} %get-tuple-element.85), channel_id=1, source_target_pairs={{0,4},{1,5},{2,6},{3,7},{4,0},{5,1},{6,2},{7,3},{8,12},{9,13},{10,... | collective-permute-start | bytes 626696 | tf_op jit(solution)/shard_map/ppermute | solution.py:816
  21.2 7.2 %collective-permute-start.35 = (f32[80,128]{1,0:T(8,128)S(1)}, f32[80,128]{1,0:T(8,128)S(1)}, u32[]{:S(2)}, u32[]{:S(2)}) collective-permute-start(f32[80,128]{1,0:T(8,128)S(1)} %get-tuple-element.87), channel_id=1, source_target_pairs={{1,0},{5,4},{9,8},{13,12},{17,16},{21,20},{25,24},{29,28}} | collective-permute-start | bytes 122888 | tf_op jit(solution)/shard_map/ppermute | solution.py:837
  22.5 7.7 %collective-permute-start.37 = (f32[80,128]{1,0:T(8,128)S(1)}, f32[80,128]{1,0:T(8,128)S(1)}, u32[]{:S(2)}, u32[]{:S(2)}) collective-permute-start(f32[80,128]{1,0:T(8,128)S(1)} %get-tuple-element.87), channel_id=1, source_target_pairs={{3,0},{7,4},{11,8},{15,12},{19,16},{23,20},{27,24},{31,28}} | collective-permute-start | bytes 122888 | tf_op jit(solution)/shard_map/ppermute | solution.py:837
  23.8 5.0 %collective-permute-start.36 = (f32[80,128]{1,0:T(8,128)S(1)}, f32[80,128]{1,0:T(8,128)S(1)}, u32[]{:S(2)}, u32[]{:S(2)}) collective-permute-start(f32[80,128]{1,0:T(8,128)S(1)} %get-tuple-element.87), channel_id=1, source_target_pairs={{2,0},{6,4},{10,8},{14,12},{18,16},{22,20},{26,24},{30,28},{5,1},{... | collective-permute-start | bytes 122888 | tf_op jit(solution)/shard_map/ppermute | solution.py:837
  30.2 4.9 %collective-permute-start.41 = (f32[80,384]{1,0:T(8,128)S(1)}, f32[80,384]{1,0:T(8,128)S(1)}, u32[]{:S(2)}, u32[]{:S(2)}) collective-permute-start(f32[80,384]{1,0:T(8,128)S(1)} %constant_dynamic-update-slice_fusion.refs_0_), channel_id=1, source_target_pairs={{0,16},{1,17},{2,18},{3,19},{4,20},{5,21},{6,22},{7,23},{8,24},{9,... | collective-permute-start | bytes 368648 | tf_op jit(solution)/shard_map/ppermute | solution.py:844
  32.0 5.2 %collective-permute-start.40 = (f32[80,384]{1,0:T(8,128)S(1)}, f32[80,384]{1,0:T(8,128)S(1)}, u32[]{:S(2)}, u32[]{:S(2)}) collective-permute-start(f32[80,384]{1,0:T(8,128)S(1)} %constant_dynamic-update-slice_fusion.refs_0_), channel_id=1, source_target_pairs={{0,12},{1,13},{2,14},{3,15},{4,24},{5,25},{6,26},{7,27},{8,20},{9,... | collective-permute-start | bytes 368648 | tf_op jit(solution)/shard_map/ppermute | solution.py:844
  33.3 6.0 %collective-permute-start.39 = (f32[80,384]{1,0:T(8,128)S(1)}, f32[80,384]{1,0:T(8,128)S(1)}, u32[]{:S(2)}, u32[]{:S(2)}) collective-permute-start(f32[80,384]{1,0:T(8,128)S(1)} %constant_dynamic-update-slice_fusion.refs_0_), channel_id=1, source_target_pairs={{0,28},{1,29},{2,30},{3,31},{4,8},{5,9},{6,10},{7,11},{8,4},{9,5},... | collective-permute-start | bytes 368648 | tf_op jit(solution)/shard_map/ppermute | solution.py:844
  33.4 6.6 %collective-permute-start.38 = (f32[80,384]{1,0:T(8,128)S(1)}, f32[80,384]{1,0:T(8,128)S(1)}, u32[]{:S(2)}, u32[]{:S(2)}) collective-permute-start(f32[80,384]{1,0:T(8,128)S(1)} %constant_dynamic-update-slice_fusion.refs_0_), channel_id=1, source_target_pairs={{0,4},{1,5},{2,6},{3,7},{4,0},{5,1},{6,2},{7,3},{8,12},{9,13},{10,... | collective-permute-start | bytes 368648 | tf_op jit(solution)/shard_map/ppermute | solution.py:844
  35.1 5.0 %collective-permute-start.44 = (f32[80,384]{1,0:T(8,128)S(1)}, f32[80,384]{1,0:T(8,128)S(1)}, u32[]{:S(2)}, u32[]{:S(2)}) collective-permute-start(f32[80,384]{1,0:T(8,128)S(1)} %collective-permute-done.41.refs_4_), channel_id=1, source_target_pairs={{0,4},{1,5},{2,6},{3,7},{4,0},{5,1},{6,2},{7,3},{8,12},{9,13},{10,... | collective-permute-start | bytes 368648 | tf_op jit(solution)/shard_map/ppermute | solution.py:844
  37.2 2.8 %collective-permute-start.43 = (f32[80,384]{1,0:T(8,128)S(1)}, f32[80,384]{1,0:T(8,128)S(1)}, u32[]{:S(2)}, u32[]{:S(2)}) collective-permute-start(f32[80,384]{1,0:T(8,128)S(1)} %collective-permute-done.40.refs_3_), channel_id=1, source_target_pairs={{0,4},{1,5},{2,6},{3,7},{4,0},{5,1},{6,2},{7,3},{8,12},{9,13},{10,... | collective-permute-start | bytes 368648 | tf_op jit(solution)/shard_map/ppermute | solution.py:844
  39.3 1.7 %collective-permute-start.42 = (f32[80,384]{1,0:T(8,128)S(1)}, f32[80,384]{1,0:T(8,128)S(1)}, u32[]{:S(2)}, u32[]{:S(2)}) collective-permute-start(f32[80,384]{1,0:T(8,128)S(1)} %collective-permute-done.39.refs_2_), channel_id=1, source_target_pairs={{0,4},{1,5},{2,6},{3,7},{4,0},{5,1},{6,2},{7,3},{8,12},{9,13},{10,... | collective-permute-start | bytes 368648 | tf_op jit(solution)/shard_map/ppermute | solution.py:844
  (5 other events, 4.9 us)

commit v8 on v7

--- a/solution.py
+++ b/solution.py
@@ -693,7 +693,7 @@
 def hops(one, two):
     (t, s), (u, r) = divmod(one, 4), divmod(two, 4)
     links = abs((t >> 2) - (u >> 2)) + abs(((t >> 1) & 1) - ((u >> 1) & 1)) + abs(s - r)
-    return links or 0.3
+    return links or 0.8
 
 
 def completed(pairs, valid):
@@ -702,7 +702,7 @@
 
     def cost(a, b):
         from_parent = a % 4 == 0 and b % 4 > 0
-        return 1e3 if a == b or from_parent or (a, b) in valid else hops(a, b) ** 2
+        return 1e3 if a == b or from_parent or (a, b) in valid else hops(a, b) ** 3
 
     n = len(senders)
     row_price, column_price = [0.0] * (n + 1), [0.0] * (n + 1)
@@ -752,16 +752,18 @@
         middle.append([(device(0, 0), device(0, 2)), (device(2, 0), device(6, 1))])
         middle.append([(device(2, 0), device(6, 3))])
     groups = []
-    for section, inner in ((1, ((2, 1), (3, 2))), (3, ((1, 2), (2, 3)))):
-        edges = [(device(start + a, 0), device(b, section)) for a, b in sends[section]]
+    for section, inner, order in (
+        (1, ((2, 1), (3, 2)), (2, 0, 1)),
+        (3, ((1, 2), (2, 3)), (1, 2, 0)),
+    ):
+        edges = [(device(t, a), device(t, b)) for a, b in inner for t in range(8)]
+        edges += [(device(corners[t], a), device(t, b)) for a, b in inner for t in corners]
+        edges = [pair for pair in edges if pair not in crowded]
+        edges += [(device(start + a, 0), device(b, section)) for a, b in sends[section]]
         if start == 1:
             edges.append((device(0, 0), device(0, section)))
-        for a, b in inner:
-            edges += [(device(t, a), device(t, b)) for t in range(8)]
-            edges += [(device(corners[t], a), device(t, b)) for t in corners]
-        edges = [pair for pair in edges if pair not in crowded]
-        rounds = in_rounds(edges, 3)[::-1]
-        groups.append([completed(pairs, edges) for pairs in rounds])
+        rounds = in_rounds(edges, 3)
+        groups.append([completed(rounds[i], edges) for i in order])
     middle = [completed(pairs, []) for pairs in middle]
     return groups[0], middle, groups[1]
 

time: 42.1 us -> 42.3 us (level)
    ppermute x3, starting transfers between devices: 4.92 us -> 7.5 us  [gather_from(): return lax.ppermute(means, BOTH, pairs)]
    ppermute x1, starting transfers between devices: 1.73 us -> 0.34 us  [send_rims(): from_cross = lax.ppermute(to_cross, BOTH, cross_map)]
    ppermute x1, starting transfers between devices: 1.87 us -> 0.9 us  [on_device(): from_pair = lax.ppermute(to_pair, BOTH, pair_map)]
    ppermute x7, waiting for transfers between devices: 6.06 us -> 5.26 us  [across(): return lax.ppermute(value, BOTH, pairs)]
    ppermute x7, waiting for transfers between devices: 1.72 us -> 2.48 us  [send_rims(): lax.ppermute(value, BOTH, pairs)]
  transfers between devices with their start and end apart: 19 -> 19, of which waited for: 10 -> 9; matrix products, arithmetic and copies ran while one was open for 0% -> 0% of each run, Pallas kernels for 0% -> 0%
where the time goes in v8:
time: 42.3 us; the launch traced here: 42.1 us
  starting transfers between devices  23.5 us (56%)
  waiting for transfers between devices  12.7 us (30%)
  Pallas kernels  4.32 us (10%)
  between operations  0.76 us (2%)
  local copies, waits for them, and re-layouts  0.65 us (2%)
    ppermute x7, starting transfers between devices, send_rims(): lax.ppermute(value, BOTH, pairs)  9.62 us
    ppermute x3, starting transfers between devices, gather_from(): return lax.ppermute(means, BOTH, pairs)  7.5 us
    ppermute x7, waiting for transfers between devices, across(): return lax.ppermute(value, BOTH, pairs)  5.26 us
    ppermute x7, starting transfers between devices, across(): return lax.ppermute(value, BOTH, pairs)  5.16 us
    ppermute x3, waiting for transfers between devices, gather_from(): return lax.ppermute(means, BOTH, pairs)  3.89 us
    ppermute x7, waiting for transfers between devices, send_rims(): lax.ppermute(value, BOTH, pairs)  2.48 us
    pallas_call x1, Pallas kernels, on_device(): pl.pallas_call(pack_kernel, out_shape=[shaped(SLOTS, 2 * LANE)] * 3 + [sh...  1.44 us
    pallas_call x1, Pallas kernels, send_rims(): pl.pallas_call(functools.partial(relay_kernel, max(case, 1), len(middle))...  1.18 us
  transfers between devices with their start and end apart: 19, of which 9 were waited for; matrix products, arithmetic and copies ran while one was open for 0% of the time, Pallas kernels for 0%

profile of v8, /device:TPU:0, one launch (start us, length us, event | category | flops | bytes accessed | tf_op | source)
XLA Modules:
  0.0 42.1 jit_solution(4403841089680259486)
XLA Ops:
  0.7 1.4 %pack.1 = (f32[56,256]{1,0:T(8,128)S(1)}, f32[56,256]{1,0:T(8,128)S(1)}, f32[56,256]{1,0:T(8,128)S(1)}, f32[56,384]{1,0:T(8,128)S(1)}, f32[56,384]{1,0:T(8,128)S(1)}) custom-call(s32[1]{0:T(128)S(6)} %copy.26.offset_ref, f32[10,24,384]{2,1,0:T(8,128)} %bitcast.5, f32[4,24,384]{2,1,0:T(8,128)} %bitcast.7), custom_call_target="tpu_custom_call" | custom-call | tf_op jit(solution)/shard_map/pack/pallas_call | solution.py:778
  2.1 14.3 %conditional.1 = ((f32[32,128]{1,0:T(8,128)S(1)}, f32[32,128]{1,0:T(8,128)S(1)}, f32[72,256]{1,0:T(8,128)S(1)}, f32[136,384]{1,0:T(8,128)S(1)}, f32[56,384]{1,0:T(8,128)S(1)})) conditional(s32[]{:T(128)} %clamp.3, (f32[56,384]{1,0:T(8,128)S(1)}, f32[56,256]{1,0:T(8,128)S(1)}, f32[56,256]{1,0:T(8,128)S(1)}, ...), branch_computations={%region_0.1_spmd, %region_1.2_spmd, %region_2.3_spmd, %region_3.4_... | conditional | bytes 4817584 | solution.py:811
  2.2 2.5 %collective-permute-start.22 = (f32[56,256]{1,0:T(8,128)S(1)}, f32[56,256]{1,0:T(8,128)S(1)}, u32[]{:S(2)}, u32[]{:S(2)}) collective-permute-start(f32[56,256]{1,0:T(8,128)S(1)} %get-tuple-element.58), channel_id=1, source_target_pairs={{8,2},{12,6},{16,26},{20,30},{18,13},{14,17},{6,11},{26,23},{4,0},... | collective-permute-start | bytes 172040 | tf_op jit(solution)/shard_map/cond/branch_2_fun/ppermute | solution.py:794
  4.6 4.1 %collective-permute-start.21 = (f32[56,256]{1,0:T(8,128)S(1)}, f32[56,256]{1,0:T(8,128)S(1)}, u32[]{:S(2)}, u32[]{:S(2)}) collective-permute-start(f32[56,256]{1,0:T(8,128)S(1)} %get-tuple-element.57), channel_id=1, source_target_pairs={{1,2},{5,6},{8,3},{9,10},{12,7},{13,14},{14,15},{16,11},{17,18},{1... | collective-permute-start | bytes 172040 | tf_op jit(solution)/shard_map/cond/branch_2_fun/ppermute | solution.py:794
  9.2 0.8 %collective-permute-start.25 = (f32[56,256]{1,0:T(8,128)S(1)}, f32[56,256]{1,0:T(8,128)S(1)}, u32[]{:S(2)}, u32[]{:S(2)}) collective-permute-start(f32[56,256]{1,0:T(8,128)S(1)} %get-tuple-element.59), channel_id=1, source_target_pairs={{2,1},{6,5},{7,10},{8,9},{11,6},{12,13},{15,18},{16,17},{19,14},{2... | collective-permute-start | bytes 172040 | tf_op jit(solution)/shard_map/cond/branch_2_fun/ppermute | solution.py:794
  10.0 0.9 %collective-permute-done.21.refs_2_ = f32[56,256]{1,0:T(8,128)S(1)} collective-permute-done((f32[56,256]{1,0:T(8,128)S(1)}, f32[56,256]{1,0:T(8,128)S(1)}, u32[]{:S(2)}, u32[]{:S(2)}) %collective-permute-start.21) | collective-permute-done | bytes 57376 | tf_op jit(solution)/shard_map/cond/branch_2_fun/ppermute | solution.py:794
  10.9 1.9 %collective-permute-start.24 = (f32[56,256]{1,0:T(8,128)S(1)}, f32[56,256]{1,0:T(8,128)S(1)}, u32[]{:S(2)}, u32[]{:S(2)}) collective-permute-start(f32[56,256]{1,0:T(8,128)S(1)} %get-tuple-element.59), channel_id=1, source_target_pairs={{3,2},{7,6},{8,1},{10,9},{11,10},{12,5},{15,14},{16,13},{19,18},{2... | collective-permute-start | bytes 172040 | tf_op jit(solution)/shard_map/cond/branch_2_fun/ppermute | solution.py:794
  13.2 1.4 %collective-permute-done.24.refs_5_ = f32[56,256]{1,0:T(8,128)S(1)} collective-permute-done((f32[56,256]{1,0:T(8,128)S(1)}, f32[56,256]{1,0:T(8,128)S(1)}, u32[]{:S(2)}, u32[]{:S(2)}) %collective-permute-start.24) | collective-permute-done | bytes 57376 | tf_op jit(solution)/shard_map/cond/branch_2_fun/ppermute | solution.py:794
  15.3 1.2 %relay.6 = (f32[32,128]{1,0:T(8,128)S(1)}, f32[32,128]{1,0:T(8,128)S(1)}, f32[72,256]{1,0:T(8,128)S(1)}, f32[136,384]{1,0:T(8,128)S(1)}, f32[56,384]{1,0:T(8,128)S(1)}) custom-call(f32[56,384]{1,0:T(8,128)S(1)} %get-tuple-element.55.to_pair_ref, f32[56,384]{1,0:T(8,128)} %copy-done.3, f32[56,256]{1,0:T(8,128)} %copy-done.16, f32[56,256]{1,0:T(8,128)} %copy-done.13, ...), custom_call_target="tpu_custom_call" | custom-call | tf_op jit(solution)/shard_map/cond/branch_2_fun/relay/pallas_call | solution.py:797
  16.5 0.9 %collective-permute-start.34 = (f32[136,384]{1,0:T(8,128)S(1)}, f32[136,384]{1,0:T(8,128)S(1)}, u32[]{:S(2)}, u32[]{:S(2)}) collective-permute-start(f32[136,384]{1,0:T(8,128)S(1)} %get-tuple-element.85), channel_id=1, source_target_pairs={{0,4},{1,5},{2,6},{3,7},{4,0},{5,1},{6,2},{7,3},{8,12},{9,13},{10,... | collective-permute-start | bytes 626696 | tf_op jit(solution)/shard_map/ppermute | solution.py:818
  17.4 1.1 %collective-permute-done.34.pair_ref = f32[136,384]{1,0:T(8,128)S(1)} collective-permute-done((f32[136,384]{1,0:T(8,128)S(1)}, f32[136,384]{1,0:T(8,128)S(1)}, u32[]{:S(2)}, u32[]{:S(2)}) %collective-permute-start.34) | collective-permute-done | bytes 208928 | tf_op jit(solution)/shard_map/ppermute | solution.py:818
  18.5 0.9 %nest.1 = (f32[10,24,384]{2,1,0:T(8,128)S(1)}, f32[80,128]{1,0:T(8,128)S(1)}) custom-call(s32[1]{0:T(128)S(6)} %copy.26.offset_ref, f32[10,24,384]{2,1,0:T(8,128)S(1)} %bitcast.6, f32[4,24,384]{2,1,0:T(8,128)S(1)} %bitcast.8, f32[32,128]{1,0:T(8,128)S(1)} %get-tuple-element.82.west_ref, f32[32,128]{1,0:T(8,128)S(1)} %get-tuple-element.83.east_ref, ...), custom_call_target="tpu_custom_call" | custom-call | tf_op jit(solution)/shard_map/nest/pallas_call | solution.py:819
  19.4 1.3 %collective-permute-start.35 = (f32[80,128]{1,0:T(8,128)S(1)}, f32[80,128]{1,0:T(8,128)S(1)}, u32[]{:S(2)}, u32[]{:S(2)}) collective-permute-start(f32[80,128]{1,0:T(8,128)S(1)} %get-tuple-element.87), channel_id=1, source_target_pairs={{1,0},{5,4},{9,8},{13,12},{17,16},{21,20},{25,24},{29,28}} | collective-permute-start | bytes 122888 | tf_op jit(solution)/shard_map/ppermute | solution.py:839
  20.7 1.3 %collective-permute-start.37 = (f32[80,128]{1,0:T(8,128)S(1)}, f32[80,128]{1,0:T(8,128)S(1)}, u32[]{:S(2)}, u32[]{:S(2)}) collective-permute-start(f32[80,128]{1,0:T(8,128)S(1)} %get-tuple-element.87), channel_id=1, source_target_pairs={{3,0},{7,4},{11,8},{15,12},{19,16},{23,20},{27,24},{31,28}} | collective-permute-start | bytes 122888 | tf_op jit(solution)/shard_map/ppermute | solution.py:839
  22.0 4.9 %collective-permute-start.36 = (f32[80,128]{1,0:T(8,128)S(1)}, f32[80,128]{1,0:T(8,128)S(1)}, u32[]{:S(2)}, u32[]{:S(2)}) collective-permute-start(f32[80,128]{1,0:T(8,128)S(1)} %get-tuple-element.87), channel_id=1, source_target_pairs={{2,0},{6,4},{10,8},{14,12},{18,16},{22,20},{26,24},{30,28},{5,1},{... | collective-permute-start | bytes 122888 | tf_op jit(solution)/shard_map/ppermute | solution.py:839
  26.9 3.9 %collective-permute-done.35 = f32[80,128]{1,0:T(8,128)S(1)} collective-permute-done((f32[80,128]{1,0:T(8,128)S(1)}, f32[80,128]{1,0:T(8,128)S(1)}, u32[]{:S(2)}, u32[]{:S(2)}) %collective-permute-start.35) | collective-permute-done | bytes 40992 | tf_op jit(solution)/shard_map/ppermute | solution.py:839
  30.8 1.8 %collective-permute-start.41 = (f32[80,384]{1,0:T(8,128)S(1)}, f32[80,384]{1,0:T(8,128)S(1)}, u32[]{:S(2)}, u32[]{:S(2)}) collective-permute-start(f32[80,384]{1,0:T(8,128)S(1)} %constant_dynamic-update-slice_fusion.refs_0_), channel_id=1, source_target_pairs={{0,16},{1,17},{2,18},{3,19},{4,20},{5,21},{6,22},{7,23},{8,24},{9,... | collective-permute-start | bytes 368648 | tf_op jit(solution)/shard_map/ppermute | solution.py:846
  32.6 1.5 %collective-permute-start.39 = (f32[80,384]{1,0:T(8,128)S(1)}, f32[80,384]{1,0:T(8,128)S(1)}, u32[]{:S(2)}, u32[]{:S(2)}) collective-permute-start(f32[80,384]{1,0:T(8,128)S(1)} %constant_dynamic-update-slice_fusion.refs_0_), channel_id=1, source_target_pairs={{0,28},{1,29},{2,30},{3,31},{4,8},{5,9},{6,10},{7,11},{8,4},{9,5},... | collective-permute-start | bytes 368648 | tf_op jit(solution)/shard_map/ppermute | solution.py:846
  34.1 2.5 %collective-permute-done.41.refs_4_ = f32[80,384]{1,0:T(8,128)S(1)} collective-permute-done((f32[80,384]{1,0:T(8,128)S(1)}, f32[80,384]{1,0:T(8,128)S(1)}, u32[]{:S(2)}, u32[]{:S(2)}) %collective-permute-start.41) | collective-permute-done | bytes 122912 | tf_op jit(solution)/shard_map/ppermute | solution.py:846
  36.6 1.6 %collective-permute-done.40.refs_3_ = f32[80,384]{1,0:T(8,128)S(1)} collective-permute-done((f32[80,384]{1,0:T(8,128)S(1)}, f32[80,384]{1,0:T(8,128)S(1)}, u32[]{:S(2)}, u32[]{:S(2)}) %collective-permute-start.40) | collective-permute-done | bytes 122912 | tf_op jit(solution)/shard_map/ppermute | solution.py:846
  38.2 1.0 %collective-permute-start.43 = (f32[80,384]{1,0:T(8,128)S(1)}, f32[80,384]{1,0:T(8,128)S(1)}, u32[]{:S(2)}, u32[]{:S(2)}) collective-permute-start(f32[80,384]{1,0:T(8,128)S(1)} %collective-permute-done.40.refs_3_), channel_id=1, source_target_pairs={{0,4},{1,5},{2,6},{3,7},{4,0},{5,1},{6,2},{7,3},{8,12},{9,13},{10,... | collective-permute-start | bytes 368648 | tf_op jit(solution)/shard_map/ppermute | solution.py:846
  39.4 0.9 %collective-permute-start.42 = (f32[80,384]{1,0:T(8,128)S(1)}, f32[80,384]{1,0:T(8,128)S(1)}, u32[]{:S(2)}, u32[]{:S(2)}) collective-permute-start(f32[80,384]{1,0:T(8,128)S(1)} %collective-permute-done.39.refs_2_), channel_id=1, source_target_pairs={{0,4},{1,5},{2,6},{3,7},{4,0},{5,1},{6,2},{7,3},{8,12},{9,13},{10,... | collective-permute-start | bytes 368648 | tf_op jit(solution)/shard_map/ppermute | solution.py:846
  40.3 1.0 %collective-permute-done.42.refs_5_ = f32[80,384]{1,0:T(8,128)S(1)} collective-permute-done((f32[80,384]{1,0:T(8,128)S(1)}, f32[80,384]{1,0:T(8,128)S(1)}, u32[]{:S(2)}, u32[]{:S(2)}) %collective-permute-start.42) | collective-permute-done | bytes 122912 | tf_op jit(solution)/shard_map/ppermute | solution.py:846
  41.2 0.8 %merge.1 = f32[10,24,384]{2,1,0:T(8,128)} custom-call(s32[1]{0:T(128)S(6)} %copy.26.offset_ref, f32[80,384]{1,0:T(8,128)S(1)} %constant_dynamic-update-slice_fusion.refs_0_, f32[80,384]{1,0:T(8,128)S(1)} %collective-permute-done.38.refs_1_, f32[80,384]{1,0:T(8,128)S(1)} %collective-permute-done.39.refs_2_, f32[80,384]{1,0:T(8,128)S(1)} %collective-permute-done.40.refs_3_, ...), custom_call_target="tpu_custom_call" | custom-call | tf_op jit(solution)/shard_map/merge/pallas_call | solution.py:855
  (42 shorter events, 1.8 us)
Async XLA Ops:
  2.1 16.4 %copy-start = (f32[5,2,24,384]{3,2,1,0:T(8,128)S(1)}, f32[5,2,24,384]{3,2,1,0:T(8,128)}, u32[]{:S(2)}) copy-start(f32[5,2,24,384]{3,2,1,0:T(8,128)} %param.7) | copy-start | bytes 1105924
  2.1 16.4 %copy-start.1 = (f32[2,2,24,384]{3,2,1,0:T(8,128)S(1)}, f32[2,2,24,384]{3,2,1,0:T(8,128)}, u32[]{:S(2)}) copy-start(f32[2,2,24,384]{3,2,1,0:T(8,128)} %param.8) | copy-start | bytes 442372
  2.2 7.1 %collective-permute-start.22 = (f32[56,256]{1,0:T(8,128)S(1)}, f32[56,256]{1,0:T(8,128)S(1)}, u32[]{:S(2)}, u32[]{:S(2)}) collective-permute-start(f32[56,256]{1,0:T(8,128)S(1)} %get-tuple-element.58), channel_id=1, source_target_pairs={{8,2},{12,6},{16,26},{20,30},{18,13},{14,17},{6,11},{26,23},{4,0},... | collective-permute-start | bytes 172040 | tf_op jit(solution)/shard_map/cond/branch_2_fun/ppermute | solution.py:794
  4.6 6.2 %collective-permute-start.21 = (f32[56,256]{1,0:T(8,128)S(1)}, f32[56,256]{1,0:T(8,128)S(1)}, u32[]{:S(2)}, u32[]{:S(2)}) collective-permute-start(f32[56,256]{1,0:T(8,128)S(1)} %get-tuple-element.57), channel_id=1, source_target_pairs={{1,2},{5,6},{8,3},{9,10},{12,7},{13,14},{14,15},{16,11},{17,18},{1... | collective-permute-start | bytes 172040 | tf_op jit(solution)/shard_map/cond/branch_2_fun/ppermute | solution.py:794
  8.7 4.1 %collective-permute-start.20 = (f32[56,256]{1,0:T(8,128)S(1)}, f32[56,256]{1,0:T(8,128)S(1)}, u32[]{:S(2)}, u32[]{:S(2)}) collective-permute-start(f32[56,256]{1,0:T(8,128)S(1)} %get-tuple-element.57), channel_id=1, source_target_pairs={{6,7},{10,11},{12,23},{14,19},{16,27},{18,15},{4,0},{5,1},{3,2},{7... | collective-permute-start | bytes 172040 | tf_op jit(solution)/shard_map/cond/branch_2_fun/ppermute | solution.py:794
  8.7 5.9 %collective-permute-start.18 = (f32[56,384]{1,0:T(8,128)S(1)}, f32[56,384]{1,0:T(8,128)S(1)}, u32[]{:S(2)}, u32[]{:S(2)}) collective-permute-start(f32[56,384]{1,0:T(8,128)S(1)} %get-tuple-element.56), channel_id=1, source_target_pairs={{0,28},{1,29},{2,30},{3,31},{4,8},{5,9},{6,10},{7,11},{8,4},{9,5},... | collective-permute-start | bytes 258056 | tf_op jit(solution)/shard_map/cond/branch_2_fun/ppermute | solution.py:791
  9.0 4.2 %collective-permute-start.19 = (f32[56,256]{1,0:T(8,128)S(1)}, f32[56,256]{1,0:T(8,128)S(1)}, u32[]{:S(2)}, u32[]{:S(2)}) collective-permute-start(f32[56,256]{1,0:T(8,128)S(1)} %get-tuple-element.57), channel_id=1, source_target_pairs={{2,3},{5,10},{8,11},{9,6},{10,7},{12,15},{13,18},{16,19},{17,14},{... | collective-permute-start | bytes 172040 | tf_op jit(solution)/shard_map/cond/branch_2_fun/ppermute | solution.py:794
  9.2 5.4 %copy-start.7 = (f32[56,256]{1,0:T(8,128)}, f32[56,256]{1,0:T(8,128)S(1)}, u32[]{:S(2)}) copy-start(f32[56,256]{1,0:T(8,128)S(1)} %collective-permute-done.22.refs_3_) | copy-start | bytes 172036 | tf_op jit(solution)/shard_map/cond
  9.2 4.0 %collective-permute-start.25 = (f32[56,256]{1,0:T(8,128)S(1)}, f32[56,256]{1,0:T(8,128)S(1)}, u32[]{:S(2)}, u32[]{:S(2)}) collective-permute-start(f32[56,256]{1,0:T(8,128)S(1)} %get-tuple-element.59), channel_id=1, source_target_pairs={{2,1},{6,5},{7,10},{8,9},{11,6},{12,13},{15,18},{16,17},{19,14},{2... | collective-permute-start | bytes 172040 | tf_op jit(solution)/shard_map/cond/branch_2_fun/ppermute | solution.py:794
  10.9 3.8 %copy-start.10 = (f32[56,256]{1,0:T(8,128)}, f32[56,256]{1,0:T(8,128)S(1)}, u32[]{:S(2)}) copy-start(f32[56,256]{1,0:T(8,128)S(1)} %collective-permute-done.21.refs_2_) | copy-start | bytes 172036 | tf_op jit(solution)/shard_map/cond
  10.9 3.7 %collective-permute-start.24 = (f32[56,256]{1,0:T(8,128)S(1)}, f32[56,256]{1,0:T(8,128)S(1)}, u32[]{:S(2)}, u32[]{:S(2)}) collective-permute-start(f32[56,256]{1,0:T(8,128)S(1)} %get-tuple-element.59), channel_id=1, source_target_pairs={{3,2},{7,6},{8,1},{10,9},{11,10},{12,5},{15,14},{16,13},{19,18},{2... | collective-permute-start | bytes 172040 | tf_op jit(solution)/shard_map/cond/branch_2_fun/ppermute | solution.py:794
  12.8 1.9 %copy-start.13 = (f32[56,256]{1,0:T(8,128)}, f32[56,256]{1,0:T(8,128)S(1)}, u32[]{:S(2)}) copy-start(f32[56,256]{1,0:T(8,128)S(1)} %collective-permute-done.20.refs_1_) | copy-start | bytes 172036 | tf_op jit(solution)/shard_map/cond
  12.8 1.8 %collective-permute-start.23 = (f32[56,256]{1,0:T(8,128)S(1)}, f32[56,256]{1,0:T(8,128)S(1)}, u32[]{:S(2)}, u32[]{:S(2)}) collective-permute-start(f32[56,256]{1,0:T(8,128)S(1)} %get-tuple-element.59), channel_id=1, source_target_pairs={{6,9},{10,5},{12,21},{14,13},{16,25},{18,17},{4,0},{5,1},{1,2},{7,... | collective-permute-start | bytes 172040 | tf_op jit(solution)/shard_map/cond/branch_2_fun/ppermute | solution.py:794
  16.5 2.0 %collective-permute-start.34 = (f32[136,384]{1,0:T(8,128)S(1)}, f32[136,384]{1,0:T(8,128)S(1)}, u32[]{:S(2)}, u32[]{:S(2)}) collective-permute-start(f32[136,384]{1,0:T(8,128)S(1)} %get-tuple-element.85), channel_id=1, source_target_pairs={{0,4},{1,5},{2,6},{3,7},{4,0},{5,1},{6,2},{7,3},{8,12},{9,13},{10,... | collective-permute-start | bytes 626696 | tf_op jit(solution)/shard_map/ppermute | solution.py:818
  19.4 11.4 %collective-permute-start.35 = (f32[80,128]{1,0:T(8,128)S(1)}, f32[80,128]{1,0:T(8,128)S(1)}, u32[]{:S(2)}, u32[]{:S(2)}) collective-permute-start(f32[80,128]{1,0:T(8,128)S(1)} %get-tuple-element.87), channel_id=1, source_target_pairs={{1,0},{5,4},{9,8},{13,12},{17,16},{21,20},{25,24},{29,28}} | collective-permute-start | bytes 122888 | tf_op jit(solution)/shard_map/ppermute | solution.py:839
  20.7 10.1 %collective-permute-start.37 = (f32[80,128]{1,0:T(8,128)S(1)}, f32[80,128]{1,0:T(8,128)S(1)}, u32[]{:S(2)}, u32[]{:S(2)}) collective-permute-start(f32[80,128]{1,0:T(8,128)S(1)} %get-tuple-element.87), channel_id=1, source_target_pairs={{3,0},{7,4},{11,8},{15,12},{19,16},{23,20},{27,24},{31,28}} | collective-permute-start | bytes 122888 | tf_op jit(solution)/shard_map/ppermute | solution.py:839
  22.0 8.8 %collective-permute-start.36 = (f32[80,128]{1,0:T(8,128)S(1)}, f32[80,128]{1,0:T(8,128)S(1)}, u32[]{:S(2)}, u32[]{:S(2)}) collective-permute-start(f32[80,128]{1,0:T(8,128)S(1)} %get-tuple-element.87), channel_id=1, source_target_pairs={{2,0},{6,4},{10,8},{14,12},{18,16},{22,20},{26,24},{30,28},{5,1},{... | collective-permute-start | bytes 122888 | tf_op jit(solution)/shard_map/ppermute | solution.py:839
  30.8 5.8 %collective-permute-start.41 = (f32[80,384]{1,0:T(8,128)S(1)}, f32[80,384]{1,0:T(8,128)S(1)}, u32[]{:S(2)}, u32[]{:S(2)}) collective-permute-start(f32[80,384]{1,0:T(8,128)S(1)} %constant_dynamic-update-slice_fusion.refs_0_), channel_id=1, source_target_pairs={{0,16},{1,17},{2,18},{3,19},{4,20},{5,21},{6,22},{7,23},{8,24},{9,... | collective-permute-start | bytes 368648 | tf_op jit(solution)/shard_map/ppermute | solution.py:846
  32.6 5.6 %collective-permute-start.40 = (f32[80,384]{1,0:T(8,128)S(1)}, f32[80,384]{1,0:T(8,128)S(1)}, u32[]{:S(2)}, u32[]{:S(2)}) collective-permute-start(f32[80,384]{1,0:T(8,128)S(1)} %constant_dynamic-update-slice_fusion.refs_0_), channel_id=1, source_target_pairs={{0,12},{1,13},{2,14},{3,15},{4,24},{5,25},{6,26},{7,27},{8,20},{9,... | collective-permute-start | bytes 368648 | tf_op jit(solution)/shard_map/ppermute | solution.py:846
  32.6 6.8 %collective-permute-start.39 = (f32[80,384]{1,0:T(8,128)S(1)}, f32[80,384]{1,0:T(8,128)S(1)}, u32[]{:S(2)}, u32[]{:S(2)}) collective-permute-start(f32[80,384]{1,0:T(8,128)S(1)} %constant_dynamic-update-slice_fusion.refs_0_), channel_id=1, source_target_pairs={{0,28},{1,29},{2,30},{3,31},{4,8},{5,9},{6,10},{7,11},{8,4},{9,5},... | collective-permute-start | bytes 368648 | tf_op jit(solution)/shard_map/ppermute | solution.py:846
  34.1 6.2 %collective-permute-start.38 = (f32[80,384]{1,0:T(8,128)S(1)}, f32[80,384]{1,0:T(8,128)S(1)}, u32[]{:S(2)}, u32[]{:S(2)}) collective-permute-start(f32[80,384]{1,0:T(8,128)S(1)} %constant_dynamic-update-slice_fusion.refs_0_), channel_id=1, source_target_pairs={{0,4},{1,5},{2,6},{3,7},{4,0},{5,1},{6,2},{7,3},{8,12},{9,13},{10,... | collective-permute-start | bytes 368648 | tf_op jit(solution)/shard_map/ppermute | solution.py:846
  36.6 3.7 %collective-permute-start.44 = (f32[80,384]{1,0:T(8,128)S(1)}, f32[80,384]{1,0:T(8,128)S(1)}, u32[]{:S(2)}, u32[]{:S(2)}) collective-permute-start(f32[80,384]{1,0:T(8,128)S(1)} %collective-permute-done.41.refs_4_), channel_id=1, source_target_pairs={{0,4},{1,5},{2,6},{3,7},{4,0},{5,1},{6,2},{7,3},{8,12},{9,13},{10,... | collective-permute-start | bytes 368648 | tf_op jit(solution)/shard_map/ppermute | solution.py:846
  38.2 2.0 %collective-permute-start.43 = (f32[80,384]{1,0:T(8,128)S(1)}, f32[80,384]{1,0:T(8,128)S(1)}, u32[]{:S(2)}, u32[]{:S(2)}) collective-permute-start(f32[80,384]{1,0:T(8,128)S(1)} %collective-permute-done.40.refs_3_), channel_id=1, source_target_pairs={{0,4},{1,5},{2,6},{3,7},{4,0},{5,1},{6,2},{7,3},{8,12},{9,13},{10,... | collective-permute-start | bytes 368648 | tf_op jit(solution)/shard_map/ppermute | solution.py:846
  39.4 1.8 %collective-permute-start.42 = (f32[80,384]{1,0:T(8,128)S(1)}, f32[80,384]{1,0:T(8,128)S(1)}, u32[]{:S(2)}, u32[]{:S(2)}) collective-permute-start(f32[80,384]{1,0:T(8,128)S(1)} %collective-permute-done.39.refs_2_), channel_id=1, source_target_pairs={{0,4},{1,5},{2,6},{3,7},{4,0},{5,1},{6,2},{7,3},{8,12},{9,13},{10,... | collective-permute-start | bytes 368648 | tf_op jit(solution)/shard_map/ppermute | solution.py:846
  (5 other events, 4.8 us)

commit v9 on v8

--- a/solution.py
+++ b/solution.py
@@ -578,7 +578,7 @@
                 target[2 * field + level] = result
             return carry
 
-        lax.fori_loop(0, STATES // 2, per_field, 0)
+        lax.fori_loop(0, STATES // 2, per_field, 0, unroll=True)
 
         def push(force, rows, lanes, part):
             def per_plane(p, carry):
@@ -586,7 +586,7 @@
                 target[p, rows, lanes] = target[p, rows, lanes] + amount
                 return carry
 
-            lax.fori_loop(0, STATES, per_plane, 0, unroll=2)
+            lax.fori_loop(0, STATES, per_plane, 0, unroll=True)
 
         for where, section_lanes in ((on_left, slice(0, LANE)), (on_right, slice(2 * LANE, COLS))):
 

time: 42.3 us -> 41.5 us (0.981)
  starting transfers between devices: 23.5 us -> 20.4 us
  waiting for transfers between devices: 12.7 us -> 15.4 us
    ppermute x7, waiting for transfers between devices: 5.26 us -> 7.54 us  [across(): return lax.ppermute(value, BOTH, pairs)]
    ppermute x3, starting transfers between devices: 7.5 us -> 5.82 us  [gather_from(): return lax.ppermute(means, BOTH, pairs)]
    ppermute x7, starting transfers between devices: 5.16 us -> 3.67 us  [across(): return lax.ppermute(value, BOTH, pairs)]
    ppermute x1, starting transfers between devices: 0.34 us -> 1.49 us  [send_rims(): from_cross = lax.ppermute(to_cross, BOTH, cross_map)]
    ppermute x7, starting transfers between devices: 9.62 us -> 8.74 us  [send_rims(): lax.ppermute(value, BOTH, pairs)]
    ppermute x3, waiting for transfers between devices: 3.89 us -> 4.36 us  [gather_from(): return lax.ppermute(means, BOTH, pairs)]
where the time goes in v9:
time: 41.5 us; the launch traced here: 41.4 us
  starting transfers between devices  20.4 us (49%)
  waiting for transfers between devices  15.4 us (37%)
  Pallas kernels  4.03 us (10%)
  between operations  0.76 us (2%)
  local copies, waits for them, and re-layouts  0.65 us (2%)
    ppermute x7, starting transfers between devices, send_rims(): lax.ppermute(value, BOTH, pairs)  8.74 us
    ppermute x7, waiting for transfers between devices, across(): return lax.ppermute(value, BOTH, pairs)  7.54 us
    ppermute x3, starting transfers between devices, gather_from(): return lax.ppermute(means, BOTH, pairs)  5.82 us
    ppermute x3, waiting for transfers between devices, gather_from(): return lax.ppermute(means, BOTH, pairs)  4.36 us
    ppermute x7, starting transfers between devices, across(): return lax.ppermute(value, BOTH, pairs)  3.67 us
    ppermute x7, waiting for transfers between devices, send_rims(): lax.ppermute(value, BOTH, pairs)  2.46 us
    ppermute x1, starting transfers between devices, send_rims(): from_cross = lax.ppermute(to_cross, BOTH, cross_map)  1.49 us
    pallas_call x1, Pallas kernels, on_device(): pl.pallas_call(pack_kernel, out_shape=[shaped(SLOTS, 2 * LANE)] * 3 + [sh...  1.44 us
  transfers between devices with their start and end apart: 19, of which 9 were waited for; matrix products, arithmetic and copies ran while one was open for 0% of the time, Pallas kernels for 0%

profile of v9, /device:TPU:0, one launch (start us, length us, event | category | flops | bytes accessed | tf_op | source)
XLA Modules:
  0.0 41.4 jit_solution(5752491229681441534)
XLA Ops:
  0.7 1.4 %pack.1 = (f32[56,256]{1,0:T(8,128)S(1)}, f32[56,256]{1,0:T(8,128)S(1)}, f32[56,256]{1,0:T(8,128)S(1)}, f32[56,384]{1,0:T(8,128)S(1)}, f32[56,384]{1,0:T(8,128)S(1)}) custom-call(s32[1]{0:T(128)S(6)} %copy.26.offset_ref, f32[10,24,384]{2,1,0:T(8,128)} %bitcast.5, f32[4,24,384]{2,1,0:T(8,128)} %bitcast.7), custom_call_target="tpu_custom_call" | custom-call | tf_op jit(solution)/shard_map/pack/pallas_call | solution.py:778
  2.1 14.6 %conditional.1 = ((f32[32,128]{1,0:T(8,128)S(1)}, f32[32,128]{1,0:T(8,128)S(1)}, f32[72,256]{1,0:T(8,128)S(1)}, f32[136,384]{1,0:T(8,128)S(1)}, f32[56,384]{1,0:T(8,128)S(1)})) conditional(s32[]{:T(128)} %clamp.3, (f32[56,384]{1,0:T(8,128)S(1)}, f32[56,256]{1,0:T(8,128)S(1)}, f32[56,256]{1,0:T(8,128)S(1)}, ...), branch_computations={%region_0.1_spmd, %region_1.2_spmd, %region_2.3_spmd, %region_3.4_... | conditional | bytes 4817584 | solution.py:811
  2.7 5.7 %collective-permute-start.29 = (f32[56,256]{1,0:T(8,128)S(1)}, f32[56,256]{1,0:T(8,128)S(1)}, u32[]{:S(2)}, u32[]{:S(2)}) collective-permute-start(f32[56,256]{1,0:T(8,128)S(1)} %get-tuple-element.62), channel_id=1, source_target_pairs={{1,2},{5,6},{9,10},{12,3},{13,14},{14,15},{16,7},{17,18},{18,19},{... | collective-permute-start | bytes 172040 | tf_op jit(solution)/shard_map/cond/branch_3_fun/ppermute | solution.py:794
  8.4 1.5 %collective-permute-start.26 = (f32[56,384]{1,0:T(8,128)S(1)}, f32[56,384]{1,0:T(8,128)S(1)}, u32[]{:S(2)}, u32[]{:S(2)}) collective-permute-start(f32[56,384]{1,0:T(8,128)S(1)} %get-tuple-element.61), channel_id=1, source_target_pairs={{0,28},{1,29},{2,30},{3,31},{4,8},{5,9},{6,10},{7,11},{8,4},{9,5},... | collective-permute-start | bytes 258056 | tf_op jit(solution)/shard_map/cond/branch_3_fun/ppermute | solution.py:791
  10.2 1.1 %collective-permute-done.29.refs_2_ = f32[56,256]{1,0:T(8,128)S(1)} collective-permute-done((f32[56,256]{1,0:T(8,128)S(1)}, f32[56,256]{1,0:T(8,128)S(1)}, u32[]{:S(2)}, u32[]{:S(2)}) %collective-permute-start.29) | collective-permute-done | bytes 57376 | tf_op jit(solution)/shard_map/cond/branch_3_fun/ppermute | solution.py:794
  11.7 1.7 %collective-permute-start.31 = (f32[56,256]{1,0:T(8,128)S(1)}, f32[56,256]{1,0:T(8,128)S(1)}, u32[]{:S(2)}, u32[]{:S(2)}) collective-permute-start(f32[56,256]{1,0:T(8,128)S(1)} %get-tuple-element.64), channel_id=1, source_target_pairs={{6,9},{10,5},{14,13},{16,21},{18,17},{20,25},{4,0},{5,1},{1,2},{7,... | collective-permute-start | bytes 172040 | tf_op jit(solution)/shard_map/cond/branch_3_fun/ppermute | solution.py:794
  13.5 0.6 %collective-permute-done.27.refs_0_ = f32[56,256]{1,0:T(8,128)S(1)} collective-permute-done((f32[56,256]{1,0:T(8,128)S(1)}, f32[56,256]{1,0:T(8,128)S(1)}, u32[]{:S(2)}, u32[]{:S(2)}) %collective-permute-start.27) | collective-permute-done | bytes 57376 | tf_op jit(solution)/shard_map/cond/branch_3_fun/ppermute | solution.py:794
  14.1 0.8 %collective-permute-done.32.refs_5_ = f32[56,256]{1,0:T(8,128)S(1)} collective-permute-done((f32[56,256]{1,0:T(8,128)S(1)}, f32[56,256]{1,0:T(8,128)S(1)}, u32[]{:S(2)}, u32[]{:S(2)}) %collective-permute-start.32) | collective-permute-done | bytes 57376 | tf_op jit(solution)/shard_map/cond/branch_3_fun/ppermute | solution.py:794
  14.9 0.5 %copy-done.23 = f32[56,256]{1,0:T(8,128)} copy-done((f32[56,256]{1,0:T(8,128)}, f32[56,256]{1,0:T(8,128)S(1)}, u32[]{:S(2)}) %copy-start.23) | copy-done | bytes 57368 | tf_op jit(solution)/shard_map/cond
  15.5 1.2 %relay.7 = (f32[32,128]{1,0:T(8,128)S(1)}, f32[32,128]{1,0:T(8,128)S(1)}, f32[72,256]{1,0:T(8,128)S(1)}, f32[136,384]{1,0:T(8,128)S(1)}, f32[56,384]{1,0:T(8,128)S(1)}) custom-call(f32[56,384]{1,0:T(8,128)S(1)} %get-tuple-element.60.to_pair_ref, f32[56,384]{1,0:T(8,128)} %copy-done.4, f32[56,256]{1,0:T(8,128)} %copy-done.17, f32[56,256]{1,0:T(8,128)} %copy-done.14, ...), custom_call_target="tpu_custom_call" | custom-call | tf_op jit(solution)/shard_map/cond/branch_3_fun/relay/pallas_call | solution.py:797
  16.7 0.6 %collective-permute-start.34 = (f32[136,384]{1,0:T(8,128)S(1)}, f32[136,384]{1,0:T(8,128)S(1)}, u32[]{:S(2)}, u32[]{:S(2)}) collective-permute-start(f32[136,384]{1,0:T(8,128)S(1)} %get-tuple-element.85), channel_id=1, source_target_pairs={{0,4},{1,5},{2,6},{3,7},{4,0},{5,1},{6,2},{7,3},{8,12},{9,13},{10,... | collective-permute-start | bytes 626696 | tf_op jit(solution)/shard_map/ppermute | solution.py:818
  17.4 1.1 %collective-permute-done.34.pair_ref = f32[136,384]{1,0:T(8,128)S(1)} collective-permute-done((f32[136,384]{1,0:T(8,128)S(1)}, f32[136,384]{1,0:T(8,128)S(1)}, u32[]{:S(2)}, u32[]{:S(2)}) %collective-permute-start.34) | collective-permute-done | bytes 208928 | tf_op jit(solution)/shard_map/ppermute | solution.py:818
  18.5 0.6 %nest.1 = (f32[10,24,384]{2,1,0:T(8,128)S(1)}, f32[80,128]{1,0:T(8,128)S(1)}) custom-call(s32[1]{0:T(128)S(6)} %copy.26.offset_ref, f32[10,24,384]{2,1,0:T(8,128)S(1)} %bitcast.6, f32[4,24,384]{2,1,0:T(8,128)S(1)} %bitcast.8, f32[32,128]{1,0:T(8,128)S(1)} %get-tuple-element.82.west_ref, f32[32,128]{1,0:T(8,128)S(1)} %get-tuple-element.83.east_ref, ...), custom_call_target="tpu_custom_call" | custom-call | tf_op jit(solution)/shard_map/nest/pallas_call | solution.py:819
  19.1 1.3 %collective-permute-start.35 = (f32[80,128]{1,0:T(8,128)S(1)}, f32[80,128]{1,0:T(8,128)S(1)}, u32[]{:S(2)}, u32[]{:S(2)}) collective-permute-start(f32[80,128]{1,0:T(8,128)S(1)} %get-tuple-element.87), channel_id=1, source_target_pairs={{1,0},{5,4},{9,8},{13,12},{17,16},{21,20},{25,24},{29,28}} | collective-permute-start | bytes 122888 | tf_op jit(solution)/shard_map/ppermute | solution.py:839
  20.4 1.3 %collective-permute-start.37 = (f32[80,128]{1,0:T(8,128)S(1)}, f32[80,128]{1,0:T(8,128)S(1)}, u32[]{:S(2)}, u32[]{:S(2)}) collective-permute-start(f32[80,128]{1,0:T(8,128)S(1)} %get-tuple-element.87), channel_id=1, source_target_pairs={{3,0},{7,4},{11,8},{15,12},{19,16},{23,20},{27,24},{31,28}} | collective-permute-start | bytes 122888 | tf_op jit(solution)/shard_map/ppermute | solution.py:839
  21.7 3.2 %collective-permute-start.36 = (f32[80,128]{1,0:T(8,128)S(1)}, f32[80,128]{1,0:T(8,128)S(1)}, u32[]{:S(2)}, u32[]{:S(2)}) collective-permute-start(f32[80,128]{1,0:T(8,128)S(1)} %get-tuple-element.87), channel_id=1, source_target_pairs={{2,0},{6,4},{10,8},{14,12},{18,16},{22,20},{26,24},{30,28},{5,1},{... | collective-permute-start | bytes 122888 | tf_op jit(solution)/shard_map/ppermute | solution.py:839
  24.9 4.4 %collective-permute-done.35 = f32[80,128]{1,0:T(8,128)S(1)} collective-permute-done((f32[80,128]{1,0:T(8,128)S(1)}, f32[80,128]{1,0:T(8,128)S(1)}, u32[]{:S(2)}, u32[]{:S(2)}) %collective-permute-start.35) | collective-permute-done | bytes 40992 | tf_op jit(solution)/shard_map/ppermute | solution.py:839
  29.3 2.4 %collective-permute-start.41 = (f32[80,384]{1,0:T(8,128)S(1)}, f32[80,384]{1,0:T(8,128)S(1)}, u32[]{:S(2)}, u32[]{:S(2)}) collective-permute-start(f32[80,384]{1,0:T(8,128)S(1)} %constant_dynamic-update-slice_fusion.refs_0_), channel_id=1, source_target_pairs={{0,16},{1,17},{2,18},{3,19},{4,20},{5,21},{6,22},{7,23},{8,24},{9,... | collective-permute-start | bytes 368648 | tf_op jit(solution)/shard_map/ppermute | solution.py:846
  31.7 1.2 %collective-permute-start.39 = (f32[80,384]{1,0:T(8,128)S(1)}, f32[80,384]{1,0:T(8,128)S(1)}, u32[]{:S(2)}, u32[]{:S(2)}) collective-permute-start(f32[80,384]{1,0:T(8,128)S(1)} %constant_dynamic-update-slice_fusion.refs_0_), channel_id=1, source_target_pairs={{0,28},{1,29},{2,30},{3,31},{4,8},{5,9},{6,10},{7,11},{8,4},{9,5},... | collective-permute-start | bytes 368648 | tf_op jit(solution)/shard_map/ppermute | solution.py:846
  33.0 2.4 %collective-permute-done.41.refs_4_ = f32[80,384]{1,0:T(8,128)S(1)} collective-permute-done((f32[80,384]{1,0:T(8,128)S(1)}, f32[80,384]{1,0:T(8,128)S(1)}, u32[]{:S(2)}, u32[]{:S(2)}) %collective-permute-start.41) | collective-permute-done | bytes 122912 | tf_op jit(solution)/shard_map/ppermute | solution.py:846
  35.4 1.9 %collective-permute-done.40.refs_3_ = f32[80,384]{1,0:T(8,128)S(1)} collective-permute-done((f32[80,384]{1,0:T(8,128)S(1)}, f32[80,384]{1,0:T(8,128)S(1)}, u32[]{:S(2)}, u32[]{:S(2)}) %collective-permute-start.40) | collective-permute-done | bytes 122912 | tf_op jit(solution)/shard_map/ppermute | solution.py:846
  37.3 1.9 %collective-permute-done.39.refs_2_ = f32[80,384]{1,0:T(8,128)S(1)} collective-permute-done((f32[80,384]{1,0:T(8,128)S(1)}, f32[80,384]{1,0:T(8,128)S(1)}, u32[]{:S(2)}, u32[]{:S(2)}) %collective-permute-start.39) | collective-permute-done | bytes 122912 | tf_op jit(solution)/shard_map/ppermute | solution.py:846
  39.2 1.3 %collective-permute-done.42.refs_5_ = f32[80,384]{1,0:T(8,128)S(1)} collective-permute-done((f32[80,384]{1,0:T(8,128)S(1)}, f32[80,384]{1,0:T(8,128)S(1)}, u32[]{:S(2)}, u32[]{:S(2)}) %collective-permute-start.42) | collective-permute-done | bytes 122912 | tf_op jit(solution)/shard_map/ppermute | solution.py:846
  40.5 0.8 %merge.1 = f32[10,24,384]{2,1,0:T(8,128)} custom-call(s32[1]{0:T(128)S(6)} %copy.26.offset_ref, f32[80,384]{1,0:T(8,128)S(1)} %constant_dynamic-update-slice_fusion.refs_0_, f32[80,384]{1,0:T(8,128)S(1)} %collective-permute-done.38.refs_1_, f32[80,384]{1,0:T(8,128)S(1)} %collective-permute-done.39.refs_2_, f32[80,384]{1,0:T(8,128)S(1)} %collective-permute-done.40.refs_3_, ...), custom_call_target="tpu_custom_call" | custom-call | tf_op jit(solution)/shard_map/merge/pallas_call | solution.py:855
  (42 shorter events, 1.4 us)
Async XLA Ops:
  2.1 16.4 %copy-start = (f32[5,2,24,384]{3,2,1,0:T(8,128)S(1)}, f32[5,2,24,384]{3,2,1,0:T(8,128)}, u32[]{:S(2)}) copy-start(f32[5,2,24,384]{3,2,1,0:T(8,128)} %param.7) | copy-start | bytes 1105924
  2.1 16.4 %copy-start.1 = (f32[2,2,24,384]{3,2,1,0:T(8,128)S(1)}, f32[2,2,24,384]{3,2,1,0:T(8,128)}, u32[]{:S(2)}) copy-start(f32[2,2,24,384]{3,2,1,0:T(8,128)} %param.8) | copy-start | bytes 442372
  2.2 7.8 %collective-permute-start.30 = (f32[56,256]{1,0:T(8,128)S(1)}, f32[56,256]{1,0:T(8,128)S(1)}, u32[]{:S(2)}, u32[]{:S(2)}) collective-permute-start(f32[56,256]{1,0:T(8,128)S(1)} %get-tuple-element.63), channel_id=1, source_target_pairs={{12,2},{16,6},{20,26},{24,30},{18,13},{14,17},{6,11},{26,23},{5,0}... | collective-permute-start | bytes 172040 | tf_op jit(solution)/shard_map/cond/branch_3_fun/ppermute | solution.py:794
  2.7 8.6 %collective-permute-start.29 = (f32[56,256]{1,0:T(8,128)S(1)}, f32[56,256]{1,0:T(8,128)S(1)}, u32[]{:S(2)}, u32[]{:S(2)}) collective-permute-start(f32[56,256]{1,0:T(8,128)S(1)} %get-tuple-element.62), channel_id=1, source_target_pairs={{1,2},{5,6},{9,10},{12,3},{13,14},{14,15},{16,7},{17,18},{18,19},{... | collective-permute-start | bytes 172040 | tf_op jit(solution)/shard_map/cond/branch_3_fun/ppermute | solution.py:794
  8.4 3.3 %collective-permute-start.28 = (f32[56,256]{1,0:T(8,128)S(1)}, f32[56,256]{1,0:T(8,128)S(1)}, u32[]{:S(2)}, u32[]{:S(2)}) collective-permute-start(f32[56,256]{1,0:T(8,128)S(1)} %get-tuple-element.62), channel_id=1, source_target_pairs={{6,7},{10,11},{14,19},{16,23},{18,15},{20,27},{4,0},{5,1},{3,2},{7... | collective-permute-start | bytes 172040 | tf_op jit(solution)/shard_map/cond/branch_3_fun/ppermute | solution.py:794
  8.4 6.5 %collective-permute-start.26 = (f32[56,384]{1,0:T(8,128)S(1)}, f32[56,384]{1,0:T(8,128)S(1)}, u32[]{:S(2)}, u32[]{:S(2)}) collective-permute-start(f32[56,384]{1,0:T(8,128)S(1)} %get-tuple-element.61), channel_id=1, source_target_pairs={{0,28},{1,29},{2,30},{3,31},{4,8},{5,9},{6,10},{7,11},{8,4},{9,5},... | collective-permute-start | bytes 258056 | tf_op jit(solution)/shard_map/cond/branch_3_fun/ppermute | solution.py:791
  9.9 4.2 %collective-permute-start.27 = (f32[56,256]{1,0:T(8,128)S(1)}, f32[56,256]{1,0:T(8,128)S(1)}, u32[]{:S(2)}, u32[]{:S(2)}) collective-permute-start(f32[56,256]{1,0:T(8,128)S(1)} %get-tuple-element.62), channel_id=1, source_target_pairs={{2,3},{5,10},{9,6},{10,7},{12,11},{13,18},{16,15},{17,14},{20,19},... | collective-permute-start | bytes 172040 | tf_op jit(solution)/shard_map/cond/branch_3_fun/ppermute | solution.py:794
  9.9 5.0 %copy-start.8 = (f32[56,256]{1,0:T(8,128)}, f32[56,256]{1,0:T(8,128)S(1)}, u32[]{:S(2)}) copy-start(f32[56,256]{1,0:T(8,128)S(1)} %collective-permute-done.30.refs_3_) | copy-start | bytes 172036 | tf_op jit(solution)/shard_map/cond
  9.9 4.2 %collective-permute-start.33 = (f32[56,256]{1,0:T(8,128)S(1)}, f32[56,256]{1,0:T(8,128)S(1)}, u32[]{:S(2)}, u32[]{:S(2)}) collective-permute-start(f32[56,256]{1,0:T(8,128)S(1)} %get-tuple-element.64), channel_id=1, source_target_pairs={{2,1},{6,5},{7,10},{11,6},{12,9},{15,18},{16,13},{19,14},{20,17},{... | collective-permute-start | bytes 172040 | tf_op jit(solution)/shard_map/cond/branch_3_fun/ppermute | solution.py:794
  11.3 3.6 %copy-start.11 = (f32[56,256]{1,0:T(8,128)}, f32[56,256]{1,0:T(8,128)S(1)}, u32[]{:S(2)}) copy-start(f32[56,256]{1,0:T(8,128)S(1)} %collective-permute-done.29.refs_2_) | copy-start | bytes 172036 | tf_op jit(solution)/shard_map/cond
  11.3 3.6 %collective-permute-start.32 = (f32[56,256]{1,0:T(8,128)S(1)}, f32[56,256]{1,0:T(8,128)S(1)}, u32[]{:S(2)}, u32[]{:S(2)}) collective-permute-start(f32[56,256]{1,0:T(8,128)S(1)} %get-tuple-element.64), channel_id=1, source_target_pairs={{3,2},{7,6},{10,9},{11,10},{12,1},{15,14},{16,5},{19,18},{20,13},{... | collective-permute-start | bytes 172040 | tf_op jit(solution)/shard_map/cond/branch_3_fun/ppermute | solution.py:794
  11.7 3.2 %copy-start.14 = (f32[56,256]{1,0:T(8,128)}, f32[56,256]{1,0:T(8,128)S(1)}, u32[]{:S(2)}) copy-start(f32[56,256]{1,0:T(8,128)S(1)} %collective-permute-done.28.refs_1_) | copy-start | bytes 172036 | tf_op jit(solution)/shard_map/cond
  11.7 3.1 %collective-permute-start.31 = (f32[56,256]{1,0:T(8,128)S(1)}, f32[56,256]{1,0:T(8,128)S(1)}, u32[]{:S(2)}, u32[]{:S(2)}) collective-permute-start(f32[56,256]{1,0:T(8,128)S(1)} %get-tuple-element.64), channel_id=1, source_target_pairs={{6,9},{10,5},{14,13},{16,21},{18,17},{20,25},{4,0},{5,1},{1,2},{7,... | collective-permute-start | bytes 172040 | tf_op jit(solution)/shard_map/cond/branch_3_fun/ppermute | solution.py:794
  16.7 1.7 %collective-permute-start.34 = (f32[136,384]{1,0:T(8,128)S(1)}, f32[136,384]{1,0:T(8,128)S(1)}, u32[]{:S(2)}, u32[]{:S(2)}) collective-permute-start(f32[136,384]{1,0:T(8,128)S(1)} %get-tuple-element.85), channel_id=1, source_target_pairs={{0,4},{1,5},{2,6},{3,7},{4,0},{5,1},{6,2},{7,3},{8,12},{9,13},{10,... | collective-permute-start | bytes 626696 | tf_op jit(solution)/shard_map/ppermute | solution.py:818
  19.1 10.2 %collective-permute-start.35 = (f32[80,128]{1,0:T(8,128)S(1)}, f32[80,128]{1,0:T(8,128)S(1)}, u32[]{:S(2)}, u32[]{:S(2)}) collective-permute-start(f32[80,128]{1,0:T(8,128)S(1)} %get-tuple-element.87), channel_id=1, source_target_pairs={{1,0},{5,4},{9,8},{13,12},{17,16},{21,20},{25,24},{29,28}} | collective-permute-start | bytes 122888 | tf_op jit(solution)/shard_map/ppermute | solution.py:839
  20.4 8.9 %collective-permute-start.37 = (f32[80,128]{1,0:T(8,128)S(1)}, f32[80,128]{1,0:T(8,128)S(1)}, u32[]{:S(2)}, u32[]{:S(2)}) collective-permute-start(f32[80,128]{1,0:T(8,128)S(1)} %get-tuple-element.87), channel_id=1, source_target_pairs={{3,0},{7,4},{11,8},{15,12},{19,16},{23,20},{27,24},{31,28}} | collective-permute-start | bytes 122888 | tf_op jit(solution)/shard_map/ppermute | solution.py:839
  21.7 7.6 %collective-permute-start.36 = (f32[80,128]{1,0:T(8,128)S(1)}, f32[80,128]{1,0:T(8,128)S(1)}, u32[]{:S(2)}, u32[]{:S(2)}) collective-permute-start(f32[80,128]{1,0:T(8,128)S(1)} %get-tuple-element.87), channel_id=1, source_target_pairs={{2,0},{6,4},{10,8},{14,12},{18,16},{22,20},{26,24},{30,28},{5,1},{... | collective-permute-start | bytes 122888 | tf_op jit(solution)/shard_map/ppermute | solution.py:839
  29.3 6.1 %collective-permute-start.41 = (f32[80,384]{1,0:T(8,128)S(1)}, f32[80,384]{1,0:T(8,128)S(1)}, u32[]{:S(2)}, u32[]{:S(2)}) collective-permute-start(f32[80,384]{1,0:T(8,128)S(1)} %constant_dynamic-update-slice_fusion.refs_0_), channel_id=1, source_target_pairs={{0,16},{1,17},{2,18},{3,19},{4,20},{5,21},{6,22},{7,23},{8,24},{9,... | collective-permute-start | bytes 368648 | tf_op jit(solution)/shard_map/ppermute | solution.py:846
  31.7 5.6 %collective-permute-start.40 = (f32[80,384]{1,0:T(8,128)S(1)}, f32[80,384]{1,0:T(8,128)S(1)}, u32[]{:S(2)}, u32[]{:S(2)}) collective-permute-start(f32[80,384]{1,0:T(8,128)S(1)} %constant_dynamic-update-slice_fusion.refs_0_), channel_id=1, source_target_pairs={{0,12},{1,13},{2,14},{3,15},{4,24},{5,25},{6,26},{7,27},{8,20},{9,... | collective-permute-start | bytes 368648 | tf_op jit(solution)/shard_map/ppermute | solution.py:846
  31.7 7.5 %collective-permute-start.39 = (f32[80,384]{1,0:T(8,128)S(1)}, f32[80,384]{1,0:T(8,128)S(1)}, u32[]{:S(2)}, u32[]{:S(2)}) collective-permute-start(f32[80,384]{1,0:T(8,128)S(1)} %constant_dynamic-update-slice_fusion.refs_0_), channel_id=1, source_target_pairs={{0,28},{1,29},{2,30},{3,31},{4,8},{5,9},{6,10},{7,11},{8,4},{9,5},... | collective-permute-start | bytes 368648 | tf_op jit(solution)/shard_map/ppermute | solution.py:846
  33.0 6.2 %collective-permute-start.38 = (f32[80,384]{1,0:T(8,128)S(1)}, f32[80,384]{1,0:T(8,128)S(1)}, u32[]{:S(2)}, u32[]{:S(2)}) collective-permute-start(f32[80,384]{1,0:T(8,128)S(1)} %constant_dynamic-update-slice_fusion.refs_0_), channel_id=1, source_target_pairs={{0,4},{1,5},{2,6},{3,7},{4,0},{5,1},{6,2},{7,3},{8,12},{9,13},{10,... | collective-permute-start | bytes 368648 | tf_op jit(solution)/shard_map/ppermute | solution.py:846
  35.4 3.8 %collective-permute-start.44 = (f32[80,384]{1,0:T(8,128)S(1)}, f32[80,384]{1,0:T(8,128)S(1)}, u32[]{:S(2)}, u32[]{:S(2)}) collective-permute-start(f32[80,384]{1,0:T(8,128)S(1)} %collective-permute-done.41.refs_4_), channel_id=1, source_target_pairs={{0,4},{1,5},{2,6},{3,7},{4,0},{5,1},{6,2},{7,3},{8,12},{9,13},{10,... | collective-permute-start | bytes 368648 | tf_op jit(solution)/shard_map/ppermute | solution.py:846
  37.3 1.9 %collective-permute-start.43 = (f32[80,384]{1,0:T(8,128)S(1)}, f32[80,384]{1,0:T(8,128)S(1)}, u32[]{:S(2)}, u32[]{:S(2)}) collective-permute-start(f32[80,384]{1,0:T(8,128)S(1)} %collective-permute-done.40.refs_3_), channel_id=1, source_target_pairs={{0,4},{1,5},{2,6},{3,7},{4,0},{5,1},{6,2},{7,3},{8,12},{9,13},{10,... | collective-permute-start | bytes 368648 | tf_op jit(solution)/shard_map/ppermute | solution.py:846
  39.2 1.3 %collective-permute-start.42 = (f32[80,384]{1,0:T(8,128)S(1)}, f32[80,384]{1,0:T(8,128)S(1)}, u32[]{:S(2)}, u32[]{:S(2)}) collective-permute-start(f32[80,384]{1,0:T(8,128)S(1)} %collective-permute-done.39.refs_2_), channel_id=1, source_target_pairs={{0,4},{1,5},{2,6},{3,7},{4,0},{5,1},{6,2},{7,3},{8,12},{9,13},{10,... | collective-permute-start | bytes 368648 | tf_op jit(solution)/shard_map/ppermute | solution.py:846
  (5 other events, 3.6 us)

commit v10 on v9

--- a/solution.py
+++ b/solution.py
@@ -696,13 +696,13 @@
     return links or 0.8
 
 
-def completed(pairs, valid):
+def completed(pairs, valid, power=3):
     senders = [d for d in range(32) if d not in {a for a, _ in pairs}]
     takers = [d for d in range(32) if d not in {b for _, b in pairs}]
 
     def cost(a, b):
         from_parent = a % 4 == 0 and b % 4 > 0
-        return 1e3 if a == b or from_parent or (a, b) in valid else hops(a, b) ** 3
+        return 1e3 if a == b or from_parent or (a, b) in valid else hops(a, b) ** power
 
     n = len(senders)
     row_price, column_price = [0.0] * (n + 1), [0.0] * (n + 1)
@@ -751,9 +751,10 @@
     if case == 0:
         middle.append([(device(0, 0), device(0, 2)), (device(2, 0), device(6, 1))])
         middle.append([(device(2, 0), device(6, 3))])
+    power = 2 if start == 2 else 3
     groups = []
     for section, inner, order in (
-        (1, ((2, 1), (3, 2)), (2, 0, 1)),
+        (1, ((2, 1), (3, 2)), (1, 2, 0) if start == 2 else (2, 0, 1)),
         (3, ((1, 2), (2, 3)), (1, 2, 0)),
     ):
         edges = [(device(t, a), device(t, b)) for a, b in inner for t in range(8)]
@@ -763,8 +764,8 @@
         if start == 1:
             edges.append((device(0, 0), device(0, section)))
         rounds = in_rounds(edges, 3)
-        groups.append([completed(rounds[i], edges) for i in order])
-    middle = [completed(pairs, []) for pairs in middle]
+        groups.append([completed(rounds[i], edges, power) for i in order])
+    middle = [completed(pairs, [], power) for pairs in middle]
     return groups[0], middle, groups[1]
 
 

time: 41.5 us -> 41.4 us (level)
  waiting for transfers between devices: 15.4 us -> 14.8 us
  starting transfers between devices: 20.4 us -> 20.9 us
    ppermute x7, waiting for transfers between devices: 7.54 us -> 4.89 us  [across(): return lax.ppermute(value, BOTH, pairs)]
    ppermute x7, starting transfers between devices: 3.67 us -> 5.43 us  [across(): return lax.ppermute(value, BOTH, pairs)]
    ppermute x3, starting transfers between devices: 5.82 us -> 4.15 us  [gather_from(): return lax.ppermute(means, BOTH, pairs)]
    ppermute x7, starting transfers between devices: 8.74 us -> 10.4 us  [send_rims(): lax.ppermute(value, BOTH, pairs)]
    ppermute x7, waiting for transfers between devices: 2.46 us -> 3.63 us  [send_rims(): lax.ppermute(value, BOTH, pairs)]
    ppermute x1, starting transfers between devices: 1.49 us -> 0.89 us  [send_rims(): from_cross = lax.ppermute(to_cross, BOTH, cross_map)]
    ppermute x1, starting transfers between devices: 0.65 us -> 0.07 us  [on_device(): from_pair = lax.ppermute(to_pair, BOTH, pair_map)]
    ppermute x3, waiting for transfers between devices: 4.36 us -> 4.81 us  [gather_from(): return lax.ppermute(means, BOTH, pairs)]
  transfers between devices with their start and end apart: 19 -> 19, of which waited for: 9 -> 11; matrix products, arithmetic and copies ran while one was open for 0% -> 0% of each run, Pallas kernels for 0% -> 0%
where the time goes in v10:
time: 41.4 us; the launch traced here: 41.2 us
  starting transfers between devices  20.9 us (50%)
  waiting for transfers between devices  14.8 us (36%)
  Pallas kernels  4.03 us (10%)
  between operations  0.75 us (2%)
  local copies, waits for them, and re-layouts  0.64 us (2%)
    ppermute x7, starting transfers between devices, send_rims(): lax.ppermute(value, BOTH, pairs)  10.4 us
    ppermute x7, starting transfers between devices, across(): return lax.ppermute(value, BOTH, pairs)  5.43 us
    ppermute x7, waiting for transfers between devices, across(): return lax.ppermute(value, BOTH, pairs)  4.89 us
    ppermute x3, waiting for transfers between devices, gather_from(): return lax.ppermute(means, BOTH, pairs)  4.81 us
    ppermute x3, starting transfers between devices, gather_from(): return lax.ppermute(means, BOTH, pairs)  4.15 us
    ppermute x7, waiting for transfers between devices, send_rims(): lax.ppermute(value, BOTH, pairs)  3.63 us
    ppermute x1, waiting for transfers between devices, on_device(): from_pair = lax.ppermute(to_pair, BOTH, pair_map)  1.45 us
    pallas_call x1, Pallas kernels, on_device(): pl.pallas_call(pack_kernel, out_shape=[shaped(SLOTS, 2 * LANE)] * 3 + [sh...  1.44 us
  transfers between devices with their start and end apart: 19, of which 11 were waited for; matrix products, arithmetic and copies ran while one was open for 0% of the time, Pallas kernels for 0%

profile of v10, /device:TPU:0, one launch (start us, length us, event | category | flops | bytes accessed | tf_op | source)
XLA Modules:
  0.0 41.2 jit_solution(16800199106266818785)
XLA Ops:
  0.7 1.4 %pack.1 = (f32[56,256]{1,0:T(8,128)S(1)}, f32[56,256]{1,0:T(8,128)S(1)}, f32[56,256]{1,0:T(8,128)S(1)}, f32[56,384]{1,0:T(8,128)S(1)}, f32[56,384]{1,0:T(8,128)S(1)}) custom-call(s32[1]{0:T(128)S(6)} %copy.26.offset_ref, f32[10,24,384]{2,1,0:T(8,128)} %bitcast.5, f32[4,24,384]{2,1,0:T(8,128)} %bitcast.7), custom_call_target="tpu_custom_call" | custom-call | tf_op jit(solution)/shard_map/pack/pallas_call | solution.py:779
  2.1 16.8 %conditional.1 = ((f32[32,128]{1,0:T(8,128)S(1)}, f32[32,128]{1,0:T(8,128)S(1)}, f32[72,256]{1,0:T(8,128)S(1)}, f32[136,384]{1,0:T(8,128)S(1)}, f32[56,384]{1,0:T(8,128)S(1)})) conditional(s32[]{:T(128)} %clamp.3, (f32[56,384]{1,0:T(8,128)S(1)}, f32[56,256]{1,0:T(8,128)S(1)}, f32[56,256]{1,0:T(8,128)S(1)}, ...), branch_computations={%region_0.1_spmd, %region_1.2_spmd, %region_2.3_spmd, %region_3.4_... | conditional | bytes 4817584 | solution.py:812
  2.7 4.7 %collective-permute-start.13 = (f32[56,256]{1,0:T(8,128)S(1)}, f32[56,256]{1,0:T(8,128)S(1)}, u32[]{:S(2)}, u32[]{:S(2)}) collective-permute-start(f32[56,256]{1,0:T(8,128)S(1)} %get-tuple-element.52), channel_id=1, source_target_pairs={{0,3},{1,2},{5,6},{8,7},{9,10},{12,11},{13,14},{14,15},{16,23},{17... | collective-permute-start | bytes 172040 | tf_op jit(solution)/shard_map/cond/branch_1_fun/ppermute | solution.py:795
  7.3 1.5 %collective-permute-start.12 = (f32[56,256]{1,0:T(8,128)S(1)}, f32[56,256]{1,0:T(8,128)S(1)}, u32[]{:S(2)}, u32[]{:S(2)}) collective-permute-start(f32[56,256]{1,0:T(8,128)S(1)} %get-tuple-element.52), channel_id=1, source_target_pairs={{4,3},{6,7},{8,23},{10,11},{12,27},{14,19},{18,15},{5,0},{21,1},{3... | collective-permute-start | bytes 172040 | tf_op jit(solution)/shard_map/cond/branch_1_fun/ppermute | solution.py:795
  8.8 0.9 %collective-permute-start.10 = (f32[56,384]{1,0:T(8,128)S(1)}, f32[56,384]{1,0:T(8,128)S(1)}, u32[]{:S(2)}, u32[]{:S(2)}) collective-permute-start(f32[56,384]{1,0:T(8,128)S(1)} %get-tuple-element.51), channel_id=1, source_target_pairs={{0,28},{1,29},{2,30},{3,31},{4,8},{5,9},{6,10},{7,11},{8,4},{9,5},... | collective-permute-start | bytes 258056 | tf_op jit(solution)/shard_map/cond/branch_1_fun/ppermute | solution.py:792
  9.9 1.4 %collective-permute-start.17 = (f32[56,256]{1,0:T(8,128)S(1)}, f32[56,256]{1,0:T(8,128)S(1)}, u32[]{:S(2)}, u32[]{:S(2)}) collective-permute-start(f32[56,256]{1,0:T(8,128)S(1)} %get-tuple-element.54), channel_id=1, source_target_pairs={{2,1},{4,9},{6,5},{7,10},{8,13},{11,6},{12,17},{15,18},{16,29},{19... | collective-permute-start | bytes 172040 | tf_op jit(solution)/shard_map/cond/branch_1_fun/ppermute | solution.py:795
  11.4 2.1 %collective-permute-start.16 = (f32[56,256]{1,0:T(8,128)S(1)}, f32[56,256]{1,0:T(8,128)S(1)}, u32[]{:S(2)}, u32[]{:S(2)}) collective-permute-start(f32[56,256]{1,0:T(8,128)S(1)} %get-tuple-element.54), channel_id=1, source_target_pairs={{0,1},{3,2},{7,6},{8,5},{10,9},{11,10},{12,13},{15,14},{16,17},{19... | collective-permute-start | bytes 172040 | tf_op jit(solution)/shard_map/cond/branch_1_fun/ppermute | solution.py:795
  14.3 1.0 %collective-permute-done.16.refs_5_ = f32[56,256]{1,0:T(8,128)S(1)} collective-permute-done((f32[56,256]{1,0:T(8,128)S(1)}, f32[56,256]{1,0:T(8,128)S(1)}, u32[]{:S(2)}, u32[]{:S(2)}) %collective-permute-start.16) | collective-permute-done | bytes 57376 | tf_op jit(solution)/shard_map/cond/branch_1_fun/ppermute | solution.py:795
  15.3 1.8 %collective-permute-done.15.refs_4_ = f32[56,256]{1,0:T(8,128)S(1)} collective-permute-done((f32[56,256]{1,0:T(8,128)S(1)}, f32[56,256]{1,0:T(8,128)S(1)}, u32[]{:S(2)}, u32[]{:S(2)}) %collective-permute-start.15) | collective-permute-done | bytes 57376 | tf_op jit(solution)/shard_map/cond/branch_1_fun/ppermute | solution.py:795
  17.7 1.2 %relay.5 = (f32[32,128]{1,0:T(8,128)S(1)}, f32[32,128]{1,0:T(8,128)S(1)}, f32[72,256]{1,0:T(8,128)S(1)}, f32[136,384]{1,0:T(8,128)S(1)}, f32[56,384]{1,0:T(8,128)S(1)}) custom-call(f32[56,384]{1,0:T(8,128)S(1)} %get-tuple-element.50.to_pair_ref, f32[56,384]{1,0:T(8,128)} %copy-done.2, f32[56,256]{1,0:T(8,128)} %copy-done.15, f32[56,256]{1,0:T(8,128)} %copy-done.12, ...), custom_call_target="tpu_custom_call" | custom-call | tf_op jit(solution)/shard_map/cond/branch_1_fun/relay/pallas_call | solution.py:798
  19.0 1.4 %collective-permute-done.34.pair_ref = f32[136,384]{1,0:T(8,128)S(1)} collective-permute-done((f32[136,384]{1,0:T(8,128)S(1)}, f32[136,384]{1,0:T(8,128)S(1)}, u32[]{:S(2)}, u32[]{:S(2)}) %collective-permute-start.34) | collective-permute-done | bytes 208928 | tf_op jit(solution)/shard_map/ppermute | solution.py:819
  20.5 0.6 %nest.1 = (f32[10,24,384]{2,1,0:T(8,128)S(1)}, f32[80,128]{1,0:T(8,128)S(1)}) custom-call(s32[1]{0:T(128)S(6)} %copy.26.offset_ref, f32[10,24,384]{2,1,0:T(8,128)S(1)} %bitcast.6, f32[4,24,384]{2,1,0:T(8,128)S(1)} %bitcast.8, f32[32,128]{1,0:T(8,128)S(1)} %get-tuple-element.82.west_ref, f32[32,128]{1,0:T(8,128)S(1)} %get-tuple-element.83.east_ref, ...), custom_call_target="tpu_custom_call" | custom-call | tf_op jit(solution)/shard_map/nest/pallas_call | solution.py:820
  21.1 1.3 %collective-permute-start.35 = (f32[80,128]{1,0:T(8,128)S(1)}, f32[80,128]{1,0:T(8,128)S(1)}, u32[]{:S(2)}, u32[]{:S(2)}) collective-permute-start(f32[80,128]{1,0:T(8,128)S(1)} %get-tuple-element.87), channel_id=1, source_target_pairs={{1,0},{5,4},{9,8},{13,12},{17,16},{21,20},{25,24},{29,28}} | collective-permute-start | bytes 122888 | tf_op jit(solution)/shard_map/ppermute | solution.py:840
  22.4 1.3 %collective-permute-start.37 = (f32[80,128]{1,0:T(8,128)S(1)}, f32[80,128]{1,0:T(8,128)S(1)}, u32[]{:S(2)}, u32[]{:S(2)}) collective-permute-start(f32[80,128]{1,0:T(8,128)S(1)} %get-tuple-element.87), channel_id=1, source_target_pairs={{3,0},{7,4},{11,8},{15,12},{19,16},{23,20},{27,24},{31,28}} | collective-permute-start | bytes 122888 | tf_op jit(solution)/shard_map/ppermute | solution.py:840
  23.7 1.6 %collective-permute-start.36 = (f32[80,128]{1,0:T(8,128)S(1)}, f32[80,128]{1,0:T(8,128)S(1)}, u32[]{:S(2)}, u32[]{:S(2)}) collective-permute-start(f32[80,128]{1,0:T(8,128)S(1)} %get-tuple-element.87), channel_id=1, source_target_pairs={{2,0},{6,4},{10,8},{14,12},{18,16},{22,20},{26,24},{30,28},{5,1},{... | collective-permute-start | bytes 122888 | tf_op jit(solution)/shard_map/ppermute | solution.py:840
  25.2 4.2 %collective-permute-done.35 = f32[80,128]{1,0:T(8,128)S(1)} collective-permute-done((f32[80,128]{1,0:T(8,128)S(1)}, f32[80,128]{1,0:T(8,128)S(1)}, u32[]{:S(2)}, u32[]{:S(2)}) %collective-permute-start.35) | collective-permute-done | bytes 40992 | tf_op jit(solution)/shard_map/ppermute | solution.py:840
  30.1 1.5 %collective-permute-start.41 = (f32[80,384]{1,0:T(8,128)S(1)}, f32[80,384]{1,0:T(8,128)S(1)}, u32[]{:S(2)}, u32[]{:S(2)}) collective-permute-start(f32[80,384]{1,0:T(8,128)S(1)} %constant_dynamic-update-slice_fusion.refs_0_), channel_id=1, source_target_pairs={{0,16},{1,17},{2,18},{3,19},{4,20},{5,21},{6,22},{7,23},{8,24},{9,... | collective-permute-start | bytes 368648 | tf_op jit(solution)/shard_map/ppermute | solution.py:847
  31.6 1.7 %collective-permute-start.39 = (f32[80,384]{1,0:T(8,128)S(1)}, f32[80,384]{1,0:T(8,128)S(1)}, u32[]{:S(2)}, u32[]{:S(2)}) collective-permute-start(f32[80,384]{1,0:T(8,128)S(1)} %constant_dynamic-update-slice_fusion.refs_0_), channel_id=1, source_target_pairs={{0,28},{1,29},{2,30},{3,31},{4,8},{5,9},{6,10},{7,11},{8,4},{9,5},... | collective-permute-start | bytes 368648 | tf_op jit(solution)/shard_map/ppermute | solution.py:847
  33.7 1.8 %collective-permute-done.41.refs_4_ = f32[80,384]{1,0:T(8,128)S(1)} collective-permute-done((f32[80,384]{1,0:T(8,128)S(1)}, f32[80,384]{1,0:T(8,128)S(1)}, u32[]{:S(2)}, u32[]{:S(2)}) %collective-permute-start.41) | collective-permute-done | bytes 122912 | tf_op jit(solution)/shard_map/ppermute | solution.py:847
  35.6 1.4 %collective-permute-done.40.refs_3_ = f32[80,384]{1,0:T(8,128)S(1)} collective-permute-done((f32[80,384]{1,0:T(8,128)S(1)}, f32[80,384]{1,0:T(8,128)S(1)}, u32[]{:S(2)}, u32[]{:S(2)}) %collective-permute-start.40) | collective-permute-done | bytes 122912 | tf_op jit(solution)/shard_map/ppermute | solution.py:847
  37.0 1.2 %collective-permute-start.43 = (f32[80,384]{1,0:T(8,128)S(1)}, f32[80,384]{1,0:T(8,128)S(1)}, u32[]{:S(2)}, u32[]{:S(2)}) collective-permute-start(f32[80,384]{1,0:T(8,128)S(1)} %collective-permute-done.40.refs_3_), channel_id=1, source_target_pairs={{0,4},{1,5},{2,6},{3,7},{4,0},{5,1},{6,2},{7,3},{8,12},{9,13},{10,... | collective-permute-start | bytes 368648 | tf_op jit(solution)/shard_map/ppermute | solution.py:847
  38.2 0.6 %collective-permute-done.39.refs_2_ = f32[80,384]{1,0:T(8,128)S(1)} collective-permute-done((f32[80,384]{1,0:T(8,128)S(1)}, f32[80,384]{1,0:T(8,128)S(1)}, u32[]{:S(2)}, u32[]{:S(2)}) %collective-permute-start.39) | collective-permute-done | bytes 122912 | tf_op jit(solution)/shard_map/ppermute | solution.py:847
  39.4 1.0 %collective-permute-done.42.refs_5_ = f32[80,384]{1,0:T(8,128)S(1)} collective-permute-done((f32[80,384]{1,0:T(8,128)S(1)}, f32[80,384]{1,0:T(8,128)S(1)}, u32[]{:S(2)}, u32[]{:S(2)}) %collective-permute-start.42) | collective-permute-done | bytes 122912 | tf_op jit(solution)/shard_map/ppermute | solution.py:847
  40.4 0.8 %merge.1 = f32[10,24,384]{2,1,0:T(8,128)} custom-call(s32[1]{0:T(128)S(6)} %copy.26.offset_ref, f32[80,384]{1,0:T(8,128)S(1)} %constant_dynamic-update-slice_fusion.refs_0_, f32[80,384]{1,0:T(8,128)S(1)} %collective-permute-done.38.refs_1_, f32[80,384]{1,0:T(8,128)S(1)} %collective-permute-done.39.refs_2_, f32[80,384]{1,0:T(8,128)S(1)} %collective-permute-done.40.refs_3_, ...), custom_call_target="tpu_custom_call" | custom-call | tf_op jit(solution)/shard_map/merge/pallas_call | solution.py:856
  (42 shorter events, 3.9 us)
Async XLA Ops:
  2.1 18.3 %copy-start = (f32[5,2,24,384]{3,2,1,0:T(8,128)S(1)}, f32[5,2,24,384]{3,2,1,0:T(8,128)}, u32[]{:S(2)}) copy-start(f32[5,2,24,384]{3,2,1,0:T(8,128)} %param.7) | copy-start | bytes 1105924
  2.1 18.3 %copy-start.1 = (f32[2,2,24,384]{3,2,1,0:T(8,128)S(1)}, f32[2,2,24,384]{3,2,1,0:T(8,128)}, u32[]{:S(2)}) copy-start(f32[2,2,24,384]{3,2,1,0:T(8,128)} %param.8) | copy-start | bytes 442372
  2.2 7.8 %collective-permute-start.14 = (f32[56,256]{1,0:T(8,128)S(1)}, f32[56,256]{1,0:T(8,128)S(1)}, u32[]{:S(2)}, u32[]{:S(2)}) collective-permute-start(f32[56,256]{1,0:T(8,128)S(1)} %get-tuple-element.53), channel_id=1, source_target_pairs={{4,2},{8,6},{12,26},{16,30},{18,13},{14,17},{6,11},{26,23},{5,0},{... | collective-permute-start | bytes 172040 | tf_op jit(solution)/shard_map/cond/branch_1_fun/ppermute | solution.py:795
  2.7 8.7 %collective-permute-start.13 = (f32[56,256]{1,0:T(8,128)S(1)}, f32[56,256]{1,0:T(8,128)S(1)}, u32[]{:S(2)}, u32[]{:S(2)}) collective-permute-start(f32[56,256]{1,0:T(8,128)S(1)} %get-tuple-element.52), channel_id=1, source_target_pairs={{0,3},{1,2},{5,6},{8,7},{9,10},{12,11},{13,14},{14,15},{16,23},{17... | collective-permute-start | bytes 172040 | tf_op jit(solution)/shard_map/cond/branch_1_fun/ppermute | solution.py:795
  7.3 6.1 %collective-permute-start.12 = (f32[56,256]{1,0:T(8,128)S(1)}, f32[56,256]{1,0:T(8,128)S(1)}, u32[]{:S(2)}, u32[]{:S(2)}) collective-permute-start(f32[56,256]{1,0:T(8,128)S(1)} %get-tuple-element.52), channel_id=1, source_target_pairs={{4,3},{6,7},{8,23},{10,11},{12,27},{14,19},{18,15},{5,0},{21,1},{3... | collective-permute-start | bytes 172040 | tf_op jit(solution)/shard_map/cond/branch_1_fun/ppermute | solution.py:795
  8.8 8.2 %collective-permute-start.10 = (f32[56,384]{1,0:T(8,128)S(1)}, f32[56,384]{1,0:T(8,128)S(1)}, u32[]{:S(2)}, u32[]{:S(2)}) collective-permute-start(f32[56,384]{1,0:T(8,128)S(1)} %get-tuple-element.51), channel_id=1, source_target_pairs={{0,28},{1,29},{2,30},{3,31},{4,8},{5,9},{6,10},{7,11},{8,4},{9,5},... | collective-permute-start | bytes 258056 | tf_op jit(solution)/shard_map/cond/branch_1_fun/ppermute | solution.py:792
  9.7 4.2 %collective-permute-start.11 = (f32[56,256]{1,0:T(8,128)S(1)}, f32[56,256]{1,0:T(8,128)S(1)}, u32[]{:S(2)}, u32[]{:S(2)}) collective-permute-start(f32[56,256]{1,0:T(8,128)S(1)} %get-tuple-element.52), channel_id=1, source_target_pairs={{2,3},{4,11},{5,10},{8,15},{9,6},{10,7},{12,19},{13,18},{16,31},{1... | collective-permute-start | bytes 172040 | tf_op jit(solution)/shard_map/cond/branch_1_fun/ppermute | solution.py:795
  9.9 7.2 %copy-start.6 = (f32[56,256]{1,0:T(8,128)}, f32[56,256]{1,0:T(8,128)S(1)}, u32[]{:S(2)}) copy-start(f32[56,256]{1,0:T(8,128)S(1)} %collective-permute-done.14.refs_3_) | copy-start | bytes 172036 | tf_op jit(solution)/shard_map/cond
  9.9 4.4 %collective-permute-start.17 = (f32[56,256]{1,0:T(8,128)S(1)}, f32[56,256]{1,0:T(8,128)S(1)}, u32[]{:S(2)}, u32[]{:S(2)}) collective-permute-start(f32[56,256]{1,0:T(8,128)S(1)} %get-tuple-element.54), channel_id=1, source_target_pairs={{2,1},{4,9},{6,5},{7,10},{8,13},{11,6},{12,17},{15,18},{16,29},{19... | collective-permute-start | bytes 172040 | tf_op jit(solution)/shard_map/cond/branch_1_fun/ppermute | solution.py:795
  11.4 5.7 %copy-start.9 = (f32[56,256]{1,0:T(8,128)}, f32[56,256]{1,0:T(8,128)S(1)}, u32[]{:S(2)}) copy-start(f32[56,256]{1,0:T(8,128)S(1)} %collective-permute-done.13.refs_2_) | copy-start | bytes 172036 | tf_op jit(solution)/shard_map/cond
  11.4 3.9 %collective-permute-start.16 = (f32[56,256]{1,0:T(8,128)S(1)}, f32[56,256]{1,0:T(8,128)S(1)}, u32[]{:S(2)}, u32[]{:S(2)}) collective-permute-start(f32[56,256]{1,0:T(8,128)S(1)} %get-tuple-element.54), channel_id=1, source_target_pairs={{0,1},{3,2},{7,6},{8,5},{10,9},{11,10},{12,13},{15,14},{16,17},{19... | collective-permute-start | bytes 172040 | tf_op jit(solution)/shard_map/cond/branch_1_fun/ppermute | solution.py:795
  13.5 3.6 %copy-start.12 = (f32[56,256]{1,0:T(8,128)}, f32[56,256]{1,0:T(8,128)S(1)}, u32[]{:S(2)}) copy-start(f32[56,256]{1,0:T(8,128)S(1)} %collective-permute-done.12.refs_1_) | copy-start | bytes 172036 | tf_op jit(solution)/shard_map/cond
  13.5 3.6 %collective-permute-start.15 = (f32[56,256]{1,0:T(8,128)S(1)}, f32[56,256]{1,0:T(8,128)S(1)}, u32[]{:S(2)}, u32[]{:S(2)}) collective-permute-start(f32[56,256]{1,0:T(8,128)S(1)} %get-tuple-element.54), channel_id=1, source_target_pairs={{4,1},{6,9},{8,21},{10,5},{12,25},{14,13},{18,17},{20,0},{1,2},{7,... | collective-permute-start | bytes 172040 | tf_op jit(solution)/shard_map/cond/branch_1_fun/ppermute | solution.py:795
  18.9 1.5 %collective-permute-start.34 = (f32[136,384]{1,0:T(8,128)S(1)}, f32[136,384]{1,0:T(8,128)S(1)}, u32[]{:S(2)}, u32[]{:S(2)}) collective-permute-start(f32[136,384]{1,0:T(8,128)S(1)} %get-tuple-element.85), channel_id=1, source_target_pairs={{0,4},{1,5},{2,6},{3,7},{4,0},{5,1},{6,2},{7,3},{8,12},{9,13},{10,... | collective-permute-start | bytes 626696 | tf_op jit(solution)/shard_map/ppermute | solution.py:819
  21.1 8.4 %collective-permute-start.35 = (f32[80,128]{1,0:T(8,128)S(1)}, f32[80,128]{1,0:T(8,128)S(1)}, u32[]{:S(2)}, u32[]{:S(2)}) collective-permute-start(f32[80,128]{1,0:T(8,128)S(1)} %get-tuple-element.87), channel_id=1, source_target_pairs={{1,0},{5,4},{9,8},{13,12},{17,16},{21,20},{25,24},{29,28}} | collective-permute-start | bytes 122888 | tf_op jit(solution)/shard_map/ppermute | solution.py:840
  22.4 7.7 %collective-permute-start.37 = (f32[80,128]{1,0:T(8,128)S(1)}, f32[80,128]{1,0:T(8,128)S(1)}, u32[]{:S(2)}, u32[]{:S(2)}) collective-permute-start(f32[80,128]{1,0:T(8,128)S(1)} %get-tuple-element.87), channel_id=1, source_target_pairs={{3,0},{7,4},{11,8},{15,12},{19,16},{23,20},{27,24},{31,28}} | collective-permute-start | bytes 122888 | tf_op jit(solution)/shard_map/ppermute | solution.py:840
  23.7 5.8 %collective-permute-start.36 = (f32[80,128]{1,0:T(8,128)S(1)}, f32[80,128]{1,0:T(8,128)S(1)}, u32[]{:S(2)}, u32[]{:S(2)}) collective-permute-start(f32[80,128]{1,0:T(8,128)S(1)} %get-tuple-element.87), channel_id=1, source_target_pairs={{2,0},{6,4},{10,8},{14,12},{18,16},{22,20},{26,24},{30,28},{5,1},{... | collective-permute-start | bytes 122888 | tf_op jit(solution)/shard_map/ppermute | solution.py:840
  30.1 5.5 %collective-permute-start.41 = (f32[80,384]{1,0:T(8,128)S(1)}, f32[80,384]{1,0:T(8,128)S(1)}, u32[]{:S(2)}, u32[]{:S(2)}) collective-permute-start(f32[80,384]{1,0:T(8,128)S(1)} %constant_dynamic-update-slice_fusion.refs_0_), channel_id=1, source_target_pairs={{0,16},{1,17},{2,18},{3,19},{4,20},{5,21},{6,22},{7,23},{8,24},{9,... | collective-permute-start | bytes 368648 | tf_op jit(solution)/shard_map/ppermute | solution.py:847
  31.6 5.4 %collective-permute-start.40 = (f32[80,384]{1,0:T(8,128)S(1)}, f32[80,384]{1,0:T(8,128)S(1)}, u32[]{:S(2)}, u32[]{:S(2)}) collective-permute-start(f32[80,384]{1,0:T(8,128)S(1)} %constant_dynamic-update-slice_fusion.refs_0_), channel_id=1, source_target_pairs={{0,12},{1,13},{2,14},{3,15},{4,24},{5,25},{6,26},{7,27},{8,20},{9,... | collective-permute-start | bytes 368648 | tf_op jit(solution)/shard_map/ppermute | solution.py:847
  31.6 7.3 %collective-permute-start.39 = (f32[80,384]{1,0:T(8,128)S(1)}, f32[80,384]{1,0:T(8,128)S(1)}, u32[]{:S(2)}, u32[]{:S(2)}) collective-permute-start(f32[80,384]{1,0:T(8,128)S(1)} %constant_dynamic-update-slice_fusion.refs_0_), channel_id=1, source_target_pairs={{0,28},{1,29},{2,30},{3,31},{4,8},{5,9},{6,10},{7,11},{8,4},{9,5},... | collective-permute-start | bytes 368648 | tf_op jit(solution)/shard_map/ppermute | solution.py:847
  33.3 6.1 %collective-permute-start.38 = (f32[80,384]{1,0:T(8,128)S(1)}, f32[80,384]{1,0:T(8,128)S(1)}, u32[]{:S(2)}, u32[]{:S(2)}) collective-permute-start(f32[80,384]{1,0:T(8,128)S(1)} %constant_dynamic-update-slice_fusion.refs_0_), channel_id=1, source_target_pairs={{0,4},{1,5},{2,6},{3,7},{4,0},{5,1},{6,2},{7,3},{8,12},{9,13},{10,... | collective-permute-start | bytes 368648 | tf_op jit(solution)/shard_map/ppermute | solution.py:847
  35.6 3.9 %collective-permute-start.44 = (f32[80,384]{1,0:T(8,128)S(1)}, f32[80,384]{1,0:T(8,128)S(1)}, u32[]{:S(2)}, u32[]{:S(2)}) collective-permute-start(f32[80,384]{1,0:T(8,128)S(1)} %collective-permute-done.41.refs_4_), channel_id=1, source_target_pairs={{0,4},{1,5},{2,6},{3,7},{4,0},{5,1},{6,2},{7,3},{8,12},{9,13},{10,... | collective-permute-start | bytes 368648 | tf_op jit(solution)/shard_map/ppermute | solution.py:847
  37.0 2.4 %collective-permute-start.43 = (f32[80,384]{1,0:T(8,128)S(1)}, f32[80,384]{1,0:T(8,128)S(1)}, u32[]{:S(2)}, u32[]{:S(2)}) collective-permute-start(f32[80,384]{1,0:T(8,128)S(1)} %collective-permute-done.40.refs_3_), channel_id=1, source_target_pairs={{0,4},{1,5},{2,6},{3,7},{4,0},{5,1},{6,2},{7,3},{8,12},{9,13},{10,... | collective-permute-start | bytes 368648 | tf_op jit(solution)/shard_map/ppermute | solution.py:847
  38.9 1.5 %collective-permute-start.42 = (f32[80,384]{1,0:T(8,128)S(1)}, f32[80,384]{1,0:T(8,128)S(1)}, u32[]{:S(2)}, u32[]{:S(2)}) collective-permute-start(f32[80,384]{1,0:T(8,128)S(1)} %collective-permute-done.39.refs_2_), channel_id=1, source_target_pairs={{0,4},{1,5},{2,6},{3,7},{4,0},{5,1},{6,2},{7,3},{8,12},{9,13},{10,... | collective-permute-start | bytes 368648 | tf_op jit(solution)/shard_map/ppermute | solution.py:847
  (5 other events, 9.1 us)
